TPU v7x, 256 devices: a whole 4x4x8 slice. The times are simulated.
256 devices in a mesh: bucket: 64 (over y, z, core), nbr: 4 (over x).
Axes of the slice: x: 4, y: 4, z: 8, core: 2. Of those that a mesh axis runs over, the one named last changes fastest.
Arguments:
- embeddings: bfloat16 [1024, 64, 1152], P('bucket'), may hold values from -6 to 6
- prior_scores: bfloat16 [1024, 64, 128], P('bucket'), may hold values from -6 to 6
- frame_valid: int32 [1024, 64], P('bucket'), may hold values 0 or 1
- neighbour_ids: int32 [1024, 32], P('bucket', 'nbr'), may hold values from 0 to 1023, as said below
- neighbour_count: int32 [1024], P('bucket'), may hold values from 1 to 32, as said below
- block_home: int32 [1024], replicated, may hold values from 0 to 1023, as said below
Outputs:
- spread_scores: bfloat16 [1024, 64, 128], P(('bucket', 'nbr'))
Inputs may be any that keep to these rules, and one draw needn't show every extreme that they name: block_home is a permutation of 0 to 1023; the block stored at position q lies in bucket q // 16. `neighbour_ids`: over the 16 rows of one bucket and the 8 columns of one index of nbr, at most 2 entries name blocks stored in any one bucket, and one bucket is named exactly 2 times by every such group. No entry names its own row's block; entries may repeat. `neighbour_count`: some block has all 32 entries.
All inputs are finite; a program needn't handle non-finite values. No bound on the sum of `frame_valid` on one device may be relied on, other than what follows from the above.
Results may differ from a plain program's by a relative error of at most 0.011.
Values may be sent and summed in bfloat16 or wider, within the bound.
No kernel may reach another device: no remote copies, remote signals or barrier semaphores. Data moves between devices by JAX's collectives and lax.ppermute only.
A program may use at most 320 MiB of HBM per device.

v0:
```python
import math

import jax
import jax.numpy as jnp
from jax import lax
from jax.sharding import PartitionSpec as P

epsilon = 1e-06
keep_share = 0.9


def normalize(values):
    floats = values.astype(jnp.float32)
    return (floats * lax.rsqrt(jnp.sum(floats * floats, axis=-1, keepdims=True) + epsilon)).astype(
        jnp.bfloat16
    )


def body(embeddings, prior_scores, frame_valid, neighbour_ids, neighbour_count, block_home):
    blocks, frames, feat_width = embeddings.shape
    channels = prior_scores.shape[2]
    per_list = neighbour_ids.shape[1]
    buckets = lax.axis_size("bucket")
    groups = lax.axis_size("nbr")
    nbr_index = lax.axis_index("nbr")
    quarter = blocks // groups
    requests = blocks * per_list
    capacity = max(2, (requests + buckets - 1) // buckets)
    slot_total = buckets * capacity
    sharpness = 2.0 * math.sqrt(feat_width)
    normed = normalize(embeddings)
    valid_float = frame_valid.astype(jnp.float32)
    target = jnp.take(block_home, neighbour_ids.reshape(requests), axis=0)
    column = nbr_index * per_list + jnp.arange(per_list, dtype=jnp.int32)
    in_list = (column[None, :] < neighbour_count[:, None]).astype(jnp.float32)
    owner_bucket = target // blocks
    key_slot = target % blocks
    entry_order = jnp.arange(requests, dtype=jnp.int32)
    same_owner = owner_bucket[:, None] == owner_bucket[None, :]
    rank_in = jnp.sum(
        (same_owner & (entry_order[:, None] > entry_order[None, :])).astype(jnp.int32), axis=1
    )
    slot_of = owner_bucket * capacity + rank_in
    slot_hits = slot_of[None, :] == jnp.arange(slot_total, dtype=jnp.int32)[:, None]
    filled = jnp.any(slot_hits, axis=1)
    entry_of = jnp.sum(jnp.where(slot_hits, entry_order[None, :], 0), axis=1)
    wanted = jnp.where(filled, jnp.take(key_slot, entry_of, axis=0), 0)
    first_block = nbr_index * quarter
    own_units = lax.dynamic_slice_in_dim(normed, first_block, quarter, 0)
    own_valid = lax.dynamic_slice_in_dim(valid_float, first_block, quarter, 0)
    own_prior = lax.dynamic_slice_in_dim(prior_scores, first_block, quarter, 0)
    own_affinity = jnp.einsum(
        "bfd,bgd->bfg", own_units, own_units, preferred_element_type=jnp.float32
    )
    off_diagonal = 1.0 - jnp.eye(frames, dtype=jnp.float32)
    own_weights = (jnp.exp(sharpness * own_affinity) * own_valid[:, None, :] * off_diagonal).astype(
        jnp.bfloat16
    )
    own_mass = jnp.sum(own_weights.astype(jnp.float32), axis=2)

    def list_sum(numerator, list_mass):
        return (
            lax.psum_scatter(numerator, "nbr", scatter_dimension=0, tiled=True),
            lax.psum_scatter(list_mass, "nbr", scatter_dimension=0, tiled=True),
        )

    def finish(list_total, list_mass, own_scores):
        own_total = jnp.einsum(
            "bfg,bgc->bfc", own_weights, own_scores, preferred_element_type=jnp.float32
        )
        denominator = 1.0 + list_mass + own_mass
        mixed = keep_share * (list_total + own_total) / denominator[:, :, None]
        return (mixed + (1.0 - keep_share) * own_prior.astype(jnp.float32)).astype(jnp.bfloat16)

    query_rows = jnp.take(normed, entry_of // per_list, axis=0).reshape(
        buckets, capacity, frames, feat_width
    )
    wanted_marks = wanted.astype(jnp.bfloat16).reshape(buckets, capacity)
    got_queries, got_marks = (
        lax.all_to_all(query_rows, "bucket", split_axis=0, concat_axis=0, tiled=True),
        lax.all_to_all(wanted_marks, "bucket", split_axis=0, concat_axis=0, tiled=True),
    )
    served_slot = got_marks.reshape(slot_total).astype(jnp.int32)
    affinity = jnp.einsum(
        "sfd,sgd->sfg",
        got_queries.reshape(slot_total, frames, feat_width),
        jnp.take(normed, served_slot, axis=0),
        preferred_element_type=jnp.float32,
    )
    served_weights = (
        jnp.exp(sharpness * affinity) * jnp.take(valid_float, served_slot, axis=0)[:, None, :]
    ).astype(jnp.bfloat16)
    served_mass = jnp.sum(served_weights.astype(jnp.float32), axis=2)

    def neighbour(bucket_rows):
        served_total = jnp.einsum(
            "sfg,sgc->sfc",
            served_weights,
            jnp.take(bucket_rows, served_slot, axis=0),
            preferred_element_type=jnp.float32,
        )
        back_total, back_mass = (
            lax.all_to_all(
                served_total.reshape(buckets, capacity, frames, channels),
                "bucket",
                split_axis=0,
                concat_axis=0,
                tiled=True,
            ),
            lax.all_to_all(
                served_mass.reshape(buckets, capacity, frames),
                "bucket",
                split_axis=0,
                concat_axis=0,
                tiled=True,
            ),
        )
        entry_total = jnp.take(
            back_total.reshape(slot_total, frames, channels), slot_of, axis=0
        ).reshape(blocks, per_list, frames, channels)
        entry_mass = jnp.take(back_mass.reshape(slot_total, frames), slot_of, axis=0).reshape(
            blocks, per_list, frames
        )
        return (
            jnp.sum(entry_total * in_list[:, :, None, None], axis=1),
            jnp.sum(entry_mass * in_list[:, :, None], axis=1),
        )

    list_terms = neighbour(prior_scores)
    round_one = finish(*list_sum(*list_terms), own_prior)
    bucket_rows = lax.all_gather(round_one, "nbr", axis=0, tiled=True)
    list_terms = neighbour(bucket_rows)
    return finish(*list_sum(*list_terms), round_one)


def solution(mesh):
    in_specs = (
        P("bucket", None, None),
        P("bucket", None, None),
        P("bucket", None),
        P("bucket", "nbr"),
        P("bucket"),
        P(),
    )
    out_specs = P(("bucket", "nbr"), None, None)
    return jax.shard_map(body, mesh=mesh, in_specs=in_specs, out_specs=out_specs, check_vma=False)
```

profile of v0, /device:TPU:1, one launch (start us, length us, event | category | flops | bytes accessed | tf_op | source)
XLA Modules:
  0.0 789.7 jit_solution(7987947378964988468)
XLA Ops:
  6.5 0.8 copy.33
  7.5 1.0 gather_fusion
  8.5 0.2 convert_reduce_fusion.2
  8.7 0.1 fusion.30
  8.8 0.1 select_reduce_fusion
  9.0 0.1 reduce_sum.83
  9.1 0.2 reduce_or.12
  9.4 1.2 gather_fusion.1
  10.6 0.1 gather.28
  10.9 0.7 copy.40
  11.7 13.2 %all-to-all-start.1 = ((bf16[64,1,2]{2,1,0:T(2,128)(2,1)}), bf16[64,1,2]{2,1,0:T(2,128)(2,1)S(1)}, u32[]{:S(2)}, u32[]{:S(2)}) async-start(bf16[64,1,2]{2,1,0:T(2,128)(2,1)} %copy.40), calls=%async_computation.1 | async-start | bytes 65536 | tf_op jit(solution)/shard_map/all_to_all | solution.py:81
  24.9 2.2 fusion.4
  27.1 2.1 fusion.5
  29.2 9.1 %gather_fusion.3 = bf16[128,64,1152]{2,1,0:T(8,128)(2,1)} fusion(bf16[16,64,1152]{2,1,0:T(8,128)(2,1)S(1)} %fusion.5, s32[1024]{0:T(1024)S(1)} %pad_clamp_fusion.4), kind=kCustom, calls=%fused_computation.clone | custom fusion | bytes 37749248 | tf_op jit(solution)/shard_map/jit(_take)/gather | solution.py:75
  38.3 17.4 %broadcast_select_fusion = bf16[128,64,1152]{2,1,0:T(8,128)(2,1)} fusion(bf16[128,64,1152]{2,1,0:T(8,128)(2,1)} %gather_fusion.3, pred[128]{0:T(512)(128)(4,1)S(1)} %get-tuple-element.10), kind=kLoop, calls=%fused_computation.13 | loop fusion | flops 9437184 | bytes 37748864 | tf_op jit(solution)/shard_map/jit(_take)/select_n | solution.py:75
  55.8 10.6 %all-to-all-start = ((bf16[64,2,64,1152]{3,2,1,0:T(8,128)(2,1)}), bf16[64,2,64,1152]{3,2,1,0:T(8,128)(2,1)}, u32[]{:S(2)}, u32[]{:S(2)}) async-start(bf16[64,2,64,1152]{3,2,1,0:T(8,128)(2,1)} %bitcast.32), calls=%async_computation | async-start | bytes 37748736 | tf_op jit(solution)/shard_map/all_to_all | solution.py:80
  66.5 0.1 reshape.390
  66.6 0.1 convert_reduce_fusion.3
  66.7 0.1 reshape.389
  66.9 9.3 %gather_fusion.4 = bf16[128,64,1152]{2,1,0:T(8,128)(2,1)} fusion(bf16[16,64,1152]{2,1,0:T(8,128)(2,1)S(1)} %fusion.5, s32[1024]{0:T(1024)S(1)} %pad_clamp_fusion.2), kind=kCustom, calls=%fused_computation.4.clone | custom fusion | bytes 37749248 | tf_op jit(solution)/shard_map/jit(_take)/gather | solution.py:87
  76.2 2.1 gather_fusion.5
  78.4 0.6 gather_fusion.2
  79.1 397.8 %all-to-all-done = bf16[64,2,64,1152]{3,2,1,0:T(8,128)(2,1)} async-done(((bf16[64,2,64,1152]{3,2,1,0:T(8,128)(2,1)}), bf16[64,2,64,1152]{3,2,1,0:T(8,128)(2,1)}, u32[]{:S(2)}, u32[]{:S(2)}) %all-to-all-start) | async-done | bytes 18874400 | tf_op jit(solution)/shard_map/all_to_all | solution.py:80
  476.9 15.7 %convert_reduce_fusion = (f32[128,64]{1,0:T(8,128)S(1)}, bf16[128,64,64]{1,2,0:T(8,128)(2,1)}) fusion(f32[128,64]{1,0:T(8,128)S(1)} %broadcast_select_fusion.3, bf16[128,64,1152]{2,1,0:T(8,128)(2,1)} %bitcast.2, bf16[128,64,1152]{2,1,0:T(8,128)(2,1)} %gather_fusion.4, pred[128]{0:T(512)(128)(4,1)S(1)} %compare_and_fusion.1), kind=kOutput, calls=%fused_computation.20 | convolution fusion | flops 1220009984 | bytes 38862976 | tf_op jit(solution)/shard_map/sfd,sgd->sfg/dot_general | solution.py:84
  492.6 5.2 fusion.8
  497.8 6.4 all-to-all-start.2
  504.3 95.7 %all-to-all-done.2 = f32[64,2,64,128]{3,2,1,0:T(8,128)} async-done(((f32[64,2,64,128]{3,2,1,0:T(8,128)}), f32[64,2,64,128]{3,2,1,0:T(8,128)}, u32[]{:S(2)}, u32[]{:S(2)}) %all-to-all-start.2) | async-done | bytes 4194336 | tf_op jit(solution)/shard_map/all_to_all | solution.py:103
  600.0 5.0 gather_fusion.6
  605.0 3.7 multiply_reduce_fusion.1
  608.7 0.7 reshape.503
  609.5 5.7 all-to-all-start.3
  615.3 0.3 convert_reduce_fusion.1
  615.6 0.6 dynamic-slice
  616.9 7.6 all-to-all-done.3
  624.4 0.5 broadcast.390
  625.0 0.7 reduce.6
  625.8 0.6 gather_fusion.7
  626.4 0.1 fusion.29
  626.5 8.6 %all-reduce = f32[16,64]{1,0:T(8,128)S(1)} all-reduce(f32[16,64]{1,0:T(8,128)S(1)} %fusion.29), channel_id=3, replica_groups=mesh['bucket'=64,'nbr'=4] {'nbr'}, use_global_device_ids=true, to_apply=%region_8.13.clone | all-reduce | flops 1024 | bytes 8192
  635.2 1.1 fusion.24
  636.4 10.0 %all_gather.3 = bf16[16,64,128]{2,1,0:T(8,128)(2,1)S(1)} all-gather(bf16[4,64,128]{2,1,0:T(8,128)(2,1)S(1)} %fusion.24), channel_id=1, replica_groups=mesh['bucket'=64,'nbr'=4] {'nbr'}, dimensions={0}, use_global_device_ids=true | all-gather | bytes 327680 | tf_op jit(solution)/shard_map/all_gather | solution.py:131
  646.3 1.0 gather_fusion.8
  647.3 2.6 fusion.6
  649.9 105.2 %all_to_all.27 = f32[64,2,64,128]{3,2,1,0:T(8,128)} all-to-all(f32[64,2,64,128]{3,2,1,0:T(8,128)S(1)} %bitcast.34), channel_id=1, replica_groups=mesh['bucket'=64,'nbr'=4] {'bucket'}, dimensions={0} | all-to-all | bytes 8388608 | tf_op jit(solution)/shard_map/all_to_all | solution.py:103
  755.1 4.9 gather_fusion.9
  760.1 3.7 multiply_reduce_fusion
  763.8 17.3 %reduce-scatter.5.cloned.1.call-done = f32[4,64,128]{2,1,0:T(8,128)} async-done(((f32[16,64,128]{2,1,0:T(8,128)}), f32[4,64,128]{2,1,0:T(8,128)}) %reduce-scatter.5.cloned.1.call-update) | async-done | bytes 131088 | tf_op jit(solution)/shard_map/reduce_scatter | solution.py:63
  781.1 1.8 fusion.23
  (50 shorter events, 1.1 us)
Async XLA Ops:
  6.5 1.0 copy-start
  11.7 44.1 %all-to-all-start.1 = ((bf16[64,1,2]{2,1,0:T(2,128)(2,1)}), bf16[64,1,2]{2,1,0:T(2,128)(2,1)S(1)}, u32[]{:S(2)}, u32[]{:S(2)}) async-start(bf16[64,1,2]{2,1,0:T(2,128)(2,1)} %copy.40), calls=%async_computation.1 | async-start | bytes 65536 | tf_op jit(solution)/shard_map/all_to_all | solution.py:81
  55.8 10.7 %copy-start.3 = (s32[16,64]{1,0:T(8,128)S(1)}, s32[16,64]{1,0:T(8,128)}, u32[]{:S(2)}) copy-start(s32[16,64]{1,0:T(8,128)} %param.16) | copy-start | bytes 12292
  55.8 421.2 %all-to-all-start = ((bf16[64,2,64,1152]{3,2,1,0:T(8,128)(2,1)}), bf16[64,2,64,1152]{3,2,1,0:T(8,128)(2,1)}, u32[]{:S(2)}, u32[]{:S(2)}) async-start(bf16[64,2,64,1152]{3,2,1,0:T(8,128)(2,1)} %bitcast.32), calls=%async_computation | async-start | bytes 37748736 | tf_op jit(solution)/shard_map/all_to_all | solution.py:80
  66.9 9.3 %copy-start.2 = (bf16[16,64,128]{2,1,0:T(8,128)(2,1)S(1)}, bf16[16,64,128]{2,1,0:T(8,128)(2,1)}, u32[]{:S(2)}) copy-start(bf16[16,64,128]{2,1,0:T(8,128)(2,1)} %param.15) | copy-start | bytes 786436
  497.8 6.5 copy-start.4
  497.8 102.3 %all-to-all-start.2 = ((f32[64,2,64,128]{3,2,1,0:T(8,128)}), f32[64,2,64,128]{3,2,1,0:T(8,128)}, u32[]{:S(2)}, u32[]{:S(2)}) async-start(f32[64,2,64,128]{3,2,1,0:T(8,128)} %bitcast.33), calls=%async_computation.2 | async-start | bytes 8388608 | tf_op jit(solution)/shard_map/all_to_all | solution.py:103
  504.2 131.0 %reduce-scatter.3.cloned.1.call-start = ((), (), s32[]{:S(2)}) async-start(), calls=%async_computation.7 | async-start | bytes 655360 | tf_op jit(solution)/shard_map/reduce_scatter | solution.py:63
  605.0 10.6 %copy-start.5 = (u32[256]{0:T(256)S(1)}, u32[256]{0:T(256)}, u32[]{:S(2)}) copy-start(u32[256]{0:T(256)} %constant.153) | copy-start | bytes 3076
  609.5 15.0 %all-to-all-start.3 = ((f32[64,1,128]{2,1,0:T(1,128)}), f32[64,1,128]{2,1,0:T(1,128)S(1)}, u32[]{:S(2)}, u32[]{:S(2)}) async-start(f32[64,1,128]{2,1,0:T(1,128)} %reshape.503), calls=%async_computation.4 | async-start | bytes 65536 | tf_op jit(solution)/shard_map/all_to_all | solution.py:110
  615.2 165.9 %reduce-scatter.5.cloned.1.call-start = ((), (), s32[]{:S(2)}) async-start(), calls=%async_computation.8 | async-start | bytes 655360 | tf_op jit(solution)/shard_map/reduce_scatter | solution.py:63
  755.1 27.7 %copy-start.1 = (s32[1024]{0:T(1024)S(1)}, s32[1024]{0:T(1024)}, u32[]{:S(2)}) copy-start(s32[1024]{0:T(1024)} %param.19) | copy-start | bytes 12292
Sparse Core Ops, SparseCore 0:
  608.8 18.7 reduce-scatter.2
  763.9 17.1 reduce-scatter.4
where the time goes:
time: 791 us; the launch traced here: 790 us
  waiting for transfers between devices  518 us (65%)
  blocking collectives  124 us (16%)
  local copies, waits for them, and re-layouts  39.5 us (5%)
  starting transfers between devices  36 us (5%)
  other arithmetic  30.8 us (4%)
  matrix products  26.7 us (3%)
  between operations  14.4 us (2%)
    all_to_all x1, waiting for transfers between devices, body(): lax.all_to_all(query_rows, 'bucket', split_axis=0, concat_axis=0, tiled=T...  398 us
    all_to_all x1, blocking collectives, neighbour(): lax.all_to_all(served_total.reshape(buckets, capacity, frames, channels),...  105 us
    all_to_all x1, waiting for transfers between devices, neighbour(): lax.all_to_all(served_total.reshape(buckets, capacity, frames, channels),...  95.7 us
    select_n x1, other arithmetic, body(): jnp.take(normed, entry_of // per_list, axis=0)  17.4 us
    reduce_scatter x2, waiting for transfers between devices, list_sum(): lax.psum_scatter(numerator, 'nbr', scatter_dimension=0, tiled=True)  17.3 us
  transfers between devices with their start and end apart: 6, of which 4 were waited for; matrix products, arithmetic and copies ran while one was open for 6% of the time, Pallas kernels for 0%

commit v1 on v0

v1 whole, which is shorter than its diff:
```python
import math

import jax
import jax.numpy as jnp
from jax import lax
from jax.experimental import pallas as pl
from jax.experimental.pallas import tpu as pltpu
from jax.sharding import Mesh
from jax.sharding import PartitionSpec as P

epsilon = 1e-06
keep_share = 0.9

NY, NZ, NC, NX = 4, 8, 2, 4
ROWS = 16
FRAMES = 64
FEAT = 1152
CH = 128
PART = ROWS // NX
QBLOCKS = NY * ROWS
KBLOCKS = NZ * NC * PART
PAIRS = 512
UNROLL = 4
WIDE = FEAT + 2 * CH
PIECE = PART * FRAMES
SEND = PIECE + 16
LIST = 640
COUNT_AT = 600
SPARE = QBLOCKS
VMEM = 56 * 1024 * 1024
sharpness = 2.0 * math.sqrt(FEAT)


def shift(value, axis, step):
    size = lax.axis_size(axis)
    return lax.ppermute(value, axis, [(i, (i + step) % size) for i in range(size)])


def list_kernel(codes, out):
    def step(i, count):
        code = codes[i]
        out[count] = code
        return count + jnp.where(code >= 0, 1, 0)

    def eight(i, count):
        for u in range(8):
            count = step(i * 8 + u, count)
        return count

    count = lax.fori_loop(0, QBLOCKS * 32 // 8, eight, 0)
    for u in range(UNROLL):
        out[count + u] = SPARE
    out[COUNT_AT] = count


def own_kernel(piece, own_weights, own_base):
    row = lax.broadcasted_iota(jnp.int32, (FRAMES, FRAMES), 0)
    col = lax.broadcasted_iota(jnp.int32, (FRAMES, FRAMES), 1)
    for b in range(PART):
        block = piece[b * FRAMES:(b + 1) * FRAMES, :]
        units = block[:, :FEAT]
        affinity = lax.dot_general(
            units, units, (((1,), (1,)), ((), ())), preferred_element_type=jnp.float32
        )
        weights = jnp.where(row == col, 0.0, jnp.exp(sharpness * affinity)).astype(jnp.bfloat16)
        own_weights[b] = weights
        own_base[b] = jnp.dot(weights, block[:, FEAT:], preferred_element_type=jnp.float32)


def first_kernel(lst, queries, near_a, near_b, far_a, far_b, send, weights_out, q, k, acc, w, sems, out_sem):
    copies = [
        pltpu.make_async_copy(near_a, k.at[0, pl.ds(0, 5 * PIECE)], sems.at[0]),
        pltpu.make_async_copy(near_b, k.at[0, pl.ds(5 * PIECE, 3 * PIECE)], sems.at[1]),
        pltpu.make_async_copy(far_a, k.at[1, pl.ds(0, 5 * PIECE)], sems.at[2]),
        pltpu.make_async_copy(far_b, k.at[1, pl.ds(5 * PIECE, 3 * PIECE)], sems.at[3]),
        pltpu.make_async_copy(queries, q, sems.at[4]),
    ]
    for copy in copies:
        copy.start()
    acc[...] = jnp.zeros_like(acc)
    for copy in copies:
        copy.wait()
    steps = (lst[COUNT_AT] + UNROLL - 1) // UNROLL

    def step(i, carry):
        for u in range(UNROLL):
            code = lst[i * UNROLL + u]
            slot = code & 127
            row = pl.multiple_of(((code >> 7) & 31) * FRAMES, FRAMES)
            side = (code >> 12) & 1
            units = q[jnp.minimum(slot, QBLOCKS - 1)]
            keys = k[side, pl.ds(row, FRAMES), pl.ds(0, FEAT)]
            affinity = lax.dot_general(
                units, keys, (((1,), (1,)), ((), ())), preferred_element_type=jnp.float32
            )
            weights = jnp.exp(sharpness * affinity).astype(jnp.bfloat16)
            w[u, i] = weights
            acc[slot] += jnp.dot(
                weights, k[side, pl.ds(row, FRAMES), pl.ds(FEAT, 2 * CH)], preferred_element_type=jnp.float32
            )
        for u in range(UNROLL):
            pltpu.make_async_copy(w.at[u, i], weights_out.at[u, i], out_sem).start()
        return carry

    lax.fori_loop(0, steps, step, 0)
    row = lax.broadcasted_iota(jnp.int32, (FRAMES, CH), 0)
    lane = lax.broadcasted_iota(jnp.int32, (FRAMES, CH), 1)
    pick = row == lane % FRAMES
    low = lax.broadcasted_iota(jnp.int32, (1, CH), 1) < FRAMES

    def finish(d, carry):
        rows = []
        for b in range(PART):
            block = acc[d * PART + b]
            send[d, b * FRAMES:(b + 1) * FRAMES, :] = block[:, :CH].astype(jnp.bfloat16)
            mass = jnp.sum(jnp.where(pick, block[:, CH:], 0.0), axis=0, keepdims=True)
            coarse = mass.astype(jnp.bfloat16).astype(jnp.float32)
            rows.append(jnp.where(low, coarse, mass - coarse))
        rows.append(jnp.zeros((16 - PART, CH), jnp.float32))
        send[d, PIECE:SEND, :] = jnp.concatenate(rows, axis=0).astype(jnp.bfloat16)
        return carry

    lax.fori_loop(0, NY * NX, finish, 0)

    def drain(i, carry):
        for u in range(UNROLL):
            pltpu.make_async_copy(w.at[u, i], weights_out.at[u, i], out_sem).wait()
        return carry

    lax.fori_loop(0, steps, drain, 0)


def second_kernel(lst, weights_in, scores, send, acc, w, in_sem):
    steps = (lst[COUNT_AT] + UNROLL - 1) // UNROLL

    def fetch(i, carry):
        for u in range(UNROLL):
            pltpu.make_async_copy(weights_in.at[u, i], w.at[u, i], in_sem).start()
        return carry

    lax.fori_loop(0, steps, fetch, 0)
    acc[...] = jnp.zeros_like(acc)

    def drain(i, carry):
        for u in range(UNROLL):
            pltpu.make_async_copy(weights_in.at[u, i], w.at[u, i], in_sem).wait()
        return carry

    lax.fori_loop(0, steps, drain, 0)

    def step(i, carry):
        for u in range(UNROLL):
            code = lst[i * UNROLL + u]
            acc[code & 127] += jnp.dot(
                w[u, i], scores[(code >> 13) & 63], preferred_element_type=jnp.float32
            )
        return carry

    lax.fori_loop(0, steps, step, 0)
    for b in range(QBLOCKS):
        send[b] = acc[b].astype(jnp.bfloat16)


def mix_kernel(got, base, weights, prior, marks, masked, denominator, own_second):
    row = lax.broadcasted_iota(jnp.int32, (FRAMES, CH), 0)
    lane = lax.broadcasted_iota(jnp.int32, (FRAMES, CH), 1)
    pick = (row == lane % FRAMES).astype(jnp.float32)
    for b in range(PART):
        total = base[b, :, :CH]
        for d in range(NY * NX):
            total = total + got[d, b * FRAMES:(b + 1) * FRAMES, :].astype(jnp.float32)
        mass = jnp.sum(got[:, PIECE:SEND, :].astype(jnp.float32), axis=0)[b:b + 1, :]
        column = jnp.sum(pick * mass, axis=1, keepdims=True)
        full = 1.0 + column + base[b, :, CH:]
        denominator[b] = full
        mixed = keep_share * total / full + (1.0 - keep_share) * prior[b].astype(jnp.float32)
        keep = (mixed.astype(jnp.bfloat16).astype(jnp.float32) * marks[b].astype(jnp.float32)).astype(jnp.bfloat16)
        masked[b] = keep
        own_second[b] = jnp.dot(weights[b], keep, preferred_element_type=jnp.float32)


def last_kernel(got, own_second, denominator, prior, out):
    for b in range(PART):
        total = own_second[b]
        for d in range(NY * NX):
            total = total + got[d, b].astype(jnp.float32)
        mixed = keep_share * total / denominator[b]
        out[b] = (mixed + (1.0 - keep_share) * prior[b].astype(jnp.float32)).astype(jnp.bfloat16)


smem = pl.BlockSpec(memory_space=pltpu.SMEM)
vmem = pl.BlockSpec(memory_space=pltpu.VMEM)
hbm = pl.BlockSpec(memory_space=pl.ANY)
params = pltpu.CompilerParams(vmem_limit_bytes=VMEM)


def body(embeddings, prior_scores, frame_valid, neighbour_ids, neighbour_count, block_home):
    per_list = neighbour_ids.shape[1]
    y, z, c, x = (lax.axis_index(a) for a in ("y", "z", "c", "x"))
    first = x * PART
    mine = lax.dynamic_slice_in_dim(embeddings, first, PART, 0).astype(jnp.float32)
    prior = lax.dynamic_slice_in_dim(prior_scores, first, PART, 0)
    valid = lax.dynamic_slice_in_dim(frame_valid, first, PART, 0)
    units = (mine * lax.rsqrt(jnp.sum(mine * mine, axis=-1, keepdims=True) + epsilon)).astype(jnp.bfloat16)
    marks = jnp.broadcast_to(valid[:, :, None], prior.shape).astype(jnp.bfloat16)
    piece = jnp.concatenate([units, prior * marks, marks], axis=-1).reshape(PIECE, WIDE)

    queries = lax.all_gather(units, ("y", "x"), axis=0, tiled=True)

    target = jnp.take(block_home, neighbour_ids.reshape(-1), axis=0)
    column = x * per_list + jnp.arange(per_list, dtype=jnp.int32)
    in_list = column[None, :] < neighbour_count[:, None]
    target = jnp.where(in_list.reshape(-1), target, -1)
    target = lax.all_gather(target, ("y", "x"), axis=0).reshape(NY, NX, ROWS, per_list)
    source = (
        jnp.arange(NY, dtype=jnp.int32)[:, None, None, None] * ROWS
        + jnp.arange(ROWS, dtype=jnp.int32)[None, None, :, None]
    )
    wanted = (target >= 0) & (target // 256 == y) & ((target % 16) // PART == x)
    place = (target // 16) % 16
    apart = (place // 2 - z) % NZ
    order = jnp.where(
        apart == 0, 0, jnp.where(apart < 4, 2 * apart, jnp.where(apart == 4, 7, 2 * (NZ - apart) - 1))
    )
    inner = target % PART
    near = order * PART + inner
    side = (place % 2) ^ c
    whole = place * PART + inner
    codes = jnp.where(wanted, source | (near << 7) | (side << 12) | (whole << 13), -1).reshape(-1)
    lst = pl.pallas_call(
        list_kernel,
        out_shape=jax.ShapeDtypeStruct((LIST,), jnp.int32),
        in_specs=[smem],
        out_specs=smem,
    )(codes)

    up, down, held = piece, piece, [piece]
    for _ in range(3):
        up, down = shift(up, "z", 1), shift(down, "z", -1)
        held += [up, down]
    half = PIECE // 2
    last_up, last_down = shift(up[:half], "z", 1), shift(down[half:], "z", -1)
    near_a = jnp.concatenate(held[:5], axis=0)
    near_b = jnp.concatenate(held[5:] + [last_up, last_down], axis=0)
    far_a, far_b = shift(near_a, "c", 1), shift(near_b, "c", 1)

    own_weights, own_base = pl.pallas_call(
        own_kernel,
        out_shape=(
            jax.ShapeDtypeStruct((PART, FRAMES, FRAMES), jnp.bfloat16),
            jax.ShapeDtypeStruct((PART, FRAMES, 2 * CH), jnp.float32),
        ),
        in_specs=[vmem],
        out_specs=(vmem, vmem),
    )(piece)

    steps = PAIRS // UNROLL
    send, weights = pl.pallas_call(
        first_kernel,
        out_shape=(
            jax.ShapeDtypeStruct((NY * NX, SEND, CH), jnp.bfloat16),
            jax.ShapeDtypeStruct((UNROLL, steps, FRAMES, FRAMES), jnp.bfloat16),
        ),
        in_specs=[smem, hbm, hbm, hbm, hbm, hbm],
        out_specs=(vmem, hbm),
        scratch_shapes=[
            pltpu.VMEM((QBLOCKS, FRAMES, FEAT), jnp.bfloat16),
            pltpu.VMEM((NC, NZ * PIECE, WIDE), jnp.bfloat16),
            pltpu.VMEM((QBLOCKS + 1, FRAMES, 2 * CH), jnp.float32),
            pltpu.VMEM((UNROLL, steps, FRAMES, FRAMES), jnp.bfloat16),
            pltpu.SemaphoreType.DMA((5,)),
            pltpu.SemaphoreType.DMA,
        ],
        compiler_params=params,
    )(lst, queries, near_a, near_b, far_a, far_b)
    got = lax.all_to_all(send, ("y", "x"), split_axis=0, concat_axis=0, tiled=True)

    masked, denominator, own_second = pl.pallas_call(
        mix_kernel,
        out_shape=(
            jax.ShapeDtypeStruct((PART, FRAMES, CH), jnp.bfloat16),
            jax.ShapeDtypeStruct((PART, FRAMES, CH), jnp.float32),
            jax.ShapeDtypeStruct((PART, FRAMES, CH), jnp.float32),
        ),
        in_specs=[vmem] * 5,
        out_specs=(vmem,) * 3,
    )(got, own_base, own_weights, prior, marks)
    scores = lax.all_gather(masked, ("z", "c"), axis=0, tiled=True)

    send = pl.pallas_call(
        second_kernel,
        out_shape=jax.ShapeDtypeStruct((QBLOCKS, FRAMES, CH), jnp.bfloat16),
        in_specs=[smem, hbm, vmem],
        out_specs=vmem,
        scratch_shapes=[
            pltpu.VMEM((QBLOCKS + 1, FRAMES, CH), jnp.float32),
            pltpu.VMEM((UNROLL, steps, FRAMES, FRAMES), jnp.bfloat16),
            pltpu.SemaphoreType.DMA,
        ],
        compiler_params=params,
    )(lst, weights, scores)
    got = lax.all_to_all(send, ("y", "x"), split_axis=0, concat_axis=0, tiled=True)
    return pl.pallas_call(
        last_kernel,
        out_shape=jax.ShapeDtypeStruct((PART, FRAMES, CH), jnp.bfloat16),
        in_specs=[vmem] * 4,
        out_specs=vmem,
    )(got.reshape(NY * NX, PART, FRAMES, CH), own_second, denominator, prior)


def solution(mesh):
    fine = Mesh(mesh.devices.reshape(NY, NZ, NC, NX), ("y", "z", "c", "x"))
    bucket = ("y", "z", "c")
    in_specs = (P(bucket, None, None), P(bucket, None, None), P(bucket, None), P(bucket, "x"), P(bucket), P())
    out_specs = P(("y", "z", "c", "x"), None, None)
    return jax.shard_map(body, mesh=fine, in_specs=in_specs, out_specs=out_specs, check_vma=False)
```

time: 791 us -> 237 us (0.30)
  waiting for transfers between devices: 518 us -> 91.8 us
  blocking collectives: 124 us -> 39.4 us
  Pallas kernels: 0 us -> 48.8 us
  local copies, waits for them, and re-layouts: 39.5 us -> 7.61 us
  matrix products: 26.7 us -> 0 us
  other arithmetic: 30.8 us -> 7.54 us
  starting transfers between devices: 36 us -> 27.8 us
    all_to_all x4 -> x1, waiting for transfers between devices: 501 us -> 10.6 us  [body(): lax.all_to_all(send, ('y', 'x'), split_axis=0, concat_axis=0, tiled=True)]
    all_to_all x1, blocking collectives: 105 us -> 22.4 us  [body(): lax.all_to_all(send, ('y', 'x'), split_axis=0, concat_axis=0, tiled=True)]
    pallas_call x0 -> x6, Pallas kernels: none -> 48.8 us  [the longest x1 28 us: body(): pl.pallas_call(first_kernel, out_shape=(jax.ShapeDtypeStruct((NY * NX, SE...]
    ppermute x0 -> x10, waiting for transfers between devices: none -> 42.2 us  [shift(): lax.ppermute(value, axis, [(i, (i + step) % size) for i in range(size)])]
    all_gather x0 -> x2, waiting for transfers between devices: none -> 38.9 us  [the longest x1 38.9 us: body(): scores = lax.all_gather(masked, ('z', 'c'), axis=0, tiled=True)]
    gather x12 -> x1, local copies, waits for them, and re-layouts: 35.1 us -> 0.97 us  [body(): target = jnp.take(block_home, neighbour_ids.reshape(-1), axis=0)]
    all_to_all x4 -> x1, starting transfers between devices: 35.9 us -> 3.71 us  [body(): lax.all_to_all(send, ('y', 'x'), split_axis=0, concat_axis=0, tiled=True)]
    dot_general x6 -> x0, matrix products: 26.7 us -> none  [the longest x1 15.7 us: body(): jnp.einsum('sfd,sgd->sfg', got_queries.reshape(slot_total, frames, feat_w...]
  transfers between devices with their start and end apart: 6 -> 13, of which waited for: 4 -> 6; matrix products, arithmetic and copies ran while one was open for 6% -> 5% of each run, Pallas kernels for 0% -> 4%
where the time goes in v1:
time: 237 us
  waiting for transfers between devices  91.8 us (39%)
  Pallas kernels  48.8 us (21%)
  blocking collectives  39.4 us (17%)
  starting transfers between devices  27.8 us (12%)
  between operations  13.7 us (6%)
  local copies, waits for them, and re-layouts  7.61 us (3%)
  other arithmetic  7.54 us (3%)
    ppermute x10, waiting for transfers between devices, shift(): lax.ppermute(value, axis, [(i, (i + step) % size) for i in range(size)])  42.2 us
    all_gather x1, waiting for transfers between devices, body(): scores = lax.all_gather(masked, ('z', 'c'), axis=0, tiled=True)  38.9 us
    pallas_call x1, Pallas kernels, body(): pl.pallas_call(first_kernel, out_shape=(jax.ShapeDtypeStruct((NY * NX, SE...  28 us
    ppermute x10, starting transfers between devices, shift(): lax.ppermute(value, axis, [(i, (i + step) % size) for i in range(size)])  24 us
    all_to_all x1, blocking collectives, body(): lax.all_to_all(send, ('y', 'x'), split_axis=0, concat_axis=0, tiled=True)  22.4 us
    all_gather x1, blocking collectives, body(): lax.all_gather(target, ('y', 'x'), axis=0).reshape(NY, NX, ROWS, per_list)  17 us
    all_to_all x1, waiting for transfers between devices, body(): lax.all_to_all(send, ('y', 'x'), split_axis=0, concat_axis=0, tiled=True)  10.6 us
    pallas_call x1, Pallas kernels, body(): pl.pallas_call(second_kernel, out_shape=jax.ShapeDtypeStruct((QBLOCKS, FR...  6.78 us
  transfers between devices with their start and end apart: 13, of which 6 were waited for; matrix products, arithmetic and copies ran while one was open for 5% of the time, Pallas kernels for 4%

profile of v1, /device:TPU:1, one launch (start us, length us, event | category | flops | bytes accessed | tf_op | source)
XLA Modules:
  0.0 236.6 jit_solution(7492893373372937605)
XLA Ops:
  6.5 1.3 fusion
  7.8 2.1 fusion.1
  10.0 0.7 dynamic-slice_convert_fusion
  10.7 1.5 broadcast_multiply_fusion
  12.1 0.1 broadcast_in_dim.28.marks
  12.3 1.1 pad_maximum_fusion
  13.4 6.5 %collective-permute-start.1 = (bf16[256,1408]{1,0:T(8,128)(2,1)S(1)}, bf16[256,1408]{1,0:T(8,128)(2,1)S(1)}, u32[]{:S(2)}, u32[]{:S(2)}) collective-permute-start(bf16[256,1408]{1,0:T(8,128)(2,1)S(1)} %bitcast.13), channel_id=1, source_target_pairs={{0,56},{8,0},{16,8},{24,16},{32,24},{40,32},{48,40},{56,48},{1,57}... | collective-permute-start | bytes 2162696 | tf_op jit(solution)/shard_map/ppermute | solution.py:36
  19.9 14.8 %collective-permute-done.1 = bf16[256,1408]{1,0:T(8,128)(2,1)S(1)} collective-permute-done((bf16[256,1408]{1,0:T(8,128)(2,1)S(1)}, bf16[256,1408]{1,0:T(8,128)(2,1)S(1)}, u32[]{:S(2)}, u32[]{:S(2)}) %collective-permute-start.1) | collective-permute-done | bytes 720928 | tf_op jit(solution)/shard_map/ppermute | solution.py:36
  34.7 3.5 %collective-permute-start.3 = (bf16[256,1408]{1,0:T(8,128)(2,1)S(1)}, bf16[256,1408]{1,0:T(8,128)(2,1)S(1)}, u32[]{:S(2)}, u32[]{:S(2)}) collective-permute-start(bf16[256,1408]{1,0:T(8,128)(2,1)S(1)} %collective-permute-done.1), channel_id=1, source_target_pairs={{0,56},{8,0},{16,8},{24,16},{32,24},{40,32},{48,40},{56,48},{1,57}... | collective-permute-start | bytes 2162696 | tf_op jit(solution)/shard_map/ppermute | solution.py:36
  38.2 0.9 constant_dynamic-update-slice_fusion.4
  39.2 0.9 constant_dynamic-update-slice_fusion.3
  40.1 0.9 constant_dynamic-update-slice_fusion.2
  41.0 11.2 %collective-permute-done.3 = bf16[256,1408]{1,0:T(8,128)(2,1)S(1)} collective-permute-done((bf16[256,1408]{1,0:T(8,128)(2,1)S(1)}, bf16[256,1408]{1,0:T(8,128)(2,1)S(1)}, u32[]{:S(2)}, u32[]{:S(2)}) %collective-permute-start.3) | collective-permute-done | bytes 720928 | tf_op jit(solution)/shard_map/ppermute | solution.py:36
  52.2 3.4 %collective-permute-start.5 = (bf16[256,1408]{1,0:T(8,128)(2,1)S(1)}, bf16[256,1408]{1,0:T(8,128)(2,1)S(1)}, u32[]{:S(2)}, u32[]{:S(2)}) collective-permute-start(bf16[256,1408]{1,0:T(8,128)(2,1)S(1)} %collective-permute-done.3), channel_id=1, source_target_pairs={{0,56},{8,0},{16,8},{24,16},{32,24},{40,32},{48,40},{56,48},{1,57}... | collective-permute-start | bytes 2162696 | tf_op jit(solution)/shard_map/ppermute | solution.py:36
  55.6 0.9 constant_dynamic-update-slice_fusion.1
  56.6 1.0 constant_dynamic-update-slice_fusion.near_a
  57.5 2.6 %collective-permute-start.8 = (bf16[1280,1408]{1,0:T(8,128)(2,1)}, bf16[1280,1408]{1,0:T(8,128)(2,1)}, u32[]{:S(2)}, u32[]{:S(2)}) collective-permute-start(bf16[1280,1408]{1,0:T(8,128)(2,1)} %constant_dynamic-update-slice_fusion.near_a), channel_id=1, source_target_pairs={{0,4},{4,0},{1,5},{5,1},{2,6},{6,2},{3,7},{7,3},{8,12},{12,8},{9,1... | collective-permute-start | bytes 10813448 | tf_op jit(solution)/shard_map/ppermute | solution.py:36
  60.2 8.5 %collective-permute-done.5 = bf16[256,1408]{1,0:T(8,128)(2,1)S(1)} collective-permute-done((bf16[256,1408]{1,0:T(8,128)(2,1)S(1)}, bf16[256,1408]{1,0:T(8,128)(2,1)S(1)}, u32[]{:S(2)}, u32[]{:S(2)}) %collective-permute-start.5) | collective-permute-done | bytes 720928 | tf_op jit(solution)/shard_map/ppermute | solution.py:36
  68.7 3.6 %collective-permute-start.7 = (bf16[128,1408]{1,0:T(8,128)(2,1)S(1)}, bf16[128,1408]{1,0:T(8,128)(2,1)S(1)}, u32[]{:S(2)}, u32[]{:S(2)}) collective-permute-start(bf16[128,1408]{1,0:T(8,128)(2,1)S(1)} %slice.11), channel_id=1, source_target_pairs={{0,56},{8,0},{16,8},{24,16},{32,24},{40,32},{48,40},{56,48},{1,57}... | collective-permute-start | bytes 1081352 | tf_op jit(solution)/shard_map/ppermute | solution.py:36
  72.4 0.1 collective-permute-start.6
  72.5 0.1 constant_dynamic-update-slice_fusion.8
  72.5 0.1 constant_dynamic-update-slice_fusion.7
  72.6 7.7 %collective-permute-done.6 = bf16[128,1408]{1,0:T(8,128)(2,1)S(1)} collective-permute-done((bf16[128,1408]{1,0:T(8,128)(2,1)S(1)}, bf16[128,1408]{1,0:T(8,128)(2,1)S(1)}, u32[]{:S(2)}, u32[]{:S(2)}) %collective-permute-start.6) | collective-permute-done | bytes 360480 | tf_op jit(solution)/shard_map/ppermute | solution.py:36
  80.4 4.3 %collective-permute-start.9 = (bf16[768,1408]{1,0:T(8,128)(2,1)S(1)}, bf16[768,1408]{1,0:T(8,128)(2,1)}, u32[]{:S(2)}, u32[]{:S(2)}) collective-permute-start(bf16[768,1408]{1,0:T(8,128)(2,1)S(1)} %constant_dynamic-update-slice_fusion.5.near_b), channel_id=1, source_target_pairs={{0,4},{4,0},{1,5},{5,1},{2,6},{6,2},{3,7},{7,3},{8,12},{12,8},{9,1... | collective-permute-start | bytes 6488072 | tf_op jit(solution)/shard_map/ppermute | solution.py:36
  84.7 0.1 copy.11
  84.8 0.1 reshape.162
  84.9 0.1 reshape.161
  85.0 0.1 broadcast_compare_fusion
  85.1 0.1 lt.86
  85.2 0.1 iota_add_fusion
  85.3 0.1 or.19
  85.4 0.1 or.20
  85.5 1.0 gather_fusion
  86.5 17.0 %all-gather = s32[16,1,128]{2,1,0:T(1,128)S(1)} all-gather(s32[1,1,128]{2,1,0:T(1,128)S(1)} %fusion.22), channel_id=1, replica_groups=mesh['y'=4,'z'=8,'c'=2,'x'=4] {'y','x'}, dimensions={0}, use_global_device_ids=true | all-gather | bytes 8704 | tf_op jit(solution)/shard_map/all_gather | solution.py:214
  103.5 0.6 fusion.13.codes
  104.2 6.8 %shard_map.64.lst = s32[640]{0:T(1024)} custom-call(s32[2048]{0:T(1024)} %fusion.13.codes), custom_call_target="tpu_custom_call" | custom-call | tf_op jit(solution)/shard_map/pallas_call | solution.py:230
  110.9 0.0 all-gather.4.cloned.1.call-done.queries
  111.0 28.0 %shard_map.65 = (bf16[16,272,128]{2,1,0:T(8,128)(2,1)}, bf16[4,128,64,64]{3,2,1,0:T(8,128)(2,1)}) custom-call(s32[640]{0:T(1024)} %shard_map.64.lst, bf16[64,64,1152]{2,1,0:T(8,128)(2,1)} %all-gather.4.cloned.1.call-done.queries, bf16[1280,1408]{1,0:T(8,128)(2,1)} %constant_dynamic-update-slice_fusion.near_a, bf16[768,1408]{1,0:T(8,128)(2,1)} %copy-done.3, ...), custom_call_target="tpu_custom_call" | custom-call | tf_op jit(solution)/shard_map/pallas_call | solution.py:258
  139.0 3.7 %all-to-all-start = ((bf16[16,272,128]{2,1,0:T(8,128)(2,1)}), bf16[16,272,128]{2,1,0:T(8,128)(2,1)S(1)}, u32[]{:S(2)}, u32[]{:S(2)}) async-start(bf16[16,272,128]{2,1,0:T(8,128)(2,1)} %get-tuple-element.13), calls=%async_computation | async-start | bytes 2228224 | tf_op jit(solution)/shard_map/all_to_all | solution.py:276
  142.8 0.0 all-gather.6.cloned.1.call-start
  142.8 2.7 %shard_map.66 = (bf16[4,64,64]{2,1,0:T(8,128)(2,1)}, f32[4,64,256]{2,1,0:T(8,128)}) custom-call(bf16[256,1408]{1,0:T(8,128)(2,1)} %bitcast.16), custom_call_target="tpu_custom_call" | custom-call | tf_op jit(solution)/shard_map/pallas_call | solution.py:247
  145.5 10.6 %all-to-all-done.got = bf16[16,272,128]{2,1,0:T(8,128)(2,1)S(1)} async-done(((bf16[16,272,128]{2,1,0:T(8,128)(2,1)}), bf16[16,272,128]{2,1,0:T(8,128)(2,1)S(1)}, u32[]{:S(2)}, u32[]{:S(2)}) %all-to-all-start) | async-done | bytes 1114144 | tf_op jit(solution)/shard_map/all_to_all | solution.py:276
  156.1 1.0 copy-done.2
  157.2 2.4 %shard_map.67 = (bf16[4,64,128]{2,1,0:T(8,128)(2,1)}, f32[4,64,128]{2,1,0:T(8,128)}, f32[4,64,128]{2,1,0:T(8,128)}) custom-call(bf16[16,272,128]{2,1,0:T(8,128)(2,1)} %copy-done.2, f32[4,64,256]{2,1,0:T(8,128)} %get-tuple-element.14.base, bf16[4,64,64]{2,1,0:T(8,128)(2,1)} %get-tuple-element.15.weights, bf16[4,64,128]{2,1,0:T(8,128)(2,1)} %get-tuple-element.20.prior, ...), custom_call_target="tpu_custom_call" | custom-call | tf_op jit(solution)/shard_map/pallas_call | solution.py:278
  159.6 38.9 %all-gather.6.cloned.1.call-done.scores = bf16[64,64,128]{2,1,0:T(8,128)(2,1)} async-done(((bf16[4,64,128]{2,1,0:T(8,128)(2,1)}), bf16[64,64,128]{2,1,0:T(8,128)(2,1)}) %all-gather.6.cloned.1.call-update) | async-done | bytes 1048592 | tf_op jit(solution)/shard_map/all_gather | solution.py:288
  198.5 6.8 %shard_map.68 = bf16[64,64,128]{2,1,0:T(8,128)(2,1)} custom-call(s32[640]{0:T(1024)} %shard_map.64.lst, bf16[4,128,64,64]{3,2,1,0:T(8,128)(2,1)} %get-tuple-element.12.weights_in, bf16[64,64,128]{2,1,0:T(8,128)(2,1)} %all-gather.6.cloned.1.call-done.scores), custom_call_target="tpu_custom_call" | custom-call | tf_op jit(solution)/shard_map/pallas_call | solution.py:290
  205.2 22.4 %all_to_all.10 = bf16[64,64,128]{2,1,0:T(8,128)(2,1)} all-to-all(bf16[64,64,128]{2,1,0:T(8,128)(2,1)} %shard_map.68), channel_id=1, replica_groups=mesh['y'=4,'z'=8,'c'=2,'x'=4] {'y','x'}, dimensions={0} | all-to-all | bytes 2097152 | tf_op jit(solution)/shard_map/all_to_all | solution.py:302
  227.7 2.1 shard_map.69
  (35 shorter events, 0.2 us)
Async XLA Ops:
  6.5 79.0 %copy-start = (s32[1024]{0:T(1024)S(1)}, s32[1024]{0:T(1024)}, u32[]{:S(2)}) copy-start(s32[1024]{0:T(1024)} %param.11) | copy-start | bytes 12292
  6.5 104.4 %all-gather.4.cloned.1.call-start = ((), (), s32[]{:S(2)}) async-start(), calls=%async_computation.2 | async-start | bytes 10027008 | tf_op jit(solution)/shard_map/all_gather | solution.py:208
  12.2 27.8 %copy-start.4 = (bf16[4,64,128]{2,1,0:T(8,128)(2,1)}, bf16[4,64,128]{2,1,0:T(8,128)(2,1)S(1)}, u32[]{:S(2)}) copy-start(bf16[4,64,128]{2,1,0:T(8,128)(2,1)S(1)} %broadcast_in_dim.28.marks) | copy-start | bytes 196612
  13.4 27.6 %copy-start.1 = (bf16[4,64,1408]{2,1,0:T(8,128)(2,1)}, bf16[4,64,1408]{2,1,0:T(8,128)(2,1)S(1)}, u32[]{:S(2)}) copy-start(bf16[4,64,1408]{2,1,0:T(8,128)(2,1)S(1)} %pad_maximum_fusion) | copy-start | bytes 2162692
  13.4 21.3 %collective-permute-start.1 = (bf16[256,1408]{1,0:T(8,128)(2,1)S(1)}, bf16[256,1408]{1,0:T(8,128)(2,1)S(1)}, u32[]{:S(2)}, u32[]{:S(2)}) collective-permute-start(bf16[256,1408]{1,0:T(8,128)(2,1)S(1)} %bitcast.13), channel_id=1, source_target_pairs={{0,56},{8,0},{16,8},{24,16},{32,24},{40,32},{48,40},{56,48},{1,57}... | collective-permute-start | bytes 2162696 | tf_op jit(solution)/shard_map/ppermute | solution.py:36
  19.9 18.3 %collective-permute-start = (bf16[256,1408]{1,0:T(8,128)(2,1)S(1)}, bf16[256,1408]{1,0:T(8,128)(2,1)S(1)}, u32[]{:S(2)}, u32[]{:S(2)}) collective-permute-start(bf16[256,1408]{1,0:T(8,128)(2,1)S(1)} %bitcast.14), channel_id=1, source_target_pairs={{0,8},{8,16},{16,24},{24,32},{32,40},{40,48},{48,56},{56,0},{1,9},... | collective-permute-start | bytes 2162696 | tf_op jit(solution)/shard_map/ppermute | solution.py:36
  34.7 17.5 %collective-permute-start.3 = (bf16[256,1408]{1,0:T(8,128)(2,1)S(1)}, bf16[256,1408]{1,0:T(8,128)(2,1)S(1)}, u32[]{:S(2)}, u32[]{:S(2)}) collective-permute-start(bf16[256,1408]{1,0:T(8,128)(2,1)S(1)} %collective-permute-done.1), channel_id=1, source_target_pairs={{0,56},{8,0},{16,8},{24,16},{32,24},{40,32},{48,40},{56,48},{1,57}... | collective-permute-start | bytes 2162696 | tf_op jit(solution)/shard_map/ppermute | solution.py:36
  38.2 17.4 %collective-permute-start.2 = (bf16[256,1408]{1,0:T(8,128)(2,1)S(1)}, bf16[256,1408]{1,0:T(8,128)(2,1)S(1)}, u32[]{:S(2)}, u32[]{:S(2)}) collective-permute-start(bf16[256,1408]{1,0:T(8,128)(2,1)S(1)} %collective-permute-done), channel_id=1, source_target_pairs={{0,8},{8,16},{16,24},{24,32},{32,40},{40,48},{48,56},{56,0},{1,9},... | collective-permute-start | bytes 2162696 | tf_op jit(solution)/shard_map/ppermute | solution.py:36
  52.2 16.5 %collective-permute-start.5 = (bf16[256,1408]{1,0:T(8,128)(2,1)S(1)}, bf16[256,1408]{1,0:T(8,128)(2,1)S(1)}, u32[]{:S(2)}, u32[]{:S(2)}) collective-permute-start(bf16[256,1408]{1,0:T(8,128)(2,1)S(1)} %collective-permute-done.3), channel_id=1, source_target_pairs={{0,56},{8,0},{16,8},{24,16},{32,24},{40,32},{48,40},{56,48},{1,57}... | collective-permute-start | bytes 2162696 | tf_op jit(solution)/shard_map/ppermute | solution.py:36
  55.6 16.7 %collective-permute-start.4 = (bf16[256,1408]{1,0:T(8,128)(2,1)S(1)}, bf16[256,1408]{1,0:T(8,128)(2,1)S(1)}, u32[]{:S(2)}, u32[]{:S(2)}) collective-permute-start(bf16[256,1408]{1,0:T(8,128)(2,1)S(1)} %collective-permute-done.2), channel_id=1, source_target_pairs={{0,8},{8,16},{16,24},{24,32},{32,40},{40,48},{48,56},{56,0},{1,9},... | collective-permute-start | bytes 2162696 | tf_op jit(solution)/shard_map/ppermute | solution.py:36
  57.5 53.4 %collective-permute-start.8 = (bf16[1280,1408]{1,0:T(8,128)(2,1)}, bf16[1280,1408]{1,0:T(8,128)(2,1)}, u32[]{:S(2)}, u32[]{:S(2)}) collective-permute-start(bf16[1280,1408]{1,0:T(8,128)(2,1)} %constant_dynamic-update-slice_fusion.near_a), channel_id=1, source_target_pairs={{0,4},{4,0},{1,5},{5,1},{2,6},{6,2},{3,7},{7,3},{8,12},{12,8},{9,1... | collective-permute-start | bytes 10813448 | tf_op jit(solution)/shard_map/ppermute | solution.py:36
  68.7 11.7 %collective-permute-start.7 = (bf16[128,1408]{1,0:T(8,128)(2,1)S(1)}, bf16[128,1408]{1,0:T(8,128)(2,1)S(1)}, u32[]{:S(2)}, u32[]{:S(2)}) collective-permute-start(bf16[128,1408]{1,0:T(8,128)(2,1)S(1)} %slice.11), channel_id=1, source_target_pairs={{0,56},{8,0},{16,8},{24,16},{32,24},{40,32},{48,40},{56,48},{1,57}... | collective-permute-start | bytes 1081352 | tf_op jit(solution)/shard_map/ppermute | solution.py:36
  72.3 12.4 %copy-start.5 = (s32[16,8]{0,1:T(8,128)S(1)}, s32[16,8]{0,1:T(8,128)}, u32[]{:S(2)}) copy-start(s32[16,8]{0,1:T(8,128)} %param.9) | copy-start | bytes 1540
  72.4 12.7 %copy-start.6 = (s32[16]{0:T(128)S(1)}, s32[16]{0:T(128)}, u32[]{:S(2)}) copy-start(s32[16]{0:T(128)} %param.10) | copy-start | bytes 196
  72.4 8.0 %collective-permute-start.6 = (bf16[128,1408]{1,0:T(8,128)(2,1)S(1)}, bf16[128,1408]{1,0:T(8,128)(2,1)S(1)}, u32[]{:S(2)}, u32[]{:S(2)}) collective-permute-start(bf16[128,1408]{1,0:T(8,128)(2,1)S(1)} %slice.10), channel_id=1, source_target_pairs={{0,8},{8,16},{16,24},{24,32},{32,40},{40,48},{48,56},{56,0},{1,9},... | collective-permute-start | bytes 1081352 | tf_op jit(solution)/shard_map/ppermute | solution.py:36
  80.4 30.5 %copy-start.3 = (bf16[768,1408]{1,0:T(8,128)(2,1)}, bf16[768,1408]{1,0:T(8,128)(2,1)S(1)}, u32[]{:S(2)}) copy-start(bf16[768,1408]{1,0:T(8,128)(2,1)S(1)} %constant_dynamic-update-slice_fusion.5.near_b) | copy-start | bytes 6488068
  80.4 30.5 %collective-permute-start.9 = (bf16[768,1408]{1,0:T(8,128)(2,1)S(1)}, bf16[768,1408]{1,0:T(8,128)(2,1)}, u32[]{:S(2)}, u32[]{:S(2)}) collective-permute-start(bf16[768,1408]{1,0:T(8,128)(2,1)S(1)} %constant_dynamic-update-slice_fusion.5.near_b), channel_id=1, source_target_pairs={{0,4},{4,0},{1,5},{5,1},{2,6},{6,2},{3,7},{7,3},{8,12},{12,8},{9,1... | collective-permute-start | bytes 6488072 | tf_op jit(solution)/shard_map/ppermute | solution.py:36
  139.0 17.1 %all-to-all-start = ((bf16[16,272,128]{2,1,0:T(8,128)(2,1)}), bf16[16,272,128]{2,1,0:T(8,128)(2,1)S(1)}, u32[]{:S(2)}, u32[]{:S(2)}) async-start(bf16[16,272,128]{2,1,0:T(8,128)(2,1)} %get-tuple-element.13), calls=%async_computation | async-start | bytes 2228224 | tf_op jit(solution)/shard_map/all_to_all | solution.py:276
  142.8 55.7 %all-gather.6.cloned.1.call-start = ((), (), s32[]{:S(2)}) async-start(), calls=%async_computation.3 | async-start | bytes 1114112 | tf_op jit(solution)/shard_map/all_gather | solution.py:288
  156.1 1.0 copy-start.2
Sparse Core Ops, SparseCore 0:
  10.1 84.5 all-gather.3
  159.7 38.7 all-gather.5

commit v2 on v1

v2 whole, which is shorter than its diff:
```python
import math

import jax
import jax.numpy as jnp
from jax import lax
from jax.experimental import pallas as pl
from jax.experimental.pallas import tpu as pltpu
from jax.sharding import Mesh
from jax.sharding import PartitionSpec as P

epsilon = 1e-06
keep_share = 0.9

NY, NZ, NC, NX = 4, 8, 2, 4
ROWS = 16
FRAMES = 64
FEAT = 1152
CH = 128
PART = ROWS // NX
LATE = PART - 1
QBLOCKS = NY * ROWS
EARLY_Q = ROWS + (NY - 1) * NX
LATE_Q = NY * NX * LATE
UNROLL = 4
SLOTS = 544
WIDE = FEAT + CH
PIECE = PART * FRAMES
SEND = PIECE + 16
LIST = 640
EARLY_AT, LATE_AT = 600, 601
SPARE = QBLOCKS
VMEM = 56 * 1024 * 1024
UNREAL = 1024.0
sharpness = 2.0 * math.sqrt(FEAT)


def shift(value, axis, step):
    size = lax.axis_size(axis)
    return lax.ppermute(value, axis, [(i, (i + step) % size) for i in range(size)])


def list_kernel(codes, out, late):
    def eight(i, counts):
        early_count, late_count = counts
        for u in range(8):
            code = codes[i * 8 + u]
            out[early_count] = code
            late[late_count] = code
            is_late = (code >> 25) & 1
            real = jnp.where(code >= 0, 1, 0)
            early_count = early_count + (real & (1 - is_late))
            late_count = late_count + (real & is_late)
        return early_count, late_count

    early_count, late_count = lax.fori_loop(0, QBLOCKS * 32 // 8, eight, (0, 0))
    for u in range(UNROLL):
        out[early_count + u] = SPARE
        late[late_count + u] = SPARE
    early_steps = (early_count + UNROLL - 1) // UNROLL
    late_steps = (late_count + UNROLL - 1) // UNROLL
    start = early_steps * UNROLL

    def copy(i, carry):
        for u in range(UNROLL):
            out[start + i * UNROLL + u] = late[i * UNROLL + u]
        return carry

    lax.fori_loop(0, late_steps, copy, 0)
    out[EARLY_AT] = early_steps
    out[LATE_AT] = early_steps + late_steps


def own_kernel(piece, own_weights, own_base):
    row = lax.broadcasted_iota(jnp.int32, (FRAMES, FRAMES), 0)
    col = lax.broadcasted_iota(jnp.int32, (FRAMES, FRAMES), 1)
    for b in range(PART):
        block = piece[b * FRAMES:(b + 1) * FRAMES, :]
        units = block[:, :FEAT]
        affinity = lax.dot_general(
            units, units, (((1,), (1,)), ((), ())), preferred_element_type=jnp.float32
        )
        weights = jnp.where(row == col, 0.0, jnp.exp(sharpness * affinity)).astype(jnp.bfloat16)
        own_weights[b] = weights
        own_base[b] = jnp.dot(weights, values_of(block[:, FEAT:]), preferred_element_type=jnp.float32)


def values_of(scores):
    floats = scores.astype(jnp.float32)
    real = floats < UNREAL
    return jnp.concatenate(
        [jnp.where(real, floats, 0.0), jnp.where(real, 1.0, 0.0)], axis=1
    ).astype(jnp.bfloat16)


def key_copies(near_a, near_b, far_a, far_b, k, sems):
    return [
        pltpu.make_async_copy(near_a, k.at[0, pl.ds(0, 5 * PIECE)], sems.at[0]),
        pltpu.make_async_copy(near_b, k.at[0, pl.ds(5 * PIECE, 3 * PIECE)], sems.at[1]),
        pltpu.make_async_copy(far_a, k.at[1, pl.ds(0, 5 * PIECE)], sems.at[2]),
        pltpu.make_async_copy(far_b, k.at[1, pl.ds(5 * PIECE, 3 * PIECE)], sems.at[3]),
    ]


def work_pairs(lst, first, last, q, q_blocks, k, acc, w, weights_out, out_sem):
    def step(i, carry):
        for u in range(UNROLL):
            at = i * UNROLL + u
            code = lst[at]
            slot = code & 127
            row = pl.multiple_of(((code >> 7) & 31) * FRAMES, FRAMES)
            side = (code >> 12) & 1
            units = q[jnp.minimum((code >> 19) & 63, q_blocks - 1)]
            keys = k[side, pl.ds(row, FRAMES), pl.ds(0, FEAT)]
            affinity = lax.dot_general(
                units, keys, (((1,), (1,)), ((), ())), preferred_element_type=jnp.float32
            )
            weights = jnp.exp(sharpness * affinity).astype(jnp.bfloat16)
            w[at] = weights
            acc[slot] += jnp.dot(
                weights,
                values_of(k[side, pl.ds(row, FRAMES), pl.ds(FEAT, CH)]),
                preferred_element_type=jnp.float32,
            )
        for u in range(UNROLL):
            at = i * UNROLL + u
            pltpu.make_async_copy(w.at[at], weights_out.at[at], out_sem).start()
        return carry

    lax.fori_loop(first, last, step, 0)


def drain_pairs(first, last, w, weights_out, out_sem):
    def drain(i, carry):
        for u in range(UNROLL):
            at = i * UNROLL + u
            pltpu.make_async_copy(w.at[at], weights_out.at[at], out_sem).wait()
        return carry

    lax.fori_loop(first, last, drain, 0)


def pack_sums(acc, send, before):
    row = lax.broadcasted_iota(jnp.int32, (FRAMES, CH), 0)
    lane = lax.broadcasted_iota(jnp.int32, (FRAMES, CH), 1)
    pick = row == lane % FRAMES
    low = lax.broadcasted_iota(jnp.int32, (1, CH), 1) < FRAMES

    def finish(d, carry):
        rows = []
        for b in range(PART):
            block = acc[d * PART + b]
            sums = block[:, :CH]
            if before is not None:
                sums = sums + before[d, b * FRAMES:(b + 1) * FRAMES, :].astype(jnp.float32)
            send[d, b * FRAMES:(b + 1) * FRAMES, :] = sums.astype(jnp.bfloat16)
            mass = jnp.sum(jnp.where(pick, block[:, CH:], 0.0), axis=0, keepdims=True)
            coarse = mass.astype(jnp.bfloat16).astype(jnp.float32)
            rows.append(jnp.where(low, coarse, mass - coarse))
        rows.append(jnp.zeros((16 - PART, CH), jnp.float32))
        tail = jnp.concatenate(rows, axis=0)
        if before is not None:
            tail = tail + before[d, PIECE:SEND, :].astype(jnp.float32)
        send[d, PIECE:SEND, :] = tail.astype(jnp.bfloat16)
        return carry

    lax.fori_loop(0, NY * NX, finish, 0)


def early_kernel(lst, own_q, behind, ahead, across, near_a, near_b, far_a, far_b,
                 send, weights_out, q, k, acc, w, sems, out_sem):
    copies = key_copies(near_a, near_b, far_a, far_b, k, sems) + [
        pltpu.make_async_copy(own_q, q.at[pl.ds(0, ROWS)], sems.at[4]),
        pltpu.make_async_copy(ahead, q.at[pl.ds(ROWS, NX)], sems.at[5]),
        pltpu.make_async_copy(across, q.at[pl.ds(ROWS + NX, NX)], sems.at[6]),
        pltpu.make_async_copy(behind, q.at[pl.ds(ROWS + 2 * NX, NX)], sems.at[7]),
    ]
    for copy in copies:
        copy.start()
    acc[...] = jnp.zeros_like(acc)
    for copy in copies:
        copy.wait()
    work_pairs(lst, 0, lst[EARLY_AT], q, EARLY_Q, k, acc, w, weights_out, out_sem)
    pack_sums(acc, send, None)
    drain_pairs(0, lst[EARLY_AT], w, weights_out, out_sem)


def late_kernel(lst, queries, before, weights_in, near_a, near_b, far_a, far_b,
                send, weights_out, q, k, acc, w, sems, out_sem):
    copies = key_copies(near_a, near_b, far_a, far_b, k, sems) + [
        pltpu.make_async_copy(queries, q, sems.at[4]),
    ]
    for copy in copies:
        copy.start()
    acc[...] = jnp.zeros_like(acc)
    for copy in copies:
        copy.wait()
    work_pairs(lst, lst[EARLY_AT], lst[LATE_AT], q, LATE_Q, k, acc, w, weights_out, out_sem)
    pack_sums(acc, send, before)
    drain_pairs(lst[EARLY_AT], lst[LATE_AT], w, weights_out, out_sem)


def second_kernel(lst, weights_in, near, far, send, acc, w, in_sem):
    steps = lst[LATE_AT]

    def fetch(i, carry):
        for u in range(UNROLL):
            at = i * UNROLL + u
            pltpu.make_async_copy(weights_in.at[at], w.at[at], in_sem).start()
        return carry

    lax.fori_loop(0, steps, fetch, 0)
    acc[...] = jnp.zeros_like(acc)
    drain_pairs(0, steps, w, weights_in, in_sem)

    def step(i, carry):
        for u in range(UNROLL):
            at = i * UNROLL + u
            code = lst[at]
            block = (code >> 13) & 31
            scores = jnp.where(((code >> 12) & 1) == 0, near[block], far[block])
            acc[code & 127] += jnp.dot(w[at], scores, preferred_element_type=jnp.float32)
        return carry

    lax.fori_loop(0, steps, step, 0)
    for b in range(QBLOCKS):
        send[b] = acc[b].astype(jnp.bfloat16)


def mix_kernel(got, base, weights, prior, marks, masked, denominator, own_second):
    row = lax.broadcasted_iota(jnp.int32, (FRAMES, CH), 0)
    lane = lax.broadcasted_iota(jnp.int32, (FRAMES, CH), 1)
    pick = (row == lane % FRAMES).astype(jnp.float32)
    for b in range(PART):
        total = base[b, :, :CH]
        for d in range(NY * NX):
            total = total + got[d, b * FRAMES:(b + 1) * FRAMES, :].astype(jnp.float32)
        mass = jnp.sum(got[:, PIECE:SEND, :].astype(jnp.float32), axis=0)[b:b + 1, :]
        column = jnp.sum(pick * mass, axis=1, keepdims=True)
        full = 1.0 + column + base[b, :, CH:]
        denominator[b] = full
        mixed = keep_share * total / full + (1.0 - keep_share) * prior[b].astype(jnp.float32)
        keep = (mixed.astype(jnp.bfloat16).astype(jnp.float32) * marks[b].astype(jnp.float32)).astype(jnp.bfloat16)
        masked[b] = keep
        own_second[b] = jnp.dot(weights[b], keep, preferred_element_type=jnp.float32)


def last_kernel(got, own_second, denominator, prior, out):
    for b in range(PART):
        total = own_second[b]
        for d in range(NY * NX):
            total = total + got[d, b].astype(jnp.float32)
        mixed = keep_share * total / denominator[b]
        out[b] = (mixed + (1.0 - keep_share) * prior[b].astype(jnp.float32)).astype(jnp.bfloat16)


smem = pl.BlockSpec(memory_space=pltpu.SMEM)
vmem = pl.BlockSpec(memory_space=pltpu.VMEM)
hbm = pl.BlockSpec(memory_space=pl.ANY)
params = pltpu.CompilerParams(vmem_limit_bytes=VMEM)


def normalize(values):
    floats = values.astype(jnp.float32)
    return (floats * lax.rsqrt(jnp.sum(floats * floats, axis=-1, keepdims=True) + epsilon)).astype(jnp.bfloat16)


def body(embeddings, prior_scores, frame_valid, neighbour_ids, neighbour_count, block_home):
    per_list = neighbour_ids.shape[1]
    y, z, c, x = (lax.axis_index(a) for a in ("y", "z", "c", "x"))
    first = x * PART
    units = normalize(lax.dynamic_slice_in_dim(embeddings, first, PART, 0))
    prior = lax.dynamic_slice_in_dim(prior_scores, first, PART, 0)
    valid = lax.dynamic_slice_in_dim(frame_valid, first, PART, 0)
    marks = jnp.broadcast_to(valid[:, :, None], prior.shape).astype(jnp.bfloat16)
    marked = jnp.where(marks > 0, prior, jnp.bfloat16(2 * UNREAL))
    piece = jnp.concatenate([units, marked], axis=-1).reshape(PIECE, WIDE)

    queries = lax.all_gather(units[:LATE], ("y", "x"), axis=0, tiled=True)

    up, down = shift(piece, "z", 1), shift(piece, "z", -1)
    embeddings, piece = lax.optimization_barrier((embeddings, piece))
    all_units = normalize(embeddings)
    direct = all_units.reshape(NX, PART, FRAMES, FEAT)[:, LATE]
    behind, ahead = shift(direct, "y", 1), shift(direct, "y", -1)
    ids, _ = lax.optimization_barrier((neighbour_ids, piece))
    target = jnp.take(block_home, ids.reshape(-1), axis=0)
    column = x * per_list + jnp.arange(per_list, dtype=jnp.int32)
    in_list = column[None, :] < neighbour_count[:, None]
    target = jnp.where(in_list.reshape(-1), target, -1)
    target = lax.all_gather(target, ("y", "x"), axis=0)

    up, down, behind, ahead, target = lax.optimization_barrier((up, down, behind, ahead, target))
    held = [piece, up, down]
    half = NX // 2
    across_a, across_b = shift(behind[:half], "y", 1), shift(ahead[half:], "y", -1)
    up, down = shift(up, "z", 1), shift(down, "z", -1)
    target = target.reshape(NY, NX, ROWS, per_list)
    source_y = jnp.arange(NY, dtype=jnp.int32)[:, None, None, None]
    source_row = jnp.arange(ROWS, dtype=jnp.int32)[None, None, :, None]
    source = source_y * ROWS + source_row
    wanted = (target >= 0) & (target // 256 == y) & ((target % 16) // PART == x)
    place = (target // 16) % 16
    apart = (place // 2 - z) % NZ
    order = jnp.where(
        apart == 0, 0, jnp.where(apart < 4, 2 * apart, jnp.where(apart == 4, 7, 2 * (NZ - apart) - 1))
    )
    inner = target % PART
    near = order * PART + inner
    side = (place % 2) ^ c
    whole = (place // 2) * PART + inner
    mine = source_y == y
    straight = source_row % PART == LATE
    late = jnp.where(mine | straight, 0, 1)
    from_early = jnp.where(mine, source_row, ROWS + ((source_y - y) % NY - 1) * NX + source_row // PART)
    from_late = (source_y * NX + source_row // PART) * LATE + source_row % PART
    taken = jnp.where(late == 0, from_early, from_late)
    codes = source | (near << 7) | (side << 12) | (whole << 13) | (taken << 19) | (late << 25)
    codes = jnp.where(wanted, codes, -1).reshape(-1)
    lst = pl.pallas_call(
        list_kernel,
        out_shape=jax.ShapeDtypeStruct((LIST,), jnp.int32),
        in_specs=[smem],
        out_specs=smem,
        scratch_shapes=[pltpu.SMEM((LIST,), jnp.int32)],
    )(codes)

    up, down, across_a, across_b, lst = lax.optimization_barrier((up, down, across_a, across_b, lst))
    across = jnp.concatenate([across_a, across_b], axis=0)
    held += [up, down]
    near_a = jnp.concatenate(held, axis=0)
    up, down = shift(up, "z", 1), shift(down, "z", -1)
    far_a = shift(near_a, "c", 1)
    own_weights, own_base = pl.pallas_call(
        own_kernel,
        out_shape=(
            jax.ShapeDtypeStruct((PART, FRAMES, FRAMES), jnp.bfloat16),
            jax.ShapeDtypeStruct((PART, FRAMES, 2 * CH), jnp.float32),
        ),
        in_specs=[vmem],
        out_specs=(vmem, vmem),
    )(piece)

    up, down, own_base = lax.optimization_barrier((up, down, own_base))
    half = PIECE // 2
    last_up, last_down = shift(up[:half], "z", 1), shift(down[half:], "z", -1)
    near_b = jnp.concatenate([up, down, last_up, last_down], axis=0)
    far_b = shift(near_b, "c", 1)
    keys = (near_a, near_b, far_a, far_b)

    def scratch(q_blocks, sems):
        return [
            pltpu.VMEM((q_blocks, FRAMES, FEAT), jnp.bfloat16),
            pltpu.VMEM((NC, NZ * PIECE, WIDE), jnp.bfloat16),
            pltpu.VMEM((QBLOCKS + 1, FRAMES, 2 * CH), jnp.float32),
            pltpu.VMEM((SLOTS, FRAMES, FRAMES), jnp.bfloat16),
            pltpu.SemaphoreType.DMA((sems,)),
            pltpu.SemaphoreType.DMA,
        ]

    sums = jax.ShapeDtypeStruct((NY * NX, SEND, CH), jnp.bfloat16)
    pair_weights = jax.ShapeDtypeStruct((SLOTS, FRAMES, FRAMES), jnp.bfloat16)
    send, weights = pl.pallas_call(
        early_kernel,
        out_shape=(sums, pair_weights),
        in_specs=[smem] + [hbm] * 8,
        out_specs=(vmem, hbm),
        scratch_shapes=scratch(EARLY_Q, 8),
        compiler_params=params,
    )(lst, all_units, behind, ahead, across, *keys)
    send, weights = pl.pallas_call(
        late_kernel,
        out_shape=(sums, pair_weights),
        in_specs=[smem, hbm, vmem] + [hbm] * 5,
        out_specs=(vmem, hbm),
        scratch_shapes=scratch(LATE_Q, 5),
        input_output_aliases={3: 1},
        compiler_params=params,
    )(lst, queries, send, weights, *keys)
    got = lax.all_to_all(send, ("y", "x"), split_axis=0, concat_axis=0, tiled=True)

    masked, denominator, own_second = pl.pallas_call(
        mix_kernel,
        out_shape=(
            jax.ShapeDtypeStruct((PART, FRAMES, CH), jnp.bfloat16),
            jax.ShapeDtypeStruct((PART, FRAMES, CH), jnp.float32),
            jax.ShapeDtypeStruct((PART, FRAMES, CH), jnp.float32),
        ),
        in_specs=[vmem] * 5,
        out_specs=(vmem,) * 3,
    )(got, own_base, own_weights, prior, marks)
    near_scores = lax.all_gather(masked, "z", axis=0, tiled=True)
    far_scores = shift(near_scores, "c", 1)

    send = pl.pallas_call(
        second_kernel,
        out_shape=jax.ShapeDtypeStruct((QBLOCKS, FRAMES, CH), jnp.bfloat16),
        in_specs=[smem, hbm, vmem, vmem],
        out_specs=vmem,
        scratch_shapes=[
            pltpu.VMEM((QBLOCKS + 1, FRAMES, CH), jnp.float32),
            pltpu.VMEM((SLOTS, FRAMES, FRAMES), jnp.bfloat16),
            pltpu.SemaphoreType.DMA,
        ],
        compiler_params=params,
    )(lst, weights, near_scores, far_scores)
    got = lax.all_to_all(send, ("y", "x"), split_axis=0, concat_axis=0, tiled=True)
    return pl.pallas_call(
        last_kernel,
        out_shape=jax.ShapeDtypeStruct((PART, FRAMES, CH), jnp.bfloat16),
        in_specs=[vmem] * 4,
        out_specs=vmem,
    )(got.reshape(NY * NX, PART, FRAMES, CH), own_second, denominator, prior)


def solution(mesh):
    fine = Mesh(mesh.devices.reshape(NY, NZ, NC, NX), ("y", "z", "c", "x"))
    bucket = ("y", "z", "c")
    in_specs = (P(bucket, None, None), P(bucket, None, None), P(bucket, None), P(bucket, "x"), P(bucket), P())
    out_specs = P(("y", "z", "c", "x"), None, None)
    return jax.shard_map(body, mesh=fine, in_specs=in_specs, out_specs=out_specs, check_vma=False)
```

time: 237 us -> 241 us (1.017)
  waiting for transfers between devices: 91.8 us -> 6.13 us
  blocking collectives: 39.4 us -> 89.9 us
  starting transfers between devices: 27.8 us -> 45.6 us
  local copies, waits for them, and re-layouts: 7.61 us -> 21.2 us
  Pallas kernels: 48.8 us -> 54.4 us
    all_gather x2 -> x1, waiting for transfers between devices: 38.9 us -> 0.02 us  [body(): queries = lax.all_gather(units[:LATE], ('y', 'x'), axis=0, tiled=True)]
    ppermute x10 -> x15, waiting for transfers between devices: 42.2 us -> 6.09 us  [shift(): lax.ppermute(value, axis, [(i, (i + step) % size) for i in range(size)])]
    all_gather x1 -> x2, blocking collectives: 17 us -> 44.6 us  [the longest x1 24 us: body(): near_scores = lax.all_gather(masked, 'z', axis=0, tiled=True)]
    all_to_all x1 -> x2, blocking collectives: 22.4 us -> 45.3 us  [body(): lax.all_to_all(send, ('y', 'x'), split_axis=0, concat_axis=0, tiled=True)]
    ppermute x10 -> x15, starting transfers between devices: 24 us -> 45.6 us  [shift(): lax.ppermute(value, axis, [(i, (i + step) % size) for i in range(size)])]
    all_to_all x1 -> x0, waiting for transfers between devices: 10.6 us -> none  [body(): lax.all_to_all(send, ('y', 'x'), split_axis=0, concat_axis=0, tiled=True)]
    unnamed x22 -> x27, local copies, waits for them, and re-layouts: 5.02 us -> 10.3 us
    slice x0 -> x3, local copies, waits for them, and re-layouts: none -> 4.21 us  [the longest x1 1.71 us: body(): ahead[half:]]
  transfers between devices with their start and end apart: 13 -> 16, of which waited for: 6 -> 4; matrix products, arithmetic and copies ran while one was open for 5% -> 10% of each run, Pallas kernels for 4% -> 11%
where the time goes in v2:
time: 241 us; the launch traced here: 240 us
  blocking collectives  89.9 us (37%)
  Pallas kernels  54.4 us (23%)
  starting transfers between devices  45.6 us (19%)
  local copies, waits for them, and re-layouts  21.2 us (9%)
  between operations  13.7 us (6%)
  other arithmetic  9.55 us (4%)
  waiting for transfers between devices  6.13 us (3%)
    ppermute x15, starting transfers between devices, shift(): lax.ppermute(value, axis, [(i, (i + step) % size) for i in range(size)])  45.6 us
    all_to_all x2, blocking collectives, body(): lax.all_to_all(send, ('y', 'x'), split_axis=0, concat_axis=0, tiled=True)  45.3 us
    all_gather x1, blocking collectives, body(): near_scores = lax.all_gather(masked, 'z', axis=0, tiled=True)  24 us
    all_gather x1, blocking collectives, body(): target = lax.all_gather(target, ('y', 'x'), axis=0)  20.5 us
    pallas_call x1, Pallas kernels, body(): pl.pallas_call(late_kernel, out_shape=(sums, pair_weights), in_specs=[sme...  16.5 us
    pallas_call x1, Pallas kernels, body(): pl.pallas_call(early_kernel, out_shape=(sums, pair_weights), in_specs=[sm...  14 us
    pallas_call x1, Pallas kernels, body(): pl.pallas_call(list_kernel, out_shape=jax.ShapeDtypeStruct((LIST,), jnp.i...  10.8 us
    unnamed x27, local copies, waits for them, and re-layouts  10.3 us
  transfers between devices with their start and end apart: 16, of which 4 were waited for; matrix products, arithmetic and copies ran while one was open for 10% of the time, Pallas kernels for 11%

profile of v2, /device:TPU:1, one launch (start us, length us, event | category | flops | bytes accessed | tf_op | source)
XLA Modules:
  0.0 240.5 jit_solution(2566870502943566838)
XLA Ops:
  6.5 1.4 fusion.2
  8.0 1.2 fusion.3
  10.7 1.5 broadcast_select_fusion
  12.2 0.9 pad_maximum_fusion
  14.1 1.4 copy-done.3
  15.5 0.9 slice_bitcast_fusion
  16.4 2.1 collective-permute-start.2
  18.6 1.4 collective-permute-start.3
  20.0 1.6 collective-permute-start
  21.6 3.9 %collective-permute-start.1 = (bf16[256,1280]{1,0:T(8,128)(2,1)}, bf16[256,1280]{1,0:T(8,128)(2,1)}, u32[]{:S(2)}, u32[]{:S(2)}) collective-permute-start(bf16[256,1280]{1,0:T(8,128)(2,1)} %bitcast.piece), channel_id=1, source_target_pairs={{0,56},{8,0},{16,8},{24,16},{32,24},{40,32},{48,40},{56,48},{1,57}... | collective-permute-start | bytes 1966088 | tf_op jit(solution)/shard_map/ppermute | solution.py:39
  26.8 1.0 gather_fusion
  27.8 20.5 %all-gather = s32[16,1,128]{2,1,0:T(1,128)S(1)} all-gather(s32[1,1,128]{2,1,0:T(1,128)S(1)} %fusion.32), channel_id=1, replica_groups=mesh['y'=4,'z'=8,'c'=2,'x'=4] {'y','x'}, dimensions={0}, use_global_device_ids=true | all-gather | bytes 8704 | tf_op jit(solution)/shard_map/all_gather | solution.py:290
  48.4 1.1 constant_dynamic-update-slice_fusion.4
  49.5 2.1 collective-permute-start.4
  51.6 5.8 %collective-permute-start.5 = (bf16[256,1280]{1,0:T(8,128)(2,1)}, bf16[256,1280]{1,0:T(8,128)(2,1)}, u32[]{:S(2)}, u32[]{:S(2)}) collective-permute-start(bf16[256,1280]{1,0:T(8,128)(2,1)} %collective-permute-done.1), channel_id=1, source_target_pairs={{0,56},{8,0},{16,8},{24,16},{32,24},{40,32},{48,40},{56,48},{1,57}... | collective-permute-start | bytes 1966088 | tf_op jit(solution)/shard_map/ppermute | solution.py:39
  57.4 1.7 slice.19
  59.1 1.3 collective-permute-start.6
  60.4 1.7 slice.20
  62.1 1.4 collective-permute-start.7
  63.5 1.2 constant_dynamic-update-slice_fusion.3
  65.3 10.8 %shard_map.64.lst = s32[640]{0:T(1024)} custom-call(s32[2048]{0:T(1024)} %fusion.16.codes), custom_call_target="tpu_custom_call" | custom-call | tf_op jit(solution)/shard_map/pallas_call | solution.py:319
  76.1 1.1 constant_dynamic-update-slice_fusion.2
  77.4 2.7 %collective-permute-start.9 = (bf16[256,1280]{1,0:T(8,128)(2,1)}, bf16[256,1280]{1,0:T(8,128)(2,1)}, u32[]{:S(2)}, u32[]{:S(2)}) collective-permute-start(bf16[256,1280]{1,0:T(8,128)(2,1)} %collective-permute-done.5), channel_id=1, source_target_pairs={{0,56},{8,0},{16,8},{24,16},{32,24},{40,32},{48,40},{56,48},{1,57}... | collective-permute-start | bytes 1966088 | tf_op jit(solution)/shard_map/ppermute | solution.py:39
  80.0 1.1 constant_dynamic-update-slice_fusion.1
  81.2 1.2 constant_dynamic-update-slice_fusion.near_a
  82.3 8.4 %collective-permute-start.12 = (bf16[1280,1280]{1,0:T(8,128)(2,1)S(1)}, bf16[1280,1280]{1,0:T(8,128)(2,1)}, u32[]{:S(2)}, u32[]{:S(2)}) collective-permute-start(bf16[1280,1280]{1,0:T(8,128)(2,1)S(1)} %constant_dynamic-update-slice_fusion.near_a), channel_id=1, source_target_pairs={{0,4},{4,0},{1,5},{5,1},{2,6},{6,2},{3,7},{7,3},{8,12},{12,8},{9,1... | collective-permute-start | bytes 9830408 | tf_op jit(solution)/shard_map/ppermute | solution.py:39
  90.7 2.7 %shard_map.65 = (bf16[4,64,64]{2,1,0:T(8,128)(2,1)}, f32[4,64,256]{2,1,0:T(8,128)}) custom-call(bf16[256,1280]{1,0:T(8,128)(2,1)} %bitcast.piece), custom_call_target="tpu_custom_call" | custom-call | tf_op jit(solution)/shard_map/pallas_call | solution.py:333
  93.4 1.0 slice.22
  94.7 1.1 constant_dynamic-update-slice_fusion.8
  95.9 1.0 slice.23
  96.8 2.7 %collective-permute-start.11 = (bf16[128,1280]{1,0:T(8,128)(2,1)S(1)}, bf16[128,1280]{1,0:T(8,128)(2,1)S(1)}, u32[]{:S(2)}, u32[]{:S(2)}) collective-permute-start(bf16[128,1280]{1,0:T(8,128)(2,1)S(1)} %slice.23), channel_id=1, source_target_pairs={{0,56},{8,0},{16,8},{24,16},{32,24},{40,32},{48,40},{56,48},{1,57}... | collective-permute-start | bytes 983048 | tf_op jit(solution)/shard_map/ppermute | solution.py:39
  99.6 1.1 constant_dynamic-update-slice_fusion.7
  100.7 1.1 collective-permute-done.10
  101.9 1.7 collective-permute-done.11
  103.6 5.0 %collective-permute-start.13 = (bf16[768,1280]{1,0:T(8,128)(2,1)S(1)}, bf16[768,1280]{1,0:T(8,128)(2,1)S(1)}, u32[]{:S(2)}, u32[]{:S(2)}) collective-permute-start(bf16[768,1280]{1,0:T(8,128)(2,1)S(1)} %constant_dynamic-update-slice_fusion.5.near_b), channel_id=1, source_target_pairs={{0,4},{4,0},{1,5},{5,1},{2,6},{6,2},{3,7},{7,3},{8,12},{12,8},{9,1... | collective-permute-start | bytes 5898248 | tf_op jit(solution)/shard_map/ppermute | solution.py:39
  108.7 1.9 pad_maximum_fusion.1.across
  110.6 1.7 collective-permute-done.13.far_b
  112.3 1.2 copy-done.5
  113.5 14.0 %shard_map.66 = (bf16[16,272,128]{2,1,0:T(8,128)(2,1)}, bf16[544,64,64]{2,1,0:T(8,128)(2,1)}) custom-call(s32[640]{0:T(1024)} %shard_map.64.lst, bf16[16,64,1152]{2,1,0:T(8,128)(2,1)} %copy-done.3, bf16[4,64,1152]{2,1,0:T(8,128)(2,1)} %collective-permute-done.2.behind, bf16[4,64,1152]{2,1,0:T(8,128)(2,1)} %collective-permute-done.3.ahead, ...), custom_call_target="tpu_custom_call" | custom-call | tf_op jit(solution)/shard_map/pallas_call | solution.py:362
  127.6 16.5 %shard_map.67 = (bf16[16,272,128]{2,1,0:T(8,128)(2,1)}, bf16[544,64,64]{2,1,0:T(8,128)(2,1)}) custom-call(s32[640]{0:T(1024)} %shard_map.64.lst, bf16[48,64,1152]{2,1,0:T(8,128)(2,1)} %all-gather.3.cloned.1.call-done.queries, bf16[16,272,128]{2,1,0:T(8,128)(2,1)} %get-tuple-element.46.before, ...), custom_call_target="tpu_custom_call", output_to_operand_aliasing={{1}: (3, {})} | custom-call | tf_op jit(solution)/shard_map/pallas_call | solution.py:370
  144.1 24.9 %all_to_all.10.got = bf16[16,272,128]{2,1,0:T(8,128)(2,1)} all-to-all(bf16[16,272,128]{2,1,0:T(8,128)(2,1)} %get-tuple-element.49), channel_id=1, replica_groups=mesh['y'=4,'z'=8,'c'=2,'x'=4] {'y','x'}, dimensions={0} | all-to-all | bytes 2228224 | tf_op jit(solution)/shard_map/all_to_all | solution.py:379
  169.7 2.4 shard_map.68
  172.1 24.0 %all_gather.12.near = bf16[32,64,128]{2,1,0:T(8,128)(2,1)S(1)} all-gather(bf16[4,64,128]{2,1,0:T(8,128)(2,1)} %get-tuple-element.52), channel_id=1, replica_groups=mesh['y'=4,'z'=8,'c'=2,'x'=4] {'z'}, dimensions={0}, use_global_device_ids=true | all-gather | bytes 589824 | tf_op jit(solution)/shard_map/all_gather | solution.py:391
  196.1 6.7 %collective-permute-start.14 = (bf16[32,64,128]{2,1,0:T(8,128)(2,1)S(1)}, bf16[32,64,128]{2,1,0:T(8,128)(2,1)S(1)}, u32[]{:S(2)}, u32[]{:S(2)}) collective-permute-start(bf16[32,64,128]{2,1,0:T(8,128)(2,1)S(1)} %all_gather.12.near), channel_id=1, source_target_pairs={{0,4},{4,0},{1,5},{5,1},{2,6},{6,2},{3,7},{7,3},{8,12},{12,8},{9,1... | collective-permute-start | bytes 1572872 | tf_op jit(solution)/shard_map/ppermute | solution.py:39
  202.9 1.5 collective-permute-done.14.far
  205.2 5.9 %shard_map.69 = bf16[64,64,128]{2,1,0:T(8,128)(2,1)} custom-call(s32[640]{0:T(1024)} %shard_map.64.lst, bf16[544,64,64]{2,1,0:T(8,128)(2,1)} %get-tuple-element.48.weights_in, bf16[32,64,128]{2,1,0:T(8,128)(2,1)} %copy-done.6, bf16[32,64,128]{2,1,0:T(8,128)(2,1)} %copy-done.7), custom_call_target="tpu_custom_call" | custom-call | tf_op jit(solution)/shard_map/pallas_call | solution.py:394
  211.1 20.5 %all_to_all.11 = bf16[64,64,128]{2,1,0:T(8,128)(2,1)} all-to-all(bf16[64,64,128]{2,1,0:T(8,128)(2,1)} %shard_map.69), channel_id=1, replica_groups=mesh['y'=4,'z'=8,'c'=2,'x'=4] {'y','x'}, dimensions={0} | all-to-all | bytes 2097152 | tf_op jit(solution)/shard_map/all_to_all | solution.py:406
  231.5 2.1 shard_map.70
  (66 shorter events, 6.4 us)
Async XLA Ops:
  6.5 20.3 %copy-start = (s32[1024]{0:T(1024)S(1)}, s32[1024]{0:T(1024)}, u32[]{:S(2)}) copy-start(s32[1024]{0:T(1024)} %param.11) | copy-start | bytes 12292
  6.5 6.5 %copy-start.2 = (bf16[16,64,1152]{2,1,0:T(8,128)(2,1)S(1)}, bf16[16,64,1152]{2,1,0:T(8,128)(2,1)}, u32[]{:S(2)}) copy-start(bf16[16,64,1152]{2,1,0:T(8,128)(2,1)} %param.6) | copy-start | bytes 7077892
  6.5 121.0 %all-gather.3.cloned.1.call-start = ((), (), s32[]{:S(2)}) async-start(), calls=%async_computation.2 | async-start | bytes 7520256 | tf_op jit(solution)/shard_map/all_gather | solution.py:278
  13.6 12.0 %copy-start.8 = (s32[16,8]{0,1:T(8,128)S(1)}, s32[16,8]{0,1:T(8,128)}, u32[]{:S(2)}) copy-start(s32[16,8]{0,1:T(8,128)} %param.9) | copy-start | bytes 1540
  13.6 12.3 %copy-start.9 = (s32[16]{0:T(128)S(1)}, s32[16]{0:T(128)}, u32[]{:S(2)}) copy-start(s32[16]{0:T(128)} %param.10) | copy-start | bytes 196
  14.1 1.4 copy-start.3
  16.4 33.1 %collective-permute-start.2 = (bf16[4,64,1152]{2,1,0:T(8,128)(2,1)}, bf16[4,64,1152]{2,1,0:T(8,128)(2,1)}, u32[]{:S(2)}, u32[]{:S(2)}) collective-permute-start(bf16[4,64,1152]{2,1,0:T(8,128)(2,1)} %slice_bitcast_fusion), channel_id=1, source_target_pairs={{0,64},{64,128},{128,192},{192,0},{1,65},{65,129},{129,193},{193,1... | collective-permute-start | bytes 1769480 | tf_op jit(solution)/shard_map/ppermute | solution.py:39
  18.6 31.0 %collective-permute-start.3 = (bf16[4,64,1152]{2,1,0:T(8,128)(2,1)}, bf16[4,64,1152]{2,1,0:T(8,128)(2,1)}, u32[]{:S(2)}, u32[]{:S(2)}) collective-permute-start(bf16[4,64,1152]{2,1,0:T(8,128)(2,1)} %slice_bitcast_fusion), channel_id=1, source_target_pairs={{0,192},{64,0},{128,64},{192,128},{1,193},{65,1},{129,65},{193,129... | collective-permute-start | bytes 1769480 | tf_op jit(solution)/shard_map/ppermute | solution.py:39
  20.0 29.5 %collective-permute-start = (bf16[256,1280]{1,0:T(8,128)(2,1)}, bf16[256,1280]{1,0:T(8,128)(2,1)}, u32[]{:S(2)}, u32[]{:S(2)}) collective-permute-start(bf16[256,1280]{1,0:T(8,128)(2,1)} %bitcast.piece), channel_id=1, source_target_pairs={{0,8},{8,16},{16,24},{24,32},{32,40},{40,48},{48,56},{56,0},{1,9},... | collective-permute-start | bytes 1966088 | tf_op jit(solution)/shard_map/ppermute | solution.py:39
  21.6 27.9 %collective-permute-start.1 = (bf16[256,1280]{1,0:T(8,128)(2,1)}, bf16[256,1280]{1,0:T(8,128)(2,1)}, u32[]{:S(2)}, u32[]{:S(2)}) collective-permute-start(bf16[256,1280]{1,0:T(8,128)(2,1)} %bitcast.piece), channel_id=1, source_target_pairs={{0,56},{8,0},{16,8},{24,16},{32,24},{40,32},{48,40},{56,48},{1,57}... | collective-permute-start | bytes 1966088 | tf_op jit(solution)/shard_map/ppermute | solution.py:39
  49.5 27.7 %collective-permute-start.4 = (bf16[256,1280]{1,0:T(8,128)(2,1)}, bf16[256,1280]{1,0:T(8,128)(2,1)}, u32[]{:S(2)}, u32[]{:S(2)}) collective-permute-start(bf16[256,1280]{1,0:T(8,128)(2,1)} %collective-permute-done), channel_id=1, source_target_pairs={{0,8},{8,16},{16,24},{24,32},{32,40},{40,48},{48,56},{56,0},{1,9},... | collective-permute-start | bytes 1966088 | tf_op jit(solution)/shard_map/ppermute | solution.py:39
  51.6 25.6 %collective-permute-start.5 = (bf16[256,1280]{1,0:T(8,128)(2,1)}, bf16[256,1280]{1,0:T(8,128)(2,1)}, u32[]{:S(2)}, u32[]{:S(2)}) collective-permute-start(bf16[256,1280]{1,0:T(8,128)(2,1)} %collective-permute-done.1), channel_id=1, source_target_pairs={{0,56},{8,0},{16,8},{24,16},{32,24},{40,32},{48,40},{56,48},{1,57}... | collective-permute-start | bytes 1966088 | tf_op jit(solution)/shard_map/ppermute | solution.py:39
  59.1 18.1 %collective-permute-start.6 = (bf16[2,64,1152]{2,1,0:T(8,128)(2,1)}, bf16[2,64,1152]{2,1,0:T(8,128)(2,1)}, u32[]{:S(2)}, u32[]{:S(2)}) collective-permute-start(bf16[2,64,1152]{2,1,0:T(8,128)(2,1)} %slice.19), channel_id=1, source_target_pairs={{0,64},{64,128},{128,192},{192,0},{1,65},{65,129},{129,193},{193,1... | collective-permute-start | bytes 884744 | tf_op jit(solution)/shard_map/ppermute | solution.py:39
  62.1 15.1 %collective-permute-start.7 = (bf16[2,64,1152]{2,1,0:T(8,128)(2,1)}, bf16[2,64,1152]{2,1,0:T(8,128)(2,1)}, u32[]{:S(2)}, u32[]{:S(2)}) collective-permute-start(bf16[2,64,1152]{2,1,0:T(8,128)(2,1)} %slice.20), channel_id=1, source_target_pairs={{0,192},{64,0},{128,64},{192,128},{1,193},{65,1},{129,65},{193,129... | collective-permute-start | bytes 884744 | tf_op jit(solution)/shard_map/ppermute | solution.py:39
  77.3 16.2 %collective-permute-start.8 = (bf16[256,1280]{1,0:T(8,128)(2,1)}, bf16[256,1280]{1,0:T(8,128)(2,1)}, u32[]{:S(2)}, u32[]{:S(2)}) collective-permute-start(bf16[256,1280]{1,0:T(8,128)(2,1)} %collective-permute-done.4), channel_id=1, source_target_pairs={{0,8},{8,16},{16,24},{24,32},{32,40},{40,48},{48,56},{56,0},{1,9},... | collective-permute-start | bytes 1966088 | tf_op jit(solution)/shard_map/ppermute | solution.py:39
  77.4 16.1 %collective-permute-start.9 = (bf16[256,1280]{1,0:T(8,128)(2,1)}, bf16[256,1280]{1,0:T(8,128)(2,1)}, u32[]{:S(2)}, u32[]{:S(2)}) collective-permute-start(bf16[256,1280]{1,0:T(8,128)(2,1)} %collective-permute-done.5), channel_id=1, source_target_pairs={{0,56},{8,0},{16,8},{24,16},{32,24},{40,32},{48,40},{56,48},{1,57}... | collective-permute-start | bytes 1966088 | tf_op jit(solution)/shard_map/ppermute | solution.py:39
  82.3 19.5 %copy-start.1 = (bf16[1280,1280]{1,0:T(8,128)(2,1)}, bf16[1280,1280]{1,0:T(8,128)(2,1)S(1)}, u32[]{:S(2)}) copy-start(bf16[1280,1280]{1,0:T(8,128)(2,1)S(1)} %constant_dynamic-update-slice_fusion.near_a) | copy-start | bytes 9830404
  82.3 29.9 %collective-permute-start.12 = (bf16[1280,1280]{1,0:T(8,128)(2,1)S(1)}, bf16[1280,1280]{1,0:T(8,128)(2,1)}, u32[]{:S(2)}, u32[]{:S(2)}) collective-permute-start(bf16[1280,1280]{1,0:T(8,128)(2,1)S(1)} %constant_dynamic-update-slice_fusion.near_a), channel_id=1, source_target_pairs={{0,4},{4,0},{1,5},{5,1},{2,6},{6,2},{3,7},{7,3},{8,12},{12,8},{9,1... | collective-permute-start | bytes 9830408 | tf_op jit(solution)/shard_map/ppermute | solution.py:39
  94.4 7.4 %collective-permute-start.10 = (bf16[128,1280]{1,0:T(8,128)(2,1)S(1)}, bf16[128,1280]{1,0:T(8,128)(2,1)S(1)}, u32[]{:S(2)}, u32[]{:S(2)}) collective-permute-start(bf16[128,1280]{1,0:T(8,128)(2,1)S(1)} %slice.22), channel_id=1, source_target_pairs={{0,8},{8,16},{16,24},{24,32},{32,40},{40,48},{48,56},{56,0},{1,9},... | collective-permute-start | bytes 983048 | tf_op jit(solution)/shard_map/ppermute | solution.py:39
  96.8 6.8 %collective-permute-start.11 = (bf16[128,1280]{1,0:T(8,128)(2,1)S(1)}, bf16[128,1280]{1,0:T(8,128)(2,1)S(1)}, u32[]{:S(2)}, u32[]{:S(2)}) collective-permute-start(bf16[128,1280]{1,0:T(8,128)(2,1)S(1)} %slice.23), channel_id=1, source_target_pairs={{0,56},{8,0},{16,8},{24,16},{32,24},{40,32},{48,40},{56,48},{1,57}... | collective-permute-start | bytes 983048 | tf_op jit(solution)/shard_map/ppermute | solution.py:39
  103.6 8.6 %copy-start.4 = (bf16[768,1280]{1,0:T(8,128)(2,1)}, bf16[768,1280]{1,0:T(8,128)(2,1)S(1)}, u32[]{:S(2)}) copy-start(bf16[768,1280]{1,0:T(8,128)(2,1)S(1)} %constant_dynamic-update-slice_fusion.5.near_b) | copy-start | bytes 5898244
  103.6 8.6 %collective-permute-start.13 = (bf16[768,1280]{1,0:T(8,128)(2,1)S(1)}, bf16[768,1280]{1,0:T(8,128)(2,1)S(1)}, u32[]{:S(2)}, u32[]{:S(2)}) collective-permute-start(bf16[768,1280]{1,0:T(8,128)(2,1)S(1)} %constant_dynamic-update-slice_fusion.5.near_b), channel_id=1, source_target_pairs={{0,4},{4,0},{1,5},{5,1},{2,6},{6,2},{3,7},{7,3},{8,12},{12,8},{9,1... | collective-permute-start | bytes 5898248 | tf_op jit(solution)/shard_map/ppermute | solution.py:39
  112.3 1.3 copy-start.5
  196.1 8.3 %copy-start.6 = (bf16[32,64,128]{2,1,0:T(8,128)(2,1)}, bf16[32,64,128]{2,1,0:T(8,128)(2,1)S(1)}, u32[]{:S(2)}) copy-start(bf16[32,64,128]{2,1,0:T(8,128)(2,1)S(1)} %all_gather.12.near) | copy-start | bytes 1572868
  196.1 8.2 %collective-permute-start.14 = (bf16[32,64,128]{2,1,0:T(8,128)(2,1)S(1)}, bf16[32,64,128]{2,1,0:T(8,128)(2,1)S(1)}, u32[]{:S(2)}, u32[]{:S(2)}) collective-permute-start(bf16[32,64,128]{2,1,0:T(8,128)(2,1)S(1)} %all_gather.12.near), channel_id=1, source_target_pairs={{0,4},{4,0},{1,5},{5,1},{2,6},{6,2},{3,7},{7,3},{8,12},{12,8},{9,1... | collective-permute-start | bytes 1572872 | tf_op jit(solution)/shard_map/ppermute | solution.py:39
  204.4 0.8 copy-start.7
Sparse Core Ops, SparseCore 0:
  10.2 82.8 all-gather.2

commit v3 on v1

v3 whole, which is shorter than its diff:
```python
import math

import jax
import jax.numpy as jnp
from jax import lax
from jax.experimental import pallas as pl
from jax.experimental.pallas import tpu as pltpu
from jax.sharding import Mesh
from jax.sharding import PartitionSpec as P

epsilon = 1e-06
keep_share = 0.9

NY, NZ, NC, NX = 4, 8, 2, 4
ROWS = 16
FRAMES = 64
FEAT = 1152
CH = 128
PART = ROWS // NX
SHARED = 2
STRAIGHT = NX * (PART - SHARED)
QBLOCKS = NY * ROWS
Q_SHARED = ROWS + (NY - 1) * STRAIGHT
Q_ALL = Q_SHARED + NY * NX * SHARED
UNROLL = 8
SLOTS = 520
WIDE = FEAT + CH
PIECE = PART * FRAMES
HALF = PIECE // 2
SEND = PIECE + 16
LIST = 640
STEPS_AT = 600
SPARE = QBLOCKS
VMEM = 56 * 1024 * 1024
UNREAL = 1024.0
sharpness = 2.0 * math.sqrt(FEAT)


def shift(value, axis, step):
    size = lax.axis_size(axis)
    return lax.ppermute(value, axis, [(i, (i + step) % size) for i in range(size)])


def list_kernel(codes, out):
    def eight(i, count):
        for u in range(8):
            code = codes[i * 8 + u]
            out[count] = code
            count = count + jnp.where(code >= 0, 1, 0)
        return count

    count = lax.fori_loop(0, QBLOCKS * 32 // 8, eight, 0)
    for u in range(UNROLL):
        out[count + u] = SPARE
    out[STEPS_AT] = (count + UNROLL - 1) // UNROLL


def own_kernel(piece, own_weights, own_base):
    row = lax.broadcasted_iota(jnp.int32, (FRAMES, FRAMES), 0)
    col = lax.broadcasted_iota(jnp.int32, (FRAMES, FRAMES), 1)
    for b in range(PART):
        block = piece[b * FRAMES:(b + 1) * FRAMES, :]
        units = block[:, :FEAT]
        affinity = lax.dot_general(
            units, units, (((1,), (1,)), ((), ())), preferred_element_type=jnp.float32
        )
        weights = jnp.where(row == col, 0.0, jnp.exp(sharpness * affinity)).astype(jnp.bfloat16)
        own_weights[b] = weights
        own_base[b] = jnp.dot(weights, values_of(block[:, FEAT:]), preferred_element_type=jnp.float32)


def values_of(scores):
    floats = scores.astype(jnp.float32)
    real = floats < UNREAL
    return jnp.concatenate(
        [jnp.where(real, floats, 0.0), jnp.where(real, 1.0, 0.0)], axis=1
    ).astype(jnp.bfloat16)


def first_kernel(lst, *refs):
    near, far, queries = refs[:9], refs[9:18], refs[18:23]
    send, weights_out, q, k, acc, w, sems, out_sem = refs[23:]
    copies = []
    for side, held in enumerate((near, far)):
        at = 0
        for piece in held:
            rows = piece.shape[0]
            copies.append(pltpu.make_async_copy(piece, k.at[side, pl.ds(at, rows)], sems.at[len(copies)]))
            at += rows
    at = 0
    for part in queries:
        rows = part.shape[0]
        copies.append(pltpu.make_async_copy(part, q.at[pl.ds(at, rows)], sems.at[len(copies)]))
        at += rows
    for copy in copies:
        copy.start()
    acc[...] = jnp.zeros_like(acc)
    for copy in copies:
        copy.wait()
    steps = lst[STEPS_AT]

    def step(i, carry):
        codes = [lst[i * UNROLL + u] for u in range(UNROLL)]
        sides = [(code >> 12) & 1 for code in codes]
        rows = [pl.multiple_of(((code >> 7) & 31) * FRAMES, FRAMES) for code in codes]
        weights = []
        for code, side, row in zip(codes, sides, rows):
            units = q[(code >> 18) & 127]
            keys = k[side, pl.ds(row, FRAMES), pl.ds(0, FEAT)]
            affinity = lax.dot_general(
                units, keys, (((1,), (1,)), ((), ())), preferred_element_type=jnp.float32
            )
            weights.append(jnp.exp(sharpness * affinity).astype(jnp.bfloat16))
        for u in range(UNROLL):
            w[i * UNROLL + u] = weights[u]
        sums = []
        for u, (side, row) in enumerate(zip(sides, rows)):
            values = values_of(k[side, pl.ds(row, FRAMES), pl.ds(FEAT, CH)])
            sums.append(jnp.dot(weights[u], values, preferred_element_type=jnp.float32))
        for u, code in enumerate(codes):
            acc[code & 127] += sums[u]
        group = pl.ds(i * UNROLL, UNROLL)
        pltpu.make_async_copy(w.at[group], weights_out.at[group], out_sem).start()
        return carry

    lax.fori_loop(0, steps, step, 0)
    row = lax.broadcasted_iota(jnp.int32, (FRAMES, CH), 0)
    lane = lax.broadcasted_iota(jnp.int32, (FRAMES, CH), 1)
    pick = row == lane % FRAMES
    low = lax.broadcasted_iota(jnp.int32, (1, CH), 1) < FRAMES

    def finish(d, carry):
        rows = []
        for b in range(PART):
            block = acc[d * PART + b]
            send[d, b * FRAMES:(b + 1) * FRAMES, :] = block[:, :CH].astype(jnp.bfloat16)
            mass = jnp.sum(jnp.where(pick, block[:, CH:], 0.0), axis=0, keepdims=True)
            coarse = mass.astype(jnp.bfloat16).astype(jnp.float32)
            rows.append(jnp.where(low, coarse, mass - coarse))
        rows.append(jnp.zeros((16 - PART, CH), jnp.float32))
        send[d, PIECE:SEND, :] = jnp.concatenate(rows, axis=0).astype(jnp.bfloat16)
        return carry

    lax.fori_loop(0, NY * NX, finish, 0)

    def drain(i, carry):
        group = pl.ds(i * UNROLL, UNROLL)
        pltpu.make_async_copy(w.at[group], weights_out.at[group], out_sem).wait()
        return carry

    lax.fori_loop(0, steps, drain, 0)


def second_kernel(lst, weights_in, near, far, send, acc, w, in_sem):
    steps = lst[STEPS_AT]

    def fetch(i, carry):
        group = pl.ds(i * UNROLL, UNROLL)
        pltpu.make_async_copy(weights_in.at[group], w.at[group], in_sem).start()
        return carry

    lax.fori_loop(0, steps, fetch, 0)
    acc[...] = jnp.zeros_like(acc)

    def drain(i, carry):
        group = pl.ds(i * UNROLL, UNROLL)
        pltpu.make_async_copy(weights_in.at[group], w.at[group], in_sem).wait()
        return carry

    lax.fori_loop(0, steps, drain, 0)

    def step(i, carry):
        codes = [lst[i * UNROLL + u] for u in range(UNROLL)]
        sums = []
        for u, code in enumerate(codes):
            block = (code >> 13) & 31
            scores = jnp.where(((code >> 12) & 1) == 0, near[block], far[block])
            sums.append(jnp.dot(w[i * UNROLL + u], scores, preferred_element_type=jnp.float32))
        for u, code in enumerate(codes):
            acc[code & 127] += sums[u]
        return carry

    lax.fori_loop(0, steps, step, 0)
    for b in range(QBLOCKS):
        send[b] = acc[b].astype(jnp.bfloat16)


def mix_kernel(got, base, weights, prior, marks, masked, denominator, own_second):
    row = lax.broadcasted_iota(jnp.int32, (FRAMES, CH), 0)
    lane = lax.broadcasted_iota(jnp.int32, (FRAMES, CH), 1)
    pick = (row == lane % FRAMES).astype(jnp.float32)
    for b in range(PART):
        total = base[b, :, :CH]
        for d in range(NY * NX):
            total = total + got[d, b * FRAMES:(b + 1) * FRAMES, :].astype(jnp.float32)
        mass = jnp.sum(got[:, PIECE:SEND, :].astype(jnp.float32), axis=0)[b:b + 1, :]
        column = jnp.sum(pick * mass, axis=1, keepdims=True)
        full = 1.0 + column + base[b, :, CH:]
        denominator[b] = full
        mixed = keep_share * total / full + (1.0 - keep_share) * prior[b].astype(jnp.float32)
        keep = (mixed.astype(jnp.bfloat16).astype(jnp.float32) * marks[b].astype(jnp.float32)).astype(jnp.bfloat16)
        masked[b] = keep
        own_second[b] = jnp.dot(weights[b], keep, preferred_element_type=jnp.float32)


def last_kernel(got, own_second, denominator, prior, out):
    for b in range(PART):
        total = own_second[b]
        for d in range(NY * NX):
            total = total + got[d, b].astype(jnp.float32)
        mixed = keep_share * total / denominator[b]
        out[b] = (mixed + (1.0 - keep_share) * prior[b].astype(jnp.float32)).astype(jnp.bfloat16)


smem = pl.BlockSpec(memory_space=pltpu.SMEM)
vmem = pl.BlockSpec(memory_space=pltpu.VMEM)
hbm = pl.BlockSpec(memory_space=pl.ANY)
params = pltpu.CompilerParams(vmem_limit_bytes=VMEM)


def normalize(values):
    floats = values.astype(jnp.float32)
    return (floats * lax.rsqrt(jnp.sum(floats * floats, axis=-1, keepdims=True) + epsilon)).astype(jnp.bfloat16)


def body(embeddings, prior_scores, frame_valid, neighbour_ids, neighbour_count, block_home):
    per_list = neighbour_ids.shape[1]
    y, z, c, x = (lax.axis_index(a) for a in ("y", "z", "c", "x"))
    first = x * PART
    units = normalize(lax.dynamic_slice_in_dim(embeddings, first, PART, 0))
    prior = lax.dynamic_slice_in_dim(prior_scores, first, PART, 0)
    valid = lax.dynamic_slice_in_dim(frame_valid, first, PART, 0)
    marks = jnp.broadcast_to(valid[:, :, None], prior.shape).astype(jnp.bfloat16)
    marked = jnp.where(marks > 0, prior, jnp.bfloat16(2 * UNREAL))
    piece = jnp.concatenate([units, marked], axis=-1).reshape(PIECE, WIDE)

    target = jnp.take(block_home, neighbour_ids.reshape(-1), axis=0)
    column = x * per_list + jnp.arange(per_list, dtype=jnp.int32)
    in_list = column[None, :] < neighbour_count[:, None]
    target = jnp.where(in_list.reshape(-1), target, -1).reshape(1, ROWS * per_list)

    shared = lax.all_gather(units[:SHARED], ("y", "x"), axis=0, tiled=True)
    up, down = shift(piece, "z", 1), shift(piece, "z", -1)
    embeddings, piece = lax.optimization_barrier((embeddings, piece))
    all_units = normalize(embeddings)
    straight = all_units.reshape(NX, PART, FRAMES, FEAT)[:, SHARED:].reshape(STRAIGHT, FRAMES, FEAT)
    behind, ahead = shift(straight, "y", 1), shift(straight, "y", -1)
    targets = [target, shift(target, "y", -1), shift(target, "y", 2), shift(target, "y", 1)]

    up, down, targets = lax.optimization_barrier((up, down, targets))
    near = [piece, up, down]
    far = [shift(v, "c", 1) for v in near]
    up, down = shift(up, "z", 1), shift(down, "z", -1)
    target = jnp.concatenate(targets, axis=0)
    targets = [target, shift(target, "x", -1), shift(target, "x", 2), shift(target, "x", 1)]

    up, down, behind, ahead, targets = lax.optimization_barrier((up, down, behind, ahead, targets))
    half = STRAIGHT // 2
    across_a, across_b = shift(behind[:half], "y", 1), shift(ahead[half:], "y", -1)
    held = [up, down]
    up, down = shift(up, "z", 1), shift(down, "z", -1)
    near += held
    far += [shift(v, "c", 1) for v in held]
    target = jnp.stack(targets, axis=0).reshape(NX, NY, ROWS, per_list)
    distance = jnp.arange(NY, dtype=jnp.int32)[None, :, None, None]
    source_row = jnp.arange(ROWS, dtype=jnp.int32)[None, None, :, None]
    source_y = (y + distance) % NY
    source = source_y * ROWS + source_row
    wanted = (target >= 0) & (target // 256 == y) & ((target % 16) // PART == x)
    place = (target // 16) % 16
    apart = (place // 2 - z) % NZ
    order = jnp.where(
        apart == 0, 0, jnp.where(apart < 4, 2 * apart, jnp.where(apart == 4, 7, 2 * (NZ - apart) - 1))
    )
    inner = target % PART
    side = (place % 2) ^ c
    quarter, within = source_row // PART, source_row % PART
    taken = jnp.where(
        distance == 0,
        source_row,
        jnp.where(
            within < SHARED,
            Q_SHARED + (source_y * NX + quarter) * SHARED + within,
            ROWS + (distance - 1) * STRAIGHT + quarter * (PART - SHARED) + within - SHARED,
        ),
    )
    codes = source | ((order * PART + inner) << 7) | (side << 12) | (((place // 2) * PART + inner) << 13) | (taken << 18)
    codes = jnp.where(wanted, codes, -1).reshape(-1)
    lst = pl.pallas_call(
        list_kernel,
        out_shape=jax.ShapeDtypeStruct((LIST,), jnp.int32),
        in_specs=[smem],
        out_specs=smem,
    )(codes)

    up, down, lst = lax.optimization_barrier((up, down, lst))
    last_up, last_down = shift(up[:HALF], "z", 1), shift(down[HALF:], "z", -1)
    near += [up, down]
    far += [shift(up, "c", 1), shift(down, "c", 1)]
    own_weights, own_base = pl.pallas_call(
        own_kernel,
        out_shape=(
            jax.ShapeDtypeStruct((PART, FRAMES, FRAMES), jnp.bfloat16),
            jax.ShapeDtypeStruct((PART, FRAMES, 2 * CH), jnp.float32),
        ),
        in_specs=[vmem],
        out_specs=(vmem, vmem),
    )(piece)
    near += [last_up, last_down]
    far += [shift(last_up, "c", 1), shift(last_down, "c", 1)]
    across = jnp.concatenate([across_a, across_b], axis=0)

    send, weights = pl.pallas_call(
        first_kernel,
        out_shape=(
            jax.ShapeDtypeStruct((NY * NX, SEND, CH), jnp.bfloat16),
            jax.ShapeDtypeStruct((SLOTS, FRAMES, FRAMES), jnp.bfloat16),
        ),
        in_specs=[smem] + [hbm] * 23,
        out_specs=(vmem, hbm),
        scratch_shapes=[
            pltpu.VMEM((Q_ALL, FRAMES, FEAT), jnp.bfloat16),
            pltpu.VMEM((NC, NZ * PIECE, WIDE), jnp.bfloat16),
            pltpu.VMEM((QBLOCKS + 1, FRAMES, 2 * CH), jnp.float32),
            pltpu.VMEM((SLOTS, FRAMES, FRAMES), jnp.bfloat16),
            pltpu.SemaphoreType.DMA((23,)),
            pltpu.SemaphoreType.DMA,
        ],
        compiler_params=params,
    )(lst, *near, *far, all_units, ahead, across, behind, shared)
    got = lax.all_to_all(send, ("y", "x"), split_axis=0, concat_axis=0, tiled=True)

    masked, denominator, own_second = pl.pallas_call(
        mix_kernel,
        out_shape=(
            jax.ShapeDtypeStruct((PART, FRAMES, CH), jnp.bfloat16),
            jax.ShapeDtypeStruct((PART, FRAMES, CH), jnp.float32),
            jax.ShapeDtypeStruct((PART, FRAMES, CH), jnp.float32),
        ),
        in_specs=[vmem] * 5,
        out_specs=(vmem,) * 3,
    )(got, own_base, own_weights, prior, marks)
    near_scores = lax.all_gather(masked, "z", axis=0, tiled=True)
    far_scores = shift(near_scores, "c", 1)

    send = pl.pallas_call(
        second_kernel,
        out_shape=jax.ShapeDtypeStruct((QBLOCKS, FRAMES, CH), jnp.bfloat16),
        in_specs=[smem, hbm, vmem, vmem],
        out_specs=vmem,
        scratch_shapes=[
            pltpu.VMEM((QBLOCKS + 1, FRAMES, CH), jnp.float32),
            pltpu.VMEM((SLOTS, FRAMES, FRAMES), jnp.bfloat16),
            pltpu.SemaphoreType.DMA,
        ],
        compiler_params=params,
    )(lst, weights, near_scores, far_scores)
    got = lax.all_to_all(send, ("y", "x"), split_axis=0, concat_axis=0, tiled=True)
    return pl.pallas_call(
        last_kernel,
        out_shape=jax.ShapeDtypeStruct((PART, FRAMES, CH), jnp.bfloat16),
        in_specs=[vmem] * 4,
        out_specs=vmem,
    )(got.reshape(NY * NX, PART, FRAMES, CH), own_second, denominator, prior)


def solution(mesh):
    fine = Mesh(mesh.devices.reshape(NY, NZ, NC, NX), ("y", "z", "c", "x"))
    bucket = ("y", "z", "c")
    in_specs = (P(bucket, None, None), P(bucket, None, None), P(bucket, None), P(bucket, "x"), P(bucket), P())
    out_specs = P(("y", "z", "c", "x"), None, None)
    return jax.shard_map(body, mesh=fine, in_specs=in_specs, out_specs=out_specs, check_vma=False)
```

time: 237 us -> 247 us (1.042)
  starting transfers between devices: 27.8 us -> 49.9 us
  Pallas kernels: 48.8 us -> 35.4 us
  waiting for transfers between devices: 91.8 us -> 80.8 us
  local copies, waits for them, and re-layouts: 7.61 us -> 14.5 us
  blocking collectives: 39.4 us -> 42.8 us
  other arithmetic: 7.54 us -> 10.2 us
    all_gather x2 -> x1, waiting for transfers between devices: 38.9 us -> 0.01 us  [body(): shared = lax.all_gather(units[:SHARED], ('y', 'x'), axis=0, tiled=True)]
    ppermute x10 -> x28, starting transfers between devices: 24 us -> 45.8 us  [shift(): lax.ppermute(value, axis, [(i, (i + step) % size) for i in range(size)])]
    ppermute x10 -> x28, waiting for transfers between devices: 42.2 us -> 62.9 us  [shift(): lax.ppermute(value, axis, [(i, (i + step) % size) for i in range(size)])]
    pallas_call x1, Pallas kernels: 28 us -> 15.8 us  [body(): pl.pallas_call(first_kernel, out_shape=(jax.ShapeDtypeStruct((NY * NX, SE...]
    all_to_all x1, waiting for transfers between devices: 10.6 us -> 17.8 us  [body(): lax.all_to_all(send, ('y', 'x'), split_axis=0, concat_axis=0, tiled=True)]
    slice x2 -> x6, local copies, waits for them, and re-layouts: 0.05 us -> 5.66 us  [the longest x2 1.99 us: body(): last_up, last_down = (shift(up[:HALF], 'z', 1), shift(down[HALF:], 'z', -1))]
    all_gather x1, blocking collectives: 17 us -> 20.3 us  [body(): near_scores = lax.all_gather(masked, 'z', axis=0, tiled=True)]
    unnamed x22 -> x43, local copies, waits for them, and re-layouts: 5.02 us -> 5.92 us
  transfers between devices with their start and end apart: 13 -> 30, of which waited for: 6 -> 11; matrix products, arithmetic and copies ran while one was open for 5% -> 6% of each run, Pallas kernels for 4% -> 4%
where the time goes in v3:
time: 247 us
  waiting for transfers between devices  80.8 us (33%)
  starting transfers between devices  49.9 us (20%)
  blocking collectives  42.8 us (17%)
  Pallas kernels  35.4 us (14%)
  local copies, waits for them, and re-layouts  14.5 us (6%)
  between operations  13.8 us (6%)
  other arithmetic  10.2 us (4%)
    ppermute x28, waiting for transfers between devices, shift(): lax.ppermute(value, axis, [(i, (i + step) % size) for i in range(size)])  62.9 us
    ppermute x28, starting transfers between devices, shift(): lax.ppermute(value, axis, [(i, (i + step) % size) for i in range(size)])  45.8 us
    all_to_all x1, blocking collectives, body(): lax.all_to_all(send, ('y', 'x'), split_axis=0, concat_axis=0, tiled=True)  22.5 us
    all_gather x1, blocking collectives, body(): near_scores = lax.all_gather(masked, 'z', axis=0, tiled=True)  20.3 us
    all_to_all x1, waiting for transfers between devices, body(): lax.all_to_all(send, ('y', 'x'), split_axis=0, concat_axis=0, tiled=True)  17.8 us
    pallas_call x1, Pallas kernels, body(): pl.pallas_call(first_kernel, out_shape=(jax.ShapeDtypeStruct((NY * NX, SE...  15.8 us
    pallas_call x1, Pallas kernels, body(): pl.pallas_call(list_kernel, out_shape=jax.ShapeDtypeStruct((LIST,), jnp.i...  6.77 us
    unnamed x43, local copies, waits for them, and re-layouts  5.92 us
  transfers between devices with their start and end apart: 30, of which 11 were waited for; matrix products, arithmetic and copies ran while one was open for 6% of the time, Pallas kernels for 4%

profile of v3, /device:TPU:1, one launch (start us, length us, event | category | flops | bytes accessed | tf_op | source)
XLA Modules:
  0.0 247.3 jit_solution(9115523705060292378)
XLA Ops:
  6.5 1.3 fusion.2
  7.8 1.2 fusion.3
  11.4 1.5 broadcast_select_fusion
  12.9 1.1 pad_maximum_fusion.1
  14.0 2.5 %collective-permute-start = (bf16[256,1280]{1,0:T(8,128)(2,1)S(1)}, bf16[256,1280]{1,0:T(8,128)(2,1)}, u32[]{:S(2)}, u32[]{:S(2)}) collective-permute-start(bf16[256,1280]{1,0:T(8,128)(2,1)S(1)} %bitcast.15), channel_id=1, source_target_pairs={{0,8},{8,16},{16,24},{24,32},{32,40},{40,48},{48,56},{56,0},{1,9},... | collective-permute-start | bytes 1966088 | tf_op jit(solution)/shard_map/ppermute | solution.py:41
  16.5 4.0 %collective-permute-start.1 = (bf16[256,1280]{1,0:T(8,128)(2,1)S(1)}, bf16[256,1280]{1,0:T(8,128)(2,1)}, u32[]{:S(2)}, u32[]{:S(2)}) collective-permute-start(bf16[256,1280]{1,0:T(8,128)(2,1)S(1)} %bitcast.16), channel_id=1, source_target_pairs={{0,56},{8,0},{16,8},{24,16},{32,24},{40,32},{48,40},{56,48},{1,57}... | collective-permute-start | bytes 1966088 | tf_op jit(solution)/shard_map/ppermute | solution.py:41
  21.6 1.4 copy-done.2
  23.0 1.2 slice.26
  24.2 1.3 collective-permute-start.7
  25.4 1.4 collective-permute-start.8
  27.4 1.0 gather_fusion
  28.4 1.5 collective-permute-start.2
  29.9 29.7 %collective-permute-done.2 = s32[1,128]{1,0:T(1,128)S(1)} collective-permute-done((s32[1,128]{1,0:T(1,128)S(1)}, s32[1,128]{1,0:T(1,128)S(1)}, u32[]{:S(2)}, u32[]{:S(2)}) %collective-permute-start.2) | collective-permute-done | bytes 544 | tf_op jit(solution)/shard_map/ppermute | solution.py:41
  60.1 3.5 %collective-permute-done.3 = s32[1,128]{1,0:T(1,128)S(1)} collective-permute-done((s32[1,128]{1,0:T(1,128)S(1)}, s32[1,128]{1,0:T(1,128)S(1)}, u32[]{:S(2)}, u32[]{:S(2)}) %collective-permute-start.3) | collective-permute-done | bytes 544 | tf_op jit(solution)/shard_map/ppermute | solution.py:41
  63.5 1.3 collective-permute-start.4
  64.9 3.4 %collective-permute-done.4 = s32[1,128]{1,0:T(1,128)S(1)} collective-permute-done((s32[1,128]{1,0:T(1,128)S(1)}, s32[1,128]{1,0:T(1,128)S(1)}, u32[]{:S(2)}, u32[]{:S(2)}) %collective-permute-start.4) | collective-permute-done | bytes 544 | tf_op jit(solution)/shard_map/ppermute | solution.py:41
  68.3 2.7 %collective-permute-start.6 = (bf16[256,1280]{1,0:T(8,128)(2,1)}, bf16[256,1280]{1,0:T(8,128)(2,1)}, u32[]{:S(2)}, u32[]{:S(2)}) collective-permute-start(bf16[256,1280]{1,0:T(8,128)(2,1)} %collective-permute-done.1.refs_2_), channel_id=1, source_target_pairs={{0,56},{8,0},{16,8},{24,16},{32,24},{40,32},{48,40},{56,48},{1,57}... | collective-permute-start | bytes 1966088 | tf_op jit(solution)/shard_map/ppermute | solution.py:41
  71.0 2.8 %collective-permute-start.10 = (s32[4,128]{1,0:T(4,128)S(1)}, s32[4,128]{1,0:T(4,128)S(1)}, u32[]{:S(2)}, u32[]{:S(2)}) collective-permute-start(s32[4,128]{1,0:T(4,128)S(1)} %pad_add_fusion.1), channel_id=1, source_target_pairs={{0,2},{1,3},{2,0},{3,1},{4,6},{5,7},{6,4},{7,5},{8,10},{9,11},{10,... | collective-permute-start | bytes 6152 | tf_op jit(solution)/shard_map/ppermute | solution.py:41
  73.8 1.3 collective-permute-done.10
  75.1 1.5 collective-permute-start.11
  76.6 2.6 %collective-permute-done.11 = s32[4,128]{1,0:T(4,128)S(1)} collective-permute-done((s32[4,128]{1,0:T(4,128)S(1)}, s32[4,128]{1,0:T(4,128)S(1)}, u32[]{:S(2)}, u32[]{:S(2)}) %collective-permute-start.11) | collective-permute-done | bytes 2080 | tf_op jit(solution)/shard_map/ppermute | solution.py:41
  79.1 1.3 collective-permute-start.9
  80.4 1.6 collective-permute-done.9
  82.0 7.6 %collective-permute-start.16 = (bf16[256,1280]{1,0:T(8,128)(2,1)S(1)}, bf16[256,1280]{1,0:T(8,128)(2,1)S(1)}, u32[]{:S(2)}, u32[]{:S(2)}) collective-permute-start(bf16[256,1280]{1,0:T(8,128)(2,1)S(1)} %bitcast.17), channel_id=1, source_target_pairs={{0,4},{4,0},{1,5},{5,1},{2,6},{6,2},{3,7},{7,3},{8,12},{12,8},{9,1... | collective-permute-start | bytes 1966088 | tf_op jit(solution)/shard_map/ppermute | solution.py:41
  89.9 2.7 %collective-permute-start.13 = (bf16[256,1280]{1,0:T(8,128)(2,1)}, bf16[256,1280]{1,0:T(8,128)(2,1)}, u32[]{:S(2)}, u32[]{:S(2)}) collective-permute-start(bf16[256,1280]{1,0:T(8,128)(2,1)} %collective-permute-done.6.refs_4_), channel_id=1, source_target_pairs={{0,56},{8,0},{16,8},{24,16},{32,24},{40,32},{48,40},{56,48},{1,57}... | collective-permute-start | bytes 1966088 | tf_op jit(solution)/shard_map/ppermute | solution.py:41
  93.4 0.9 slice.21
  96.4 11.4 %collective-permute-done.12.refs_5_ = bf16[256,1280]{1,0:T(8,128)(2,1)} collective-permute-done((bf16[256,1280]{1,0:T(8,128)(2,1)}, bf16[256,1280]{1,0:T(8,128)(2,1)}, u32[]{:S(2)}, u32[]{:S(2)}) %collective-permute-start.12) | collective-permute-done | bytes 655392 | tf_op jit(solution)/shard_map/ppermute | solution.py:41
  107.9 2.6 %collective-permute-start.26 = (bf16[4,64,1152]{2,1,0:T(8,128)(2,1)}, bf16[4,64,1152]{2,1,0:T(8,128)(2,1)}, u32[]{:S(2)}, u32[]{:S(2)}) collective-permute-start(bf16[4,64,1152]{2,1,0:T(8,128)(2,1)} %slice.22), channel_id=1, source_target_pairs={{0,192},{64,0},{128,64},{192,128},{1,193},{65,1},{129,65},{193,129... | collective-permute-start | bytes 1769480 | tf_op jit(solution)/shard_map/ppermute | solution.py:41
  112.2 6.8 %shard_map.64.lst = s32[640]{0:T(1024)} custom-call(s32[2048]{0:T(1024)} %fusion.15.codes), custom_call_target="tpu_custom_call" | custom-call | tf_op jit(solution)/shard_map/pallas_call | solution.py:289
  119.0 1.0 slice.19
  119.9 1.0 slice.20
  121.0 1.4 collective-permute-start.20
  122.4 1.0 collective-permute-done.25
  123.4 1.7 collective-permute-start.15
  125.9 7.0 %collective-permute-done.14.refs_7_ = bf16[128,1280]{1,0:T(8,128)(2,1)S(1)} collective-permute-done((bf16[128,1280]{1,0:T(8,128)(2,1)S(1)}, bf16[128,1280]{1,0:T(8,128)(2,1)S(1)}, u32[]{:S(2)}, u32[]{:S(2)}) %collective-permute-start.14) | collective-permute-done | bytes 327712 | tf_op jit(solution)/shard_map/ppermute | solution.py:41
  132.9 0.9 collective-permute-start.23
  133.9 2.4 pad_maximum_fusion.refs_20_
  138.2 15.8 %shard_map.65 = (bf16[16,272,128]{2,1,0:T(8,128)(2,1)}, bf16[520,64,64]{2,1,0:T(8,128)(2,1)}) custom-call(s32[640]{0:T(1024)} %shard_map.64.lst, bf16[256,1280]{1,0:T(8,128)(2,1)} %bitcast.18, bf16[256,1280]{1,0:T(8,128)(2,1)} %collective-permute-done.refs_1_, bf16[256,1280]{1,0:T(8,128)(2,1)} %collective-permute-done.1.refs_2_, ...), custom_call_target="tpu_custom_call" | custom-call | tf_op jit(solution)/shard_map/pallas_call | solution.py:313
  154.0 4.1 %all-to-all-start = ((bf16[16,272,128]{2,1,0:T(8,128)(2,1)}), bf16[16,272,128]{2,1,0:T(8,128)(2,1)S(1)}, u32[]{:S(2)}, u32[]{:S(2)}) async-start(bf16[16,272,128]{2,1,0:T(8,128)(2,1)} %get-tuple-element.51), calls=%async_computation | async-start | bytes 2228224 | tf_op jit(solution)/shard_map/all_to_all | solution.py:331
  158.1 2.7 %shard_map.66 = (bf16[4,64,64]{2,1,0:T(8,128)(2,1)}, f32[4,64,256]{2,1,0:T(8,128)}) custom-call(bf16[256,1280]{1,0:T(8,128)(2,1)} %bitcast.19), custom_call_target="tpu_custom_call" | custom-call | tf_op jit(solution)/shard_map/pallas_call | solution.py:300
  160.8 17.8 %all-to-all-done.got = bf16[16,272,128]{2,1,0:T(8,128)(2,1)S(1)} async-done(((bf16[16,272,128]{2,1,0:T(8,128)(2,1)}), bf16[16,272,128]{2,1,0:T(8,128)(2,1)S(1)}, u32[]{:S(2)}, u32[]{:S(2)}) %all-to-all-start) | async-done | bytes 1114144 | tf_op jit(solution)/shard_map/all_to_all | solution.py:331
  179.6 2.4 shard_map.67
  182.0 20.3 %all_gather.7.near = bf16[32,64,128]{2,1,0:T(8,128)(2,1)S(1)} all-gather(bf16[4,64,128]{2,1,0:T(8,128)(2,1)} %get-tuple-element.54), channel_id=1, replica_groups=mesh['y'=4,'z'=8,'c'=2,'x'=4] {'z'}, dimensions={0}, use_global_device_ids=true | all-gather | bytes 589824 | tf_op jit(solution)/shard_map/all_gather | solution.py:343
  202.3 5.6 %collective-permute-start.27 = (bf16[32,64,128]{2,1,0:T(8,128)(2,1)S(1)}, bf16[32,64,128]{2,1,0:T(8,128)(2,1)S(1)}, u32[]{:S(2)}, u32[]{:S(2)}) collective-permute-start(bf16[32,64,128]{2,1,0:T(8,128)(2,1)S(1)} %all_gather.7.near), channel_id=1, source_target_pairs={{0,4},{4,0},{1,5},{5,1},{2,6},{6,2},{3,7},{7,3},{8,12},{12,8},{9,1... | collective-permute-start | bytes 1572872 | tf_op jit(solution)/shard_map/ppermute | solution.py:41
  207.9 1.5 collective-permute-done.27.far
  210.3 5.6 %shard_map.68 = bf16[64,64,128]{2,1,0:T(8,128)(2,1)} custom-call(s32[640]{0:T(1024)} %shard_map.64.lst, bf16[520,64,64]{2,1,0:T(8,128)(2,1)} %get-tuple-element.50.weights_in, bf16[32,64,128]{2,1,0:T(8,128)(2,1)} %copy-done.8, bf16[32,64,128]{2,1,0:T(8,128)(2,1)} %copy-done.14), custom_call_target="tpu_custom_call" | custom-call | tf_op jit(solution)/shard_map/pallas_call | solution.py:346
  215.9 22.5 %all_to_all.10 = bf16[64,64,128]{2,1,0:T(8,128)(2,1)} all-to-all(bf16[64,64,128]{2,1,0:T(8,128)(2,1)} %shard_map.68), channel_id=1, replica_groups=mesh['y'=4,'z'=8,'c'=2,'x'=4] {'y','x'}, dimensions={0} | all-to-all | bytes 2097152 | tf_op jit(solution)/shard_map/all_to_all | solution.py:358
  238.4 2.1 shard_map.69
  (110 shorter events, 13.8 us)
Async XLA Ops:
  6.5 20.8 %copy-start = (s32[1024]{0:T(1024)S(1)}, s32[1024]{0:T(1024)}, u32[]{:S(2)}) copy-start(s32[1024]{0:T(1024)} %param.11) | copy-start | bytes 12292
  6.5 130.5 %all-gather.2.cloned.1.call-start = ((), (), s32[]{:S(2)}) async-start(), calls=%async_computation.2 | async-start | bytes 5013504 | tf_op jit(solution)/shard_map/all_gather | solution.py:242
  9.9 10.7 %copy-start.1 = (bf16[16,64,1152]{2,1,0:T(8,128)(2,1)S(1)}, bf16[16,64,1152]{2,1,0:T(8,128)(2,1)}, u32[]{:S(2)}) copy-start(bf16[16,64,1152]{2,1,0:T(8,128)(2,1)} %param.6) | copy-start | bytes 7077892
  14.0 68.0 %copy-start.3 = (bf16[4,64,1280]{2,1,0:T(8,128)(2,1)}, bf16[4,64,1280]{2,1,0:T(8,128)(2,1)S(1)}, u32[]{:S(2)}) copy-start(bf16[4,64,1280]{2,1,0:T(8,128)(2,1)S(1)} %pad_maximum_fusion.1) | copy-start | bytes 1966084
  14.0 54.3 %collective-permute-start = (bf16[256,1280]{1,0:T(8,128)(2,1)S(1)}, bf16[256,1280]{1,0:T(8,128)(2,1)}, u32[]{:S(2)}, u32[]{:S(2)}) collective-permute-start(bf16[256,1280]{1,0:T(8,128)(2,1)S(1)} %bitcast.15), channel_id=1, source_target_pairs={{0,8},{8,16},{16,24},{24,32},{32,40},{40,48},{48,56},{56,0},{1,9},... | collective-permute-start | bytes 1966088 | tf_op jit(solution)/shard_map/ppermute | solution.py:41
  16.5 51.7 %collective-permute-start.1 = (bf16[256,1280]{1,0:T(8,128)(2,1)S(1)}, bf16[256,1280]{1,0:T(8,128)(2,1)}, u32[]{:S(2)}, u32[]{:S(2)}) collective-permute-start(bf16[256,1280]{1,0:T(8,128)(2,1)S(1)} %bitcast.16), channel_id=1, source_target_pairs={{0,56},{8,0},{16,8},{24,16},{32,24},{40,32},{48,40},{56,48},{1,57}... | collective-permute-start | bytes 1966088 | tf_op jit(solution)/shard_map/ppermute | solution.py:41
  21.6 1.4 copy-start.2
  21.6 5.3 %copy-start.20 = (s32[16]{0:T(128)S(1)}, s32[16]{0:T(128)}, u32[]{:S(2)}) copy-start(s32[16]{0:T(128)} %param.10) | copy-start | bytes 196
  21.6 5.4 %copy-start.19 = (s32[16,8]{0,1:T(8,128)S(1)}, s32[16,8]{0,1:T(8,128)}, u32[]{:S(2)}) copy-start(s32[16,8]{0,1:T(8,128)} %param.9) | copy-start | bytes 1540
  24.2 65.5 %collective-permute-start.7 = (bf16[8,64,1152]{2,1,0:T(8,128)(2,1)}, bf16[8,64,1152]{2,1,0:T(8,128)(2,1)S(1)}, u32[]{:S(2)}, u32[]{:S(2)}) collective-permute-start(bf16[8,64,1152]{2,1,0:T(8,128)(2,1)} %bitcast.4), channel_id=1, source_target_pairs={{0,64},{64,128},{128,192},{192,0},{1,65},{65,129},{129,193},{193,1... | collective-permute-start | bytes 3538952 | tf_op jit(solution)/shard_map/ppermute | solution.py:41
  25.4 64.2 %collective-permute-start.8 = (bf16[8,64,1152]{2,1,0:T(8,128)(2,1)}, bf16[8,64,1152]{2,1,0:T(8,128)(2,1)S(1)}, u32[]{:S(2)}, u32[]{:S(2)}) collective-permute-start(bf16[8,64,1152]{2,1,0:T(8,128)(2,1)} %bitcast.4), channel_id=1, source_target_pairs={{0,192},{64,0},{128,64},{192,128},{1,193},{65,1},{129,65},{193,129... | collective-permute-start | bytes 3538952 | tf_op jit(solution)/shard_map/ppermute | solution.py:41
  28.4 31.2 %collective-permute-start.2 = (s32[1,128]{1,0:T(1,128)S(1)}, s32[1,128]{1,0:T(1,128)S(1)}, u32[]{:S(2)}, u32[]{:S(2)}) collective-permute-start(s32[1,128]{1,0:T(1,128)S(1)} %fusion.22), channel_id=1, source_target_pairs={{0,192},{64,0},{128,64},{192,128},{1,193},{65,1},{129,65},{193,129... | collective-permute-start | bytes 1544 | tf_op jit(solution)/shard_map/ppermute | solution.py:41
  59.6 4.0 %collective-permute-start.3 = (s32[1,128]{1,0:T(1,128)S(1)}, s32[1,128]{1,0:T(1,128)S(1)}, u32[]{:S(2)}, u32[]{:S(2)}) collective-permute-start(s32[1,128]{1,0:T(1,128)S(1)} %fusion.22), channel_id=1, source_target_pairs={{0,128},{64,192},{128,0},{192,64},{1,129},{65,193},{129,1},{193,65... | collective-permute-start | bytes 1544 | tf_op jit(solution)/shard_map/ppermute | solution.py:41
  63.5 4.7 %collective-permute-start.4 = (s32[1,128]{1,0:T(1,128)S(1)}, s32[1,128]{1,0:T(1,128)S(1)}, u32[]{:S(2)}, u32[]{:S(2)}) collective-permute-start(s32[1,128]{1,0:T(1,128)S(1)} %fusion.22), channel_id=1, source_target_pairs={{0,64},{64,128},{128,192},{192,0},{1,65},{65,129},{129,193},{193,1... | collective-permute-start | bytes 1544 | tf_op jit(solution)/shard_map/ppermute | solution.py:41
  68.3 21.4 %collective-permute-start.5 = (bf16[256,1280]{1,0:T(8,128)(2,1)}, bf16[256,1280]{1,0:T(8,128)(2,1)}, u32[]{:S(2)}, u32[]{:S(2)}) collective-permute-start(bf16[256,1280]{1,0:T(8,128)(2,1)} %collective-permute-done.refs_1_), channel_id=1, source_target_pairs={{0,8},{8,16},{16,24},{24,32},{32,40},{40,48},{48,56},{56,0},{1,9},... | collective-permute-start | bytes 1966088 | tf_op jit(solution)/shard_map/ppermute | solution.py:41
  68.3 21.4 %collective-permute-start.6 = (bf16[256,1280]{1,0:T(8,128)(2,1)}, bf16[256,1280]{1,0:T(8,128)(2,1)}, u32[]{:S(2)}, u32[]{:S(2)}) collective-permute-start(bf16[256,1280]{1,0:T(8,128)(2,1)} %collective-permute-done.1.refs_2_), channel_id=1, source_target_pairs={{0,56},{8,0},{16,8},{24,16},{32,24},{40,32},{48,40},{56,48},{1,57}... | collective-permute-start | bytes 1966088 | tf_op jit(solution)/shard_map/ppermute | solution.py:41
  71.0 4.1 %collective-permute-start.10 = (s32[4,128]{1,0:T(4,128)S(1)}, s32[4,128]{1,0:T(4,128)S(1)}, u32[]{:S(2)}, u32[]{:S(2)}) collective-permute-start(s32[4,128]{1,0:T(4,128)S(1)} %pad_add_fusion.1), channel_id=1, source_target_pairs={{0,2},{1,3},{2,0},{3,1},{4,6},{5,7},{6,4},{7,5},{8,10},{9,11},{10,... | collective-permute-start | bytes 6152 | tf_op jit(solution)/shard_map/ppermute | solution.py:41
  75.1 4.0 %collective-permute-start.11 = (s32[4,128]{1,0:T(4,128)S(1)}, s32[4,128]{1,0:T(4,128)S(1)}, u32[]{:S(2)}, u32[]{:S(2)}) collective-permute-start(s32[4,128]{1,0:T(4,128)S(1)} %pad_add_fusion.1), channel_id=1, source_target_pairs={{0,1},{1,2},{2,3},{3,0},{4,5},{5,6},{6,7},{7,4},{8,9},{9,10},{10,1... | collective-permute-start | bytes 6152 | tf_op jit(solution)/shard_map/ppermute | solution.py:41
  79.1 2.8 %collective-permute-start.9 = (s32[4,128]{1,0:T(4,128)S(1)}, s32[4,128]{1,0:T(4,128)S(1)}, u32[]{:S(2)}, u32[]{:S(2)}) collective-permute-start(s32[4,128]{1,0:T(4,128)S(1)} %pad_add_fusion.1), channel_id=1, source_target_pairs={{0,3},{1,0},{2,1},{3,2},{4,7},{5,4},{6,5},{7,6},{8,11},{9,8},{10,9... | collective-permute-start | bytes 6152 | tf_op jit(solution)/shard_map/ppermute | solution.py:41
  82.0 13.2 %collective-permute-start.16 = (bf16[256,1280]{1,0:T(8,128)(2,1)S(1)}, bf16[256,1280]{1,0:T(8,128)(2,1)S(1)}, u32[]{:S(2)}, u32[]{:S(2)}) collective-permute-start(bf16[256,1280]{1,0:T(8,128)(2,1)S(1)} %bitcast.17), channel_id=1, source_target_pairs={{0,4},{4,0},{1,5},{5,1},{2,6},{6,2},{3,7},{7,3},{8,12},{12,8},{9,1... | collective-permute-start | bytes 1966088 | tf_op jit(solution)/shard_map/ppermute | solution.py:41
  89.6 21.1 %copy-start.6 = (bf16[8,64,1152]{2,1,0:T(8,128)(2,1)}, bf16[8,64,1152]{2,1,0:T(8,128)(2,1)S(1)}, u32[]{:S(2)}) copy-start(bf16[8,64,1152]{2,1,0:T(8,128)(2,1)S(1)} %collective-permute-done.7.refs_21_) | copy-start | bytes 3538948
  89.6 21.1 %copy-start.7 = (bf16[8,64,1152]{2,1,0:T(8,128)(2,1)}, bf16[8,64,1152]{2,1,0:T(8,128)(2,1)S(1)}, u32[]{:S(2)}) copy-start(bf16[8,64,1152]{2,1,0:T(8,128)(2,1)S(1)} %collective-permute-done.8.refs_19_) | copy-start | bytes 3538948
  89.7 18.1 %collective-permute-start.12 = (bf16[256,1280]{1,0:T(8,128)(2,1)}, bf16[256,1280]{1,0:T(8,128)(2,1)}, u32[]{:S(2)}, u32[]{:S(2)}) collective-permute-start(bf16[256,1280]{1,0:T(8,128)(2,1)} %collective-permute-done.5.refs_3_), channel_id=1, source_target_pairs={{0,8},{8,16},{16,24},{24,32},{32,40},{40,48},{48,56},{56,0},{1,9},... | collective-permute-start | bytes 1966088 | tf_op jit(solution)/shard_map/ppermute | solution.py:41
  89.9 18.0 %collective-permute-start.13 = (bf16[256,1280]{1,0:T(8,128)(2,1)}, bf16[256,1280]{1,0:T(8,128)(2,1)}, u32[]{:S(2)}, u32[]{:S(2)}) collective-permute-start(bf16[256,1280]{1,0:T(8,128)(2,1)} %collective-permute-done.6.refs_4_), channel_id=1, source_target_pairs={{0,56},{8,0},{16,8},{24,16},{32,24},{40,32},{48,40},{56,48},{1,57}... | collective-permute-start | bytes 1966088 | tf_op jit(solution)/shard_map/ppermute | solution.py:41
  92.6 28.3 %collective-permute-start.17 = (bf16[256,1280]{1,0:T(8,128)(2,1)}, bf16[256,1280]{1,0:T(8,128)(2,1)}, u32[]{:S(2)}, u32[]{:S(2)}) collective-permute-start(bf16[256,1280]{1,0:T(8,128)(2,1)} %collective-permute-done.refs_1_), channel_id=1, source_target_pairs={{0,4},{4,0},{1,5},{5,1},{2,6},{6,2},{3,7},{7,3},{8,12},{12,8},{9,1... | collective-permute-start | bytes 1966088 | tf_op jit(solution)/shard_map/ppermute | solution.py:41
  93.3 29.1 %collective-permute-start.18 = (bf16[256,1280]{1,0:T(8,128)(2,1)}, bf16[256,1280]{1,0:T(8,128)(2,1)}, u32[]{:S(2)}, u32[]{:S(2)}) collective-permute-start(bf16[256,1280]{1,0:T(8,128)(2,1)} %collective-permute-done.1.refs_2_), channel_id=1, source_target_pairs={{0,4},{4,0},{1,5},{5,1},{2,6},{6,2},{3,7},{7,3},{8,12},{12,8},{9,1... | collective-permute-start | bytes 1966088 | tf_op jit(solution)/shard_map/ppermute | solution.py:41
  95.2 0.9 copy-start.9
  96.0 29.7 %collective-permute-start.19 = (bf16[256,1280]{1,0:T(8,128)(2,1)}, bf16[256,1280]{1,0:T(8,128)(2,1)S(1)}, u32[]{:S(2)}, u32[]{:S(2)}) collective-permute-start(bf16[256,1280]{1,0:T(8,128)(2,1)} %collective-permute-done.5.refs_3_), channel_id=1, source_target_pairs={{0,4},{4,0},{1,5},{5,1},{2,6},{6,2},{3,7},{7,3},{8,12},{12,8},{9,1... | collective-permute-start | bytes 1966088 | tf_op jit(solution)/shard_map/ppermute | solution.py:41
  107.8 15.6 %collective-permute-start.25 = (bf16[4,64,1152]{2,1,0:T(8,128)(2,1)}, bf16[4,64,1152]{2,1,0:T(8,128)(2,1)}, u32[]{:S(2)}, u32[]{:S(2)}) collective-permute-start(bf16[4,64,1152]{2,1,0:T(8,128)(2,1)} %slice.21), channel_id=1, source_target_pairs={{0,64},{64,128},{128,192},{192,0},{1,65},{65,129},{129,193},{193,1... | collective-permute-start | bytes 1769480 | tf_op jit(solution)/shard_map/ppermute | solution.py:41
  107.9 17.2 %collective-permute-start.26 = (bf16[4,64,1152]{2,1,0:T(8,128)(2,1)}, bf16[4,64,1152]{2,1,0:T(8,128)(2,1)}, u32[]{:S(2)}, u32[]{:S(2)}) collective-permute-start(bf16[4,64,1152]{2,1,0:T(8,128)(2,1)} %slice.22), channel_id=1, source_target_pairs={{0,192},{64,0},{128,64},{192,128},{1,193},{65,1},{129,65},{193,129... | collective-permute-start | bytes 1769480 | tf_op jit(solution)/shard_map/ppermute | solution.py:41
  121.0 15.3 %collective-permute-start.20 = (bf16[256,1280]{1,0:T(8,128)(2,1)}, bf16[256,1280]{1,0:T(8,128)(2,1)S(1)}, u32[]{:S(2)}, u32[]{:S(2)}) collective-permute-start(bf16[256,1280]{1,0:T(8,128)(2,1)} %collective-permute-done.6.refs_4_), channel_id=1, source_target_pairs={{0,4},{4,0},{1,5},{5,1},{2,6},{6,2},{3,7},{7,3},{8,12},{12,8},{9,1... | collective-permute-start | bytes 1966088 | tf_op jit(solution)/shard_map/ppermute | solution.py:41
  122.4 10.5 %collective-permute-start.14 = (bf16[128,1280]{1,0:T(8,128)(2,1)S(1)}, bf16[128,1280]{1,0:T(8,128)(2,1)S(1)}, u32[]{:S(2)}, u32[]{:S(2)}) collective-permute-start(bf16[128,1280]{1,0:T(8,128)(2,1)S(1)} %slice.19), channel_id=1, source_target_pairs={{0,8},{8,16},{16,24},{24,32},{32,40},{40,48},{48,56},{56,0},{1,9},... | collective-permute-start | bytes 983048 | tf_op jit(solution)/shard_map/ppermute | solution.py:41
  123.4 10.4 %collective-permute-start.15 = (bf16[128,1280]{1,0:T(8,128)(2,1)S(1)}, bf16[128,1280]{1,0:T(8,128)(2,1)S(1)}, u32[]{:S(2)}, u32[]{:S(2)}) collective-permute-start(bf16[128,1280]{1,0:T(8,128)(2,1)S(1)} %slice.20), channel_id=1, source_target_pairs={{0,56},{8,0},{16,8},{24,16},{32,24},{40,32},{48,40},{56,48},{1,57}... | collective-permute-start | bytes 983048 | tf_op jit(solution)/shard_map/ppermute | solution.py:41
  125.1 11.2 %collective-permute-start.21 = (bf16[256,1280]{1,0:T(8,128)(2,1)}, bf16[256,1280]{1,0:T(8,128)(2,1)S(1)}, u32[]{:S(2)}, u32[]{:S(2)}) collective-permute-start(bf16[256,1280]{1,0:T(8,128)(2,1)} %collective-permute-done.12.refs_5_), channel_id=1, source_target_pairs={{0,4},{4,0},{1,5},{5,1},{2,6},{6,2},{3,7},{7,3},{8,12},{12,8},{9,1... | collective-permute-start | bytes 1966088 | tf_op jit(solution)/shard_map/ppermute | solution.py:41
  125.8 11.3 %copy-start.10 = (bf16[256,1280]{1,0:T(8,128)(2,1)}, bf16[256,1280]{1,0:T(8,128)(2,1)S(1)}, u32[]{:S(2)}) copy-start(bf16[256,1280]{1,0:T(8,128)(2,1)S(1)} %collective-permute-done.19.refs_12_) | copy-start | bytes 1966084
  125.8 11.3 %collective-permute-start.22 = (bf16[256,1280]{1,0:T(8,128)(2,1)}, bf16[256,1280]{1,0:T(8,128)(2,1)S(1)}, u32[]{:S(2)}, u32[]{:S(2)}) collective-permute-start(bf16[256,1280]{1,0:T(8,128)(2,1)} %collective-permute-done.13.refs_6_), channel_id=1, source_target_pairs={{0,4},{4,0},{1,5},{5,1},{2,6},{6,2},{3,7},{7,3},{8,12},{12,8},{9,1... | collective-permute-start | bytes 1966088 | tf_op jit(solution)/shard_map/ppermute | solution.py:41
  132.9 4.2 %copy-start.15 = (bf16[128,1280]{1,0:T(8,128)(2,1)}, bf16[128,1280]{1,0:T(8,128)(2,1)S(1)}, u32[]{:S(2)}) copy-start(bf16[128,1280]{1,0:T(8,128)(2,1)S(1)} %collective-permute-done.14.refs_7_) | copy-start | bytes 983044
  132.9 3.4 %collective-permute-start.23 = (bf16[128,1280]{1,0:T(8,128)(2,1)S(1)}, bf16[128,1280]{1,0:T(8,128)(2,1)S(1)}, u32[]{:S(2)}, u32[]{:S(2)}) collective-permute-start(bf16[128,1280]{1,0:T(8,128)(2,1)S(1)} %collective-permute-done.14.refs_7_), channel_id=1, source_target_pairs={{0,4},{4,0},{1,5},{5,1},{2,6},{6,2},{3,7},{7,3},{8,12},{12,8},{9,1... | collective-permute-start | bytes 983048 | tf_op jit(solution)/shard_map/ppermute | solution.py:41
  133.8 2.6 %copy-start.16 = (bf16[128,1280]{1,0:T(8,128)(2,1)}, bf16[128,1280]{1,0:T(8,128)(2,1)S(1)}, u32[]{:S(2)}) copy-start(bf16[128,1280]{1,0:T(8,128)(2,1)S(1)} %collective-permute-done.15.refs_8_) | copy-start | bytes 983044
  133.8 2.6 %collective-permute-start.24 = (bf16[128,1280]{1,0:T(8,128)(2,1)S(1)}, bf16[128,1280]{1,0:T(8,128)(2,1)S(1)}, u32[]{:S(2)}, u32[]{:S(2)}) collective-permute-start(bf16[128,1280]{1,0:T(8,128)(2,1)S(1)} %collective-permute-done.15.refs_8_), channel_id=1, source_target_pairs={{0,4},{4,0},{1,5},{5,1},{2,6},{6,2},{3,7},{7,3},{8,12},{12,8},{9,1... | collective-permute-start | bytes 983048 | tf_op jit(solution)/shard_map/ppermute | solution.py:41
  136.3 0.9 copy-start.11
  136.3 1.0 copy-start.18
  137.1 0.8 copy-start.12
  137.1 1.1 copy-start.13
  154.0 24.6 %all-to-all-start = ((bf16[16,272,128]{2,1,0:T(8,128)(2,1)}), bf16[16,272,128]{2,1,0:T(8,128)(2,1)S(1)}, u32[]{:S(2)}, u32[]{:S(2)}) async-start(bf16[16,272,128]{2,1,0:T(8,128)(2,1)} %get-tuple-element.51), calls=%async_computation | async-start | bytes 2228224 | tf_op jit(solution)/shard_map/all_to_all | solution.py:331
  178.6 1.0 copy-start.4
  202.3 7.2 %copy-start.8 = (bf16[32,64,128]{2,1,0:T(8,128)(2,1)}, bf16[32,64,128]{2,1,0:T(8,128)(2,1)S(1)}, u32[]{:S(2)}) copy-start(bf16[32,64,128]{2,1,0:T(8,128)(2,1)S(1)} %all_gather.7.near) | copy-start | bytes 1572868
  202.3 7.2 %collective-permute-start.27 = (bf16[32,64,128]{2,1,0:T(8,128)(2,1)S(1)}, bf16[32,64,128]{2,1,0:T(8,128)(2,1)S(1)}, u32[]{:S(2)}, u32[]{:S(2)}) collective-permute-start(bf16[32,64,128]{2,1,0:T(8,128)(2,1)S(1)} %all_gather.7.near), channel_id=1, source_target_pairs={{0,4},{4,0},{1,5},{5,1},{2,6},{6,2},{3,7},{7,3},{8,12},{12,8},{9,1... | collective-permute-start | bytes 1572872 | tf_op jit(solution)/shard_map/ppermute | solution.py:41
  (3 other events, 2.4 us)
Sparse Core Ops, SparseCore 0:
  10.8 66.9 all-gather.1

commit v4 on v3

--- a/solution.py
+++ b/solution.py
@@ -28,6 +28,8 @@
 PIECE = PART * FRAMES
 HALF = PIECE // 2
 SEND = PIECE + 16
+SHARED_ROWS = SHARED * FRAMES
+CELL = SHARED_ROWS + 16
 LIST = 640
 STEPS_AT = 600
 SPARE = QBLOCKS
@@ -88,10 +90,17 @@
             copies.append(pltpu.make_async_copy(piece, k.at[side, pl.ds(at, rows)], sems.at[len(copies)]))
             at += rows
     at = 0
-    for part in queries:
+    for part in queries[:4]:
         rows = part.shape[0]
         copies.append(pltpu.make_async_copy(part, q.at[pl.ds(at, rows)], sems.at[len(copies)]))
         at += rows
+    for d in range(NY * NX):
+        copies.append(
+            pltpu.make_async_copy(
+                queries[4].at[d, pl.ds(0, SHARED_ROWS)], q.at[pl.ds(at, SHARED_ROWS)], sems.at[len(copies)]
+            )
+        )
+        at += SHARED_ROWS
     for copy in copies:
         copy.start()
     acc[...] = jnp.zeros_like(acc)
@@ -105,7 +114,7 @@
         rows = [pl.multiple_of(((code >> 7) & 31) * FRAMES, FRAMES) for code in codes]
         weights = []
         for code, side, row in zip(codes, sides, rows):
-            units = q[(code >> 18) & 127]
+            units = q[pl.ds(pl.multiple_of(((code >> 18) & 127) * FRAMES, FRAMES), FRAMES), :]
             keys = k[side, pl.ds(row, FRAMES), pl.ds(0, FEAT)]
             affinity = lax.dot_general(
                 units, keys, (((1,), (1,)), ((), ())), preferred_element_type=jnp.float32
@@ -199,7 +208,8 @@
         denominator[b] = full
         mixed = keep_share * total / full + (1.0 - keep_share) * prior[b].astype(jnp.float32)
         keep = (mixed.astype(jnp.bfloat16).astype(jnp.float32) * marks[b].astype(jnp.float32)).astype(jnp.bfloat16)
-        masked[b] = keep
+        for d in range(NZ):
+            masked[d, b] = keep
         own_second[b] = jnp.dot(weights[b], keep, preferred_element_type=jnp.float32)
 
 
@@ -236,35 +246,52 @@
 
     target = jnp.take(block_home, neighbour_ids.reshape(-1), axis=0)
     column = x * per_list + jnp.arange(per_list, dtype=jnp.int32)
-    in_list = column[None, :] < neighbour_count[:, None]
-    target = jnp.where(in_list.reshape(-1), target, -1).reshape(1, ROWS * per_list)
-
-    shared = lax.all_gather(units[:SHARED], ("y", "x"), axis=0, tiled=True)
+    in_list = (column[None, :] < neighbour_count[:, None]).reshape(-1)
+    numbers = jnp.concatenate([jnp.where(in_list, target // 32, -1), target % 32]).astype(jnp.bfloat16)
+    numbers = jnp.pad(numbers[None, :], ((0, CELL - SHARED_ROWS - 1), (0, FEAT - 2 * ROWS * per_list)))
+    shared = jnp.concatenate([units[:SHARED].reshape(SHARED_ROWS, FEAT), numbers], axis=0)
+
+    shared = lax.all_gather(shared, ("y", "x"), axis=0)
     up, down = shift(piece, "z", 1), shift(piece, "z", -1)
     embeddings, piece = lax.optimization_barrier((embeddings, piece))
     all_units = normalize(embeddings)
-    straight = all_units.reshape(NX, PART, FRAMES, FEAT)[:, SHARED:].reshape(STRAIGHT, FRAMES, FEAT)
+    straight = all_units.reshape(NX, PART, FRAMES, FEAT)[:, SHARED:].reshape(STRAIGHT * FRAMES, FEAT)
     behind, ahead = shift(straight, "y", 1), shift(straight, "y", -1)
-    targets = [target, shift(target, "y", -1), shift(target, "y", 2), shift(target, "y", 1)]
-
-    up, down, targets = lax.optimization_barrier((up, down, targets))
+
+    up, down = lax.optimization_barrier((up, down))
     near = [piece, up, down]
     far = [shift(v, "c", 1) for v in near]
     up, down = shift(up, "z", 1), shift(down, "z", -1)
-    target = jnp.concatenate(targets, axis=0)
-    targets = [target, shift(target, "x", -1), shift(target, "x", 2), shift(target, "x", 1)]
-
-    up, down, behind, ahead, targets = lax.optimization_barrier((up, down, behind, ahead, targets))
-    half = STRAIGHT // 2
+
+    up, down, behind, ahead = lax.optimization_barrier((up, down, behind, ahead))
+    half = STRAIGHT * FRAMES // 2
     across_a, across_b = shift(behind[:half], "y", 1), shift(ahead[half:], "y", -1)
     held = [up, down]
     up, down = shift(up, "z", 1), shift(down, "z", -1)
     near += held
     far += [shift(v, "c", 1) for v in held]
-    target = jnp.stack(targets, axis=0).reshape(NX, NY, ROWS, per_list)
-    distance = jnp.arange(NY, dtype=jnp.int32)[None, :, None, None]
+    own_weights, own_base = pl.pallas_call(
+        own_kernel,
+        out_shape=(
+            jax.ShapeDtypeStruct((PART, FRAMES, FRAMES), jnp.bfloat16),
+            jax.ShapeDtypeStruct((PART, FRAMES, 2 * CH), jnp.float32),
+        ),
+        in_specs=[vmem],
+        out_specs=(vmem, vmem),
+    )(piece)
+
+    last_up, last_down = shift(up[:HALF], "z", 1), shift(down[HALF:], "z", -1)
+    near += [up, down]
+    far += [shift(up, "c", 1), shift(down, "c", 1)]
+    across = jnp.concatenate([across_a, across_b], axis=0)
+
+    shared, _, own_base = lax.optimization_barrier((shared, up, own_base))
+    entries = ROWS * per_list
+    numbers = shared[:, SHARED_ROWS, :2 * entries].astype(jnp.int32)
+    target = (numbers[:, :entries] * 32 + numbers[:, entries:]).reshape(NY, NX, ROWS, per_list)
+    source_y = jnp.arange(NY, dtype=jnp.int32)[:, None, None, None]
     source_row = jnp.arange(ROWS, dtype=jnp.int32)[None, None, :, None]
-    source_y = (y + distance) % NY
+    distance = (source_y - y) % NY
     source = source_y * ROWS + source_row
     wanted = (target >= 0) & (target // 256 == y) & ((target % 16) // PART == x)
     place = (target // 16) % 16
@@ -293,22 +320,9 @@
         out_specs=smem,
     )(codes)
 
-    up, down, lst = lax.optimization_barrier((up, down, lst))
-    last_up, last_down = shift(up[:HALF], "z", 1), shift(down[HALF:], "z", -1)
-    near += [up, down]
-    far += [shift(up, "c", 1), shift(down, "c", 1)]
-    own_weights, own_base = pl.pallas_call(
-        own_kernel,
-        out_shape=(
-            jax.ShapeDtypeStruct((PART, FRAMES, FRAMES), jnp.bfloat16),
-            jax.ShapeDtypeStruct((PART, FRAMES, 2 * CH), jnp.float32),
-        ),
-        in_specs=[vmem],
-        out_specs=(vmem, vmem),
-    )(piece)
+    last_up, last_down, lst = lax.optimization_barrier((last_up, last_down, lst))
     near += [last_up, last_down]
     far += [shift(last_up, "c", 1), shift(last_down, "c", 1)]
-    across = jnp.concatenate([across_a, across_b], axis=0)
 
     send, weights = pl.pallas_call(
         first_kernel,
@@ -319,28 +333,29 @@
         in_specs=[smem] + [hbm] * 23,
         out_specs=(vmem, hbm),
         scratch_shapes=[
-            pltpu.VMEM((Q_ALL, FRAMES, FEAT), jnp.bfloat16),
+            pltpu.VMEM((Q_ALL * FRAMES, FEAT), jnp.bfloat16),
             pltpu.VMEM((NC, NZ * PIECE, WIDE), jnp.bfloat16),
             pltpu.VMEM((QBLOCKS + 1, FRAMES, 2 * CH), jnp.float32),
             pltpu.VMEM((SLOTS, FRAMES, FRAMES), jnp.bfloat16),
-            pltpu.SemaphoreType.DMA((23,)),
+            pltpu.SemaphoreType.DMA((22 + NY * NX,)),
             pltpu.SemaphoreType.DMA,
         ],
         compiler_params=params,
-    )(lst, *near, *far, all_units, ahead, across, behind, shared)
+    )(lst, *near, *far, all_units.reshape(ROWS * FRAMES, FEAT), ahead, across, behind, shared)
     got = lax.all_to_all(send, ("y", "x"), split_axis=0, concat_axis=0, tiled=True)
 
     masked, denominator, own_second = pl.pallas_call(
         mix_kernel,
         out_shape=(
-            jax.ShapeDtypeStruct((PART, FRAMES, CH), jnp.bfloat16),
+            jax.ShapeDtypeStruct((NZ, PART, FRAMES, CH), jnp.bfloat16),
             jax.ShapeDtypeStruct((PART, FRAMES, CH), jnp.float32),
             jax.ShapeDtypeStruct((PART, FRAMES, CH), jnp.float32),
         ),
         in_specs=[vmem] * 5,
         out_specs=(vmem,) * 3,
     )(got, own_base, own_weights, prior, marks)
-    near_scores = lax.all_gather(masked, "z", axis=0, tiled=True)
+    near_scores = lax.all_to_all(masked, "z", split_axis=0, concat_axis=0, tiled=True)
+    near_scores = near_scores.reshape(NZ * PART, FRAMES, CH)
     far_scores = shift(near_scores, "c", 1)
 
     send = pl.pallas_call(

time: 247 us -> 213 us (0.86)
  waiting for transfers between devices: 80.8 us -> 38.8 us
  blocking collectives: 42.8 us -> 65.7 us
  starting transfers between devices: 49.9 us -> 32.6 us
  other arithmetic: 10.2 us -> 12.8 us
    ppermute x28 -> x22, waiting for transfers between devices: 62.9 us -> 38.8 us  [shift(): lax.ppermute(value, axis, [(i, (i + step) % size) for i in range(size)])]
    all_to_all x0 -> x1, blocking collectives: none -> 22.1 us  [body(): lax.all_to_all(masked, 'z', split_axis=0, concat_axis=0, tiled=True)]
    all_to_all x1 -> x2, blocking collectives: 22.5 us -> 43.6 us  [body(): lax.all_to_all(send, ('y', 'x'), split_axis=0, concat_axis=0, tiled=True)]
    all_gather x1 -> x0, blocking collectives: 20.3 us -> none  [body(): near_scores = lax.all_gather(masked, 'z', axis=0, tiled=True)]
    all_to_all x1 -> x0, waiting for transfers between devices: 17.8 us -> none  [body(): lax.all_to_all(send, ('y', 'x'), split_axis=0, concat_axis=0, tiled=True)]
    ppermute x28 -> x22, starting transfers between devices: 45.8 us -> 32.6 us  [shift(): lax.ppermute(value, axis, [(i, (i + step) % size) for i in range(size)])]
    all_to_all x1 -> x0, starting transfers between devices: 4.06 us -> none  [body(): lax.all_to_all(send, ('y', 'x'), split_axis=0, concat_axis=0, tiled=True)]
    unnamed x43 -> x44, local copies, waits for them, and re-layouts: 5.92 us -> 6.39 us
  transfers between devices with their start and end apart: 30 -> 23, of which waited for: 11 -> 6; matrix products, arithmetic and copies ran while one was open for 6% -> 7% of each run, Pallas kernels for 4% -> 4%
where the time goes in v4:
time: 213 us; the launch traced here: 212 us
  blocking collectives  65.7 us (31%)
  waiting for transfers between devices  38.8 us (18%)
  Pallas kernels  33.8 us (16%)
  starting transfers between devices  32.6 us (15%)
  local copies, waits for them, and re-layouts  14.5 us (7%)
  between operations  13.8 us (6%)
  other arithmetic  12.8 us (6%)
    all_to_all x2, blocking collectives, body(): lax.all_to_all(send, ('y', 'x'), split_axis=0, concat_axis=0, tiled=True)  43.6 us
    ppermute x22, waiting for transfers between devices, shift(): lax.ppermute(value, axis, [(i, (i + step) % size) for i in range(size)])  38.8 us
    ppermute x22, starting transfers between devices, shift(): lax.ppermute(value, axis, [(i, (i + step) % size) for i in range(size)])  32.6 us
    all_to_all x1, blocking collectives, body(): lax.all_to_all(masked, 'z', split_axis=0, concat_axis=0, tiled=True)  22.1 us
    pallas_call x1, Pallas kernels, body(): pl.pallas_call(first_kernel, out_shape=(jax.ShapeDtypeStruct((NY * NX, SE...  14.6 us
    pallas_call x1, Pallas kernels, body(): pl.pallas_call(list_kernel, out_shape=jax.ShapeDtypeStruct((LIST,), jnp.i...  6.77 us
    unnamed x44, local copies, waits for them, and re-layouts  6.39 us
    pallas_call x1, Pallas kernels, body(): pl.pallas_call(second_kernel, out_shape=jax.ShapeDtypeStruct((QBLOCKS, FR...  5.11 us
  transfers between devices with their start and end apart: 23, of which 6 were waited for; matrix products, arithmetic and copies ran while one was open for 7% of the time, Pallas kernels for 4%

profile of v4, /device:TPU:1, one launch (start us, length us, event | category | flops | bytes accessed | tf_op | source)
XLA Modules:
  0.0 212.0 jit_solution(8950352864766868339)
XLA Ops:
  6.5 0.8 copy.9
  7.5 1.3 fusion.2
  8.8 1.4 fusion.3
  10.2 0.8 copy-done.5
  11.3 1.0 gather_fusion
  12.3 0.7 pad_maximum_fusion.2
  13.1 0.9 broadcast_compare_fusion.1
  13.9 1.5 broadcast_select_fusion
  15.4 1.1 pad_maximum_fusion.1
  16.5 2.5 %collective-permute-start = (bf16[256,1280]{1,0:T(8,128)(2,1)S(1)}, bf16[256,1280]{1,0:T(8,128)(2,1)S(1)}, u32[]{:S(2)}, u32[]{:S(2)}) collective-permute-start(bf16[256,1280]{1,0:T(8,128)(2,1)S(1)} %bitcast.27), channel_id=1, source_target_pairs={{0,8},{8,16},{16,24},{24,32},{32,40},{40,48},{48,56},{56,0},{1,9},... | collective-permute-start | bytes 1966088 | tf_op jit(solution)/shard_map/ppermute | solution.py:43
  19.1 4.0 %collective-permute-start.1 = (bf16[256,1280]{1,0:T(8,128)(2,1)S(1)}, bf16[256,1280]{1,0:T(8,128)(2,1)S(1)}, u32[]{:S(2)}, u32[]{:S(2)}) collective-permute-start(bf16[256,1280]{1,0:T(8,128)(2,1)S(1)} %bitcast.28), channel_id=1, source_target_pairs={{0,56},{8,0},{16,8},{24,16},{32,24},{40,32},{48,40},{56,48},{1,57}... | collective-permute-start | bytes 1966088 | tf_op jit(solution)/shard_map/ppermute | solution.py:43
  24.2 1.4 collective-permute-start.4
  25.6 1.5 collective-permute-start.5
  27.1 10.4 %collective-permute-done.refs_1_ = bf16[256,1280]{1,0:T(8,128)(2,1)S(1)} collective-permute-done((bf16[256,1280]{1,0:T(8,128)(2,1)S(1)}, bf16[256,1280]{1,0:T(8,128)(2,1)S(1)}, u32[]{:S(2)}, u32[]{:S(2)}) %collective-permute-start) | collective-permute-done | bytes 655392 | tf_op jit(solution)/shard_map/ppermute | solution.py:43
  37.7 2.7 %collective-permute-start.3 = (bf16[256,1280]{1,0:T(8,128)(2,1)S(1)}, bf16[256,1280]{1,0:T(8,128)(2,1)S(1)}, u32[]{:S(2)}, u32[]{:S(2)}) collective-permute-start(bf16[256,1280]{1,0:T(8,128)(2,1)S(1)} %collective-permute-done.1.refs_2_), channel_id=1, source_target_pairs={{0,56},{8,0},{16,8},{24,16},{32,24},{40,32},{48,40},{56,48},{1,57}... | collective-permute-start | bytes 1966088 | tf_op jit(solution)/shard_map/ppermute | solution.py:43
  40.3 17.2 %collective-permute-done.4.refs_21_ = bf16[512,1152]{1,0:T(8,128)(2,1)S(1)} collective-permute-done((bf16[512,1152]{1,0:T(8,128)(2,1)S(1)}, bf16[512,1152]{1,0:T(8,128)(2,1)S(1)}, u32[]{:S(2)}, u32[]{:S(2)}) %collective-permute-start.4) | collective-permute-done | bytes 1179680 | tf_op jit(solution)/shard_map/ppermute | solution.py:43
  57.5 1.0 copy-done.6
  59.4 3.0 %collective-permute-start.10 = (bf16[256,1280]{1,0:T(8,128)(2,1)S(1)}, bf16[256,1280]{1,0:T(8,128)(2,1)}, u32[]{:S(2)}, u32[]{:S(2)}) collective-permute-start(bf16[256,1280]{1,0:T(8,128)(2,1)S(1)} %bitcast.29), channel_id=1, source_target_pairs={{0,4},{4,0},{1,5},{5,1},{2,6},{6,2},{3,7},{7,3},{8,12},{12,8},{9,1... | collective-permute-start | bytes 1966088 | tf_op jit(solution)/shard_map/ppermute | solution.py:43
  62.4 2.0 collective-permute-start.8
  65.0 1.9 slice.34
  67.0 6.6 %collective-permute-done.6.refs_5_ = bf16[256,1280]{1,0:T(8,128)(2,1)} collective-permute-done((bf16[256,1280]{1,0:T(8,128)(2,1)}, bf16[256,1280]{1,0:T(8,128)(2,1)}, u32[]{:S(2)}, u32[]{:S(2)}) %collective-permute-start.6) | collective-permute-done | bytes 655392 | tf_op jit(solution)/shard_map/ppermute | solution.py:43
  74.2 2.7 %shard_map.64 = (bf16[4,64,64]{2,1,0:T(8,128)(2,1)}, f32[4,64,256]{2,1,0:T(8,128)}) custom-call(bf16[256,1280]{1,0:T(8,128)(2,1)} %bitcast.30), custom_call_target="tpu_custom_call" | custom-call | tf_op jit(solution)/shard_map/pallas_call | solution.py:273
  77.1 1.0 slice.39
  78.2 1.0 collective-permute-done.8.refs_6_
  79.2 1.0 slice.40
  80.2 3.2 %collective-permute-start.9 = (bf16[128,1280]{1,0:T(8,128)(2,1)S(1)}, bf16[128,1280]{1,0:T(8,128)(2,1)}, u32[]{:S(2)}, u32[]{:S(2)}) collective-permute-start(bf16[128,1280]{1,0:T(8,128)(2,1)S(1)} %slice.40), channel_id=1, source_target_pairs={{0,56},{8,0},{16,8},{24,16},{32,24},{40,32},{48,40},{56,48},{1,57}... | collective-permute-start | bytes 983048 | tf_op jit(solution)/shard_map/ppermute | solution.py:43
  83.4 1.1 slice.35
  84.5 2.8 %collective-permute-start.13 = (bf16[256,1280]{1,0:T(8,128)(2,1)}, bf16[256,1280]{1,0:T(8,128)(2,1)S(1)}, u32[]{:S(2)}, u32[]{:S(2)}) collective-permute-start(bf16[256,1280]{1,0:T(8,128)(2,1)} %collective-permute-done.2.refs_3_), channel_id=1, source_target_pairs={{0,4},{4,0},{1,5},{5,1},{2,6},{6,2},{3,7},{7,3},{8,12},{12,8},{9,1... | collective-permute-start | bytes 1966088 | tf_op jit(solution)/shard_map/ppermute | solution.py:43
  87.3 2.7 %collective-permute-start.20 = (bf16[256,1152]{1,0:T(8,128)(2,1)S(1)}, bf16[256,1152]{1,0:T(8,128)(2,1)}, u32[]{:S(2)}, u32[]{:S(2)}) collective-permute-start(bf16[256,1152]{1,0:T(8,128)(2,1)S(1)} %slice.35), channel_id=1, source_target_pairs={{0,192},{64,0},{128,64},{192,128},{1,193},{65,1},{129,65},{193,129... | collective-permute-start | bytes 1769480 | tf_op jit(solution)/shard_map/ppermute | solution.py:43
  90.1 0.7 or.31
  90.8 2.1 collective-permute-done.19
  92.9 1.8 collective-permute-start.14
  95.4 0.9 slice_convert_fusion
  96.3 1.3 fusion.21.codes
  97.6 6.8 %shard_map.65.lst = s32[640]{0:T(1024)} custom-call(s32[2048]{0:T(1024)} %fusion.21.codes), custom_call_target="tpu_custom_call" | custom-call | tf_op jit(solution)/shard_map/pallas_call | solution.py:316
  105.1 2.5 %pad_maximum_fusion.refs_20_ = bf16[512,1152]{1,0:T(8,128)(2,1)} fusion(bf16[256,1152]{1,0:T(8,128)(2,1)} %collective-permute-done.20, bf16[256,1152]{1,0:T(8,128)(2,1)} %collective-permute-done.19), kind=kLoop, calls=%fused_computation.9 | loop fusion | flops 2359296 | bytes 2359296 | tf_op jit(solution)/shard_map/concatenate | solution.py:286
  107.7 0.8 copy-done.13
  109.2 14.6 %shard_map.66 = (bf16[16,272,128]{2,1,0:T(8,128)(2,1)}, bf16[520,64,64]{2,1,0:T(8,128)(2,1)}) custom-call(s32[640]{0:T(1024)} %shard_map.65.lst, bf16[256,1280]{1,0:T(8,128)(2,1)} %bitcast.31, bf16[256,1280]{1,0:T(8,128)(2,1)} %copy-done.9, bf16[256,1280]{1,0:T(8,128)(2,1)} %copy-done.10, bf16[256,1280]{1,0:T(8,128)(2,1)} %collective-permute-done.2.refs_3_, ...), custom_call_target="tpu_custom_call" | custom-call | tf_op jit(solution)/shard_map/pallas_call | solution.py:327
  123.8 22.6 %all_to_all.15.got = bf16[16,272,128]{2,1,0:T(8,128)(2,1)} all-to-all(bf16[16,272,128]{2,1,0:T(8,128)(2,1)} %get-tuple-element.39), channel_id=1, replica_groups=mesh['y'=4,'z'=8,'c'=2,'x'=4] {'y','x'}, dimensions={0} | all-to-all | bytes 2228224 | tf_op jit(solution)/shard_map/all_to_all | solution.py:345
  146.4 0.7 broadcast_in_dim.59.marks
  147.1 2.5 %shard_map.67 = (bf16[8,4,64,128]{3,2,1,0:T(8,128)(2,1)}, f32[4,64,128]{2,1,0:T(8,128)}, f32[4,64,128]{2,1,0:T(8,128)}) custom-call(bf16[16,272,128]{2,1,0:T(8,128)(2,1)} %all_to_all.15.got, f32[4,64,256]{2,1,0:T(8,128)} %get-tuple-element.40.base, bf16[4,64,64]{2,1,0:T(8,128)(2,1)} %get-tuple-element.41.weights, ...), custom_call_target="tpu_custom_call" | custom-call | tf_op jit(solution)/shard_map/pallas_call | solution.py:347
  149.6 22.1 %all_to_all.16 = bf16[8,4,64,128]{3,2,1,0:T(8,128)(2,1)S(1)} all-to-all(bf16[8,4,64,128]{3,2,1,0:T(8,128)(2,1)} %get-tuple-element.42), channel_id=1, replica_groups=mesh['y'=4,'z'=8,'c'=2,'x'=4] {'z'}, dimensions={0} | all-to-all | bytes 1048576 | tf_op jit(solution)/shard_map/all_to_all | solution.py:357
  171.7 2.9 %collective-permute-start.21 = (bf16[32,64,128]{2,1,0:T(8,128)(2,1)S(1)}, bf16[32,64,128]{2,1,0:T(8,128)(2,1)S(1)}, u32[]{:S(2)}, u32[]{:S(2)}) collective-permute-start(bf16[32,64,128]{2,1,0:T(8,128)(2,1)S(1)} %bitcast.35), channel_id=1, source_target_pairs={{0,4},{4,0},{1,5},{5,1},{2,6},{6,2},{3,7},{7,3},{8,12},{12,8},{9,1... | collective-permute-start | bytes 1572872 | tf_op jit(solution)/shard_map/ppermute | solution.py:43
  174.6 1.5 collective-permute-done.21.far
  176.2 0.8 copy-done.16
  177.0 5.1 %shard_map.68 = bf16[64,64,128]{2,1,0:T(8,128)(2,1)} custom-call(s32[640]{0:T(1024)} %shard_map.65.lst, bf16[520,64,64]{2,1,0:T(8,128)(2,1)} %get-tuple-element.38.weights_in, bf16[32,64,128]{2,1,0:T(8,128)(2,1)} %bitcast.36, bf16[32,64,128]{2,1,0:T(8,128)(2,1)} %copy-done.16), custom_call_target="tpu_custom_call" | custom-call | tf_op jit(solution)/shard_map/pallas_call | solution.py:361
  182.1 21.0 %all_to_all.17 = bf16[64,64,128]{2,1,0:T(8,128)(2,1)} all-to-all(bf16[64,64,128]{2,1,0:T(8,128)(2,1)} %shard_map.68), channel_id=1, replica_groups=mesh['y'=4,'z'=8,'c'=2,'x'=4] {'y','x'}, dimensions={0} | all-to-all | bytes 2097152 | tf_op jit(solution)/shard_map/all_to_all | solution.py:373
  203.1 2.1 shard_map.69
  (95 shorter events, 6.4 us)
Async XLA Ops:
  6.5 4.7 %copy-start = (s32[1024]{0:T(1024)S(1)}, s32[1024]{0:T(1024)}, u32[]{:S(2)}) copy-start(s32[1024]{0:T(1024)} %param.11) | copy-start | bytes 12292
  6.5 4.5 %copy-start.20 = (s32[16]{0:T(128)S(1)}, s32[16]{0:T(128)}, u32[]{:S(2)}) copy-start(s32[16]{0:T(128)} %param.10) | copy-start | bytes 196
  6.5 84.3 %all-gather.3.cloned.1.call-start = ((), (), s32[]{:S(2)}) async-start(), calls=%async_computation.3 | async-start | bytes 5640192 | tf_op jit(solution)/shard_map/all_gather | solution.py:254
  8.8 14.3 %copy-start.2 = (bf16[16,64,1152]{2,1,0:T(8,128)(2,1)S(1)}, bf16[16,64,1152]{2,1,0:T(8,128)(2,1)}, u32[]{:S(2)}) copy-start(bf16[16,64,1152]{2,1,0:T(8,128)(2,1)} %param.6) | copy-start | bytes 7077892
  10.2 0.8 copy-start.5
  13.1 10.6 %copy-start.3 = (bf16[16,64,1152]{2,1,0:T(8,128)(2,1)S(1)}, bf16[16,64,1152]{2,1,0:T(8,128)(2,1)}, u32[]{:S(2)}) copy-start(bf16[16,64,1152]{2,1,0:T(8,128)(2,1)} %param.6) | copy-start | bytes 7077892
  16.5 42.0 %copy-start.4 = (bf16[4,64,1280]{2,1,0:T(8,128)(2,1)}, bf16[4,64,1280]{2,1,0:T(8,128)(2,1)S(1)}, u32[]{:S(2)}) copy-start(bf16[4,64,1280]{2,1,0:T(8,128)(2,1)S(1)} %pad_maximum_fusion.1) | copy-start | bytes 1966084
  16.5 21.0 %collective-permute-start = (bf16[256,1280]{1,0:T(8,128)(2,1)S(1)}, bf16[256,1280]{1,0:T(8,128)(2,1)S(1)}, u32[]{:S(2)}, u32[]{:S(2)}) collective-permute-start(bf16[256,1280]{1,0:T(8,128)(2,1)S(1)} %bitcast.27), channel_id=1, source_target_pairs={{0,8},{8,16},{16,24},{24,32},{32,40},{40,48},{48,56},{56,0},{1,9},... | collective-permute-start | bytes 1966088 | tf_op jit(solution)/shard_map/ppermute | solution.py:43
  19.1 18.5 %collective-permute-start.1 = (bf16[256,1280]{1,0:T(8,128)(2,1)S(1)}, bf16[256,1280]{1,0:T(8,128)(2,1)S(1)}, u32[]{:S(2)}, u32[]{:S(2)}) collective-permute-start(bf16[256,1280]{1,0:T(8,128)(2,1)S(1)} %bitcast.28), channel_id=1, source_target_pairs={{0,56},{8,0},{16,8},{24,16},{32,24},{40,32},{48,40},{56,48},{1,57}... | collective-permute-start | bytes 1966088 | tf_op jit(solution)/shard_map/ppermute | solution.py:43
  24.1 54.0 %copy-start.1 = (bf16[16,64,1152]{2,1,0:T(8,128)(2,1)}, bf16[16,64,1152]{2,1,0:T(8,128)(2,1)S(1)}, u32[]{:S(2)}) copy-start(bf16[16,64,1152]{2,1,0:T(8,128)(2,1)S(1)} %fusion.1) | copy-start | bytes 7077892
  24.2 33.3 %collective-permute-start.4 = (bf16[512,1152]{1,0:T(8,128)(2,1)S(1)}, bf16[512,1152]{1,0:T(8,128)(2,1)S(1)}, u32[]{:S(2)}, u32[]{:S(2)}) collective-permute-start(bf16[512,1152]{1,0:T(8,128)(2,1)S(1)} %bitcast.37), channel_id=1, source_target_pairs={{0,64},{64,128},{128,192},{192,0},{1,65},{65,129},{129,193},{193,1... | collective-permute-start | bytes 3538952 | tf_op jit(solution)/shard_map/ppermute | solution.py:43
  25.6 31.9 %collective-permute-start.5 = (bf16[512,1152]{1,0:T(8,128)(2,1)S(1)}, bf16[512,1152]{1,0:T(8,128)(2,1)S(1)}, u32[]{:S(2)}, u32[]{:S(2)}) collective-permute-start(bf16[512,1152]{1,0:T(8,128)(2,1)S(1)} %bitcast.38), channel_id=1, source_target_pairs={{0,192},{64,0},{128,64},{192,128},{1,193},{65,1},{129,65},{193,129... | collective-permute-start | bytes 3538952 | tf_op jit(solution)/shard_map/ppermute | solution.py:43
  37.6 21.0 %copy-start.9 = (bf16[256,1280]{1,0:T(8,128)(2,1)}, bf16[256,1280]{1,0:T(8,128)(2,1)S(1)}, u32[]{:S(2)}) copy-start(bf16[256,1280]{1,0:T(8,128)(2,1)S(1)} %collective-permute-done.refs_1_) | copy-start | bytes 1966084
  37.6 21.0 %copy-start.10 = (bf16[256,1280]{1,0:T(8,128)(2,1)}, bf16[256,1280]{1,0:T(8,128)(2,1)S(1)}, u32[]{:S(2)}) copy-start(bf16[256,1280]{1,0:T(8,128)(2,1)S(1)} %collective-permute-done.1.refs_2_) | copy-start | bytes 1966084
  37.6 19.9 %collective-permute-start.2 = (bf16[256,1280]{1,0:T(8,128)(2,1)S(1)}, bf16[256,1280]{1,0:T(8,128)(2,1)}, u32[]{:S(2)}, u32[]{:S(2)}) collective-permute-start(bf16[256,1280]{1,0:T(8,128)(2,1)S(1)} %collective-permute-done.refs_1_), channel_id=1, source_target_pairs={{0,8},{8,16},{16,24},{24,32},{32,40},{40,48},{48,56},{56,0},{1,9},... | collective-permute-start | bytes 1966088 | tf_op jit(solution)/shard_map/ppermute | solution.py:43
  37.7 19.8 %collective-permute-start.3 = (bf16[256,1280]{1,0:T(8,128)(2,1)S(1)}, bf16[256,1280]{1,0:T(8,128)(2,1)S(1)}, u32[]{:S(2)}, u32[]{:S(2)}) collective-permute-start(bf16[256,1280]{1,0:T(8,128)(2,1)S(1)} %collective-permute-done.1.refs_2_), channel_id=1, source_target_pairs={{0,56},{8,0},{16,8},{24,16},{32,24},{40,32},{48,40},{56,48},{1,57}... | collective-permute-start | bytes 1966088 | tf_op jit(solution)/shard_map/ppermute | solution.py:43
  57.5 1.0 copy-start.6
  57.5 1.4 copy-start.7
  58.5 0.8 copy-start.11
  58.5 15.0 %collective-permute-start.6 = (bf16[256,1280]{1,0:T(8,128)(2,1)}, bf16[256,1280]{1,0:T(8,128)(2,1)}, u32[]{:S(2)}, u32[]{:S(2)}) collective-permute-start(bf16[256,1280]{1,0:T(8,128)(2,1)} %collective-permute-done.2.refs_3_), channel_id=1, source_target_pairs={{0,8},{8,16},{16,24},{24,32},{32,40},{40,48},{48,56},{56,0},{1,9},... | collective-permute-start | bytes 1966088 | tf_op jit(solution)/shard_map/ppermute | solution.py:43
  59.4 20.8 %collective-permute-start.10 = (bf16[256,1280]{1,0:T(8,128)(2,1)S(1)}, bf16[256,1280]{1,0:T(8,128)(2,1)}, u32[]{:S(2)}, u32[]{:S(2)}) collective-permute-start(bf16[256,1280]{1,0:T(8,128)(2,1)S(1)} %bitcast.29), channel_id=1, source_target_pairs={{0,4},{4,0},{1,5},{5,1},{2,6},{6,2},{3,7},{7,3},{8,12},{12,8},{9,1... | collective-permute-start | bytes 1966088 | tf_op jit(solution)/shard_map/ppermute | solution.py:43
  62.4 16.8 %collective-permute-start.8 = (bf16[256,1280]{1,0:T(8,128)(2,1)}, bf16[256,1280]{1,0:T(8,128)(2,1)}, u32[]{:S(2)}, u32[]{:S(2)}) collective-permute-start(bf16[256,1280]{1,0:T(8,128)(2,1)} %copy-done.11), channel_id=1, source_target_pairs={{0,56},{8,0},{16,8},{24,16},{32,24},{40,32},{48,40},{56,48},{1,57}... | collective-permute-start | bytes 1966088 | tf_op jit(solution)/shard_map/ppermute | solution.py:43
  64.4 20.1 %collective-permute-start.11 = (bf16[256,1280]{1,0:T(8,128)(2,1)}, bf16[256,1280]{1,0:T(8,128)(2,1)}, u32[]{:S(2)}, u32[]{:S(2)}) collective-permute-start(bf16[256,1280]{1,0:T(8,128)(2,1)} %copy-done.9), channel_id=1, source_target_pairs={{0,4},{4,0},{1,5},{5,1},{2,6},{6,2},{3,7},{7,3},{8,12},{12,8},{9,1... | collective-permute-start | bytes 1966088 | tf_op jit(solution)/shard_map/ppermute | solution.py:43
  64.8 22.5 %collective-permute-start.12 = (bf16[256,1280]{1,0:T(8,128)(2,1)}, bf16[256,1280]{1,0:T(8,128)(2,1)}, u32[]{:S(2)}, u32[]{:S(2)}) collective-permute-start(bf16[256,1280]{1,0:T(8,128)(2,1)} %copy-done.10), channel_id=1, source_target_pairs={{0,4},{4,0},{1,5},{5,1},{2,6},{6,2},{3,7},{7,3},{8,12},{12,8},{9,1... | collective-permute-start | bytes 1966088 | tf_op jit(solution)/shard_map/ppermute | solution.py:43
  73.5 19.4 %collective-permute-start.19 = (bf16[256,1152]{1,0:T(8,128)(2,1)}, bf16[256,1152]{1,0:T(8,128)(2,1)}, u32[]{:S(2)}, u32[]{:S(2)}) collective-permute-start(bf16[256,1152]{1,0:T(8,128)(2,1)} %slice.34), channel_id=1, source_target_pairs={{0,64},{64,128},{128,192},{192,0},{1,65},{65,129},{129,193},{193,1... | collective-permute-start | bytes 1769480 | tf_op jit(solution)/shard_map/ppermute | solution.py:43
  79.2 15.5 %collective-permute-start.7 = (bf16[128,1280]{1,0:T(8,128)(2,1)S(1)}, bf16[128,1280]{1,0:T(8,128)(2,1)S(1)}, u32[]{:S(2)}, u32[]{:S(2)}) collective-permute-start(bf16[128,1280]{1,0:T(8,128)(2,1)S(1)} %slice.39), channel_id=1, source_target_pairs={{0,8},{8,16},{16,24},{24,32},{32,40},{40,48},{48,56},{56,0},{1,9},... | collective-permute-start | bytes 983048 | tf_op jit(solution)/shard_map/ppermute | solution.py:43
  80.2 15.2 %collective-permute-start.9 = (bf16[128,1280]{1,0:T(8,128)(2,1)S(1)}, bf16[128,1280]{1,0:T(8,128)(2,1)}, u32[]{:S(2)}, u32[]{:S(2)}) collective-permute-start(bf16[128,1280]{1,0:T(8,128)(2,1)S(1)} %slice.40), channel_id=1, source_target_pairs={{0,56},{8,0},{16,8},{24,16},{32,24},{40,32},{48,40},{56,48},{1,57}... | collective-permute-start | bytes 983048 | tf_op jit(solution)/shard_map/ppermute | solution.py:43
  84.5 20.5 %collective-permute-start.13 = (bf16[256,1280]{1,0:T(8,128)(2,1)}, bf16[256,1280]{1,0:T(8,128)(2,1)S(1)}, u32[]{:S(2)}, u32[]{:S(2)}) collective-permute-start(bf16[256,1280]{1,0:T(8,128)(2,1)} %collective-permute-done.2.refs_3_), channel_id=1, source_target_pairs={{0,4},{4,0},{1,5},{5,1},{2,6},{6,2},{3,7},{7,3},{8,12},{12,8},{9,1... | collective-permute-start | bytes 1966088 | tf_op jit(solution)/shard_map/ppermute | solution.py:43
  87.3 17.1 %collective-permute-start.20 = (bf16[256,1152]{1,0:T(8,128)(2,1)S(1)}, bf16[256,1152]{1,0:T(8,128)(2,1)}, u32[]{:S(2)}, u32[]{:S(2)}) collective-permute-start(bf16[256,1152]{1,0:T(8,128)(2,1)S(1)} %slice.35), channel_id=1, source_target_pairs={{0,192},{64,0},{128,64},{192,128},{1,193},{65,1},{129,65},{193,129... | collective-permute-start | bytes 1769480 | tf_op jit(solution)/shard_map/ppermute | solution.py:43
  92.9 14.7 %collective-permute-start.14 = (bf16[256,1280]{1,0:T(8,128)(2,1)}, bf16[256,1280]{1,0:T(8,128)(2,1)S(1)}, u32[]{:S(2)}, u32[]{:S(2)}) collective-permute-start(bf16[256,1280]{1,0:T(8,128)(2,1)} %copy-done.11), channel_id=1, source_target_pairs={{0,4},{4,0},{1,5},{5,1},{2,6},{6,2},{3,7},{7,3},{8,12},{12,8},{9,1... | collective-permute-start | bytes 1966088 | tf_op jit(solution)/shard_map/ppermute | solution.py:43
  94.7 0.7 copy-start.17
  94.7 13.0 %collective-permute-start.15 = (bf16[256,1280]{1,0:T(8,128)(2,1)}, bf16[256,1280]{1,0:T(8,128)(2,1)S(1)}, u32[]{:S(2)}, u32[]{:S(2)}) collective-permute-start(bf16[256,1280]{1,0:T(8,128)(2,1)} %collective-permute-done.6.refs_5_), channel_id=1, source_target_pairs={{0,4},{4,0},{1,5},{5,1},{2,6},{6,2},{3,7},{7,3},{8,12},{12,8},{9,1... | collective-permute-start | bytes 1966088 | tf_op jit(solution)/shard_map/ppermute | solution.py:43
  95.4 12.2 %collective-permute-start.16 = (bf16[256,1280]{1,0:T(8,128)(2,1)}, bf16[256,1280]{1,0:T(8,128)(2,1)S(1)}, u32[]{:S(2)}, u32[]{:S(2)}) collective-permute-start(bf16[256,1280]{1,0:T(8,128)(2,1)} %collective-permute-done.8.refs_6_), channel_id=1, source_target_pairs={{0,4},{4,0},{1,5},{5,1},{2,6},{6,2},{3,7},{7,3},{8,12},{12,8},{9,1... | collective-permute-start | bytes 1966088 | tf_op jit(solution)/shard_map/ppermute | solution.py:43
  104.4 3.3 %collective-permute-start.17 = (bf16[128,1280]{1,0:T(8,128)(2,1)}, bf16[128,1280]{1,0:T(8,128)(2,1)S(1)}, u32[]{:S(2)}, u32[]{:S(2)}) collective-permute-start(bf16[128,1280]{1,0:T(8,128)(2,1)} %copy-done.17), channel_id=1, source_target_pairs={{0,4},{4,0},{1,5},{5,1},{2,6},{6,2},{3,7},{7,3},{8,12},{12,8},{9,1... | collective-permute-start | bytes 983048 | tf_op jit(solution)/shard_map/ppermute | solution.py:43
  105.0 2.7 %copy-start.12 = (bf16[256,1280]{1,0:T(8,128)(2,1)}, bf16[256,1280]{1,0:T(8,128)(2,1)S(1)}, u32[]{:S(2)}) copy-start(bf16[256,1280]{1,0:T(8,128)(2,1)S(1)} %collective-permute-done.13.refs_12_) | copy-start | bytes 1966084
  105.0 2.7 %collective-permute-start.18 = (bf16[128,1280]{1,0:T(8,128)(2,1)}, bf16[128,1280]{1,0:T(8,128)(2,1)S(1)}, u32[]{:S(2)}, u32[]{:S(2)}) collective-permute-start(bf16[128,1280]{1,0:T(8,128)(2,1)} %collective-permute-done.9.refs_8_), channel_id=1, source_target_pairs={{0,4},{4,0},{1,5},{5,1},{2,6},{6,2},{3,7},{7,3},{8,12},{12,8},{9,1... | collective-permute-start | bytes 983048 | tf_op jit(solution)/shard_map/ppermute | solution.py:43
  107.6 0.8 copy-start.13
  107.6 1.1 copy-start.14
  107.7 1.4 copy-start.15
  107.7 1.4 copy-start.18
  107.7 1.5 copy-start.19
  171.7 4.4 %copy-start.8 = (bf16[8,4,64,128]{3,2,1,0:T(8,128)(2,1)}, bf16[8,4,64,128]{3,2,1,0:T(8,128)(2,1)S(1)}, u32[]{:S(2)}) copy-start(bf16[8,4,64,128]{3,2,1,0:T(8,128)(2,1)S(1)} %all_to_all.16) | copy-start | bytes 1572868
  171.7 4.4 %collective-permute-start.21 = (bf16[32,64,128]{2,1,0:T(8,128)(2,1)S(1)}, bf16[32,64,128]{2,1,0:T(8,128)(2,1)S(1)}, u32[]{:S(2)}, u32[]{:S(2)}) collective-permute-start(bf16[32,64,128]{2,1,0:T(8,128)(2,1)S(1)} %bitcast.35), channel_id=1, source_target_pairs={{0,4},{4,0},{1,5},{5,1},{2,6},{6,2},{3,7},{7,3},{8,12},{12,8},{9,1... | collective-permute-start | bytes 1572872 | tf_op jit(solution)/shard_map/ppermute | solution.py:43
  176.1 0.8 copy-start.16
Sparse Core Ops, SparseCore 0:
  13.2 70.8 all-gather.2

commit v5 on v3

--- a/solution.py
+++ b/solution.py
@@ -17,16 +17,13 @@
 FEAT = 1152
 CH = 128
 PART = ROWS // NX
-SHARED = 2
-STRAIGHT = NX * (PART - SHARED)
+STRAIGHT = NX * (PART - 1)
 QBLOCKS = NY * ROWS
-Q_SHARED = ROWS + (NY - 1) * STRAIGHT
-Q_ALL = Q_SHARED + NY * NX * SHARED
+Q_TURN = ROWS + (NY - 1) * STRAIGHT
 UNROLL = 8
 SLOTS = 520
 WIDE = FEAT + CH
 PIECE = PART * FRAMES
-HALF = PIECE // 2
 SEND = PIECE + 16
 LIST = 640
 STEPS_AT = 600
@@ -77,16 +74,10 @@
     ).astype(jnp.bfloat16)
 
 
-def first_kernel(lst, *refs):
-    near, far, queries = refs[:9], refs[9:18], refs[18:23]
-    send, weights_out, q, k, acc, w, sems, out_sem = refs[23:]
-    copies = []
-    for side, held in enumerate((near, far)):
-        at = 0
-        for piece in held:
-            rows = piece.shape[0]
-            copies.append(pltpu.make_async_copy(piece, k.at[side, pl.ds(at, rows)], sems.at[len(copies)]))
-            at += rows
+def first_kernel(lst, keys, *refs):
+    queries = refs[:9]
+    send, weights_out, q, k, acc, w, sems, out_sem = refs[9:]
+    copies = [pltpu.make_async_copy(keys, k, sems.at[0])]
     at = 0
     for part in queries:
         rows = part.shape[0]
@@ -101,21 +92,22 @@
 
     def step(i, carry):
         codes = [lst[i * UNROLL + u] for u in range(UNROLL)]
-        sides = [(code >> 12) & 1 for code in codes]
-        rows = [pl.multiple_of(((code >> 7) & 31) * FRAMES, FRAMES) for code in codes]
+        key_rows = [pl.multiple_of(((code >> 7) & 63) * FRAMES, FRAMES) for code in codes]
+        query_rows = [pl.multiple_of(((code >> 13) & 63) * FRAMES, FRAMES) for code in codes]
         weights = []
-        for code, side, row in zip(codes, sides, rows):
-            units = q[(code >> 18) & 127]
-            keys = k[side, pl.ds(row, FRAMES), pl.ds(0, FEAT)]
+        for query_row, key_row in zip(query_rows, key_rows):
             affinity = lax.dot_general(
-                units, keys, (((1,), (1,)), ((), ())), preferred_element_type=jnp.float32
+                q[pl.ds(query_row, FRAMES), :],
+                k[pl.ds(key_row, FRAMES), pl.ds(0, FEAT)],
+                (((1,), (1,)), ((), ())),
+                preferred_element_type=jnp.float32,
             )
             weights.append(jnp.exp(sharpness * affinity).astype(jnp.bfloat16))
         for u in range(UNROLL):
             w[i * UNROLL + u] = weights[u]
         sums = []
-        for u, (side, row) in enumerate(zip(sides, rows)):
-            values = values_of(k[side, pl.ds(row, FRAMES), pl.ds(FEAT, CH)])
+        for u, key_row in enumerate(key_rows):
+            values = values_of(k[pl.ds(key_row, FRAMES), pl.ds(FEAT, CH)])
             sums.append(jnp.dot(weights[u], values, preferred_element_type=jnp.float32))
         for u, code in enumerate(codes):
             acc[code & 127] += sums[u]
@@ -173,8 +165,8 @@
         codes = [lst[i * UNROLL + u] for u in range(UNROLL)]
         sums = []
         for u, code in enumerate(codes):
-            block = (code >> 13) & 31
-            scores = jnp.where(((code >> 12) & 1) == 0, near[block], far[block])
+            block = (code >> 21) & 31
+            scores = jnp.where(((code >> 20) & 1) == 0, near[block], far[block])
             sums.append(jnp.dot(w[i * UNROLL + u], scores, preferred_element_type=jnp.float32))
         for u, code in enumerate(codes):
             acc[code & 127] += sums[u]
@@ -199,7 +191,8 @@
         denominator[b] = full
         mixed = keep_share * total / full + (1.0 - keep_share) * prior[b].astype(jnp.float32)
         keep = (mixed.astype(jnp.bfloat16).astype(jnp.float32) * marks[b].astype(jnp.float32)).astype(jnp.bfloat16)
-        masked[b] = keep
+        for d in range(NZ):
+            masked[d, b] = keep
         own_second[b] = jnp.dot(weights[b], keep, preferred_element_type=jnp.float32)
 
 
@@ -234,44 +227,34 @@
     marked = jnp.where(marks > 0, prior, jnp.bfloat16(2 * UNREAL))
     piece = jnp.concatenate([units, marked], axis=-1).reshape(PIECE, WIDE)
 
-    target = jnp.take(block_home, neighbour_ids.reshape(-1), axis=0)
+    keys = lax.all_gather(piece, ("z", "c"), axis=0, tiled=True)
+
+    embeddings, piece = lax.optimization_barrier((embeddings, piece))
+    turn = units[0]
+    turned = [shift(turn, "y", -1), shift(turn, "y", 2), shift(turn, "y", 1)]
+    all_units = normalize(embeddings)
+    straight = all_units.reshape(NX, PART, FRAMES, FEAT)[:, 1:].reshape(STRAIGHT * FRAMES, FEAT)
+    turned, straight = lax.optimization_barrier((turned, straight))
+    behind, ahead = shift(straight, "y", 1), shift(straight, "y", -1)
+
+    turned = jnp.concatenate(turned, axis=0)
+    ids, block_home, turned = lax.optimization_barrier((neighbour_ids, block_home, turned))
+    target = jnp.take(block_home, ids.reshape(-1), axis=0)
     column = x * per_list + jnp.arange(per_list, dtype=jnp.int32)
-    in_list = column[None, :] < neighbour_count[:, None]
-    target = jnp.where(in_list.reshape(-1), target, -1).reshape(1, ROWS * per_list)
-
-    shared = lax.all_gather(units[:SHARED], ("y", "x"), axis=0, tiled=True)
-    up, down = shift(piece, "z", 1), shift(piece, "z", -1)
-    embeddings, piece = lax.optimization_barrier((embeddings, piece))
-    all_units = normalize(embeddings)
-    straight = all_units.reshape(NX, PART, FRAMES, FEAT)[:, SHARED:].reshape(STRAIGHT, FRAMES, FEAT)
-    behind, ahead = shift(straight, "y", 1), shift(straight, "y", -1)
-    targets = [target, shift(target, "y", -1), shift(target, "y", 2), shift(target, "y", 1)]
-
-    up, down, targets = lax.optimization_barrier((up, down, targets))
-    near = [piece, up, down]
-    far = [shift(v, "c", 1) for v in near]
-    up, down = shift(up, "z", 1), shift(down, "z", -1)
-    target = jnp.concatenate(targets, axis=0)
-    targets = [target, shift(target, "x", -1), shift(target, "x", 2), shift(target, "x", 1)]
-
-    up, down, behind, ahead, targets = lax.optimization_barrier((up, down, behind, ahead, targets))
-    half = STRAIGHT // 2
-    across_a, across_b = shift(behind[:half], "y", 1), shift(ahead[half:], "y", -1)
-    held = [up, down]
-    up, down = shift(up, "z", 1), shift(down, "z", -1)
-    near += held
-    far += [shift(v, "c", 1) for v in held]
-    target = jnp.stack(targets, axis=0).reshape(NX, NY, ROWS, per_list)
-    distance = jnp.arange(NY, dtype=jnp.int32)[None, :, None, None]
+    in_list = (column[None, :] < neighbour_count[:, None]).reshape(-1)
+    target = lax.all_gather(jnp.where(in_list, target, -1), ("y", "x"), axis=0)
+
+    turned = [turned, shift(turned, "x", -1), shift(turned, "x", 2), shift(turned, "x", 1)]
+    half = STRAIGHT * FRAMES // 2
+    across = [shift(behind[:half], "y", 1), shift(ahead[half:], "y", -1)]
+
+    target = target.reshape(NY, NX, ROWS, per_list)
+    source_y = jnp.arange(NY, dtype=jnp.int32)[:, None, None, None]
     source_row = jnp.arange(ROWS, dtype=jnp.int32)[None, None, :, None]
-    source_y = (y + distance) % NY
+    distance = (source_y - y) % NY
     source = source_y * ROWS + source_row
     wanted = (target >= 0) & (target // 256 == y) & ((target % 16) // PART == x)
     place = (target // 16) % 16
-    apart = (place // 2 - z) % NZ
-    order = jnp.where(
-        apart == 0, 0, jnp.where(apart < 4, 2 * apart, jnp.where(apart == 4, 7, 2 * (NZ - apart) - 1))
-    )
     inner = target % PART
     side = (place % 2) ^ c
     quarter, within = source_row // PART, source_row % PART
@@ -279,12 +262,12 @@
         distance == 0,
         source_row,
         jnp.where(
-            within < SHARED,
-            Q_SHARED + (source_y * NX + quarter) * SHARED + within,
-            ROWS + (distance - 1) * STRAIGHT + quarter * (PART - SHARED) + within - SHARED,
+            within == 0,
+            Q_TURN + ((quarter - x) % NX) * (NY - 1) + distance - 1,
+            ROWS + (distance - 1) * STRAIGHT + quarter * (PART - 1) + within - 1,
         ),
     )
-    codes = source | ((order * PART + inner) << 7) | (side << 12) | (((place // 2) * PART + inner) << 13) | (taken << 18)
+    codes = source | ((place * PART + inner) << 7) | (taken << 13) | (side << 20) | (((place // 2) * PART + inner) << 21)
     codes = jnp.where(wanted, codes, -1).reshape(-1)
     lst = pl.pallas_call(
         list_kernel,
@@ -292,11 +275,6 @@
         in_specs=[smem],
         out_specs=smem,
     )(codes)
-
-    up, down, lst = lax.optimization_barrier((up, down, lst))
-    last_up, last_down = shift(up[:HALF], "z", 1), shift(down[HALF:], "z", -1)
-    near += [up, down]
-    far += [shift(up, "c", 1), shift(down, "c", 1)]
     own_weights, own_base = pl.pallas_call(
         own_kernel,
         out_shape=(
@@ -306,9 +284,6 @@
         in_specs=[vmem],
         out_specs=(vmem, vmem),
     )(piece)
-    near += [last_up, last_down]
-    far += [shift(last_up, "c", 1), shift(last_down, "c", 1)]
-    across = jnp.concatenate([across_a, across_b], axis=0)
 
     send, weights = pl.pallas_call(
         first_kernel,
@@ -316,31 +291,32 @@
             jax.ShapeDtypeStruct((NY * NX, SEND, CH), jnp.bfloat16),
             jax.ShapeDtypeStruct((SLOTS, FRAMES, FRAMES), jnp.bfloat16),
         ),
-        in_specs=[smem] + [hbm] * 23,
+        in_specs=[smem] + [hbm] * 10,
         out_specs=(vmem, hbm),
         scratch_shapes=[
-            pltpu.VMEM((Q_ALL, FRAMES, FEAT), jnp.bfloat16),
-            pltpu.VMEM((NC, NZ * PIECE, WIDE), jnp.bfloat16),
+            pltpu.VMEM((QBLOCKS * FRAMES, FEAT), jnp.bfloat16),
+            pltpu.VMEM((NZ * NC * PIECE, WIDE), jnp.bfloat16),
             pltpu.VMEM((QBLOCKS + 1, FRAMES, 2 * CH), jnp.float32),
             pltpu.VMEM((SLOTS, FRAMES, FRAMES), jnp.bfloat16),
-            pltpu.SemaphoreType.DMA((23,)),
+            pltpu.SemaphoreType.DMA((10,)),
             pltpu.SemaphoreType.DMA,
         ],
         compiler_params=params,
-    )(lst, *near, *far, all_units, ahead, across, behind, shared)
+    )(lst, keys, all_units.reshape(ROWS * FRAMES, FEAT), ahead, *across, behind, *turned)
     got = lax.all_to_all(send, ("y", "x"), split_axis=0, concat_axis=0, tiled=True)
 
     masked, denominator, own_second = pl.pallas_call(
         mix_kernel,
         out_shape=(
-            jax.ShapeDtypeStruct((PART, FRAMES, CH), jnp.bfloat16),
+            jax.ShapeDtypeStruct((NZ, PART, FRAMES, CH), jnp.bfloat16),
             jax.ShapeDtypeStruct((PART, FRAMES, CH), jnp.float32),
             jax.ShapeDtypeStruct((PART, FRAMES, CH), jnp.float32),
         ),
         in_specs=[vmem] * 5,
         out_specs=(vmem,) * 3,
     )(got, own_base, own_weights, prior, marks)
-    near_scores = lax.all_gather(masked, "z", axis=0, tiled=True)
+    near_scores = lax.all_to_all(masked, "z", split_axis=0, concat_axis=0, tiled=True)
+    near_scores = near_scores.reshape(NZ * PART, FRAMES, CH)
     far_scores = shift(near_scores, "c", 1)
 
     send = pl.pallas_call(

time: 247 us -> 216 us (0.87)
  waiting for transfers between devices: 80.8 us -> 51 us
  blocking collectives: 42.8 us -> 69.6 us
  starting transfers between devices: 49.9 us -> 28 us
  local copies, waits for them, and re-layouts: 14.5 us -> 10.4 us
    ppermute x28 -> x11, waiting for transfers between devices: 62.9 us -> 39.7 us  [shift(): lax.ppermute(value, axis, [(i, (i + step) % size) for i in range(size)])]
    ppermute x28 -> x11, starting transfers between devices: 45.8 us -> 24.3 us  [shift(): lax.ppermute(value, axis, [(i, (i + step) % size) for i in range(size)])]
    all_to_all x0 -> x1, blocking collectives: none -> 20.9 us  [body(): lax.all_to_all(masked, 'z', split_axis=0, concat_axis=0, tiled=True)]
    all_gather x1, blocking collectives: 20.3 us -> 27.8 us  [body(): target = lax.all_gather(jnp.where(in_list, target, -1), ('y', 'x'), axis=0)]
    all_to_all x1, waiting for transfers between devices: 17.8 us -> 11.3 us  [body(): lax.all_to_all(send, ('y', 'x'), split_axis=0, concat_axis=0, tiled=True)]
    unnamed x43 -> x26, local copies, waits for them, and re-layouts: 5.92 us -> 1.91 us
    slice x6 -> x3, local copies, waits for them, and re-layouts: 5.66 us -> 4.07 us  [the longest x2 2.55 us: body(): across = [shift(behind[:half], 'y', 1), shift(ahead[half:], 'y', -1)]]
  transfers between devices with their start and end apart: 30 -> 13, of which waited for: 11 -> 4; matrix products, arithmetic and copies ran while one was open for 6% -> 5% of each run, Pallas kernels for 4% -> 4%
where the time goes in v5:
time: 216 us; the launch traced here: 215 us
  blocking collectives  69.6 us (32%)
  waiting for transfers between devices  51 us (24%)
  Pallas kernels  34.2 us (16%)
  starting transfers between devices  28 us (13%)
  between operations  13.7 us (6%)
  local copies, waits for them, and re-layouts  10.4 us (5%)
  other arithmetic  8.31 us (4%)
    ppermute x11, waiting for transfers between devices, shift(): lax.ppermute(value, axis, [(i, (i + step) % size) for i in range(size)])  39.7 us
    all_gather x1, blocking collectives, body(): target = lax.all_gather(jnp.where(in_list, target, -1), ('y', 'x'), axis=0)  27.8 us
    ppermute x11, starting transfers between devices, shift(): lax.ppermute(value, axis, [(i, (i + step) % size) for i in range(size)])  24.3 us
    all_to_all x1, blocking collectives, body(): lax.all_to_all(send, ('y', 'x'), split_axis=0, concat_axis=0, tiled=True)  21 us
    all_to_all x1, blocking collectives, body(): lax.all_to_all(masked, 'z', split_axis=0, concat_axis=0, tiled=True)  20.9 us
    pallas_call x1, Pallas kernels, body(): pl.pallas_call(first_kernel, out_shape=(jax.ShapeDtypeStruct((NY * NX, SE...  14.7 us
    all_to_all x1, waiting for transfers between devices, body(): lax.all_to_all(send, ('y', 'x'), split_axis=0, concat_axis=0, tiled=True)  11.3 us
    pallas_call x1, Pallas kernels, body(): pl.pallas_call(list_kernel, out_shape=jax.ShapeDtypeStruct((LIST,), jnp.i...  6.77 us
  transfers between devices with their start and end apart: 13, of which 4 were waited for; matrix products, arithmetic and copies ran while one was open for 5% of the time, Pallas kernels for 4%

profile of v5, /device:TPU:1, one launch (start us, length us, event | category | flops | bytes accessed | tf_op | source)
XLA Modules:
  0.0 215.2 jit_solution(13751855915121469235)
XLA Ops:
  6.5 0.8 broadcast_compare_fusion.1
  7.4 1.3 fusion.2
  8.7 1.2 fusion.3
  9.9 1.5 broadcast_select_fusion
  11.4 0.9 pad_maximum_fusion
  12.3 2.2 %collective-permute-start.2 = (bf16[64,1152]{1,0:T(8,128)(2,1)S(1)}, bf16[64,1152]{1,0:T(8,128)(2,1)S(1)}, u32[]{:S(2)}, u32[]{:S(2)}) collective-permute-start(bf16[64,1152]{1,0:T(8,128)(2,1)S(1)} %slice_bitcast_fusion), channel_id=1, source_target_pairs={{0,64},{64,128},{128,192},{192,0},{1,65},{65,129},{129,193},{193,1... | collective-permute-start | bytes 442376 | tf_op jit(solution)/shard_map/ppermute | solution.py:38
  14.5 2.6 %collective-permute-start.1 = (bf16[64,1152]{1,0:T(8,128)(2,1)S(1)}, bf16[64,1152]{1,0:T(8,128)(2,1)S(1)}, u32[]{:S(2)}, u32[]{:S(2)}) collective-permute-start(bf16[64,1152]{1,0:T(8,128)(2,1)S(1)} %slice_bitcast_fusion), channel_id=1, source_target_pairs={{0,128},{64,192},{128,0},{192,64},{1,129},{65,193},{129,1},{193,65... | collective-permute-start | bytes 442376 | tf_op jit(solution)/shard_map/ppermute | solution.py:38
  17.1 1.1 collective-permute-start
  18.2 0.5 fusion
  18.7 0.5 fusion.1
  19.2 1.5 slice.19
  20.7 2.8 %collective-permute-done.1 = bf16[64,1152]{1,0:T(8,128)(2,1)S(1)} collective-permute-done((bf16[64,1152]{1,0:T(8,128)(2,1)S(1)}, bf16[64,1152]{1,0:T(8,128)(2,1)S(1)}, u32[]{:S(2)}, u32[]{:S(2)}) %collective-permute-start.1) | collective-permute-done | bytes 147488 | tf_op jit(solution)/shard_map/ppermute | solution.py:38
  23.5 0.7 collective-permute-start.4
  24.2 2.0 collective-permute-start.3
  26.3 0.7 lt.96
  27.1 0.1 or.31
  27.5 0.7 or.34
  28.2 35.4 %collective-permute-done.4.refs_4_ = bf16[768,1152]{1,0:T(8,128)(2,1)} collective-permute-done((bf16[768,1152]{1,0:T(8,128)(2,1)}, bf16[768,1152]{1,0:T(8,128)(2,1)}, u32[]{:S(2)}, u32[]{:S(2)}) %collective-permute-start.4) | collective-permute-done | bytes 1769504 | tf_op jit(solution)/shard_map/ppermute | solution.py:38
  63.6 1.3 slice.20
  64.8 0.1 collective-permute-start.5
  65.0 1.3 slice.21
  66.3 2.7 %collective-permute-start.6 = (bf16[384,1152]{1,0:T(8,128)(2,1)S(1)}, bf16[384,1152]{1,0:T(8,128)(2,1)S(1)}, u32[]{:S(2)}, u32[]{:S(2)}) collective-permute-start(bf16[384,1152]{1,0:T(8,128)(2,1)S(1)} %slice.21), channel_id=1, source_target_pairs={{0,192},{64,0},{128,64},{192,128},{1,193},{65,1},{129,65},{193,129... | collective-permute-start | bytes 2654216 | tf_op jit(solution)/shard_map/ppermute | solution.py:38
  69.0 0.8 copy.11
  69.8 0.1 reshape.426
  69.9 0.1 reshape.425
  70.0 1.3 collective-permute-start.9
  71.3 2.5 %collective-permute-start.8 = (bf16[192,1152]{1,0:T(8,128)(2,1)S(1)}, bf16[192,1152]{1,0:T(8,128)(2,1)}, u32[]{:S(2)}, u32[]{:S(2)}) collective-permute-start(bf16[192,1152]{1,0:T(8,128)(2,1)S(1)} %pad_maximum_fusion.1.refs_5_), channel_id=1, source_target_pairs={{0,2},{1,3},{2,0},{3,1},{4,6},{5,7},{6,4},{7,5},{8,10},{9,11},{10,... | collective-permute-start | bytes 1327112 | tf_op jit(solution)/shard_map/ppermute | solution.py:38
  73.7 1.2 collective-permute-start.7
  74.9 1.0 gather_fusion
  75.9 0.7 fusion.31
  76.6 27.8 %all-gather = s32[16,1,128]{2,1,0:T(1,128)S(1)} all-gather(s32[1,1,128]{2,1,0:T(1,128)S(1)} %fusion.31), channel_id=1, replica_groups=mesh['y'=4,'z'=8,'c'=2,'x'=4] {'y','x'}, dimensions={0}, use_global_device_ids=true | all-gather | bytes 8704 | tf_op jit(solution)/shard_map/all_gather | solution.py:245
  104.3 0.6 fusion.13.codes
  105.0 6.8 %shard_map.64.lst = s32[640]{0:T(1024)} custom-call(s32[2048]{0:T(1024)} %fusion.13.codes), custom_call_target="tpu_custom_call" | custom-call | tf_op jit(solution)/shard_map/pallas_call | solution.py:272
  111.8 0.9 copy-done.7
  112.7 14.7 %shard_map.65 = (bf16[16,272,128]{2,1,0:T(8,128)(2,1)}, bf16[520,64,64]{2,1,0:T(8,128)(2,1)}) custom-call(s32[640]{0:T(1024)} %shard_map.64.lst, bf16[4096,1280]{1,0:T(8,128)(2,1)} %all-gather.3.cloned.1.call-done.keys, bf16[1024,1152]{1,0:T(8,128)(2,1)} %bitcast.22, bf16[768,1152]{1,0:T(8,128)(2,1)} %collective-permute-done.3.refs_1_, ...), custom_call_target="tpu_custom_call" | custom-call | tf_op jit(solution)/shard_map/pallas_call | solution.py:288
  127.4 3.7 %all-to-all-start = ((bf16[16,272,128]{2,1,0:T(8,128)(2,1)}), bf16[16,272,128]{2,1,0:T(8,128)(2,1)S(1)}, u32[]{:S(2)}, u32[]{:S(2)}) async-start(bf16[16,272,128]{2,1,0:T(8,128)(2,1)} %get-tuple-element.30), calls=%async_computation | async-start | bytes 2228224 | tf_op jit(solution)/shard_map/all_to_all | solution.py:306
  131.1 2.7 %shard_map.66 = (bf16[4,64,64]{2,1,0:T(8,128)(2,1)}, f32[4,64,256]{2,1,0:T(8,128)}) custom-call(bf16[256,1280]{1,0:T(8,128)(2,1)} %bitcast.24), custom_call_target="tpu_custom_call" | custom-call | tf_op jit(solution)/shard_map/pallas_call | solution.py:278
  133.9 11.3 %all-to-all-done.got = bf16[16,272,128]{2,1,0:T(8,128)(2,1)S(1)} async-done(((bf16[16,272,128]{2,1,0:T(8,128)(2,1)}), bf16[16,272,128]{2,1,0:T(8,128)(2,1)S(1)}, u32[]{:S(2)}, u32[]{:S(2)}) %all-to-all-start) | async-done | bytes 1114144 | tf_op jit(solution)/shard_map/all_to_all | solution.py:306
  145.1 0.8 broadcast_in_dim.58.marks
  146.0 0.2 copy-done.4
  146.2 2.5 %shard_map.67 = (bf16[8,4,64,128]{3,2,1,0:T(8,128)(2,1)}, f32[4,64,128]{2,1,0:T(8,128)}, f32[4,64,128]{2,1,0:T(8,128)}) custom-call(bf16[16,272,128]{2,1,0:T(8,128)(2,1)} %copy-done.4, f32[4,64,256]{2,1,0:T(8,128)} %get-tuple-element.32.base, bf16[4,64,64]{2,1,0:T(8,128)(2,1)} %get-tuple-element.33.weights, bf16[4,64,128]{2,1,0:T(8,128)(2,1)} %get-tuple-element.38.prior, ...), custom_call_target="tpu_custom_call" | custom-call | tf_op jit(solution)/shard_map/pallas_call | solution.py:308
  148.7 20.9 %all_to_all.15 = bf16[8,4,64,128]{3,2,1,0:T(8,128)(2,1)S(1)} all-to-all(bf16[8,4,64,128]{3,2,1,0:T(8,128)(2,1)} %get-tuple-element.34), channel_id=1, replica_groups=mesh['y'=4,'z'=8,'c'=2,'x'=4] {'z'}, dimensions={0} | all-to-all | bytes 1048576 | tf_op jit(solution)/shard_map/all_to_all | solution.py:318
  169.5 8.0 %collective-permute-start.10 = (bf16[32,64,128]{2,1,0:T(8,128)(2,1)S(1)}, bf16[32,64,128]{2,1,0:T(8,128)(2,1)S(1)}, u32[]{:S(2)}, u32[]{:S(2)}) collective-permute-start(bf16[32,64,128]{2,1,0:T(8,128)(2,1)S(1)} %bitcast.26), channel_id=1, source_target_pairs={{0,4},{4,0},{1,5},{5,1},{2,6},{6,2},{3,7},{7,3},{8,12},{12,8},{9,1... | collective-permute-start | bytes 1572872 | tf_op jit(solution)/shard_map/ppermute | solution.py:38
  177.5 1.5 collective-permute-done.10.far
  179.0 0.8 copy-done.8
  179.8 5.4 %shard_map.68 = bf16[64,64,128]{2,1,0:T(8,128)(2,1)} custom-call(s32[640]{0:T(1024)} %shard_map.64.lst, bf16[520,64,64]{2,1,0:T(8,128)(2,1)} %get-tuple-element.29.weights_in, bf16[32,64,128]{2,1,0:T(8,128)(2,1)} %bitcast.27, bf16[32,64,128]{2,1,0:T(8,128)(2,1)} %copy-done.8), custom_call_target="tpu_custom_call" | custom-call | tf_op jit(solution)/shard_map/pallas_call | solution.py:322
  185.2 21.0 %all_to_all.16 = bf16[64,64,128]{2,1,0:T(8,128)(2,1)} all-to-all(bf16[64,64,128]{2,1,0:T(8,128)(2,1)} %shard_map.68), channel_id=1, replica_groups=mesh['y'=4,'z'=8,'c'=2,'x'=4] {'y','x'}, dimensions={0} | all-to-all | bytes 2097152 | tf_op jit(solution)/shard_map/all_to_all | solution.py:334
  206.2 2.1 shard_map.69
  (52 shorter events, 0.6 us)
Async XLA Ops:
  6.5 68.4 %copy-start = (s32[1024]{0:T(1024)S(1)}, s32[1024]{0:T(1024)}, u32[]{:S(2)}) copy-start(s32[1024]{0:T(1024)} %param.11) | copy-start | bytes 12292
  6.5 11.7 %copy-start.2 = (bf16[16,64,1152]{2,1,0:T(8,128)(2,1)S(1)}, bf16[16,64,1152]{2,1,0:T(8,128)(2,1)}, u32[]{:S(2)}) copy-start(bf16[16,64,1152]{2,1,0:T(8,128)(2,1)} %param.6) | copy-start | bytes 7077892
  6.5 105.3 %all-gather.3.cloned.1.call-start = ((), (), s32[]{:S(2)}) async-start(), calls=%async_computation.3 | async-start | bytes 11141120 | tf_op jit(solution)/shard_map/all_gather | solution.py:230
  12.3 6.5 %copy-start.3 = (bf16[16,64,1152]{2,1,0:T(8,128)(2,1)S(1)}, bf16[16,64,1152]{2,1,0:T(8,128)(2,1)}, u32[]{:S(2)}) copy-start(bf16[16,64,1152]{2,1,0:T(8,128)(2,1)} %param.6) | copy-start | bytes 7077892
  12.3 8.5 %collective-permute-start.2 = (bf16[64,1152]{1,0:T(8,128)(2,1)S(1)}, bf16[64,1152]{1,0:T(8,128)(2,1)S(1)}, u32[]{:S(2)}, u32[]{:S(2)}) collective-permute-start(bf16[64,1152]{1,0:T(8,128)(2,1)S(1)} %slice_bitcast_fusion), channel_id=1, source_target_pairs={{0,64},{64,128},{128,192},{192,0},{1,65},{65,129},{129,193},{193,1... | collective-permute-start | bytes 442376 | tf_op jit(solution)/shard_map/ppermute | solution.py:38
  14.5 9.0 %collective-permute-start.1 = (bf16[64,1152]{1,0:T(8,128)(2,1)S(1)}, bf16[64,1152]{1,0:T(8,128)(2,1)S(1)}, u32[]{:S(2)}, u32[]{:S(2)}) collective-permute-start(bf16[64,1152]{1,0:T(8,128)(2,1)S(1)} %slice_bitcast_fusion), channel_id=1, source_target_pairs={{0,128},{64,192},{128,0},{192,64},{1,129},{65,193},{129,1},{193,65... | collective-permute-start | bytes 442376 | tf_op jit(solution)/shard_map/ppermute | solution.py:38
  17.1 6.4 %collective-permute-start = (bf16[64,1152]{1,0:T(8,128)(2,1)S(1)}, bf16[64,1152]{1,0:T(8,128)(2,1)S(1)}, u32[]{:S(2)}, u32[]{:S(2)}) collective-permute-start(bf16[64,1152]{1,0:T(8,128)(2,1)S(1)} %slice_bitcast_fusion), channel_id=1, source_target_pairs={{0,192},{64,0},{128,64},{192,128},{1,193},{65,1},{129,65},{193,129... | collective-permute-start | bytes 442376 | tf_op jit(solution)/shard_map/ppermute | solution.py:38
  19.2 45.6 %copy-start.1 = (bf16[16,64,1152]{2,1,0:T(8,128)(2,1)}, bf16[16,64,1152]{2,1,0:T(8,128)(2,1)S(1)}, u32[]{:S(2)}) copy-start(bf16[16,64,1152]{2,1,0:T(8,128)(2,1)S(1)} %fusion.1) | copy-start | bytes 7077892
  19.2 7.0 %copy-start.12 = (s32[16]{0:T(128)S(1)}, s32[16]{0:T(128)}, u32[]{:S(2)}) copy-start(s32[16]{0:T(128)} %param.10) | copy-start | bytes 196
  23.5 3.4 %copy-start.9 = (bf16[64,1152]{1,0:T(8,128)(2,1)}, bf16[64,1152]{1,0:T(8,128)(2,1)S(1)}, u32[]{:S(2)}) copy-start(bf16[64,1152]{1,0:T(8,128)(2,1)S(1)} %collective-permute-done) | copy-start | bytes 442372
  23.5 40.0 %collective-permute-start.4 = (bf16[768,1152]{1,0:T(8,128)(2,1)}, bf16[768,1152]{1,0:T(8,128)(2,1)}, u32[]{:S(2)}, u32[]{:S(2)}) collective-permute-start(bf16[768,1152]{1,0:T(8,128)(2,1)} %bitcast.3), channel_id=1, source_target_pairs={{0,64},{64,128},{128,192},{192,0},{1,65},{65,129},{129,193},{193,1... | collective-permute-start | bytes 5308424 | tf_op jit(solution)/shard_map/ppermute | solution.py:38
  24.2 40.7 %collective-permute-start.3 = (bf16[768,1152]{1,0:T(8,128)(2,1)}, bf16[768,1152]{1,0:T(8,128)(2,1)}, u32[]{:S(2)}, u32[]{:S(2)}) collective-permute-start(bf16[768,1152]{1,0:T(8,128)(2,1)} %bitcast.3), channel_id=1, source_target_pairs={{0,192},{64,0},{128,64},{192,128},{1,193},{65,1},{129,65},{193,129... | collective-permute-start | bytes 5308424 | tf_op jit(solution)/shard_map/ppermute | solution.py:38
  28.2 40.8 %copy-start.10 = (bf16[64,1152]{1,0:T(8,128)(2,1)S(1)}, bf16[64,1152]{1,0:T(8,128)(2,1)}, u32[]{:S(2)}) copy-start(bf16[64,1152]{1,0:T(8,128)(2,1)} %copy-done.9) | copy-start | bytes 442372
  64.8 46.9 %collective-permute-start.5 = (bf16[384,1152]{1,0:T(8,128)(2,1)S(1)}, bf16[384,1152]{1,0:T(8,128)(2,1)}, u32[]{:S(2)}, u32[]{:S(2)}) collective-permute-start(bf16[384,1152]{1,0:T(8,128)(2,1)S(1)} %slice.20), channel_id=1, source_target_pairs={{0,64},{64,128},{128,192},{192,0},{1,65},{65,129},{129,193},{193,1... | collective-permute-start | bytes 2654216 | tf_op jit(solution)/shard_map/ppermute | solution.py:38
  64.9 39.4 %copy-start.11 = (s32[2048]{0:T(1024)S(1)}, s32[2048]{0:T(1024)}, u32[]{:S(2)}) copy-start(s32[2048]{0:T(1024)} %or.34) | copy-start | bytes 24580
  66.3 45.5 %collective-permute-start.6 = (bf16[384,1152]{1,0:T(8,128)(2,1)S(1)}, bf16[384,1152]{1,0:T(8,128)(2,1)S(1)}, u32[]{:S(2)}, u32[]{:S(2)}) collective-permute-start(bf16[384,1152]{1,0:T(8,128)(2,1)S(1)} %slice.21), channel_id=1, source_target_pairs={{0,192},{64,0},{128,64},{192,128},{1,193},{65,1},{129,65},{193,129... | collective-permute-start | bytes 2654216 | tf_op jit(solution)/shard_map/ppermute | solution.py:38
  69.0 42.9 %copy-start.6 = (bf16[192,1152]{1,0:T(8,128)(2,1)}, bf16[192,1152]{1,0:T(8,128)(2,1)S(1)}, u32[]{:S(2)}) copy-start(bf16[192,1152]{1,0:T(8,128)(2,1)S(1)} %pad_maximum_fusion.1.refs_5_) | copy-start | bytes 1327108
  70.0 41.8 %collective-permute-start.9 = (bf16[192,1152]{1,0:T(8,128)(2,1)S(1)}, bf16[192,1152]{1,0:T(8,128)(2,1)}, u32[]{:S(2)}, u32[]{:S(2)}) collective-permute-start(bf16[192,1152]{1,0:T(8,128)(2,1)S(1)} %pad_maximum_fusion.1.refs_5_), channel_id=1, source_target_pairs={{0,1},{1,2},{2,3},{3,0},{4,5},{5,6},{6,7},{7,4},{8,9},{9,10},{10,1... | collective-permute-start | bytes 1327112 | tf_op jit(solution)/shard_map/ppermute | solution.py:38
  71.3 40.5 %collective-permute-start.8 = (bf16[192,1152]{1,0:T(8,128)(2,1)S(1)}, bf16[192,1152]{1,0:T(8,128)(2,1)}, u32[]{:S(2)}, u32[]{:S(2)}) collective-permute-start(bf16[192,1152]{1,0:T(8,128)(2,1)S(1)} %pad_maximum_fusion.1.refs_5_), channel_id=1, source_target_pairs={{0,2},{1,3},{2,0},{3,1},{4,6},{5,7},{6,4},{7,5},{8,10},{9,11},{10,... | collective-permute-start | bytes 1327112 | tf_op jit(solution)/shard_map/ppermute | solution.py:38
  73.7 38.0 %collective-permute-start.7 = (bf16[192,1152]{1,0:T(8,128)(2,1)S(1)}, bf16[192,1152]{1,0:T(8,128)(2,1)}, u32[]{:S(2)}, u32[]{:S(2)}) collective-permute-start(bf16[192,1152]{1,0:T(8,128)(2,1)S(1)} %pad_maximum_fusion.1.refs_5_), channel_id=1, source_target_pairs={{0,3},{1,0},{2,1},{3,2},{4,7},{5,4},{6,5},{7,6},{8,11},{9,8},{10,9... | collective-permute-start | bytes 1327112 | tf_op jit(solution)/shard_map/ppermute | solution.py:38
  111.8 0.9 copy-start.7
  127.4 17.7 %all-to-all-start = ((bf16[16,272,128]{2,1,0:T(8,128)(2,1)}), bf16[16,272,128]{2,1,0:T(8,128)(2,1)S(1)}, u32[]{:S(2)}, u32[]{:S(2)}) async-start(bf16[16,272,128]{2,1,0:T(8,128)(2,1)} %get-tuple-element.30), calls=%async_computation | async-start | bytes 2228224 | tf_op jit(solution)/shard_map/all_to_all | solution.py:306
  145.1 1.0 copy-start.4
  169.5 9.5 %copy-start.5 = (bf16[8,4,64,128]{3,2,1,0:T(8,128)(2,1)}, bf16[8,4,64,128]{3,2,1,0:T(8,128)(2,1)S(1)}, u32[]{:S(2)}) copy-start(bf16[8,4,64,128]{3,2,1,0:T(8,128)(2,1)S(1)} %all_to_all.15) | copy-start | bytes 1572868
  169.5 9.5 %collective-permute-start.10 = (bf16[32,64,128]{2,1,0:T(8,128)(2,1)S(1)}, bf16[32,64,128]{2,1,0:T(8,128)(2,1)S(1)}, u32[]{:S(2)}, u32[]{:S(2)}) collective-permute-start(bf16[32,64,128]{2,1,0:T(8,128)(2,1)S(1)} %bitcast.26), channel_id=1, source_target_pairs={{0,4},{4,0},{1,5},{5,1},{2,6},{6,2},{3,7},{7,3},{8,12},{12,8},{9,1... | collective-permute-start | bytes 1572872 | tf_op jit(solution)/shard_map/ppermute | solution.py:38
  179.0 0.8 copy-start.8
Sparse Core Ops, SparseCore 0:
  12.4 69.9 all-gather.2

commit v6 on v5

--- a/solution.py
+++ b/solution.py
@@ -28,7 +28,6 @@
 LIST = 640
 STEPS_AT = 600
 SPARE = QBLOCKS
-VMEM = 56 * 1024 * 1024
 UNREAL = 1024.0
 sharpness = 2.0 * math.sqrt(FEAT)
 
@@ -208,7 +207,10 @@
 smem = pl.BlockSpec(memory_space=pltpu.SMEM)
 vmem = pl.BlockSpec(memory_space=pltpu.VMEM)
 hbm = pl.BlockSpec(memory_space=pl.ANY)
-params = pltpu.CompilerParams(vmem_limit_bytes=VMEM)
+
+
+def limit(mebibytes):
+    return pltpu.CompilerParams(vmem_limit_bytes=mebibytes * 1024 * 1024)
 
 
 def normalize(values):
@@ -245,9 +247,6 @@
     target = lax.all_gather(jnp.where(in_list, target, -1), ("y", "x"), axis=0)
 
     turned = [turned, shift(turned, "x", -1), shift(turned, "x", 2), shift(turned, "x", 1)]
-    half = STRAIGHT * FRAMES // 2
-    across = [shift(behind[:half], "y", 1), shift(ahead[half:], "y", -1)]
-
     target = target.reshape(NY, NX, ROWS, per_list)
     source_y = jnp.arange(NY, dtype=jnp.int32)[:, None, None, None]
     source_row = jnp.arange(ROWS, dtype=jnp.int32)[None, None, :, None]
@@ -274,7 +273,11 @@
         out_shape=jax.ShapeDtypeStruct((LIST,), jnp.int32),
         in_specs=[smem],
         out_specs=smem,
+        compiler_params=limit(1),
     )(codes)
+    half = STRAIGHT * FRAMES // 2
+    behind, ahead, turned, lst = lax.optimization_barrier((behind, ahead, turned, lst))
+    across = [shift(behind[:half], "y", 1), shift(ahead[half:], "y", -1)]
     own_weights, own_base = pl.pallas_call(
         own_kernel,
         out_shape=(
@@ -283,6 +286,7 @@
         ),
         in_specs=[vmem],
         out_specs=(vmem, vmem),
+        compiler_params=limit(4),
     )(piece)
 
     send, weights = pl.pallas_call(
@@ -301,7 +305,7 @@
             pltpu.SemaphoreType.DMA((10,)),
             pltpu.SemaphoreType.DMA,
         ],
-        compiler_params=params,
+        compiler_params=limit(38),
     )(lst, keys, all_units.reshape(ROWS * FRAMES, FEAT), ahead, *across, behind, *turned)
     got = lax.all_to_all(send, ("y", "x"), split_axis=0, concat_axis=0, tiled=True)
 
@@ -314,6 +318,7 @@
         ),
         in_specs=[vmem] * 5,
         out_specs=(vmem,) * 3,
+        compiler_params=limit(8),
     )(got, own_base, own_weights, prior, marks)
     near_scores = lax.all_to_all(masked, "z", split_axis=0, concat_axis=0, tiled=True)
     near_scores = near_scores.reshape(NZ * PART, FRAMES, CH)
@@ -329,7 +334,7 @@
             pltpu.VMEM((SLOTS, FRAMES, FRAMES), jnp.bfloat16),
             pltpu.SemaphoreType.DMA,
         ],
-        compiler_params=params,
+        compiler_params=limit(16),
     )(lst, weights, near_scores, far_scores)
     got = lax.all_to_all(send, ("y", "x"), split_axis=0, concat_axis=0, tiled=True)
     return pl.pallas_call(
@@ -337,6 +342,7 @@
         out_shape=jax.ShapeDtypeStruct((PART, FRAMES, CH), jnp.bfloat16),
         in_specs=[vmem] * 4,
         out_specs=vmem,
+        compiler_params=limit(8),
     )(got.reshape(NY * NX, PART, FRAMES, CH), own_second, denominator, prior)
 
 

time: 216 us -> 205 us (0.949)
  waiting for transfers between devices: 51 us -> 32 us
  blocking collectives: 69.6 us -> 85.1 us
  Pallas kernels: 34.2 us -> 25.2 us
  local copies, waits for them, and re-layouts: 10.4 us -> 15.4 us
    ppermute x11, waiting for transfers between devices: 39.7 us -> 18.9 us  [shift(): lax.ppermute(value, axis, [(i, (i + step) % size) for i in range(size)])]
    all_gather x1, blocking collectives: 27.8 us -> 46.3 us  [body(): target = lax.all_gather(jnp.where(in_list, target, -1), ('y', 'x'), axis=0)]
    unnamed x26 -> x24, local copies, waits for them, and re-layouts: 1.91 us -> 9.75 us
    pallas_call x1, Pallas kernels: 14.7 us -> 12.1 us  [body(): pl.pallas_call(first_kernel, out_shape=(jax.ShapeDtypeStruct((NY * NX, SE...]
  transfers between devices with their start and end apart: 13 -> 13, of which waited for: 4 -> 4; matrix products, arithmetic and copies ran while one was open for 5% -> 3% of each run, Pallas kernels for 4% -> 4%
where the time goes in v6:
time: 205 us
  blocking collectives  85.1 us (42%)
  waiting for transfers between devices  32 us (16%)
  starting transfers between devices  26.8 us (13%)
  Pallas kernels  25.2 us (12%)
  local copies, waits for them, and re-layouts  15.4 us (8%)
  between operations  13.7 us (7%)
  other arithmetic  6.57 us (3%)
    all_gather x1, blocking collectives, body(): target = lax.all_gather(jnp.where(in_list, target, -1), ('y', 'x'), axis=0)  46.3 us
    ppermute x11, starting transfers between devices, shift(): lax.ppermute(value, axis, [(i, (i + step) % size) for i in range(size)])  23 us
    all_to_all x1, blocking collectives, body(): lax.all_to_all(masked, 'z', split_axis=0, concat_axis=0, tiled=True)  19.9 us
    ppermute x11, waiting for transfers between devices, shift(): lax.ppermute(value, axis, [(i, (i + step) % size) for i in range(size)])  18.9 us
    all_to_all x1, blocking collectives, body(): lax.all_to_all(send, ('y', 'x'), split_axis=0, concat_axis=0, tiled=True)  18.9 us
    all_to_all x1, waiting for transfers between devices, body(): lax.all_to_all(send, ('y', 'x'), split_axis=0, concat_axis=0, tiled=True)  13 us
    pallas_call x1, Pallas kernels, body(): pl.pallas_call(first_kernel, out_shape=(jax.ShapeDtypeStruct((NY * NX, SE...  12.1 us
    unnamed x24, local copies, waits for them, and re-layouts  9.75 us
  transfers between devices with their start and end apart: 13, of which 4 were waited for; matrix products, arithmetic and copies ran while one was open for 3% of the time, Pallas kernels for 4%

profile of v6, /device:TPU:1, one launch (start us, length us, event | category | flops | bytes accessed | tf_op | source)
XLA Modules:
  0.0 204.7 jit_solution(13253110908267616171)
XLA Ops:
  6.6 0.8 broadcast_compare_fusion.1
  7.4 1.3 fusion.2
  8.7 1.2 fusion.3
  9.9 0.9 broadcast_select_fusion
  10.9 0.9 pad_maximum_fusion
  11.8 2.2 %collective-permute-start.2 = (bf16[64,1152]{1,0:T(8,128)(2,1)S(1)}, bf16[64,1152]{1,0:T(8,128)(2,1)S(1)}, u32[]{:S(2)}, u32[]{:S(2)}) collective-permute-start(bf16[64,1152]{1,0:T(8,128)(2,1)S(1)} %slice_bitcast_fusion), channel_id=1, source_target_pairs={{0,64},{64,128},{128,192},{192,0},{1,65},{65,129},{129,193},{193,1... | collective-permute-start | bytes 442376 | tf_op jit(solution)/shard_map/ppermute | solution.py:37
  14.0 2.6 %collective-permute-start.1 = (bf16[64,1152]{1,0:T(8,128)(2,1)S(1)}, bf16[64,1152]{1,0:T(8,128)(2,1)S(1)}, u32[]{:S(2)}, u32[]{:S(2)}) collective-permute-start(bf16[64,1152]{1,0:T(8,128)(2,1)S(1)} %slice_bitcast_fusion), channel_id=1, source_target_pairs={{0,128},{64,192},{128,0},{192,64},{1,129},{65,193},{129,1},{193,65... | collective-permute-start | bytes 442376 | tf_op jit(solution)/shard_map/ppermute | solution.py:37
  16.6 1.1 collective-permute-start
  17.8 0.1 lt.97
  17.9 0.5 fusion
  18.5 1.1 copy-done.9
  19.6 0.5 fusion.1
  20.2 0.1 or.31
  20.3 1.4 slice.19
  21.7 1.3 collective-permute-done.1
  23.0 0.8 collective-permute-start.4
  23.8 0.7 collective-permute-start.3
  24.7 0.1 or.34
  25.1 0.1 reshape.425
  25.1 2.0 collective-permute-start.7
  27.1 2.5 %collective-permute-start.6 = (bf16[192,1152]{1,0:T(8,128)(2,1)S(1)}, bf16[192,1152]{1,0:T(8,128)(2,1)}, u32[]{:S(2)}, u32[]{:S(2)}) collective-permute-start(bf16[192,1152]{1,0:T(8,128)(2,1)S(1)} %pad_maximum_fusion.1.refs_5_), channel_id=1, source_target_pairs={{0,2},{1,3},{2,0},{3,1},{4,6},{5,7},{6,4},{7,5},{8,10},{9,11},{10,... | collective-permute-start | bytes 1327112 | tf_op jit(solution)/shard_map/ppermute | solution.py:37
  29.6 1.2 collective-permute-start.5
  30.8 1.0 gather_fusion
  31.8 46.3 %all-gather = s32[16,1,128]{2,1,0:T(1,128)S(1)} all-gather(s32[1,1,128]{2,1,0:T(1,128)S(1)} %fusion.31), channel_id=1, replica_groups=mesh['y'=4,'z'=8,'c'=2,'x'=4] {'y','x'}, dimensions={0}, use_global_device_ids=true | all-gather | bytes 8704 | tf_op jit(solution)/shard_map/all_gather | solution.py:247
  78.1 6.7 %shard_map.64.lst = s32[640]{0:T(1024)S(1)} custom-call(s32[2048]{0:T(1024)S(1)} %fusion.13.codes), custom_call_target="tpu_custom_call" | custom-call | tf_op jit(solution)/shard_map/pallas_call | solution.py:271
  84.9 1.2 slice.15
  86.1 1.2 slice.14
  87.4 0.1 collective-permute-start.8
  87.5 2.7 %collective-permute-start.9 = (bf16[384,1152]{1,0:T(8,128)(2,1)S(1)}, bf16[384,1152]{1,0:T(8,128)(2,1)S(1)}, u32[]{:S(2)}, u32[]{:S(2)}) collective-permute-start(bf16[384,1152]{1,0:T(8,128)(2,1)S(1)} %slice.15), channel_id=1, source_target_pairs={{0,192},{64,0},{128,64},{192,128},{1,193},{65,1},{129,65},{193,129... | collective-permute-start | bytes 2654216 | tf_op jit(solution)/shard_map/ppermute | solution.py:37
  90.1 16.0 %collective-permute-done.8.refs_2_ = bf16[384,1152]{1,0:T(8,128)(2,1)S(1)} collective-permute-done((bf16[384,1152]{1,0:T(8,128)(2,1)S(1)}, bf16[384,1152]{1,0:T(8,128)(2,1)S(1)}, u32[]{:S(2)}, u32[]{:S(2)}) %collective-permute-start.8) | collective-permute-done | bytes 884768 | tf_op jit(solution)/shard_map/ppermute | solution.py:37
  106.1 0.9 copy-done.4
  107.1 1.0 copy-done.6
  108.0 1.2 copy-done.5
  109.2 1.2 copy-done.7
  110.3 12.1 %shard_map.65 = (bf16[16,272,128]{2,1,0:T(8,128)(2,1)S(1)}, bf16[520,64,64]{2,1,0:T(8,128)(2,1)}) custom-call(s32[640]{0:T(1024)S(1)} %shard_map.64.lst, bf16[4096,1280]{1,0:T(8,128)(2,1)} %all-gather.3.cloned.1.call-done.keys, bf16[1024,1152]{1,0:T(8,128)(2,1)S(1)} %bitcast.22, bf16[768,1152]{1,0:T(8,128)(2,1)} %collective-permute-done.4.refs_1_, ...), custom_call_target="tpu_custom_call" | custom-call | tf_op jit(solution)/shard_map/pallas_call | solution.py:292
  122.5 1.0 copy-done.3
  123.5 3.8 %all-to-all-start = ((bf16[16,272,128]{2,1,0:T(8,128)(2,1)}), bf16[16,272,128]{2,1,0:T(8,128)(2,1)S(1)}, u32[]{:S(2)}, u32[]{:S(2)}) async-start(bf16[16,272,128]{2,1,0:T(8,128)(2,1)} %copy-done.3), calls=%async_computation | async-start | bytes 2228224 | tf_op jit(solution)/shard_map/all_to_all | solution.py:310
  127.3 0.9 shard_map.66
  128.3 13.0 %all-to-all-done.got = bf16[16,272,128]{2,1,0:T(8,128)(2,1)S(1)} async-done(((bf16[16,272,128]{2,1,0:T(8,128)(2,1)}), bf16[16,272,128]{2,1,0:T(8,128)(2,1)S(1)}, u32[]{:S(2)}, u32[]{:S(2)}) %all-to-all-start) | async-done | bytes 1114144 | tf_op jit(solution)/shard_map/all_to_all | solution.py:310
  141.3 0.1 broadcast_in_dim.58.marks
  141.4 0.4 shard_map.67
  141.8 19.9 %all_to_all.15 = bf16[8,4,64,128]{3,2,1,0:T(8,128)(2,1)S(1)} all-to-all(bf16[8,4,64,128]{3,2,1,0:T(8,128)(2,1)S(1)} %get-tuple-element.48), channel_id=1, replica_groups=mesh['y'=4,'z'=8,'c'=2,'x'=4] {'z'}, dimensions={0} | all-to-all | bytes 1048576 | tf_op jit(solution)/shard_map/all_to_all | solution.py:323
  161.6 7.2 %collective-permute-start.10 = (bf16[32,64,128]{2,1,0:T(8,128)(2,1)S(1)}, bf16[32,64,128]{2,1,0:T(8,128)(2,1)S(1)}, u32[]{:S(2)}, u32[]{:S(2)}) collective-permute-start(bf16[32,64,128]{2,1,0:T(8,128)(2,1)S(1)} %bitcast.26), channel_id=1, source_target_pairs={{0,4},{4,0},{1,5},{5,1},{2,6},{6,2},{3,7},{7,3},{8,12},{12,8},{9,1... | collective-permute-start | bytes 1572872 | tf_op jit(solution)/shard_map/ppermute | solution.py:37
  168.9 1.5 collective-permute-done.10.far
  170.4 3.4 %copy-done.1 = bf16[520,64,64]{2,1,0:T(8,128)(2,1)S(1)} copy-done((bf16[520,64,64]{2,1,0:T(8,128)(2,1)S(1)}, bf16[520,64,64]{2,1,0:T(8,128)(2,1)}, u32[]{:S(2)}) %copy-start.1) | copy-done | bytes 4259864
  173.8 4.3 %shard_map.68 = bf16[64,64,128]{2,1,0:T(8,128)(2,1)S(1)} custom-call(s32[640]{0:T(1024)S(1)} %shard_map.64.lst, bf16[520,64,64]{2,1,0:T(8,128)(2,1)S(1)} %copy-done.1, bf16[32,64,128]{2,1,0:T(8,128)(2,1)S(1)} %bitcast.27, bf16[32,64,128]{2,1,0:T(8,128)(2,1)S(1)} %collective-permute-done.10.far), custom_call_target="tpu_custom_call" | custom-call | tf_op jit(solution)/shard_map/pallas_call | solution.py:327
  178.1 18.9 %all_to_all.16 = bf16[64,64,128]{2,1,0:T(8,128)(2,1)S(1)} all-to-all(bf16[64,64,128]{2,1,0:T(8,128)(2,1)S(1)} %shard_map.68), channel_id=1, replica_groups=mesh['y'=4,'z'=8,'c'=2,'x'=4] {'y','x'}, dimensions={0} | all-to-all | bytes 2097152 | tf_op jit(solution)/shard_map/all_to_all | solution.py:339
  197.0 0.8 shard_map.69
  (50 shorter events, 0.8 us)
Async XLA Ops:
  6.5 24.2 %copy-start = (s32[1024]{0:T(1024)S(1)}, s32[1024]{0:T(1024)}, u32[]{:S(2)}) copy-start(s32[1024]{0:T(1024)} %param.11) | copy-start | bytes 12292
  6.5 11.4 %copy-start.8 = (bf16[16,64,1152]{2,1,0:T(8,128)(2,1)S(1)}, bf16[16,64,1152]{2,1,0:T(8,128)(2,1)}, u32[]{:S(2)}) copy-start(bf16[16,64,1152]{2,1,0:T(8,128)(2,1)} %param.6) | copy-start | bytes 7077892
  6.5 11.2 %copy-start.11 = (s32[16]{0:T(128)S(1)}, s32[16]{0:T(128)}, u32[]{:S(2)}) copy-start(s32[16]{0:T(128)} %param.10) | copy-start | bytes 196
  6.5 101.5 %all-gather.3.cloned.1.call-start = ((), (), s32[]{:S(2)}) async-start(), calls=%async_computation.3 | async-start | bytes 11141120 | tf_op jit(solution)/shard_map/all_gather | solution.py:232
  11.8 9.9 %collective-permute-start.2 = (bf16[64,1152]{1,0:T(8,128)(2,1)S(1)}, bf16[64,1152]{1,0:T(8,128)(2,1)S(1)}, u32[]{:S(2)}, u32[]{:S(2)}) collective-permute-start(bf16[64,1152]{1,0:T(8,128)(2,1)S(1)} %slice_bitcast_fusion), channel_id=1, source_target_pairs={{0,64},{64,128},{128,192},{192,0},{1,65},{65,129},{129,193},{193,1... | collective-permute-start | bytes 442376 | tf_op jit(solution)/shard_map/ppermute | solution.py:37
  14.0 9.0 %collective-permute-start.1 = (bf16[64,1152]{1,0:T(8,128)(2,1)S(1)}, bf16[64,1152]{1,0:T(8,128)(2,1)S(1)}, u32[]{:S(2)}, u32[]{:S(2)}) collective-permute-start(bf16[64,1152]{1,0:T(8,128)(2,1)S(1)} %slice_bitcast_fusion), channel_id=1, source_target_pairs={{0,128},{64,192},{128,0},{192,64},{1,129},{65,193},{129,1},{193,65... | collective-permute-start | bytes 442376 | tf_op jit(solution)/shard_map/ppermute | solution.py:37
  16.6 6.4 %collective-permute-start = (bf16[64,1152]{1,0:T(8,128)(2,1)S(1)}, bf16[64,1152]{1,0:T(8,128)(2,1)S(1)}, u32[]{:S(2)}, u32[]{:S(2)}) collective-permute-start(bf16[64,1152]{1,0:T(8,128)(2,1)S(1)} %slice_bitcast_fusion), channel_id=1, source_target_pairs={{0,192},{64,0},{128,64},{192,128},{1,193},{65,1},{129,65},{193,129... | collective-permute-start | bytes 442376 | tf_op jit(solution)/shard_map/ppermute | solution.py:37
  17.9 1.7 copy-start.9
  20.3 4.6 %copy-start.10 = (s32[16,8]{0,1:T(8,128)S(1)}, s32[16,8]{0,1:T(8,128)}, u32[]{:S(2)}) copy-start(s32[16,8]{0,1:T(8,128)} %param.9) | copy-start | bytes 1540
  23.0 61.8 %collective-permute-start.4 = (bf16[768,1152]{1,0:T(8,128)(2,1)}, bf16[768,1152]{1,0:T(8,128)(2,1)}, u32[]{:S(2)}, u32[]{:S(2)}) collective-permute-start(bf16[768,1152]{1,0:T(8,128)(2,1)} %bitcast.3), channel_id=1, source_target_pairs={{0,192},{64,0},{128,64},{192,128},{1,193},{65,1},{129,65},{193,129... | collective-permute-start | bytes 5308424 | tf_op jit(solution)/shard_map/ppermute | solution.py:37
  23.8 61.0 %collective-permute-start.3 = (bf16[768,1152]{1,0:T(8,128)(2,1)}, bf16[768,1152]{1,0:T(8,128)(2,1)}, u32[]{:S(2)}, u32[]{:S(2)}) collective-permute-start(bf16[768,1152]{1,0:T(8,128)(2,1)} %bitcast.3), channel_id=1, source_target_pairs={{0,64},{64,128},{128,192},{192,0},{1,65},{65,129},{129,193},{193,1... | collective-permute-start | bytes 5308424 | tf_op jit(solution)/shard_map/ppermute | solution.py:37
  25.1 59.7 %collective-permute-start.7 = (bf16[192,1152]{1,0:T(8,128)(2,1)S(1)}, bf16[192,1152]{1,0:T(8,128)(2,1)S(1)}, u32[]{:S(2)}, u32[]{:S(2)}) collective-permute-start(bf16[192,1152]{1,0:T(8,128)(2,1)S(1)} %pad_maximum_fusion.1.refs_5_), channel_id=1, source_target_pairs={{0,1},{1,2},{2,3},{3,0},{4,5},{5,6},{6,7},{7,4},{8,9},{9,10},{10,1... | collective-permute-start | bytes 1327112 | tf_op jit(solution)/shard_map/ppermute | solution.py:37
  27.1 57.7 %collective-permute-start.6 = (bf16[192,1152]{1,0:T(8,128)(2,1)S(1)}, bf16[192,1152]{1,0:T(8,128)(2,1)}, u32[]{:S(2)}, u32[]{:S(2)}) collective-permute-start(bf16[192,1152]{1,0:T(8,128)(2,1)S(1)} %pad_maximum_fusion.1.refs_5_), channel_id=1, source_target_pairs={{0,2},{1,3},{2,0},{3,1},{4,6},{5,7},{6,4},{7,5},{8,10},{9,11},{10,... | collective-permute-start | bytes 1327112 | tf_op jit(solution)/shard_map/ppermute | solution.py:37
  29.6 55.3 %collective-permute-start.5 = (bf16[192,1152]{1,0:T(8,128)(2,1)S(1)}, bf16[192,1152]{1,0:T(8,128)(2,1)}, u32[]{:S(2)}, u32[]{:S(2)}) collective-permute-start(bf16[192,1152]{1,0:T(8,128)(2,1)S(1)} %pad_maximum_fusion.1.refs_5_), channel_id=1, source_target_pairs={{0,3},{1,0},{2,1},{3,2},{4,7},{5,4},{6,5},{7,6},{8,11},{9,8},{10,9... | collective-permute-start | bytes 1327112 | tf_op jit(solution)/shard_map/ppermute | solution.py:37
  87.4 18.8 %collective-permute-start.8 = (bf16[384,1152]{1,0:T(8,128)(2,1)S(1)}, bf16[384,1152]{1,0:T(8,128)(2,1)S(1)}, u32[]{:S(2)}, u32[]{:S(2)}) collective-permute-start(bf16[384,1152]{1,0:T(8,128)(2,1)S(1)} %slice.14), channel_id=1, source_target_pairs={{0,64},{64,128},{128,192},{192,0},{1,65},{65,129},{129,193},{193,1... | collective-permute-start | bytes 2654216 | tf_op jit(solution)/shard_map/ppermute | solution.py:37
  87.5 19.6 %collective-permute-start.9 = (bf16[384,1152]{1,0:T(8,128)(2,1)S(1)}, bf16[384,1152]{1,0:T(8,128)(2,1)S(1)}, u32[]{:S(2)}, u32[]{:S(2)}) collective-permute-start(bf16[384,1152]{1,0:T(8,128)(2,1)S(1)} %slice.15), channel_id=1, source_target_pairs={{0,192},{64,0},{128,64},{192,128},{1,193},{65,1},{129,65},{193,129... | collective-permute-start | bytes 2654216 | tf_op jit(solution)/shard_map/ppermute | solution.py:37
  106.1 0.9 copy-start.4
  107.1 1.0 copy-start.6
  108.0 1.2 copy-start.5
  109.2 1.2 copy-start.7
  122.5 1.0 copy-start.3
  123.5 3.8 %copy-start.2 = (bf16[4,64,1280]{2,1,0:T(8,128)(2,1)S(1)}, bf16[4,64,1280]{2,1,0:T(8,128)(2,1)}, u32[]{:S(2)}) copy-start(bf16[4,64,1280]{2,1,0:T(8,128)(2,1)} %pad_maximum_fusion) | copy-start | bytes 1966084
  123.5 17.8 %all-to-all-start = ((bf16[16,272,128]{2,1,0:T(8,128)(2,1)}), bf16[16,272,128]{2,1,0:T(8,128)(2,1)S(1)}, u32[]{:S(2)}, u32[]{:S(2)}) async-start(bf16[16,272,128]{2,1,0:T(8,128)(2,1)} %copy-done.3), calls=%async_computation | async-start | bytes 2228224 | tf_op jit(solution)/shard_map/all_to_all | solution.py:310
  161.6 8.8 %collective-permute-start.10 = (bf16[32,64,128]{2,1,0:T(8,128)(2,1)S(1)}, bf16[32,64,128]{2,1,0:T(8,128)(2,1)S(1)}, u32[]{:S(2)}, u32[]{:S(2)}) collective-permute-start(bf16[32,64,128]{2,1,0:T(8,128)(2,1)S(1)} %bitcast.26), channel_id=1, source_target_pairs={{0,4},{4,0},{1,5},{5,1},{2,6},{6,2},{3,7},{7,3},{8,12},{12,8},{9,1... | collective-permute-start | bytes 1572872 | tf_op jit(solution)/shard_map/ppermute | solution.py:37
  170.4 3.4 %copy-start.1 = (bf16[520,64,64]{2,1,0:T(8,128)(2,1)S(1)}, bf16[520,64,64]{2,1,0:T(8,128)(2,1)}, u32[]{:S(2)}) copy-start(bf16[520,64,64]{2,1,0:T(8,128)(2,1)} %get-tuple-element.43.weights_in) | copy-start | bytes 12779524
Sparse Core Ops, SparseCore 0:
  11.9 69.9 all-gather.2

commit v7 on v6

--- a/solution.py
+++ b/solution.py
@@ -17,7 +17,8 @@
 FEAT = 1152
 CH = 128
 PART = ROWS // NX
-STRAIGHT = NX * (PART - 1)
+TURN = 2
+STRAIGHT = NX * (PART - TURN)
 QBLOCKS = NY * ROWS
 Q_TURN = ROWS + (NY - 1) * STRAIGHT
 UNROLL = 8
@@ -74,8 +75,8 @@
 
 
 def first_kernel(lst, keys, *refs):
-    queries = refs[:9]
-    send, weights_out, q, k, acc, w, sems, out_sem = refs[9:]
+    queries = refs[:10]
+    send, w, q, k, acc, sems = refs[10:]
     copies = [pltpu.make_async_copy(keys, k, sems.at[0])]
     at = 0
     for part in queries:
@@ -102,16 +103,14 @@
                 preferred_element_type=jnp.float32,
             )
             weights.append(jnp.exp(sharpness * affinity).astype(jnp.bfloat16))
-        for u in range(UNROLL):
-            w[i * UNROLL + u] = weights[u]
+        for u in range(UNROLL // 2):
+            w[i * (UNROLL // 2) + u] = jnp.concatenate(weights[2 * u:2 * u + 2], axis=1)
         sums = []
         for u, key_row in enumerate(key_rows):
             values = values_of(k[pl.ds(key_row, FRAMES), pl.ds(FEAT, CH)])
             sums.append(jnp.dot(weights[u], values, preferred_element_type=jnp.float32))
         for u, code in enumerate(codes):
             acc[code & 127] += sums[u]
-        group = pl.ds(i * UNROLL, UNROLL)
-        pltpu.make_async_copy(w.at[group], weights_out.at[group], out_sem).start()
         return carry
 
     lax.fori_loop(0, steps, step, 0)
@@ -134,31 +133,10 @@
 
     lax.fori_loop(0, NY * NX, finish, 0)
 
-    def drain(i, carry):
-        group = pl.ds(i * UNROLL, UNROLL)
-        pltpu.make_async_copy(w.at[group], weights_out.at[group], out_sem).wait()
-        return carry
-
-    lax.fori_loop(0, steps, drain, 0)
-
-
-def second_kernel(lst, weights_in, near, far, send, acc, w, in_sem):
+
+def second_kernel(lst, w, near, far, send, acc):
     steps = lst[STEPS_AT]
-
-    def fetch(i, carry):
-        group = pl.ds(i * UNROLL, UNROLL)
-        pltpu.make_async_copy(weights_in.at[group], w.at[group], in_sem).start()
-        return carry
-
-    lax.fori_loop(0, steps, fetch, 0)
     acc[...] = jnp.zeros_like(acc)
-
-    def drain(i, carry):
-        group = pl.ds(i * UNROLL, UNROLL)
-        pltpu.make_async_copy(weights_in.at[group], w.at[group], in_sem).wait()
-        return carry
-
-    lax.fori_loop(0, steps, drain, 0)
 
     def step(i, carry):
         codes = [lst[i * UNROLL + u] for u in range(UNROLL)]
@@ -166,7 +144,8 @@
         for u, code in enumerate(codes):
             block = (code >> 21) & 31
             scores = jnp.where(((code >> 20) & 1) == 0, near[block], far[block])
-            sums.append(jnp.dot(w[i * UNROLL + u], scores, preferred_element_type=jnp.float32))
+            weights = w[i * (UNROLL // 2) + u // 2][:, (u % 2) * FRAMES:(u % 2 + 1) * FRAMES]
+            sums.append(jnp.dot(weights, scores, preferred_element_type=jnp.float32))
         for u, code in enumerate(codes):
             acc[code & 127] += sums[u]
         return carry
@@ -231,22 +210,35 @@
 
     keys = lax.all_gather(piece, ("z", "c"), axis=0, tiled=True)
 
-    embeddings, piece = lax.optimization_barrier((embeddings, piece))
-    turn = units[0]
-    turned = [shift(turn, "y", -1), shift(turn, "y", 2), shift(turn, "y", 1)]
-    all_units = normalize(embeddings)
-    straight = all_units.reshape(NX, PART, FRAMES, FEAT)[:, 1:].reshape(STRAIGHT * FRAMES, FEAT)
-    turned, straight = lax.optimization_barrier((turned, straight))
-    behind, ahead = shift(straight, "y", 1), shift(straight, "y", -1)
-
-    turned = jnp.concatenate(turned, axis=0)
-    ids, block_home, turned = lax.optimization_barrier((neighbour_ids, block_home, turned))
+    embeddings, ids, block_home, piece = lax.optimization_barrier((embeddings, neighbour_ids, block_home, piece))
     target = jnp.take(block_home, ids.reshape(-1), axis=0)
     column = x * per_list + jnp.arange(per_list, dtype=jnp.int32)
     in_list = (column[None, :] < neighbour_count[:, None]).reshape(-1)
-    target = lax.all_gather(jnp.where(in_list, target, -1), ("y", "x"), axis=0)
-
-    turned = [turned, shift(turned, "x", -1), shift(turned, "x", 2), shift(turned, "x", 1)]
+    target = jnp.where(in_list, target, -1)
+    target = jnp.broadcast_to(target[None, :], (NY * NX, ROWS * per_list))
+    target = lax.all_to_all(target, ("y", "x"), split_axis=0, concat_axis=0, tiled=True)
+
+    units, target = lax.optimization_barrier((units, target))
+    turn = units[:TURN].reshape(TURN * FRAMES, FEAT)
+    turned = [
+        shift(turn, "y", -1), shift(turn[:FRAMES], "y", 2), shift(turn[FRAMES:], "y", -2), shift(turn, "y", 1)
+    ]
+    all_units = normalize(embeddings)
+    straight = all_units.reshape(NX, PART, FRAMES, FEAT)[:, TURN:].reshape(STRAIGHT * FRAMES, FEAT)
+    turned, straight = lax.optimization_barrier((turned, straight))
+    behind, ahead = shift(straight, "y", 1), shift(straight, "y", -1)
+    turned = jnp.concatenate(turned, axis=0)
+    half = turned.shape[0] // 2
+    turned = [
+        turned,
+        shift(turned, "x", -1),
+        shift(turned[:half], "x", 2),
+        shift(turned[half:], "x", -2),
+        shift(turned, "x", 1),
+    ]
+    half = STRAIGHT * FRAMES // 2
+    across = [shift(behind[:half], "y", 1), shift(ahead[half:], "y", -1)]
+
     target = target.reshape(NY, NX, ROWS, per_list)
     source_y = jnp.arange(NY, dtype=jnp.int32)[:, None, None, None]
     source_row = jnp.arange(ROWS, dtype=jnp.int32)[None, None, :, None]
@@ -261,9 +253,9 @@
         distance == 0,
         source_row,
         jnp.where(
-            within == 0,
-            Q_TURN + ((quarter - x) % NX) * (NY - 1) + distance - 1,
-            ROWS + (distance - 1) * STRAIGHT + quarter * (PART - 1) + within - 1,
+            within < TURN,
+            Q_TURN + (((quarter - x) % NX) * (NY - 1) + distance - 1) * TURN + within,
+            ROWS + (distance - 1) * STRAIGHT + quarter * (PART - TURN) + within - TURN,
         ),
     )
     codes = source | ((place * PART + inner) << 7) | (taken << 13) | (side << 20) | (((place // 2) * PART + inner) << 21)
@@ -275,9 +267,6 @@
         out_specs=smem,
         compiler_params=limit(1),
     )(codes)
-    half = STRAIGHT * FRAMES // 2
-    behind, ahead, turned, lst = lax.optimization_barrier((behind, ahead, turned, lst))
-    across = [shift(behind[:half], "y", 1), shift(ahead[half:], "y", -1)]
     own_weights, own_base = pl.pallas_call(
         own_kernel,
         out_shape=(
@@ -293,19 +282,17 @@
         first_kernel,
         out_shape=(
             jax.ShapeDtypeStruct((NY * NX, SEND, CH), jnp.bfloat16),
-            jax.ShapeDtypeStruct((SLOTS, FRAMES, FRAMES), jnp.bfloat16),
+            jax.ShapeDtypeStruct((SLOTS // 2, FRAMES, 2 * FRAMES), jnp.bfloat16),
         ),
-        in_specs=[smem] + [hbm] * 10,
-        out_specs=(vmem, hbm),
+        in_specs=[smem] + [hbm] * 11,
+        out_specs=(vmem, vmem),
         scratch_shapes=[
             pltpu.VMEM((QBLOCKS * FRAMES, FEAT), jnp.bfloat16),
             pltpu.VMEM((NZ * NC * PIECE, WIDE), jnp.bfloat16),
             pltpu.VMEM((QBLOCKS + 1, FRAMES, 2 * CH), jnp.float32),
-            pltpu.VMEM((SLOTS, FRAMES, FRAMES), jnp.bfloat16),
-            pltpu.SemaphoreType.DMA((10,)),
-            pltpu.SemaphoreType.DMA,
+            pltpu.SemaphoreType.DMA((11,)),
         ],
-        compiler_params=limit(38),
+        compiler_params=limit(32),
     )(lst, keys, all_units.reshape(ROWS * FRAMES, FEAT), ahead, *across, behind, *turned)
     got = lax.all_to_all(send, ("y", "x"), split_axis=0, concat_axis=0, tiled=True)
 
@@ -327,14 +314,10 @@
     send = pl.pallas_call(
         second_kernel,
         out_shape=jax.ShapeDtypeStruct((QBLOCKS, FRAMES, CH), jnp.bfloat16),
-        in_specs=[smem, hbm, vmem, vmem],
+        in_specs=[smem, vmem, vmem, vmem],
         out_specs=vmem,
-        scratch_shapes=[
-            pltpu.VMEM((QBLOCKS + 1, FRAMES, CH), jnp.float32),
-            pltpu.VMEM((SLOTS, FRAMES, FRAMES), jnp.bfloat16),
-            pltpu.SemaphoreType.DMA,
-        ],
-        compiler_params=limit(16),
+        scratch_shapes=[pltpu.VMEM((QBLOCKS + 1, FRAMES, CH), jnp.float32)],
+        compiler_params=limit(12),
     )(lst, weights, near_scores, far_scores)
     got = lax.all_to_all(send, ("y", "x"), split_axis=0, concat_axis=0, tiled=True)
     return pl.pallas_call(

time: 205 us -> 192 us (0.937)
  blocking collectives: 85.1 us -> 39.6 us
  waiting for transfers between devices: 32 us -> 43.4 us
  local copies, waits for them, and re-layouts: 15.4 us -> 26.3 us
  starting transfers between devices: 26.8 us -> 33.1 us
  other arithmetic: 6.57 us -> 10.7 us
    all_gather x1 -> x0, blocking collectives: 46.3 us -> none  [body(): target = lax.all_gather(jnp.where(in_list, target, -1), ('y', 'x'), axis=0)]
    ppermute x11 -> x13, waiting for transfers between devices: 18.9 us -> 26.6 us  [shift(): lax.ppermute(value, axis, [(i, (i + step) % size) for i in range(size)])]
    all_to_all x0 -> x1, starting transfers between devices: none -> 7.58 us  [body(): lax.all_to_all(target, ('y', 'x'), split_axis=0, concat_axis=0, tiled=True)]
    unnamed x24 -> x49, local copies, waits for them, and re-layouts: 9.75 us -> 16.8 us
    all_to_all x0 -> x1, waiting for transfers between devices: none -> 3.75 us  [body(): lax.all_to_all(target, ('y', 'x'), split_axis=0, concat_axis=0, tiled=True)]
    or x4, local copies, waits for them, and re-layouts: 0.37 us -> 2.52 us  [body(): source | place * PART + inner << 7 | taken << 13 | side << 20]
    ppermute x11 -> x13, starting transfers between devices: 23 us -> 21.6 us  [shift(): lax.ppermute(value, axis, [(i, (i + step) % size) for i in range(size)])]
  transfers between devices with their start and end apart: 13 -> 16, of which waited for: 4 -> 7; matrix products, arithmetic and copies ran while one was open for 3% -> 10% of each run, Pallas kernels for 4% -> 4%
where the time goes in v7:
time: 192 us; the launch traced here: 191 us
  waiting for transfers between devices  43.4 us (23%)
  blocking collectives  39.6 us (21%)
  starting transfers between devices  33.1 us (17%)
  local copies, waits for them, and re-layouts  26.3 us (14%)
  Pallas kernels  24.6 us (13%)
  between operations  13.7 us (7%)
  other arithmetic  10.7 us (6%)
    ppermute x13, waiting for transfers between devices, shift(): lax.ppermute(value, axis, [(i, (i + step) % size) for i in range(size)])  26.6 us
    ppermute x13, starting transfers between devices, shift(): lax.ppermute(value, axis, [(i, (i + step) % size) for i in range(size)])  21.6 us
    all_to_all x1, blocking collectives, body(): lax.all_to_all(masked, 'z', split_axis=0, concat_axis=0, tiled=True)  19.9 us
    all_to_all x1, blocking collectives, body(): lax.all_to_all(send, ('y', 'x'), split_axis=0, concat_axis=0, tiled=True)  19.7 us
    unnamed x49, local copies, waits for them, and re-layouts  16.8 us
    all_to_all x1, waiting for transfers between devices, body(): lax.all_to_all(send, ('y', 'x'), split_axis=0, concat_axis=0, tiled=True)  13 us
    pallas_call x1, Pallas kernels, body(): pl.pallas_call(first_kernel, out_shape=(jax.ShapeDtypeStruct((NY * NX, SE...  12.7 us
    all_to_all x1, starting transfers between devices, body(): lax.all_to_all(target, ('y', 'x'), split_axis=0, concat_axis=0, tiled=True)  7.58 us
  transfers between devices with their start and end apart: 16, of which 7 were waited for; matrix products, arithmetic and copies ran while one was open for 10% of the time, Pallas kernels for 4%

profile of v7, /device:TPU:1, one launch (start us, length us, event | category | flops | bytes accessed | tf_op | source)
XLA Modules:
  0.0 191.4 jit_solution(4211703427703208781)
XLA Ops:
  6.6 0.8 broadcast_compare_fusion.1
  7.4 1.3 fusion.2
  8.7 1.2 fusion.3
  10.0 1.5 broadcast_select_fusion
  11.4 0.9 pad_maximum_fusion
  12.9 1.0 gather_fusion
  14.5 7.6 %all-to-all-start = ((s32[16,1,128]{2,1,0:T(1,128)}), s32[16,1,128]{2,1,0:T(1,128)S(1)}, u32[]{:S(2)}, u32[]{:S(2)}) async-start(s32[16,1,128]{2,1,0:T(1,128)} %broadcast_in_dim.62), calls=%async_computation | async-start | bytes 16384 | tf_op jit(solution)/shard_map/all_to_all | solution.py:219
  22.7 1.0 copy-done.11
  24.7 3.8 %all-to-all-done = s32[16,1,128]{2,1,0:T(1,128)S(1)} async-done(((s32[16,1,128]{2,1,0:T(1,128)}), s32[16,1,128]{2,1,0:T(1,128)S(1)}, u32[]{:S(2)}, u32[]{:S(2)}) %all-to-all-start) | async-done | bytes 8224 | tf_op jit(solution)/shard_map/all_to_all | solution.py:219
  29.3 2.5 %collective-permute-start = (bf16[128,1152]{1,0:T(8,128)(2,1)}, bf16[128,1152]{1,0:T(8,128)(2,1)S(1)}, u32[]{:S(2)}, u32[]{:S(2)}) collective-permute-start(bf16[128,1152]{1,0:T(8,128)(2,1)} %bitcast.5), channel_id=1, source_target_pairs={{0,192},{64,0},{128,64},{192,128},{1,193},{65,1},{129,65},{193,129... | collective-permute-start | bytes 884744 | tf_op jit(solution)/shard_map/ppermute | solution.py:38
  31.9 0.7 slice_bitcast_fusion
  32.6 3.0 %collective-permute-start.1 = (bf16[64,1152]{1,0:T(8,128)(2,1)}, bf16[64,1152]{1,0:T(8,128)(2,1)S(1)}, u32[]{:S(2)}, u32[]{:S(2)}) collective-permute-start(bf16[64,1152]{1,0:T(8,128)(2,1)} %get-tuple-element.46), channel_id=1, source_target_pairs={{0,128},{64,192},{128,0},{192,64},{1,129},{65,193},{129,1},{193,65... | collective-permute-start | bytes 442376 | tf_op jit(solution)/shard_map/ppermute | solution.py:38
  36.5 3.5 %collective-permute-done.2 = bf16[64,1152]{1,0:T(8,128)(2,1)S(1)} collective-permute-done((bf16[64,1152]{1,0:T(8,128)(2,1)}, bf16[64,1152]{1,0:T(8,128)(2,1)S(1)}, u32[]{:S(2)}, u32[]{:S(2)}) %collective-permute-start.2) | collective-permute-done | bytes 147488 | tf_op jit(solution)/shard_map/ppermute | solution.py:38
  40.0 3.5 %collective-permute-done.1 = bf16[64,1152]{1,0:T(8,128)(2,1)S(1)} collective-permute-done((bf16[64,1152]{1,0:T(8,128)(2,1)}, bf16[64,1152]{1,0:T(8,128)(2,1)S(1)}, u32[]{:S(2)}, u32[]{:S(2)}) %collective-permute-start.1) | collective-permute-done | bytes 147488 | tf_op jit(solution)/shard_map/ppermute | solution.py:38
  45.6 2.0 %collective-permute-start.4 = (bf16[512,1152]{1,0:T(8,128)(2,1)S(1)}, bf16[512,1152]{1,0:T(8,128)(2,1)S(1)}, u32[]{:S(2)}, u32[]{:S(2)}) collective-permute-start(bf16[512,1152]{1,0:T(8,128)(2,1)S(1)} %bitcast.71), channel_id=1, source_target_pairs={{0,192},{64,0},{128,64},{192,128},{1,193},{65,1},{129,65},{193,129... | collective-permute-start | bytes 3538952 | tf_op jit(solution)/shard_map/ppermute | solution.py:38
  47.6 1.7 constant_dynamic-update-slice_fusion.3
  49.3 1.7 constant_dynamic-update-slice_fusion.2
  51.0 1.6 constant_dynamic-update-slice_fusion.1
  52.6 1.7 constant_dynamic-update-slice_fusion.refs_5_
  54.6 2.4 %collective-permute-start.8 = (bf16[384,1152]{1,0:T(8,128)(2,1)}, bf16[384,1152]{1,0:T(8,128)(2,1)}, u32[]{:S(2)}, u32[]{:S(2)}) collective-permute-start(bf16[384,1152]{1,0:T(8,128)(2,1)} %constant_dynamic-update-slice_fusion.refs_5_), channel_id=1, source_target_pairs={{0,3},{1,0},{2,1},{3,2},{4,7},{5,4},{6,5},{7,6},{8,11},{9,8},{10,9... | collective-permute-start | bytes 2654216 | tf_op jit(solution)/shard_map/ppermute | solution.py:38
  57.0 1.0 pad_maximum_fusion.2
  58.2 12.7 %collective-permute-done.5.refs_4_ = bf16[512,1152]{1,0:T(8,128)(2,1)S(1)} collective-permute-done((bf16[512,1152]{1,0:T(8,128)(2,1)S(1)}, bf16[512,1152]{1,0:T(8,128)(2,1)S(1)}, u32[]{:S(2)}, u32[]{:S(2)}) %collective-permute-start.5) | collective-permute-done | bytes 1179680 | tf_op jit(solution)/shard_map/ppermute | solution.py:38
  70.9 0.9 slice.41
  71.8 0.9 slice.42
  72.7 1.0 copy-done.4
  73.7 2.7 %collective-permute-start.7 = (bf16[256,1152]{1,0:T(8,128)(2,1)}, bf16[256,1152]{1,0:T(8,128)(2,1)}, u32[]{:S(2)}, u32[]{:S(2)}) collective-permute-start(bf16[256,1152]{1,0:T(8,128)(2,1)} %slice.42), channel_id=1, source_target_pairs={{0,192},{64,0},{128,64},{192,128},{1,193},{65,1},{129,65},{193,129... | collective-permute-start | bytes 1769480 | tf_op jit(solution)/shard_map/ppermute | solution.py:38
  76.3 0.8 pad_maximum_fusion.1
  77.1 5.3 %collective-permute-done.10.refs_8_ = bf16[192,1152]{1,0:T(8,128)(2,1)S(1)} collective-permute-done((bf16[192,1152]{1,0:T(8,128)(2,1)S(1)}, bf16[192,1152]{1,0:T(8,128)(2,1)S(1)}, u32[]{:S(2)}, u32[]{:S(2)}) %collective-permute-start.10) | collective-permute-done | bytes 442400 | tf_op jit(solution)/shard_map/ppermute | solution.py:38
  82.5 0.8 copy-done.8
  83.2 1.1 collective-permute-start.9
  85.2 1.6 or.34
  86.8 0.8 fusion.13.codes
  87.5 6.7 %shard_map.64.lst = s32[640]{0:T(1024)S(1)} custom-call(s32[2048]{0:T(1024)S(1)} %fusion.13.codes), custom_call_target="tpu_custom_call" | custom-call | tf_op jit(solution)/shard_map/pallas_call | solution.py:263
  94.3 1.3 copy-done.5
  95.6 1.0 copy-done.9
  96.6 12.7 %shard_map.65 = (bf16[16,272,128]{2,1,0:T(8,128)(2,1)S(1)}, bf16[260,64,128]{2,1,0:T(8,128)(2,1)S(1)}) custom-call(s32[640]{0:T(1024)S(1)} %shard_map.64.lst, bf16[4096,1280]{1,0:T(8,128)(2,1)} %all-gather.2.cloned.1.call-done.keys, bf16[1024,1152]{1,0:T(8,128)(2,1)S(1)} %bitcast.64, bf16[512,1152]{1,0:T(8,128)(2,1)S(1)} %copy-done.5, ...), custom_call_target="tpu_custom_call" | custom-call | tf_op jit(solution)/shard_map/pallas_call | solution.py:281
  109.3 2.0 %copy-done.2 = bf16[260,64,128]{2,1,0:T(8,128)(2,1)} copy-done((bf16[260,64,128]{2,1,0:T(8,128)(2,1)}, bf16[260,64,128]{2,1,0:T(8,128)(2,1)S(1)}, u32[]{:S(2)}) %copy-start.2) | copy-done | bytes 4259864
  111.3 1.0 copy-done.6
  112.3 3.8 %all-to-all-start.1 = ((bf16[16,272,128]{2,1,0:T(8,128)(2,1)}), bf16[16,272,128]{2,1,0:T(8,128)(2,1)S(1)}, u32[]{:S(2)}, u32[]{:S(2)}) async-start(bf16[16,272,128]{2,1,0:T(8,128)(2,1)} %copy-done.6), calls=%async_computation.1 | async-start | bytes 2228224 | tf_op jit(solution)/shard_map/all_to_all | solution.py:297
  116.2 0.9 shard_map.66
  117.1 13.0 %all-to-all-done.1.got = bf16[16,272,128]{2,1,0:T(8,128)(2,1)S(1)} async-done(((bf16[16,272,128]{2,1,0:T(8,128)(2,1)}), bf16[16,272,128]{2,1,0:T(8,128)(2,1)S(1)}, u32[]{:S(2)}, u32[]{:S(2)}) %all-to-all-start.1) | async-done | bytes 1114144 | tf_op jit(solution)/shard_map/all_to_all | solution.py:297
  130.6 19.9 %all_to_all.24 = bf16[8,4,64,128]{3,2,1,0:T(8,128)(2,1)S(1)} all-to-all(bf16[8,4,64,128]{3,2,1,0:T(8,128)(2,1)S(1)} %get-tuple-element.38), channel_id=1, replica_groups=mesh['y'=4,'z'=8,'c'=2,'x'=4] {'z'}, dimensions={0} | all-to-all | bytes 1048576 | tf_op jit(solution)/shard_map/all_to_all | solution.py:310
  150.5 6.7 %collective-permute-start.12 = (bf16[32,64,128]{2,1,0:T(8,128)(2,1)S(1)}, bf16[32,64,128]{2,1,0:T(8,128)(2,1)S(1)}, u32[]{:S(2)}, u32[]{:S(2)}) collective-permute-start(bf16[32,64,128]{2,1,0:T(8,128)(2,1)S(1)} %bitcast.68), channel_id=1, source_target_pairs={{0,4},{4,0},{1,5},{5,1},{2,6},{6,2},{3,7},{7,3},{8,12},{12,8},{9,1... | collective-permute-start | bytes 1572872 | tf_op jit(solution)/shard_map/ppermute | solution.py:38
  157.2 1.5 collective-permute-done.12.far
  158.7 2.2 %copy-done.3 = bf16[260,64,128]{2,1,0:T(8,128)(2,1)S(1)} copy-done((bf16[260,64,128]{2,1,0:T(8,128)(2,1)S(1)}, bf16[260,64,128]{2,1,0:T(8,128)(2,1)}, u32[]{:S(2)}) %copy-start.3) | copy-done | bytes 4259864
  160.9 3.1 %shard_map.68 = bf16[64,64,128]{2,1,0:T(8,128)(2,1)S(1)} custom-call(s32[640]{0:T(1024)S(1)} %shard_map.64.lst, bf16[260,64,128]{2,1,0:T(8,128)(2,1)S(1)} %copy-done.3, bf16[32,64,128]{2,1,0:T(8,128)(2,1)S(1)} %bitcast.69, bf16[32,64,128]{2,1,0:T(8,128)(2,1)S(1)} %collective-permute-done.12.far), custom_call_target="tpu_custom_call" | custom-call | tf_op jit(solution)/shard_map/pallas_call | solution.py:314
  164.1 19.7 %all_to_all.25 = bf16[64,64,128]{2,1,0:T(8,128)(2,1)S(1)} all-to-all(bf16[64,64,128]{2,1,0:T(8,128)(2,1)S(1)} %shard_map.68), channel_id=1, replica_groups=mesh['y'=4,'z'=8,'c'=2,'x'=4] {'y','x'}, dimensions={0} | all-to-all | bytes 2097152 | tf_op jit(solution)/shard_map/all_to_all | solution.py:322
  183.7 0.8 shard_map.69
  (84 shorter events, 8.3 us)
Async XLA Ops:
  6.5 6.3 %copy-start = (s32[1024]{0:T(1024)S(1)}, s32[1024]{0:T(1024)}, u32[]{:S(2)}) copy-start(s32[1024]{0:T(1024)} %param.11) | copy-start | bytes 12292
  6.5 15.6 %copy-start.10 = (bf16[16,64,1152]{2,1,0:T(8,128)(2,1)S(1)}, bf16[16,64,1152]{2,1,0:T(8,128)(2,1)}, u32[]{:S(2)}) copy-start(bf16[16,64,1152]{2,1,0:T(8,128)(2,1)} %param.6) | copy-start | bytes 7077892
  6.5 5.8 %copy-start.19 = (s32[16,8]{0,1:T(8,128)S(1)}, s32[16,8]{0,1:T(8,128)}, u32[]{:S(2)}) copy-start(s32[16,8]{0,1:T(8,128)} %param.9) | copy-start | bytes 1540
  6.5 6.1 %copy-start.20 = (s32[16]{0:T(128)S(1)}, s32[16]{0:T(128)}, u32[]{:S(2)}) copy-start(s32[16]{0:T(128)} %param.10) | copy-start | bytes 196
  6.5 87.8 %all-gather.2.cloned.1.call-start = ((), (), s32[]{:S(2)}) async-start(), calls=%async_computation.4 | async-start | bytes 11141120 | tf_op jit(solution)/shard_map/all_gather | solution.py:211
  14.5 14.0 %all-to-all-start = ((s32[16,1,128]{2,1,0:T(1,128)}), s32[16,1,128]{2,1,0:T(1,128)S(1)}, u32[]{:S(2)}, u32[]{:S(2)}) async-start(s32[16,1,128]{2,1,0:T(1,128)} %broadcast_in_dim.62), calls=%async_computation | async-start | bytes 16384 | tf_op jit(solution)/shard_map/all_to_all | solution.py:219
  22.0 1.7 copy-start.11
  28.5 0.7 copy-start.18
  29.2 14.3 %collective-permute-start.3 = (bf16[128,1152]{1,0:T(8,128)(2,1)}, bf16[128,1152]{1,0:T(8,128)(2,1)S(1)}, u32[]{:S(2)}, u32[]{:S(2)}) collective-permute-start(bf16[128,1152]{1,0:T(8,128)(2,1)} %bitcast.5), channel_id=1, source_target_pairs={{0,64},{64,128},{128,192},{192,0},{1,65},{65,129},{129,193},{193,1... | collective-permute-start | bytes 884744 | tf_op jit(solution)/shard_map/ppermute | solution.py:38
  29.3 14.1 %collective-permute-start = (bf16[128,1152]{1,0:T(8,128)(2,1)}, bf16[128,1152]{1,0:T(8,128)(2,1)S(1)}, u32[]{:S(2)}, u32[]{:S(2)}) collective-permute-start(bf16[128,1152]{1,0:T(8,128)(2,1)} %bitcast.5), channel_id=1, source_target_pairs={{0,192},{64,0},{128,64},{192,128},{1,193},{65,1},{129,65},{193,129... | collective-permute-start | bytes 884744 | tf_op jit(solution)/shard_map/ppermute | solution.py:38
  32.6 7.4 %collective-permute-start.2 = (bf16[64,1152]{1,0:T(8,128)(2,1)}, bf16[64,1152]{1,0:T(8,128)(2,1)S(1)}, u32[]{:S(2)}, u32[]{:S(2)}) collective-permute-start(bf16[64,1152]{1,0:T(8,128)(2,1)} %get-tuple-element.45), channel_id=1, source_target_pairs={{0,128},{64,192},{128,0},{192,64},{1,129},{65,193},{129,1},{193,65... | collective-permute-start | bytes 442376 | tf_op jit(solution)/shard_map/ppermute | solution.py:38
  32.6 10.9 %collective-permute-start.1 = (bf16[64,1152]{1,0:T(8,128)(2,1)}, bf16[64,1152]{1,0:T(8,128)(2,1)S(1)}, u32[]{:S(2)}, u32[]{:S(2)}) collective-permute-start(bf16[64,1152]{1,0:T(8,128)(2,1)} %get-tuple-element.46), channel_id=1, source_target_pairs={{0,128},{64,192},{128,0},{192,64},{1,129},{65,193},{129,1},{193,65... | collective-permute-start | bytes 442376 | tf_op jit(solution)/shard_map/ppermute | solution.py:38
  40.0 3.5 %copy-start.17 = (bf16[64,1152]{1,0:T(8,128)(2,1)}, bf16[64,1152]{1,0:T(8,128)(2,1)S(1)}, u32[]{:S(2)}) copy-start(bf16[64,1152]{1,0:T(8,128)(2,1)S(1)} %collective-permute-done.2) | copy-start | bytes 442372
  43.5 0.7 copy-start.15
  43.5 0.8 copy-start.14
  44.2 0.7 copy-start.12
  45.0 26.0 %collective-permute-start.5 = (bf16[512,1152]{1,0:T(8,128)(2,1)S(1)}, bf16[512,1152]{1,0:T(8,128)(2,1)S(1)}, u32[]{:S(2)}, u32[]{:S(2)}) collective-permute-start(bf16[512,1152]{1,0:T(8,128)(2,1)S(1)} %bitcast.70), channel_id=1, source_target_pairs={{0,64},{64,128},{128,192},{192,0},{1,65},{65,129},{129,193},{193,1... | collective-permute-start | bytes 3538952 | tf_op jit(solution)/shard_map/ppermute | solution.py:38
  45.6 26.2 %collective-permute-start.4 = (bf16[512,1152]{1,0:T(8,128)(2,1)S(1)}, bf16[512,1152]{1,0:T(8,128)(2,1)S(1)}, u32[]{:S(2)}, u32[]{:S(2)}) collective-permute-start(bf16[512,1152]{1,0:T(8,128)(2,1)S(1)} %bitcast.71), channel_id=1, source_target_pairs={{0,192},{64,0},{128,64},{192,128},{1,193},{65,1},{129,65},{193,129... | collective-permute-start | bytes 3538952 | tf_op jit(solution)/shard_map/ppermute | solution.py:38
  49.3 27.0 %copy-start.13 = (bf16[128,1152]{1,0:T(8,128)(2,1)S(1)}, bf16[128,1152]{1,0:T(8,128)(2,1)}, u32[]{:S(2)}) copy-start(bf16[128,1152]{1,0:T(8,128)(2,1)} %copy-done.12) | copy-start | bytes 884740
  49.3 27.0 %copy-start.16 = (bf16[64,1152]{1,0:T(8,128)(2,1)S(1)}, bf16[64,1152]{1,0:T(8,128)(2,1)}, u32[]{:S(2)}) copy-start(bf16[64,1152]{1,0:T(8,128)(2,1)} %copy-done.15) | copy-start | bytes 442372
  52.6 31.7 %copy-start.21 = (pred[16]{0:T(512)(128)(4,1)S(1)}, pred[16]{0:T(512)(128)(4,1)}, u32[]{:S(2)}) copy-start(pred[16]{0:T(512)(128)(4,1)} %broadcast_compare_fusion.2) | copy-start | bytes 52
  52.6 31.7 %copy-start.22 = (s32[16]{0:T(128)S(1)}, s32[16]{0:T(128)}, u32[]{:S(2)}) copy-start(s32[16]{0:T(128)} %broadcast_multiply_fusion) | copy-start | bytes 196
  54.4 39.9 %collective-permute-start.11 = (bf16[384,1152]{1,0:T(8,128)(2,1)}, bf16[384,1152]{1,0:T(8,128)(2,1)}, u32[]{:S(2)}, u32[]{:S(2)}) collective-permute-start(bf16[384,1152]{1,0:T(8,128)(2,1)} %constant_dynamic-update-slice_fusion.refs_5_), channel_id=1, source_target_pairs={{0,1},{1,2},{2,3},{3,0},{4,5},{5,6},{6,7},{7,4},{8,9},{9,10},{10,1... | collective-permute-start | bytes 2654216 | tf_op jit(solution)/shard_map/ppermute | solution.py:38
  54.6 39.7 %collective-permute-start.8 = (bf16[384,1152]{1,0:T(8,128)(2,1)}, bf16[384,1152]{1,0:T(8,128)(2,1)}, u32[]{:S(2)}, u32[]{:S(2)}) collective-permute-start(bf16[384,1152]{1,0:T(8,128)(2,1)} %constant_dynamic-update-slice_fusion.refs_5_), channel_id=1, source_target_pairs={{0,3},{1,0},{2,1},{3,2},{4,7},{5,4},{6,5},{7,6},{8,11},{9,8},{10,9... | collective-permute-start | bytes 2654216 | tf_op jit(solution)/shard_map/ppermute | solution.py:38
  58.1 24.4 %collective-permute-start.10 = (bf16[192,1152]{1,0:T(8,128)(2,1)S(1)}, bf16[192,1152]{1,0:T(8,128)(2,1)S(1)}, u32[]{:S(2)}, u32[]{:S(2)}) collective-permute-start(bf16[192,1152]{1,0:T(8,128)(2,1)S(1)} %pad_maximum_fusion.2), channel_id=1, source_target_pairs={{0,2},{1,3},{2,0},{3,1},{4,6},{5,7},{6,4},{7,5},{8,10},{9,11},{10,... | collective-permute-start | bytes 1327112 | tf_op jit(solution)/shard_map/ppermute | solution.py:38
  71.8 22.5 %collective-permute-start.6 = (bf16[256,1152]{1,0:T(8,128)(2,1)}, bf16[256,1152]{1,0:T(8,128)(2,1)}, u32[]{:S(2)}, u32[]{:S(2)}) collective-permute-start(bf16[256,1152]{1,0:T(8,128)(2,1)} %slice.41), channel_id=1, source_target_pairs={{0,64},{64,128},{128,192},{192,0},{1,65},{65,129},{129,193},{193,1... | collective-permute-start | bytes 1769480 | tf_op jit(solution)/shard_map/ppermute | solution.py:38
  72.7 1.0 copy-start.4
  73.7 20.6 %collective-permute-start.7 = (bf16[256,1152]{1,0:T(8,128)(2,1)}, bf16[256,1152]{1,0:T(8,128)(2,1)}, u32[]{:S(2)}, u32[]{:S(2)}) collective-permute-start(bf16[256,1152]{1,0:T(8,128)(2,1)} %slice.42), channel_id=1, source_target_pairs={{0,192},{64,0},{128,64},{192,128},{1,193},{65,1},{129,65},{193,129... | collective-permute-start | bytes 1769480 | tf_op jit(solution)/shard_map/ppermute | solution.py:38
  82.5 0.8 copy-start.8
  83.2 11.0 %collective-permute-start.9 = (bf16[192,1152]{1,0:T(8,128)(2,1)}, bf16[192,1152]{1,0:T(8,128)(2,1)}, u32[]{:S(2)}, u32[]{:S(2)}) collective-permute-start(bf16[192,1152]{1,0:T(8,128)(2,1)} %pad_maximum_fusion.1), channel_id=1, source_target_pairs={{0,2},{1,3},{2,0},{3,1},{4,6},{5,7},{6,4},{7,5},{8,10},{9,11},{10,... | collective-permute-start | bytes 1327112 | tf_op jit(solution)/shard_map/ppermute | solution.py:38
  94.3 1.3 copy-start.5
  95.6 1.0 copy-start.9
  109.3 2.0 %copy-start.2 = (bf16[260,64,128]{2,1,0:T(8,128)(2,1)}, bf16[260,64,128]{2,1,0:T(8,128)(2,1)S(1)}, u32[]{:S(2)}) copy-start(bf16[260,64,128]{2,1,0:T(8,128)(2,1)S(1)} %get-tuple-element.33.w) | copy-start | bytes 12779524
  111.3 1.0 copy-start.6
  112.3 3.8 %copy-start.1 = (bf16[4,64,1280]{2,1,0:T(8,128)(2,1)S(1)}, bf16[4,64,1280]{2,1,0:T(8,128)(2,1)}, u32[]{:S(2)}) copy-start(bf16[4,64,1280]{2,1,0:T(8,128)(2,1)} %pad_maximum_fusion) | copy-start | bytes 1966084
  112.3 17.9 %copy-start.7 = (bf16[4,64,128]{2,1,0:T(8,128)(2,1)S(1)}, bf16[4,64,128]{2,1,0:T(8,128)(2,1)}, u32[]{:S(2)}) copy-start(bf16[4,64,128]{2,1,0:T(8,128)(2,1)} %get-tuple-element.42.prior) | copy-start | bytes 196612
  112.3 17.8 %all-to-all-start.1 = ((bf16[16,272,128]{2,1,0:T(8,128)(2,1)}), bf16[16,272,128]{2,1,0:T(8,128)(2,1)S(1)}, u32[]{:S(2)}, u32[]{:S(2)}) async-start(bf16[16,272,128]{2,1,0:T(8,128)(2,1)} %copy-done.6), calls=%async_computation.1 | async-start | bytes 2228224 | tf_op jit(solution)/shard_map/all_to_all | solution.py:297
  150.5 8.3 %collective-permute-start.12 = (bf16[32,64,128]{2,1,0:T(8,128)(2,1)S(1)}, bf16[32,64,128]{2,1,0:T(8,128)(2,1)S(1)}, u32[]{:S(2)}, u32[]{:S(2)}) collective-permute-start(bf16[32,64,128]{2,1,0:T(8,128)(2,1)S(1)} %bitcast.68), channel_id=1, source_target_pairs={{0,4},{4,0},{1,5},{5,1},{2,6},{6,2},{3,7},{7,3},{8,12},{12,8},{9,1... | collective-permute-start | bytes 1572872 | tf_op jit(solution)/shard_map/ppermute | solution.py:38
  158.7 2.2 %copy-start.3 = (bf16[260,64,128]{2,1,0:T(8,128)(2,1)S(1)}, bf16[260,64,128]{2,1,0:T(8,128)(2,1)}, u32[]{:S(2)}) copy-start(bf16[260,64,128]{2,1,0:T(8,128)(2,1)} %copy-done.2) | copy-start | bytes 12779524
Sparse Core Ops, SparseCore 0:
  12.5 69.9 all-gather.1

commit v8 on v7

--- a/solution.py
+++ b/solution.py
@@ -74,9 +74,28 @@
     ).astype(jnp.bfloat16)
 
 
+def pairs_copy(source, target, sem, i):
+    group = pl.ds(i * (UNROLL // 2), UNROLL // 2)
+    return pltpu.make_async_copy(source.at[group], target.at[group], sem)
+
+
+def join_kernel(one, two_a, two_b, three, out, sems):
+    rows = TURN * FRAMES
+    copies = [
+        pltpu.make_async_copy(one, out.at[pl.ds(0, rows)], sems.at[0]),
+        pltpu.make_async_copy(two_a, out.at[pl.ds(rows, FRAMES)], sems.at[1]),
+        pltpu.make_async_copy(two_b, out.at[pl.ds(rows + FRAMES, FRAMES)], sems.at[2]),
+        pltpu.make_async_copy(three, out.at[pl.ds(rows + 2 * FRAMES, rows)], sems.at[3]),
+    ]
+    for copy in copies:
+        copy.start()
+    for copy in copies:
+        copy.wait()
+
+
 def first_kernel(lst, keys, *refs):
     queries = refs[:10]
-    send, w, q, k, acc, sems = refs[10:]
+    send_out, w_out, q, k, acc, send, w, sems, w_sem, send_sem = refs[10:]
     copies = [pltpu.make_async_copy(keys, k, sems.at[0])]
     at = 0
     for part in queries:
@@ -111,6 +130,7 @@
             sums.append(jnp.dot(weights[u], values, preferred_element_type=jnp.float32))
         for u, code in enumerate(codes):
             acc[code & 127] += sums[u]
+        pairs_copy(w, w_out, w_sem, i).start()
         return carry
 
     lax.fori_loop(0, steps, step, 0)
@@ -129,14 +149,39 @@
             rows.append(jnp.where(low, coarse, mass - coarse))
         rows.append(jnp.zeros((16 - PART, CH), jnp.float32))
         send[d, PIECE:SEND, :] = jnp.concatenate(rows, axis=0).astype(jnp.bfloat16)
+        pltpu.make_async_copy(send.at[d], send_out.at[d], send_sem).start()
         return carry
 
     lax.fori_loop(0, NY * NX, finish, 0)
 
-
-def second_kernel(lst, w, near, far, send, acc):
+    def drain_send(d, carry):
+        pltpu.make_async_copy(send.at[d], send_out.at[d], send_sem).wait()
+        return carry
+
+    lax.fori_loop(0, NY * NX, drain_send, 0)
+
+    def drain(i, carry):
+        pairs_copy(w, w_out, w_sem, i).wait()
+        return carry
+
+    lax.fori_loop(0, steps, drain, 0)
+
+
+def second_kernel(lst, w_in, near, far, send, acc, w, w_sem):
     steps = lst[STEPS_AT]
+
+    def fetch(i, carry):
+        pairs_copy(w_in, w, w_sem, i).start()
+        return carry
+
+    lax.fori_loop(0, steps, fetch, 0)
     acc[...] = jnp.zeros_like(acc)
+
+    def drain(i, carry):
+        pairs_copy(w_in, w, w_sem, i).wait()
+        return carry
+
+    lax.fori_loop(0, steps, drain, 0)
 
     def step(i, carry):
         codes = [lst[i * UNROLL + u] for u in range(UNROLL)]
@@ -186,6 +231,7 @@
 smem = pl.BlockSpec(memory_space=pltpu.SMEM)
 vmem = pl.BlockSpec(memory_space=pltpu.VMEM)
 hbm = pl.BlockSpec(memory_space=pl.ANY)
+far_memory = pl.BlockSpec(memory_space=pltpu.HBM)
 
 
 def limit(mebibytes):
@@ -218,26 +264,26 @@
     target = jnp.broadcast_to(target[None, :], (NY * NX, ROWS * per_list))
     target = lax.all_to_all(target, ("y", "x"), split_axis=0, concat_axis=0, tiled=True)
 
-    units, target = lax.optimization_barrier((units, target))
     turn = units[:TURN].reshape(TURN * FRAMES, FEAT)
     turned = [
         shift(turn, "y", -1), shift(turn[:FRAMES], "y", 2), shift(turn[FRAMES:], "y", -2), shift(turn, "y", 1)
     ]
     all_units = normalize(embeddings)
     straight = all_units.reshape(NX, PART, FRAMES, FEAT)[:, TURN:].reshape(STRAIGHT * FRAMES, FEAT)
-    turned, straight = lax.optimization_barrier((turned, straight))
+    turned, straight, target = lax.optimization_barrier((turned, straight, target))
     behind, ahead = shift(straight, "y", 1), shift(straight, "y", -1)
-    turned = jnp.concatenate(turned, axis=0)
-    half = turned.shape[0] // 2
-    turned = [
-        turned,
-        shift(turned, "x", -1),
-        shift(turned[:half], "x", 2),
-        shift(turned[half:], "x", -2),
-        shift(turned, "x", 1),
-    ]
-    half = STRAIGHT * FRAMES // 2
-    across = [shift(behind[:half], "y", 1), shift(ahead[half:], "y", -1)]
+    rows = (NY - 1) * TURN * FRAMES
+    turned = pl.pallas_call(
+        join_kernel,
+        out_shape=jax.ShapeDtypeStruct((rows, FEAT), jnp.bfloat16),
+        in_specs=[hbm] * 4,
+        out_specs=hbm,
+        scratch_shapes=[pltpu.SemaphoreType.DMA((4,))],
+        compiler_params=limit(1),
+    )(*turned)
+    following, leading = shift(turned, "x", -1), shift(turned, "x", 1)
+    over = [shift(leading[:rows // 2], "x", 1), shift(following[rows // 2:], "x", -1)]
+    turned = [turned, following, *over, leading]
 
     target = target.reshape(NY, NX, ROWS, per_list)
     source_y = jnp.arange(NY, dtype=jnp.int32)[:, None, None, None]
@@ -267,6 +313,9 @@
         out_specs=smem,
         compiler_params=limit(1),
     )(codes)
+    half = STRAIGHT * FRAMES // 2
+    behind, ahead, lst = lax.optimization_barrier((behind, ahead, lst))
+    across = [shift(behind[:half], "y", 1), shift(ahead[half:], "y", -1)]
     own_weights, own_base = pl.pallas_call(
         own_kernel,
         out_shape=(
@@ -285,12 +334,16 @@
             jax.ShapeDtypeStruct((SLOTS // 2, FRAMES, 2 * FRAMES), jnp.bfloat16),
         ),
         in_specs=[smem] + [hbm] * 11,
-        out_specs=(vmem, vmem),
+        out_specs=(far_memory, far_memory),
         scratch_shapes=[
             pltpu.VMEM((QBLOCKS * FRAMES, FEAT), jnp.bfloat16),
             pltpu.VMEM((NZ * NC * PIECE, WIDE), jnp.bfloat16),
             pltpu.VMEM((QBLOCKS + 1, FRAMES, 2 * CH), jnp.float32),
+            pltpu.VMEM((NY * NX, SEND, CH), jnp.bfloat16),
+            pltpu.VMEM((SLOTS // 2, FRAMES, 2 * FRAMES), jnp.bfloat16),
             pltpu.SemaphoreType.DMA((11,)),
+            pltpu.SemaphoreType.DMA,
+            pltpu.SemaphoreType.DMA,
         ],
         compiler_params=limit(32),
     )(lst, keys, all_units.reshape(ROWS * FRAMES, FEAT), ahead, *across, behind, *turned)
@@ -314,9 +367,13 @@
     send = pl.pallas_call(
         second_kernel,
         out_shape=jax.ShapeDtypeStruct((QBLOCKS, FRAMES, CH), jnp.bfloat16),
-        in_specs=[smem, vmem, vmem, vmem],
+        in_specs=[smem, far_memory, vmem, vmem],
         out_specs=vmem,
-        scratch_shapes=[pltpu.VMEM((QBLOCKS + 1, FRAMES, CH), jnp.float32)],
+        scratch_shapes=[
+            pltpu.VMEM((QBLOCKS + 1, FRAMES, CH), jnp.float32),
+            pltpu.VMEM((SLOTS // 2, FRAMES, 2 * FRAMES), jnp.bfloat16),
+            pltpu.SemaphoreType.DMA,
+        ],
         compiler_params=limit(12),
     )(lst, weights, near_scores, far_scores)
     got = lax.all_to_all(send, ("y", "x"), split_axis=0, concat_axis=0, tiled=True)

time: 192 us -> 188 us (0.979)
  waiting for transfers between devices: 43.4 us -> 35.8 us
  Pallas kernels: 24.6 us -> 29.7 us
  starting transfers between devices: 33.1 us -> 37.2 us
  other arithmetic: 10.7 us -> 6.64 us
  blocking collectives: 39.6 us -> 36.1 us
    ppermute x13, starting transfers between devices: 21.6 us -> 26.8 us  [shift(): lax.ppermute(value, axis, [(i, (i + step) % size) for i in range(size)])]
    all_to_all x1, waiting for transfers between devices: 3.75 us -> 0.01 us  [body(): lax.all_to_all(target, ('y', 'x'), split_axis=0, concat_axis=0, tiled=True)]
    ppermute x13, waiting for transfers between devices: 26.6 us -> 22.9 us  [shift(): lax.ppermute(value, axis, [(i, (i + step) % size) for i in range(size)])]
    pallas_call x1, Pallas kernels: 12.7 us -> 16 us  [body(): pl.pallas_call(first_kernel, out_shape=(jax.ShapeDtypeStruct((NY * NX, SE...]
    all_to_all x1, blocking collectives: 19.9 us -> 16.6 us  [body(): lax.all_to_all(masked, 'z', split_axis=0, concat_axis=0, tiled=True)]
    slice x0 -> x2, local copies, waits for them, and re-layouts: none -> 2.17 us  [the longest x1 1.11 us: body(): leading[:rows // 2]]
    or x4, local copies, waits for them, and re-layouts: 2.52 us -> 0.37 us  [body(): source | place * PART + inner << 7 | taken << 13 | side << 20]
    all_to_all x1, starting transfers between devices: 7.58 us -> 5.45 us  [body(): lax.all_to_all(target, ('y', 'x'), split_axis=0, concat_axis=0, tiled=True)]
  transfers between devices with their start and end apart: 16 -> 16, of which waited for: 7 -> 8; matrix products, arithmetic and copies ran while one was open for 10% -> 6% of each run, Pallas kernels for 4% -> 4%
where the time goes in v8:
time: 188 us; the launch traced here: 187 us
  starting transfers between devices  37.2 us (20%)
  blocking collectives  36.1 us (19%)
  waiting for transfers between devices  35.8 us (19%)
  Pallas kernels  29.7 us (16%)
  local copies, waits for them, and re-layouts  27.9 us (15%)
  between operations  13.7 us (7%)
  other arithmetic  6.64 us (4%)
    ppermute x13, starting transfers between devices, shift(): lax.ppermute(value, axis, [(i, (i + step) % size) for i in range(size)])  26.8 us
    ppermute x13, waiting for transfers between devices, shift(): lax.ppermute(value, axis, [(i, (i + step) % size) for i in range(size)])  22.9 us
    all_to_all x1, blocking collectives, body(): lax.all_to_all(send, ('y', 'x'), split_axis=0, concat_axis=0, tiled=True)  19.5 us
    unnamed x48, local copies, waits for them, and re-layouts  17.5 us
    all_to_all x1, blocking collectives, body(): lax.all_to_all(masked, 'z', split_axis=0, concat_axis=0, tiled=True)  16.6 us
    pallas_call x1, Pallas kernels, body(): pl.pallas_call(first_kernel, out_shape=(jax.ShapeDtypeStruct((NY * NX, SE...  16 us
    all_to_all x1, waiting for transfers between devices, body(): lax.all_to_all(send, ('y', 'x'), split_axis=0, concat_axis=0, tiled=True)  12.9 us
    pallas_call x1, Pallas kernels, body(): pl.pallas_call(list_kernel, out_shape=jax.ShapeDtypeStruct((LIST,), jnp.i...  6.69 us
  transfers between devices with their start and end apart: 16, of which 8 were waited for; matrix products, arithmetic and copies ran while one was open for 6% of the time, Pallas kernels for 4%

profile of v8, /device:TPU:1, one launch (start us, length us, event | category | flops | bytes accessed | tf_op | source)
XLA Modules:
  0.0 187.1 jit_solution(10614504608170598416)
XLA Ops:
  7.3 1.3 fusion.2
  8.6 1.4 fusion.3
  10.0 1.0 broadcast_select_fusion
  11.0 0.9 pad_maximum_fusion
  12.6 2.1 %collective-permute-start.3 = (bf16[128,1152]{1,0:T(8,128)(2,1)}, bf16[128,1152]{1,0:T(8,128)(2,1)S(1)}, u32[]{:S(2)}, u32[]{:S(2)}) collective-permute-start(bf16[128,1152]{1,0:T(8,128)(2,1)} %bitcast), channel_id=1, source_target_pairs={{0,64},{64,128},{128,192},{192,0},{1,65},{65,129},{129,193},{193,1... | collective-permute-start | bytes 884744 | tf_op jit(solution)/shard_map/ppermute | solution.py:38
  14.8 1.5 collective-permute-start
  16.7 1.0 gather_fusion
  18.3 5.5 %all-to-all-start = ((s32[16,1,128]{2,1,0:T(1,128)}), s32[16,1,128]{2,1,0:T(1,128)S(1)}, u32[]{:S(2)}, u32[]{:S(2)}) async-start(s32[16,1,128]{2,1,0:T(1,128)} %broadcast_in_dim.62), calls=%async_computation | async-start | bytes 16384 | tf_op jit(solution)/shard_map/all_to_all | solution.py:265
  23.8 1.8 slice_bitcast_fusion
  25.6 2.9 %collective-permute-start.2 = (bf16[64,1152]{1,0:T(8,128)(2,1)}, bf16[64,1152]{1,0:T(8,128)(2,1)S(1)}, u32[]{:S(2)}, u32[]{:S(2)}) collective-permute-start(bf16[64,1152]{1,0:T(8,128)(2,1)} %get-tuple-element.49), channel_id=1, source_target_pairs={{0,128},{64,192},{128,0},{192,64},{1,129},{65,193},{129,1},{193,65... | collective-permute-start | bytes 442376 | tf_op jit(solution)/shard_map/ppermute | solution.py:38
  29.6 1.1 slice.47
  30.7 0.9 collective-permute-done.2.two_b
  31.7 3.3 %collective-permute-done.1.two_a = bf16[64,1152]{1,0:T(8,128)(2,1)S(1)} collective-permute-done((bf16[64,1152]{1,0:T(8,128)(2,1)S(1)}, bf16[64,1152]{1,0:T(8,128)(2,1)S(1)}, u32[]{:S(2)}, u32[]{:S(2)}) %collective-permute-start.1) | collective-permute-done | bytes 147488 | tf_op jit(solution)/shard_map/ppermute | solution.py:38
  37.1 1.7 collective-permute-start.5
  39.1 1.0 copy-done.14
  40.0 1.0 copy-done.16
  41.0 0.9 copy-done.18
  42.5 1.9 %collective-permute-start.9 = (bf16[384,1152]{1,0:T(8,128)(2,1)S(1)}, bf16[384,1152]{1,0:T(8,128)(2,1)}, u32[]{:S(2)}, u32[]{:S(2)}) collective-permute-start(bf16[384,1152]{1,0:T(8,128)(2,1)S(1)} %shard_map.65.refs_5_), channel_id=1, source_target_pairs={{0,1},{1,2},{2,3},{3,0},{4,5},{5,6},{6,7},{7,4},{8,9},{9,10},{10,1... | collective-permute-start | bytes 2654216 | tf_op jit(solution)/shard_map/ppermute | solution.py:38
  44.4 1.3 collective-permute-start.8
  46.0 6.7 %shard_map.64.lst = s32[640]{0:T(1024)S(1)} custom-call(s32[2048]{0:T(1024)S(1)} %fusion.13.codes), custom_call_target="tpu_custom_call" | custom-call | tf_op jit(solution)/shard_map/pallas_call | solution.py:309
  52.7 9.8 %collective-permute-done.5.refs_1_ = bf16[512,1152]{1,0:T(8,128)(2,1)} collective-permute-done((bf16[512,1152]{1,0:T(8,128)(2,1)}, bf16[512,1152]{1,0:T(8,128)(2,1)}, u32[]{:S(2)}, u32[]{:S(2)}) %collective-permute-start.5) | collective-permute-done | bytes 1179680 | tf_op jit(solution)/shard_map/ppermute | solution.py:38
  62.6 2.2 %collective-permute-done.4.refs_4_ = bf16[512,1152]{1,0:T(8,128)(2,1)} collective-permute-done((bf16[512,1152]{1,0:T(8,128)(2,1)}, bf16[512,1152]{1,0:T(8,128)(2,1)}, u32[]{:S(2)}, u32[]{:S(2)}) %collective-permute-start.4) | collective-permute-done | bytes 1179680 | tf_op jit(solution)/shard_map/ppermute | solution.py:38
  64.8 1.1 slice.39
  65.9 1.1 slice.38
  67.1 2.7 %collective-permute-start.7 = (bf16[256,1152]{1,0:T(8,128)(2,1)S(1)}, bf16[256,1152]{1,0:T(8,128)(2,1)S(1)}, u32[]{:S(2)}, u32[]{:S(2)}) collective-permute-start(bf16[256,1152]{1,0:T(8,128)(2,1)S(1)} %slice.39), channel_id=1, source_target_pairs={{0,192},{64,0},{128,64},{192,128},{1,193},{65,1},{129,65},{193,129... | collective-permute-start | bytes 1769480 | tf_op jit(solution)/shard_map/ppermute | solution.py:38
  69.8 1.1 slice.48
  70.9 1.1 collective-permute-start.10
  72.0 1.1 slice.49
  73.1 1.9 collective-permute-start.11
  75.0 4.8 %collective-permute-done.10.refs_7_ = bf16[192,1152]{1,0:T(8,128)(2,1)S(1)} collective-permute-done((bf16[192,1152]{1,0:T(8,128)(2,1)S(1)}, bf16[192,1152]{1,0:T(8,128)(2,1)S(1)}, u32[]{:S(2)}, u32[]{:S(2)}) %collective-permute-start.10) | collective-permute-done | bytes 442400 | tf_op jit(solution)/shard_map/ppermute | solution.py:38
  81.6 0.8 copy-done.5
  83.2 1.1 copy-done.6
  84.3 1.1 copy-done.8
  85.3 1.0 copy-done.10
  86.3 1.0 copy-done.12
  87.3 16.0 %shard_map.66 = (bf16[16,272,128]{2,1,0:T(8,128)(2,1)S(1)}, bf16[260,64,128]{2,1,0:T(8,128)(2,1)S(1)}) custom-call(s32[640]{0:T(1024)S(1)} %shard_map.64.lst, bf16[4096,1280]{1,0:T(8,128)(2,1)} %all-gather.2.cloned.1.call-done.keys, bf16[1024,1152]{1,0:T(8,128)(2,1)S(1)} %bitcast.64, bf16[512,1152]{1,0:T(8,128)(2,1)} %collective-permute-done.5.refs_1_, ...), custom_call_target="tpu_custom_call" | custom-call | tf_op jit(solution)/shard_map/pallas_call | solution.py:330
  103.4 2.0 %copy-done.2 = bf16[260,64,128]{2,1,0:T(8,128)(2,1)} copy-done((bf16[260,64,128]{2,1,0:T(8,128)(2,1)}, bf16[260,64,128]{2,1,0:T(8,128)(2,1)S(1)}, u32[]{:S(2)}) %copy-start.2) | copy-done | bytes 4259864
  105.3 1.0 copy-done.4
  106.3 5.0 %all-to-all-start.1 = ((bf16[16,272,128]{2,1,0:T(8,128)(2,1)}), bf16[16,272,128]{2,1,0:T(8,128)(2,1)S(1)}, u32[]{:S(2)}, u32[]{:S(2)}) async-start(bf16[16,272,128]{2,1,0:T(8,128)(2,1)} %copy-done.4), calls=%async_computation.1 | async-start | bytes 2228224 | tf_op jit(solution)/shard_map/all_to_all | solution.py:350
  111.3 0.9 shard_map.67
  112.3 12.9 %all-to-all-done.1.got = bf16[16,272,128]{2,1,0:T(8,128)(2,1)S(1)} async-done(((bf16[16,272,128]{2,1,0:T(8,128)(2,1)}), bf16[16,272,128]{2,1,0:T(8,128)(2,1)S(1)}, u32[]{:S(2)}, u32[]{:S(2)}) %all-to-all-start.1) | async-done | bytes 1114144 | tf_op jit(solution)/shard_map/all_to_all | solution.py:350
  125.7 16.6 %all_to_all.24 = bf16[8,4,64,128]{3,2,1,0:T(8,128)(2,1)S(1)} all-to-all(bf16[8,4,64,128]{3,2,1,0:T(8,128)(2,1)S(1)} %get-tuple-element.42), channel_id=1, replica_groups=mesh['y'=4,'z'=8,'c'=2,'x'=4] {'z'}, dimensions={0} | all-to-all | bytes 1048576 | tf_op jit(solution)/shard_map/all_to_all | solution.py:363
  142.3 9.5 %collective-permute-start.12 = (bf16[32,64,128]{2,1,0:T(8,128)(2,1)S(1)}, bf16[32,64,128]{2,1,0:T(8,128)(2,1)S(1)}, u32[]{:S(2)}, u32[]{:S(2)}) collective-permute-start(bf16[32,64,128]{2,1,0:T(8,128)(2,1)S(1)} %bitcast.68), channel_id=1, source_target_pairs={{0,4},{4,0},{1,5},{5,1},{2,6},{6,2},{3,7},{7,3},{8,12},{12,8},{9,1... | collective-permute-start | bytes 1572872 | tf_op jit(solution)/shard_map/ppermute | solution.py:38
  151.8 1.5 collective-permute-done.12.far
  153.3 2.2 %copy-done.3 = bf16[260,64,128]{2,1,0:T(8,128)(2,1)S(1)} copy-done((bf16[260,64,128]{2,1,0:T(8,128)(2,1)S(1)}, bf16[260,64,128]{2,1,0:T(8,128)(2,1)}, u32[]{:S(2)}) %copy-start.3) | copy-done | bytes 4259864
  155.6 4.4 %shard_map.69 = bf16[64,64,128]{2,1,0:T(8,128)(2,1)S(1)} custom-call(s32[640]{0:T(1024)S(1)} %shard_map.64.lst, bf16[260,64,128]{2,1,0:T(8,128)(2,1)S(1)} %copy-done.3, bf16[32,64,128]{2,1,0:T(8,128)(2,1)S(1)} %bitcast.69, bf16[32,64,128]{2,1,0:T(8,128)(2,1)S(1)} %collective-permute-done.12.far), custom_call_target="tpu_custom_call" | custom-call | tf_op jit(solution)/shard_map/pallas_call | solution.py:367
  160.0 19.5 %all_to_all.25 = bf16[64,64,128]{2,1,0:T(8,128)(2,1)S(1)} all-to-all(bf16[64,64,128]{2,1,0:T(8,128)(2,1)S(1)} %shard_map.69), channel_id=1, replica_groups=mesh['y'=4,'z'=8,'c'=2,'x'=4] {'y','x'}, dimensions={0} | all-to-all | bytes 2097152 | tf_op jit(solution)/shard_map/all_to_all | solution.py:379
  179.4 0.8 shard_map.70
  (83 shorter events, 10.1 us)
Async XLA Ops:
  6.5 10.2 %copy-start = (s32[1024]{0:T(1024)S(1)}, s32[1024]{0:T(1024)}, u32[]{:S(2)}) copy-start(s32[1024]{0:T(1024)} %param.11) | copy-start | bytes 12292
  6.5 9.7 %copy-start.22 = (s32[16,8]{0,1:T(8,128)S(1)}, s32[16,8]{0,1:T(8,128)}, u32[]{:S(2)}) copy-start(s32[16,8]{0,1:T(8,128)} %param.9) | copy-start | bytes 1540
  6.5 10.0 %copy-start.23 = (s32[16]{0:T(128)S(1)}, s32[16]{0:T(128)}, u32[]{:S(2)}) copy-start(s32[16]{0:T(128)} %param.10) | copy-start | bytes 196
  6.5 76.6 %all-gather.2.cloned.1.call-start = ((), (), s32[]{:S(2)}) async-start(), calls=%async_computation.4 | async-start | bytes 11141120 | tf_op jit(solution)/shard_map/all_gather | solution.py:257
  8.5 20.0 %copy-start.19 = (bf16[16,64,1152]{2,1,0:T(8,128)(2,1)S(1)}, bf16[16,64,1152]{2,1,0:T(8,128)(2,1)}, u32[]{:S(2)}) copy-start(bf16[16,64,1152]{2,1,0:T(8,128)(2,1)} %param.6) | copy-start | bytes 7077892
  10.0 2.7 %copy-start.21 = (bf16[4,64,1152]{2,1,0:T(8,128)(2,1)}, bf16[4,64,1152]{2,1,0:T(8,128)(2,1)S(1)}, u32[]{:S(2)}) copy-start(bf16[4,64,1152]{2,1,0:T(8,128)(2,1)S(1)} %fusion.3) | copy-start | bytes 1769476
  12.6 23.0 %collective-permute-start.3 = (bf16[128,1152]{1,0:T(8,128)(2,1)}, bf16[128,1152]{1,0:T(8,128)(2,1)S(1)}, u32[]{:S(2)}, u32[]{:S(2)}) collective-permute-start(bf16[128,1152]{1,0:T(8,128)(2,1)} %bitcast), channel_id=1, source_target_pairs={{0,64},{64,128},{128,192},{192,0},{1,65},{65,129},{129,193},{193,1... | collective-permute-start | bytes 884744 | tf_op jit(solution)/shard_map/ppermute | solution.py:38
  14.8 21.6 %collective-permute-start = (bf16[128,1152]{1,0:T(8,128)(2,1)}, bf16[128,1152]{1,0:T(8,128)(2,1)S(1)}, u32[]{:S(2)}, u32[]{:S(2)}) collective-permute-start(bf16[128,1152]{1,0:T(8,128)(2,1)} %bitcast), channel_id=1, source_target_pairs={{0,192},{64,0},{128,64},{192,128},{1,193},{65,1},{129,65},{193,129... | collective-permute-start | bytes 884744 | tf_op jit(solution)/shard_map/ppermute | solution.py:38
  18.3 12.4 %all-to-all-start = ((s32[16,1,128]{2,1,0:T(1,128)}), s32[16,1,128]{2,1,0:T(1,128)S(1)}, u32[]{:S(2)}, u32[]{:S(2)}) async-start(s32[16,1,128]{2,1,0:T(1,128)} %broadcast_in_dim.62), calls=%async_computation | async-start | bytes 16384 | tf_op jit(solution)/shard_map/all_to_all | solution.py:265
  23.8 5.3 %copy-start.20 = (bf16[16,64,1152]{2,1,0:T(8,128)(2,1)S(1)}, bf16[16,64,1152]{2,1,0:T(8,128)(2,1)}, u32[]{:S(2)}) copy-start(bf16[16,64,1152]{2,1,0:T(8,128)(2,1)} %param.6) | copy-start | bytes 7077892
  25.6 6.0 %collective-permute-start.2 = (bf16[64,1152]{1,0:T(8,128)(2,1)}, bf16[64,1152]{1,0:T(8,128)(2,1)S(1)}, u32[]{:S(2)}, u32[]{:S(2)}) collective-permute-start(bf16[64,1152]{1,0:T(8,128)(2,1)} %get-tuple-element.49), channel_id=1, source_target_pairs={{0,128},{64,192},{128,0},{192,64},{1,129},{65,193},{129,1},{193,65... | collective-permute-start | bytes 442376 | tf_op jit(solution)/shard_map/ppermute | solution.py:38
  28.5 6.5 %collective-permute-start.1 = (bf16[64,1152]{1,0:T(8,128)(2,1)S(1)}, bf16[64,1152]{1,0:T(8,128)(2,1)S(1)}, u32[]{:S(2)}, u32[]{:S(2)}) collective-permute-start(bf16[64,1152]{1,0:T(8,128)(2,1)S(1)} %get-tuple-element.50), channel_id=1, source_target_pairs={{0,128},{64,192},{128,0},{192,64},{1,129},{65,193},{129,1},{193,65... | collective-permute-start | bytes 442376 | tf_op jit(solution)/shard_map/ppermute | solution.py:38
  34.9 0.7 copy-start.17
  35.6 0.7 copy-start.13
  36.3 0.7 copy-start.15
  37.1 25.5 %collective-permute-start.5 = (bf16[512,1152]{1,0:T(8,128)(2,1)}, bf16[512,1152]{1,0:T(8,128)(2,1)}, u32[]{:S(2)}, u32[]{:S(2)}) collective-permute-start(bf16[512,1152]{1,0:T(8,128)(2,1)} %bitcast.70), channel_id=1, source_target_pairs={{0,192},{64,0},{128,64},{192,128},{1,193},{65,1},{129,65},{193,129... | collective-permute-start | bytes 3538952 | tf_op jit(solution)/shard_map/ppermute | solution.py:38
  38.8 26.0 %collective-permute-start.4 = (bf16[512,1152]{1,0:T(8,128)(2,1)}, bf16[512,1152]{1,0:T(8,128)(2,1)}, u32[]{:S(2)}, u32[]{:S(2)}) collective-permute-start(bf16[512,1152]{1,0:T(8,128)(2,1)} %bitcast.71), channel_id=1, source_target_pairs={{0,64},{64,128},{128,192},{192,0},{1,65},{65,129},{129,193},{193,1... | collective-permute-start | bytes 3538952 | tf_op jit(solution)/shard_map/ppermute | solution.py:38
  39.1 1.0 copy-start.14
  40.0 1.0 copy-start.16
  41.0 0.9 copy-start.18
  42.5 27.3 %collective-permute-start.9 = (bf16[384,1152]{1,0:T(8,128)(2,1)S(1)}, bf16[384,1152]{1,0:T(8,128)(2,1)}, u32[]{:S(2)}, u32[]{:S(2)}) collective-permute-start(bf16[384,1152]{1,0:T(8,128)(2,1)S(1)} %shard_map.65.refs_5_), channel_id=1, source_target_pairs={{0,1},{1,2},{2,3},{3,0},{4,5},{5,6},{6,7},{7,4},{8,9},{9,10},{10,1... | collective-permute-start | bytes 2654216 | tf_op jit(solution)/shard_map/ppermute | solution.py:38
  44.4 27.7 %collective-permute-start.8 = (bf16[384,1152]{1,0:T(8,128)(2,1)S(1)}, bf16[384,1152]{1,0:T(8,128)(2,1)}, u32[]{:S(2)}, u32[]{:S(2)}) collective-permute-start(bf16[384,1152]{1,0:T(8,128)(2,1)S(1)} %shard_map.65.refs_5_), channel_id=1, source_target_pairs={{0,3},{1,0},{2,1},{3,2},{4,7},{5,4},{6,5},{7,6},{8,11},{9,8},{10,9... | collective-permute-start | bytes 2654216 | tf_op jit(solution)/shard_map/ppermute | solution.py:38
  67.0 14.6 %collective-permute-start.6 = (bf16[256,1152]{1,0:T(8,128)(2,1)S(1)}, bf16[256,1152]{1,0:T(8,128)(2,1)S(1)}, u32[]{:S(2)}, u32[]{:S(2)}) collective-permute-start(bf16[256,1152]{1,0:T(8,128)(2,1)S(1)} %slice.38), channel_id=1, source_target_pairs={{0,64},{64,128},{128,192},{192,0},{1,65},{65,129},{129,193},{193,1... | collective-permute-start | bytes 1769480 | tf_op jit(solution)/shard_map/ppermute | solution.py:38
  67.1 15.3 %collective-permute-start.7 = (bf16[256,1152]{1,0:T(8,128)(2,1)S(1)}, bf16[256,1152]{1,0:T(8,128)(2,1)S(1)}, u32[]{:S(2)}, u32[]{:S(2)}) collective-permute-start(bf16[256,1152]{1,0:T(8,128)(2,1)S(1)} %slice.39), channel_id=1, source_target_pairs={{0,192},{64,0},{128,64},{192,128},{1,193},{65,1},{129,65},{193,129... | collective-permute-start | bytes 1769480 | tf_op jit(solution)/shard_map/ppermute | solution.py:38
  70.9 8.8 %collective-permute-start.10 = (bf16[192,1152]{1,0:T(8,128)(2,1)S(1)}, bf16[192,1152]{1,0:T(8,128)(2,1)S(1)}, u32[]{:S(2)}, u32[]{:S(2)}) collective-permute-start(bf16[192,1152]{1,0:T(8,128)(2,1)S(1)} %slice.48), channel_id=1, source_target_pairs={{0,1},{1,2},{2,3},{3,0},{4,5},{5,6},{6,7},{7,4},{8,9},{9,10},{10,1... | collective-permute-start | bytes 1327112 | tf_op jit(solution)/shard_map/ppermute | solution.py:38
  73.1 7.7 %collective-permute-start.11 = (bf16[192,1152]{1,0:T(8,128)(2,1)S(1)}, bf16[192,1152]{1,0:T(8,128)(2,1)S(1)}, u32[]{:S(2)}, u32[]{:S(2)}) collective-permute-start(bf16[192,1152]{1,0:T(8,128)(2,1)S(1)} %slice.49), channel_id=1, source_target_pairs={{0,3},{1,0},{2,1},{3,2},{4,7},{5,4},{6,5},{7,6},{8,11},{9,8},{10,9... | collective-permute-start | bytes 1327112 | tf_op jit(solution)/shard_map/ppermute | solution.py:38
  79.7 0.8 copy-start.9
  80.8 0.8 copy-start.11
  81.6 0.8 copy-start.5
  82.4 0.8 copy-start.7
  83.2 1.1 copy-start.6
  84.3 1.1 copy-start.8
  85.3 1.0 copy-start.10
  86.3 1.0 copy-start.12
  103.4 2.0 %copy-start.2 = (bf16[260,64,128]{2,1,0:T(8,128)(2,1)}, bf16[260,64,128]{2,1,0:T(8,128)(2,1)S(1)}, u32[]{:S(2)}) copy-start(bf16[260,64,128]{2,1,0:T(8,128)(2,1)S(1)} %get-tuple-element.37.w_in) | copy-start | bytes 12779524
  105.3 1.0 copy-start.4
  106.3 5.0 %copy-start.1 = (bf16[4,64,1280]{2,1,0:T(8,128)(2,1)S(1)}, bf16[4,64,1280]{2,1,0:T(8,128)(2,1)}, u32[]{:S(2)}) copy-start(bf16[4,64,1280]{2,1,0:T(8,128)(2,1)} %pad_maximum_fusion) | copy-start | bytes 1966084
  106.3 18.9 %all-to-all-start.1 = ((bf16[16,272,128]{2,1,0:T(8,128)(2,1)}), bf16[16,272,128]{2,1,0:T(8,128)(2,1)S(1)}, u32[]{:S(2)}, u32[]{:S(2)}) async-start(bf16[16,272,128]{2,1,0:T(8,128)(2,1)} %copy-done.4), calls=%async_computation.1 | async-start | bytes 2228224 | tf_op jit(solution)/shard_map/all_to_all | solution.py:350
  142.3 11.0 %collective-permute-start.12 = (bf16[32,64,128]{2,1,0:T(8,128)(2,1)S(1)}, bf16[32,64,128]{2,1,0:T(8,128)(2,1)S(1)}, u32[]{:S(2)}, u32[]{:S(2)}) collective-permute-start(bf16[32,64,128]{2,1,0:T(8,128)(2,1)S(1)} %bitcast.68), channel_id=1, source_target_pairs={{0,4},{4,0},{1,5},{5,1},{2,6},{6,2},{3,7},{7,3},{8,12},{12,8},{9,1... | collective-permute-start | bytes 1572872 | tf_op jit(solution)/shard_map/ppermute | solution.py:38
  153.3 2.2 %copy-start.3 = (bf16[260,64,128]{2,1,0:T(8,128)(2,1)S(1)}, bf16[260,64,128]{2,1,0:T(8,128)(2,1)}, u32[]{:S(2)}) copy-start(bf16[260,64,128]{2,1,0:T(8,128)(2,1)} %copy-done.2) | copy-start | bytes 12779524
Sparse Core Ops, SparseCore 0:
  12.0 69.9 all-gather.1

commit v9 on v8

--- a/solution.py
+++ b/solution.py
@@ -79,13 +79,11 @@
     return pltpu.make_async_copy(source.at[group], target.at[group], sem)
 
 
-def join_kernel(one, two_a, two_b, three, out, sems):
+def join_kernel(*refs):
+    parts, out, sems = refs[:3], refs[3], refs[4]
     rows = TURN * FRAMES
     copies = [
-        pltpu.make_async_copy(one, out.at[pl.ds(0, rows)], sems.at[0]),
-        pltpu.make_async_copy(two_a, out.at[pl.ds(rows, FRAMES)], sems.at[1]),
-        pltpu.make_async_copy(two_b, out.at[pl.ds(rows + FRAMES, FRAMES)], sems.at[2]),
-        pltpu.make_async_copy(three, out.at[pl.ds(rows + 2 * FRAMES, rows)], sems.at[3]),
+        pltpu.make_async_copy(part, out.at[pl.ds(d * rows, rows)], sems.at[d]) for d, part in enumerate(parts)
     ]
     for copy in copies:
         copy.start()
@@ -265,22 +263,20 @@
     target = lax.all_to_all(target, ("y", "x"), split_axis=0, concat_axis=0, tiled=True)
 
     turn = units[:TURN].reshape(TURN * FRAMES, FEAT)
-    turned = [
-        shift(turn, "y", -1), shift(turn[:FRAMES], "y", 2), shift(turn[FRAMES:], "y", -2), shift(turn, "y", 1)
-    ]
+    one, two, three = shift(turn, "y", -1), shift(turn, "y", 2), shift(turn, "y", 1)
     all_units = normalize(embeddings)
     straight = all_units.reshape(NX, PART, FRAMES, FEAT)[:, TURN:].reshape(STRAIGHT * FRAMES, FEAT)
-    turned, straight, target = lax.optimization_barrier((turned, straight, target))
+    one, three, straight, target = lax.optimization_barrier((one, three, straight, target))
     behind, ahead = shift(straight, "y", 1), shift(straight, "y", -1)
     rows = (NY - 1) * TURN * FRAMES
     turned = pl.pallas_call(
         join_kernel,
         out_shape=jax.ShapeDtypeStruct((rows, FEAT), jnp.bfloat16),
-        in_specs=[hbm] * 4,
+        in_specs=[hbm] * 3,
         out_specs=hbm,
-        scratch_shapes=[pltpu.SemaphoreType.DMA((4,))],
+        scratch_shapes=[pltpu.SemaphoreType.DMA((3,))],
         compiler_params=limit(1),
-    )(*turned)
+    )(one, two, three)
     following, leading = shift(turned, "x", -1), shift(turned, "x", 1)
     over = [shift(leading[:rows // 2], "x", 1), shift(following[rows // 2:], "x", -1)]
     turned = [turned, following, *over, leading]
@@ -345,7 +341,7 @@
             pltpu.SemaphoreType.DMA,
             pltpu.SemaphoreType.DMA,
         ],
-        compiler_params=limit(32),
+        compiler_params=limit(58),
     )(lst, keys, all_units.reshape(ROWS * FRAMES, FEAT), ahead, *across, behind, *turned)
     got = lax.all_to_all(send, ("y", "x"), split_axis=0, concat_axis=0, tiled=True)
 
@@ -374,7 +370,7 @@
             pltpu.VMEM((SLOTS // 2, FRAMES, 2 * FRAMES), jnp.bfloat16),
             pltpu.SemaphoreType.DMA,
         ],
-        compiler_params=limit(12),
+        compiler_params=limit(57),
     )(lst, weights, near_scores, far_scores)
     got = lax.all_to_all(send, ("y", "x"), split_axis=0, concat_axis=0, tiled=True)
     return pl.pallas_call(

time: 188 us -> 182 us (0.968)
  local copies, waits for them, and re-layouts: 27.9 us -> 10.5 us
  waiting for transfers between devices: 35.8 us -> 50.1 us
  starting transfers between devices: 37.2 us -> 31.4 us
  blocking collectives: 36.1 us -> 38.3 us
    unnamed x48 -> x28, local copies, waits for them, and re-layouts: 17.5 us -> 2.98 us
    all_to_all x1, waiting for transfers between devices: 12.9 us -> 18.4 us  [body(): lax.all_to_all(send, ('y', 'x'), split_axis=0, concat_axis=0, tiled=True)]
    ppermute x13 -> x12, starting transfers between devices: 26.8 us -> 21.8 us  [shift(): lax.ppermute(value, axis, [(i, (i + step) % size) for i in range(size)])]
    all_gather x1, waiting for transfers between devices: 0.01 us -> 3.75 us  [body(): keys = lax.all_gather(piece, ('z', 'c'), axis=0, tiled=True)]
    all_to_all x1, waiting for transfers between devices: 0.01 us -> 2.8 us  [body(): lax.all_to_all(target, ('y', 'x'), split_axis=0, concat_axis=0, tiled=True)]
    ppermute x13 -> x12, waiting for transfers between devices: 22.9 us -> 25.1 us  [shift(): lax.ppermute(value, axis, [(i, (i + step) % size) for i in range(size)])]
    all_to_all x1, blocking collectives: 19.5 us -> 21.4 us  [body(): lax.all_to_all(send, ('y', 'x'), split_axis=0, concat_axis=0, tiled=True)]
  transfers between devices with their start and end apart: 16 -> 15, of which waited for: 8 -> 8; matrix products, arithmetic and copies ran while one was open for 6% -> 5% of each run, Pallas kernels for 4% -> 4%
where the time goes in v9:
time: 182 us; the launch traced here: 181 us
  waiting for transfers between devices  50.1 us (28%)
  blocking collectives  38.3 us (21%)
  starting transfers between devices  31.4 us (17%)
  Pallas kernels  30.7 us (17%)
  between operations  13.7 us (8%)
  local copies, waits for them, and re-layouts  10.5 us (6%)
  other arithmetic  6.57 us (4%)
    ppermute x12, waiting for transfers between devices, shift(): lax.ppermute(value, axis, [(i, (i + step) % size) for i in range(size)])  25.1 us
    ppermute x12, starting transfers between devices, shift(): lax.ppermute(value, axis, [(i, (i + step) % size) for i in range(size)])  21.8 us
    all_to_all x1, blocking collectives, body(): lax.all_to_all(send, ('y', 'x'), split_axis=0, concat_axis=0, tiled=True)  21.4 us
    all_to_all x1, waiting for transfers between devices, body(): lax.all_to_all(send, ('y', 'x'), split_axis=0, concat_axis=0, tiled=True)  18.4 us
    all_to_all x1, blocking collectives, body(): lax.all_to_all(masked, 'z', split_axis=0, concat_axis=0, tiled=True)  16.9 us
    pallas_call x1, Pallas kernels, body(): pl.pallas_call(first_kernel, out_shape=(jax.ShapeDtypeStruct((NY * NX, SE...  15.7 us
    pallas_call x1, Pallas kernels, body(): pl.pallas_call(list_kernel, out_shape=jax.ShapeDtypeStruct((LIST,), jnp.i...  6.69 us
    pallas_call x1, Pallas kernels, body(): pl.pallas_call(second_kernel, out_shape=jax.ShapeDtypeStruct((QBLOCKS, FR...  5.99 us
  transfers between devices with their start and end apart: 15, of which 8 were waited for; matrix products, arithmetic and copies ran while one was open for 5% of the time, Pallas kernels for 4%

profile of v9, /device:TPU:1, one launch (start us, length us, event | category | flops | bytes accessed | tf_op | source)
XLA Modules:
  0.0 181.3 jit_solution(12373484026003285000)
XLA Ops:
  6.6 0.7 broadcast_compare_fusion.1
  7.3 1.3 fusion.2
  8.6 1.4 fusion.3
  10.0 0.9 broadcast_select_fusion
  10.9 0.9 pad_maximum_fusion
  11.8 0.7 slice.26
  12.6 3.8 %collective-permute-start.6 = (bf16[128,1152]{1,0:T(8,128)(2,1)}, bf16[128,1152]{1,0:T(8,128)(2,1)S(1)}, u32[]{:S(2)}, u32[]{:S(2)}) collective-permute-start(bf16[128,1152]{1,0:T(8,128)(2,1)} %bitcast), channel_id=1, source_target_pairs={{0,128},{64,192},{128,0},{192,64},{1,129},{65,193},{129,1},{193,65... | collective-permute-start | bytes 884744 | tf_op jit(solution)/shard_map/ppermute | solution.py:38
  16.3 0.4 collective-permute-start.1
  16.7 2.3 %collective-permute-start = (bf16[128,1152]{1,0:T(8,128)(2,1)}, bf16[128,1152]{1,0:T(8,128)(2,1)S(1)}, u32[]{:S(2)}, u32[]{:S(2)}) collective-permute-start(bf16[128,1152]{1,0:T(8,128)(2,1)} %bitcast), channel_id=1, source_target_pairs={{0,192},{64,0},{128,64},{192,128},{1,193},{65,1},{129,65},{193,129... | collective-permute-start | bytes 884744 | tf_op jit(solution)/shard_map/ppermute | solution.py:38
  19.5 1.0 gather_fusion
  20.5 0.6 broadcast_in_dim.62
  21.1 4.1 %all-to-all-start = ((s32[16,1,128]{2,1,0:T(1,128)}), s32[16,1,128]{2,1,0:T(1,128)S(1)}, u32[]{:S(2)}, u32[]{:S(2)}) async-start(s32[16,1,128]{2,1,0:T(1,128)} %broadcast_in_dim.62), calls=%async_computation | async-start | bytes 16384 | tf_op jit(solution)/shard_map/all_to_all | solution.py:263
  25.2 0.5 fusion
  25.8 0.5 fusion.1
  26.2 1.4 copy-done.5
  27.6 1.1 slice.27
  28.7 2.8 %all-to-all-done = s32[16,1,128]{2,1,0:T(1,128)S(1)} async-done(((s32[16,1,128]{2,1,0:T(1,128)}), s32[16,1,128]{2,1,0:T(1,128)S(1)}, u32[]{:S(2)}, u32[]{:S(2)}) %all-to-all-start) | async-done | bytes 8224 | tf_op jit(solution)/shard_map/all_to_all | solution.py:263
  31.5 1.6 collective-permute-start.3
  33.3 0.1 or.31
  33.4 0.2 shard_map.65.refs_5_
  33.7 1.3 collective-permute-start.8
  35.0 1.5 collective-permute-start.7
  36.6 0.1 or.34
  36.8 6.7 %shard_map.64.lst = s32[640]{0:T(1024)S(1)} custom-call(s32[2048]{0:T(1024)S(1)} %fusion.13.codes), custom_call_target="tpu_custom_call" | custom-call | tf_op jit(solution)/shard_map/pallas_call | solution.py:305
  43.5 13.0 %collective-permute-done.3.refs_1_ = bf16[512,1152]{1,0:T(8,128)(2,1)S(1)} collective-permute-done((bf16[512,1152]{1,0:T(8,128)(2,1)}, bf16[512,1152]{1,0:T(8,128)(2,1)S(1)}, u32[]{:S(2)}, u32[]{:S(2)}) %collective-permute-start.3) | collective-permute-done | bytes 1179680 | tf_op jit(solution)/shard_map/ppermute | solution.py:38
  56.5 3.1 %collective-permute-done.2.refs_4_ = bf16[512,1152]{1,0:T(8,128)(2,1)} collective-permute-done((bf16[512,1152]{1,0:T(8,128)(2,1)}, bf16[512,1152]{1,0:T(8,128)(2,1)}, u32[]{:S(2)}, u32[]{:S(2)}) %collective-permute-start.2) | collective-permute-done | bytes 1179680 | tf_op jit(solution)/shard_map/ppermute | solution.py:38
  59.7 1.1 slice.20
  60.9 2.7 %collective-permute-start.5 = (bf16[256,1152]{1,0:T(8,128)(2,1)S(1)}, bf16[256,1152]{1,0:T(8,128)(2,1)}, u32[]{:S(2)}, u32[]{:S(2)}) collective-permute-start(bf16[256,1152]{1,0:T(8,128)(2,1)S(1)} %slice.21), channel_id=1, source_target_pairs={{0,192},{64,0},{128,64},{192,128},{1,193},{65,1},{129,65},{193,129... | collective-permute-start | bytes 1769480 | tf_op jit(solution)/shard_map/ppermute | solution.py:38
  63.6 1.1 slice.28
  64.6 2.3 %collective-permute-start.9 = (bf16[192,1152]{1,0:T(8,128)(2,1)S(1)}, bf16[192,1152]{1,0:T(8,128)(2,1)S(1)}, u32[]{:S(2)}, u32[]{:S(2)}) collective-permute-start(bf16[192,1152]{1,0:T(8,128)(2,1)S(1)} %slice.28), channel_id=1, source_target_pairs={{0,1},{1,2},{2,3},{3,0},{4,5},{5,6},{6,7},{7,4},{8,9},{9,10},{10,1... | collective-permute-start | bytes 1327112 | tf_op jit(solution)/shard_map/ppermute | solution.py:38
  66.9 1.1 slice.29
  67.9 2.0 %collective-permute-start.10 = (bf16[192,1152]{1,0:T(8,128)(2,1)S(1)}, bf16[192,1152]{1,0:T(8,128)(2,1)S(1)}, u32[]{:S(2)}, u32[]{:S(2)}) collective-permute-start(bf16[192,1152]{1,0:T(8,128)(2,1)S(1)} %slice.29), channel_id=1, source_target_pairs={{0,3},{1,0},{2,1},{3,2},{4,7},{5,4},{6,5},{7,6},{8,11},{9,8},{10,9... | collective-permute-start | bytes 1327112 | tf_op jit(solution)/shard_map/ppermute | solution.py:38
  70.0 6.6 %collective-permute-done.9.refs_7_ = bf16[192,1152]{1,0:T(8,128)(2,1)S(1)} collective-permute-done((bf16[192,1152]{1,0:T(8,128)(2,1)S(1)}, bf16[192,1152]{1,0:T(8,128)(2,1)S(1)}, u32[]{:S(2)}, u32[]{:S(2)}) %collective-permute-start.9) | collective-permute-done | bytes 442400 | tf_op jit(solution)/shard_map/ppermute | solution.py:38
  76.6 0.9 collective-permute-done.10.refs_8_
  77.5 0.8 copy-done.11
  78.2 3.7 %all-gather.2.cloned.1.call-done.keys = bf16[4096,1280]{1,0:T(8,128)(2,1)} async-done(((bf16[256,1280]{1,0:T(8,128)(2,1)}), bf16[4096,1280]{1,0:T(8,128)(2,1)}) %all-gather.2.cloned.1.call-update) | async-done | bytes 10485776 | tf_op jit(solution)/shard_map/all_gather | solution.py:255
  82.0 15.7 %shard_map.66 = (bf16[16,272,128]{2,1,0:T(8,128)(2,1)}, bf16[260,64,128]{2,1,0:T(8,128)(2,1)}) custom-call(s32[640]{0:T(1024)} %copy-done.3, bf16[4096,1280]{1,0:T(8,128)(2,1)} %all-gather.2.cloned.1.call-done.keys, bf16[1024,1152]{1,0:T(8,128)(2,1)} %bitcast.63, bf16[512,1152]{1,0:T(8,128)(2,1)} %copy-done.6, bf16[256,1152]{1,0:T(8,128)(2,1)} %copy-done.8, ...), custom_call_target="tpu_custom_call" | custom-call | tf_op jit(solution)/shard_map/pallas_call | solution.py:326
  97.8 5.5 %all-to-all-start.1 = ((bf16[16,272,128]{2,1,0:T(8,128)(2,1)}), bf16[16,272,128]{2,1,0:T(8,128)(2,1)S(1)}, u32[]{:S(2)}, u32[]{:S(2)}) async-start(bf16[16,272,128]{2,1,0:T(8,128)(2,1)} %get-tuple-element.34), calls=%async_computation.1 | async-start | bytes 2228224 | tf_op jit(solution)/shard_map/all_to_all | solution.py:346
  103.3 0.9 shard_map.67
  104.2 18.4 %all-to-all-done.1.got = bf16[16,272,128]{2,1,0:T(8,128)(2,1)S(1)} async-done(((bf16[16,272,128]{2,1,0:T(8,128)(2,1)}), bf16[16,272,128]{2,1,0:T(8,128)(2,1)S(1)}, u32[]{:S(2)}, u32[]{:S(2)}) %all-to-all-start.1) | async-done | bytes 1114144 | tf_op jit(solution)/shard_map/all_to_all | solution.py:346
  122.7 0.4 shard_map.68
  123.1 16.9 %all_to_all.24 = bf16[8,4,64,128]{3,2,1,0:T(8,128)(2,1)S(1)} all-to-all(bf16[8,4,64,128]{3,2,1,0:T(8,128)(2,1)S(1)} %get-tuple-element.38), channel_id=1, replica_groups=mesh['y'=4,'z'=8,'c'=2,'x'=4] {'z'}, dimensions={0} | all-to-all | bytes 1048576 | tf_op jit(solution)/shard_map/all_to_all | solution.py:359
  139.9 4.0 %collective-permute-start.11 = (bf16[32,64,128]{2,1,0:T(8,128)(2,1)S(1)}, bf16[32,64,128]{2,1,0:T(8,128)(2,1)S(1)}, u32[]{:S(2)}, u32[]{:S(2)}) collective-permute-start(bf16[32,64,128]{2,1,0:T(8,128)(2,1)S(1)} %bitcast.64), channel_id=1, source_target_pairs={{0,4},{4,0},{1,5},{5,1},{2,6},{6,2},{3,7},{7,3},{8,12},{12,8},{9,1... | collective-permute-start | bytes 1572872 | tf_op jit(solution)/shard_map/ppermute | solution.py:38
  143.9 1.5 collective-permute-done.11.far
  145.5 0.8 copy-done.9
  146.2 6.0 %shard_map.69 = bf16[64,64,128]{2,1,0:T(8,128)(2,1)} custom-call(s32[640]{0:T(1024)} %copy-done.3, bf16[260,64,128]{2,1,0:T(8,128)(2,1)} %get-tuple-element.33.w_in, bf16[32,64,128]{2,1,0:T(8,128)(2,1)} %bitcast.65, bf16[32,64,128]{2,1,0:T(8,128)(2,1)} %copy-done.9), custom_call_target="tpu_custom_call" | custom-call | tf_op jit(solution)/shard_map/pallas_call | solution.py:363
  152.2 21.4 %all_to_all.25 = bf16[64,64,128]{2,1,0:T(8,128)(2,1)S(1)} all-to-all(bf16[64,64,128]{2,1,0:T(8,128)(2,1)} %shard_map.69), channel_id=1, replica_groups=mesh['y'=4,'z'=8,'c'=2,'x'=4] {'y','x'}, dimensions={0} | all-to-all | bytes 2097152 | tf_op jit(solution)/shard_map/all_to_all | solution.py:375
  173.6 0.8 shard_map.70
  (60 shorter events, 1.2 us)
Async XLA Ops:
  6.5 13.0 %copy-start = (s32[1024]{0:T(1024)S(1)}, s32[1024]{0:T(1024)}, u32[]{:S(2)}) copy-start(s32[1024]{0:T(1024)} %param.11) | copy-start | bytes 12292
  6.5 12.5 %copy-start.12 = (s32[16,8]{0,1:T(8,128)S(1)}, s32[16,8]{0,1:T(8,128)}, u32[]{:S(2)}) copy-start(s32[16,8]{0,1:T(8,128)} %param.9) | copy-start | bytes 1540
  6.5 12.8 %copy-start.13 = (s32[16]{0:T(128)S(1)}, s32[16]{0:T(128)}, u32[]{:S(2)}) copy-start(s32[16]{0:T(128)} %param.10) | copy-start | bytes 196
  6.5 75.4 %all-gather.2.cloned.1.call-start = ((), (), s32[]{:S(2)}) async-start(), calls=%async_computation.4 | async-start | bytes 11141120 | tf_op jit(solution)/shard_map/all_gather | solution.py:255
  8.5 16.7 %copy-start.4 = (bf16[16,64,1152]{2,1,0:T(8,128)(2,1)S(1)}, bf16[16,64,1152]{2,1,0:T(8,128)(2,1)}, u32[]{:S(2)}) copy-start(bf16[16,64,1152]{2,1,0:T(8,128)(2,1)} %param.6) | copy-start | bytes 7077892
  12.6 20.9 %collective-permute-start.6 = (bf16[128,1152]{1,0:T(8,128)(2,1)}, bf16[128,1152]{1,0:T(8,128)(2,1)S(1)}, u32[]{:S(2)}, u32[]{:S(2)}) collective-permute-start(bf16[128,1152]{1,0:T(8,128)(2,1)} %bitcast), channel_id=1, source_target_pairs={{0,128},{64,192},{128,0},{192,64},{1,129},{65,193},{129,1},{193,65... | collective-permute-start | bytes 884744 | tf_op jit(solution)/shard_map/ppermute | solution.py:38
  16.3 15.2 %collective-permute-start.1 = (bf16[128,1152]{1,0:T(8,128)(2,1)}, bf16[128,1152]{1,0:T(8,128)(2,1)S(1)}, u32[]{:S(2)}, u32[]{:S(2)}) collective-permute-start(bf16[128,1152]{1,0:T(8,128)(2,1)} %bitcast), channel_id=1, source_target_pairs={{0,64},{64,128},{128,192},{192,0},{1,65},{65,129},{129,193},{193,1... | collective-permute-start | bytes 884744 | tf_op jit(solution)/shard_map/ppermute | solution.py:38
  16.7 14.8 %collective-permute-start = (bf16[128,1152]{1,0:T(8,128)(2,1)}, bf16[128,1152]{1,0:T(8,128)(2,1)S(1)}, u32[]{:S(2)}, u32[]{:S(2)}) collective-permute-start(bf16[128,1152]{1,0:T(8,128)(2,1)} %bitcast), channel_id=1, source_target_pairs={{0,192},{64,0},{128,64},{192,128},{1,193},{65,1},{129,65},{193,129... | collective-permute-start | bytes 884744 | tf_op jit(solution)/shard_map/ppermute | solution.py:38
  21.1 10.4 %all-to-all-start = ((s32[16,1,128]{2,1,0:T(1,128)}), s32[16,1,128]{2,1,0:T(1,128)S(1)}, u32[]{:S(2)}, u32[]{:S(2)}) async-start(s32[16,1,128]{2,1,0:T(1,128)} %broadcast_in_dim.62), calls=%async_computation | async-start | bytes 16384 | tf_op jit(solution)/shard_map/all_to_all | solution.py:263
  26.2 1.4 copy-start.5
  31.5 24.9 %collective-permute-start.3 = (bf16[512,1152]{1,0:T(8,128)(2,1)}, bf16[512,1152]{1,0:T(8,128)(2,1)S(1)}, u32[]{:S(2)}, u32[]{:S(2)}) collective-permute-start(bf16[512,1152]{1,0:T(8,128)(2,1)} %bitcast.66), channel_id=1, source_target_pairs={{0,192},{64,0},{128,64},{192,128},{1,193},{65,1},{129,65},{193,129... | collective-permute-start | bytes 3538952 | tf_op jit(solution)/shard_map/ppermute | solution.py:38
  33.1 26.5 %collective-permute-start.2 = (bf16[512,1152]{1,0:T(8,128)(2,1)}, bf16[512,1152]{1,0:T(8,128)(2,1)}, u32[]{:S(2)}, u32[]{:S(2)}) collective-permute-start(bf16[512,1152]{1,0:T(8,128)(2,1)} %bitcast.67), channel_id=1, source_target_pairs={{0,64},{64,128},{128,192},{192,0},{1,65},{65,129},{129,193},{193,1... | collective-permute-start | bytes 3538952 | tf_op jit(solution)/shard_map/ppermute | solution.py:38
  33.7 48.3 %copy-start.2 = (bf16[384,1152]{1,0:T(8,128)(2,1)}, bf16[384,1152]{1,0:T(8,128)(2,1)S(1)}, u32[]{:S(2)}) copy-start(bf16[384,1152]{1,0:T(8,128)(2,1)S(1)} %shard_map.65.refs_5_) | copy-start | bytes 2654212
  33.7 29.9 %collective-permute-start.8 = (bf16[384,1152]{1,0:T(8,128)(2,1)S(1)}, bf16[384,1152]{1,0:T(8,128)(2,1)}, u32[]{:S(2)}, u32[]{:S(2)}) collective-permute-start(bf16[384,1152]{1,0:T(8,128)(2,1)S(1)} %shard_map.65.refs_5_), channel_id=1, source_target_pairs={{0,1},{1,2},{2,3},{3,0},{4,5},{5,6},{6,7},{7,4},{8,9},{9,10},{10,1... | collective-permute-start | bytes 2654216 | tf_op jit(solution)/shard_map/ppermute | solution.py:38
  35.0 31.9 %collective-permute-start.7 = (bf16[384,1152]{1,0:T(8,128)(2,1)S(1)}, bf16[384,1152]{1,0:T(8,128)(2,1)}, u32[]{:S(2)}, u32[]{:S(2)}) collective-permute-start(bf16[384,1152]{1,0:T(8,128)(2,1)S(1)} %shard_map.65.refs_5_), channel_id=1, source_target_pairs={{0,3},{1,0},{2,1},{3,2},{4,7},{5,4},{6,5},{7,6},{8,11},{9,8},{10,9... | collective-permute-start | bytes 2654216 | tf_op jit(solution)/shard_map/ppermute | solution.py:38
  43.5 38.5 %copy-start.3 = (s32[640]{0:T(1024)}, s32[640]{0:T(1024)S(1)}, u32[]{:S(2)}) copy-start(s32[640]{0:T(1024)S(1)} %shard_map.64.lst) | copy-start | bytes 7684
  56.5 25.5 %copy-start.6 = (bf16[512,1152]{1,0:T(8,128)(2,1)}, bf16[512,1152]{1,0:T(8,128)(2,1)S(1)}, u32[]{:S(2)}) copy-start(bf16[512,1152]{1,0:T(8,128)(2,1)S(1)} %collective-permute-done.3.refs_1_) | copy-start | bytes 3538948
  60.8 16.7 %collective-permute-start.4 = (bf16[256,1152]{1,0:T(8,128)(2,1)S(1)}, bf16[256,1152]{1,0:T(8,128)(2,1)S(1)}, u32[]{:S(2)}, u32[]{:S(2)}) collective-permute-start(bf16[256,1152]{1,0:T(8,128)(2,1)S(1)} %slice.20), channel_id=1, source_target_pairs={{0,64},{64,128},{128,192},{192,0},{1,65},{65,129},{129,193},{193,1... | collective-permute-start | bytes 1769480 | tf_op jit(solution)/shard_map/ppermute | solution.py:38
  60.9 17.3 %collective-permute-start.5 = (bf16[256,1152]{1,0:T(8,128)(2,1)S(1)}, bf16[256,1152]{1,0:T(8,128)(2,1)}, u32[]{:S(2)}, u32[]{:S(2)}) collective-permute-start(bf16[256,1152]{1,0:T(8,128)(2,1)S(1)} %slice.21), channel_id=1, source_target_pairs={{0,192},{64,0},{128,64},{192,128},{1,193},{65,1},{129,65},{193,129... | collective-permute-start | bytes 1769480 | tf_op jit(solution)/shard_map/ppermute | solution.py:38
  64.6 12.0 %collective-permute-start.9 = (bf16[192,1152]{1,0:T(8,128)(2,1)S(1)}, bf16[192,1152]{1,0:T(8,128)(2,1)S(1)}, u32[]{:S(2)}, u32[]{:S(2)}) collective-permute-start(bf16[192,1152]{1,0:T(8,128)(2,1)S(1)} %slice.28), channel_id=1, source_target_pairs={{0,1},{1,2},{2,3},{3,0},{4,5},{5,6},{6,7},{7,4},{8,9},{9,10},{10,1... | collective-permute-start | bytes 1327112 | tf_op jit(solution)/shard_map/ppermute | solution.py:38
  67.9 9.5 %collective-permute-start.10 = (bf16[192,1152]{1,0:T(8,128)(2,1)S(1)}, bf16[192,1152]{1,0:T(8,128)(2,1)S(1)}, u32[]{:S(2)}, u32[]{:S(2)}) collective-permute-start(bf16[192,1152]{1,0:T(8,128)(2,1)S(1)} %slice.29), channel_id=1, source_target_pairs={{0,3},{1,0},{2,1},{3,2},{4,7},{5,4},{6,5},{7,6},{8,11},{9,8},{10,9... | collective-permute-start | bytes 1327112 | tf_op jit(solution)/shard_map/ppermute | solution.py:38
  76.6 5.4 %copy-start.10 = (bf16[192,1152]{1,0:T(8,128)(2,1)}, bf16[192,1152]{1,0:T(8,128)(2,1)S(1)}, u32[]{:S(2)}) copy-start(bf16[192,1152]{1,0:T(8,128)(2,1)S(1)} %collective-permute-done.9.refs_7_) | copy-start | bytes 1327108
  77.5 0.8 copy-start.11
  78.2 3.8 %copy-start.8 = (bf16[256,1152]{1,0:T(8,128)(2,1)}, bf16[256,1152]{1,0:T(8,128)(2,1)S(1)}, u32[]{:S(2)}) copy-start(bf16[256,1152]{1,0:T(8,128)(2,1)S(1)} %collective-permute-done.4.refs_2_) | copy-start | bytes 1769476
  97.8 5.5 %copy-start.1 = (bf16[4,64,1280]{2,1,0:T(8,128)(2,1)S(1)}, bf16[4,64,1280]{2,1,0:T(8,128)(2,1)}, u32[]{:S(2)}) copy-start(bf16[4,64,1280]{2,1,0:T(8,128)(2,1)} %pad_maximum_fusion) | copy-start | bytes 1966084
  97.8 24.8 %all-to-all-start.1 = ((bf16[16,272,128]{2,1,0:T(8,128)(2,1)}), bf16[16,272,128]{2,1,0:T(8,128)(2,1)S(1)}, u32[]{:S(2)}, u32[]{:S(2)}) async-start(bf16[16,272,128]{2,1,0:T(8,128)(2,1)} %get-tuple-element.34), calls=%async_computation.1 | async-start | bytes 2228224 | tf_op jit(solution)/shard_map/all_to_all | solution.py:346
  139.9 5.5 %copy-start.7 = (bf16[8,4,64,128]{3,2,1,0:T(8,128)(2,1)}, bf16[8,4,64,128]{3,2,1,0:T(8,128)(2,1)S(1)}, u32[]{:S(2)}) copy-start(bf16[8,4,64,128]{3,2,1,0:T(8,128)(2,1)S(1)} %all_to_all.24) | copy-start | bytes 1572868
  139.9 5.5 %collective-permute-start.11 = (bf16[32,64,128]{2,1,0:T(8,128)(2,1)S(1)}, bf16[32,64,128]{2,1,0:T(8,128)(2,1)S(1)}, u32[]{:S(2)}, u32[]{:S(2)}) collective-permute-start(bf16[32,64,128]{2,1,0:T(8,128)(2,1)S(1)} %bitcast.64), channel_id=1, source_target_pairs={{0,4},{4,0},{1,5},{5,1},{2,6},{6,2},{3,7},{7,3},{8,12},{12,8},{9,1... | collective-permute-start | bytes 1572872 | tf_op jit(solution)/shard_map/ppermute | solution.py:38
  145.4 0.8 copy-start.9
Sparse Core Ops, SparseCore 0:
  11.9 69.9 all-gather.1

commit v10 on v9

--- a/solution.py
+++ b/solution.py
@@ -22,12 +22,12 @@
 QBLOCKS = NY * ROWS
 Q_TURN = ROWS + (NY - 1) * STRAIGHT
 UNROLL = 8
-SLOTS = 520
+SLOTS = 528
 WIDE = FEAT + CH
 PIECE = PART * FRAMES
 SEND = PIECE + 16
 LIST = 640
-STEPS_AT = 600
+EARLY_AT, STEPS_AT = 600, 601
 SPARE = QBLOCKS
 UNREAL = 1024.0
 sharpness = 2.0 * math.sqrt(FEAT)
@@ -38,18 +38,65 @@
     return lax.ppermute(value, axis, [(i, (i + step) % size) for i in range(size)])
 
 
-def list_kernel(codes, out):
-    def eight(i, count):
+def normalize(values):
+    floats = values.astype(jnp.float32)
+    return (floats * lax.rsqrt(jnp.sum(floats * floats, axis=-1, keepdims=True) + epsilon)).astype(jnp.bfloat16)
+
+
+def prep_kernel(embeddings, prior, valid, piece, turn, e, p, sems):
+    first = lax.axis_index("x") * PART
+    copies = [
+        pltpu.make_async_copy(embeddings.at[pl.ds(first, PART)], e, sems.at[0]),
+        pltpu.make_async_copy(prior.at[pl.ds(first, PART)], p, sems.at[1]),
+    ]
+    for copy in copies:
+        copy.start()
+    for copy in copies:
+        copy.wait()
+    row = lax.broadcasted_iota(jnp.int32, (FRAMES, FRAMES), 0)
+    col = lax.broadcasted_iota(jnp.int32, (FRAMES, FRAMES), 1)
+    pick = row == col
+    for b in range(PART):
+        units = normalize(e[b])
+        real = valid[pl.ds(first + b, 1), :].astype(jnp.float32)
+        column = jnp.sum(jnp.where(pick, real, 0.0), axis=1, keepdims=True)
+        marked = jnp.where(column > 0.0, p[b].astype(jnp.float32), 2.0 * UNREAL).astype(jnp.bfloat16)
+        rows = pl.ds(b * FRAMES, FRAMES)
+        piece[rows, :FEAT] = units
+        piece[rows, FEAT:] = marked
+        if b < TURN:
+            turn[rows, :] = units
+
+
+def list_kernel(codes, out, late):
+    def eight(i, counts):
+        early_count, late_count = counts
         for u in range(8):
             code = codes[i * 8 + u]
-            out[count] = code
-            count = count + jnp.where(code >= 0, 1, 0)
-        return count
-
-    count = lax.fori_loop(0, QBLOCKS * 32 // 8, eight, 0)
+            out[early_count] = code
+            late[late_count] = code
+            is_late = (code >> 12) & 1
+            real = jnp.where(code >= 0, 1, 0)
+            early_count = early_count + (real & (1 - is_late))
+            late_count = late_count + (real & is_late)
+        return early_count, late_count
+
+    early_count, late_count = lax.fori_loop(0, QBLOCKS * 32 // 8, eight, (0, 0))
     for u in range(UNROLL):
-        out[count + u] = SPARE
-    out[STEPS_AT] = (count + UNROLL - 1) // UNROLL
+        out[early_count + u] = SPARE
+        late[late_count + u] = SPARE
+    early_steps = (early_count + UNROLL - 1) // UNROLL
+    late_steps = (late_count + UNROLL - 1) // UNROLL
+    start = early_steps * UNROLL
+
+    def copy(i, carry):
+        for u in range(UNROLL):
+            out[start + i * UNROLL + u] = late[i * UNROLL + u]
+        return carry
+
+    lax.fori_loop(0, late_steps, copy, 0)
+    out[EARLY_AT] = early_steps
+    out[STEPS_AT] = early_steps + late_steps
 
 
 def own_kernel(piece, own_weights, own_base):
@@ -94,18 +141,21 @@
 def first_kernel(lst, keys, *refs):
     queries = refs[:10]
     send_out, w_out, q, k, acc, send, w, sems, w_sem, send_sem = refs[10:]
-    copies = [pltpu.make_async_copy(keys, k, sems.at[0])]
+    half = k.shape[0] // 2
+    copies = [pltpu.make_async_copy(keys.at[pl.ds(0, half)], k.at[pl.ds(0, half)], sems.at[0])]
     at = 0
     for part in queries:
         rows = part.shape[0]
         copies.append(pltpu.make_async_copy(part, q.at[pl.ds(at, rows)], sems.at[len(copies)]))
         at += rows
+    rest = pltpu.make_async_copy(keys.at[pl.ds(half, half)], k.at[pl.ds(half, half)], sems.at[len(copies)])
     for copy in copies:
         copy.start()
+    rest.start()
     acc[...] = jnp.zeros_like(acc)
     for copy in copies:
         copy.wait()
-    steps = lst[STEPS_AT]
+    early_steps, steps = lst[EARLY_AT], lst[STEPS_AT]
 
     def step(i, carry):
         codes = [lst[i * UNROLL + u] for u in range(UNROLL)]
@@ -131,7 +181,9 @@
         pairs_copy(w, w_out, w_sem, i).start()
         return carry
 
-    lax.fori_loop(0, steps, step, 0)
+    lax.fori_loop(0, early_steps, step, 0)
+    rest.wait()
+    lax.fori_loop(early_steps, steps, step, 0)
     row = lax.broadcasted_iota(jnp.int32, (FRAMES, CH), 0)
     lane = lax.broadcasted_iota(jnp.int32, (FRAMES, CH), 1)
     pick = row == lane % FRAMES
@@ -165,8 +217,14 @@
     lax.fori_loop(0, steps, drain, 0)
 
 
-def second_kernel(lst, w_in, near, far, send, acc, w, w_sem):
+def second_kernel(lst, w_in, near, far, send_out, acc, w, scores, send, w_sem, sems, send_sem):
     steps = lst[STEPS_AT]
+    copies = [
+        pltpu.make_async_copy(near, scores.at[0], sems.at[0]),
+        pltpu.make_async_copy(far, scores.at[1], sems.at[1]),
+    ]
+    for copy in copies:
+        copy.start()
 
     def fetch(i, carry):
         pairs_copy(w_in, w, w_sem, i).start()
@@ -174,6 +232,8 @@
 
     lax.fori_loop(0, steps, fetch, 0)
     acc[...] = jnp.zeros_like(acc)
+    for copy in copies:
+        copy.wait()
 
     def drain(i, carry):
         pairs_copy(w_in, w, w_sem, i).wait()
@@ -185,17 +245,23 @@
         codes = [lst[i * UNROLL + u] for u in range(UNROLL)]
         sums = []
         for u, code in enumerate(codes):
-            block = (code >> 21) & 31
-            scores = jnp.where(((code >> 20) & 1) == 0, near[block], far[block])
             weights = w[i * (UNROLL // 2) + u // 2][:, (u % 2) * FRAMES:(u % 2 + 1) * FRAMES]
-            sums.append(jnp.dot(weights, scores, preferred_element_type=jnp.float32))
+            sums.append(
+                jnp.dot(
+                    weights, scores[(code >> 20) & 1, (code >> 21) & 31], preferred_element_type=jnp.float32
+                )
+            )
         for u, code in enumerate(codes):
             acc[code & 127] += sums[u]
         return carry
 
     lax.fori_loop(0, steps, step, 0)
-    for b in range(QBLOCKS):
-        send[b] = acc[b].astype(jnp.bfloat16)
+    groups = [pl.ds(d * PART, PART) for d in range(NY * NX)]
+    for group in groups:
+        send[group] = acc[group].astype(jnp.bfloat16)
+        pltpu.make_async_copy(send.at[group], send_out.at[group], send_sem).start()
+    for group in groups:
+        pltpu.make_async_copy(send.at[group], send_out.at[group], send_sem).wait()
 
 
 def mix_kernel(got, base, weights, prior, marks, masked, denominator, own_second):
@@ -236,25 +302,34 @@
     return pltpu.CompilerParams(vmem_limit_bytes=mebibytes * 1024 * 1024)
 
 
-def normalize(values):
-    floats = values.astype(jnp.float32)
-    return (floats * lax.rsqrt(jnp.sum(floats * floats, axis=-1, keepdims=True) + epsilon)).astype(jnp.bfloat16)
-
-
 def body(embeddings, prior_scores, frame_valid, neighbour_ids, neighbour_count, block_home):
     per_list = neighbour_ids.shape[1]
     y, z, c, x = (lax.axis_index(a) for a in ("y", "z", "c", "x"))
     first = x * PART
-    units = normalize(lax.dynamic_slice_in_dim(embeddings, first, PART, 0))
+    piece, turn = pl.pallas_call(
+        prep_kernel,
+        out_shape=(
+            jax.ShapeDtypeStruct((PIECE, WIDE), jnp.bfloat16),
+            jax.ShapeDtypeStruct((TURN * FRAMES, FEAT), jnp.bfloat16),
+        ),
+        in_specs=[hbm, hbm, vmem],
+        out_specs=(vmem, vmem),
+        scratch_shapes=[
+            pltpu.VMEM((PART, FRAMES, FEAT), jnp.bfloat16),
+            pltpu.VMEM((PART, FRAMES, CH), jnp.bfloat16),
+            pltpu.SemaphoreType.DMA((2,)),
+        ],
+        compiler_params=limit(59),
+    )(embeddings, prior_scores, frame_valid)
+
+    keys = lax.all_gather(piece, ("z", "c"), axis=0, tiled=True)
+
+    embeddings, prior_scores, ids, block_home, piece = lax.optimization_barrier(
+        (embeddings, prior_scores, neighbour_ids, block_home, piece)
+    )
     prior = lax.dynamic_slice_in_dim(prior_scores, first, PART, 0)
     valid = lax.dynamic_slice_in_dim(frame_valid, first, PART, 0)
     marks = jnp.broadcast_to(valid[:, :, None], prior.shape).astype(jnp.bfloat16)
-    marked = jnp.where(marks > 0, prior, jnp.bfloat16(2 * UNREAL))
-    piece = jnp.concatenate([units, marked], axis=-1).reshape(PIECE, WIDE)
-
-    keys = lax.all_gather(piece, ("z", "c"), axis=0, tiled=True)
-
-    embeddings, ids, block_home, piece = lax.optimization_barrier((embeddings, neighbour_ids, block_home, piece))
     target = jnp.take(block_home, ids.reshape(-1), axis=0)
     column = x * per_list + jnp.arange(per_list, dtype=jnp.int32)
     in_list = (column[None, :] < neighbour_count[:, None]).reshape(-1)
@@ -262,7 +337,6 @@
     target = jnp.broadcast_to(target[None, :], (NY * NX, ROWS * per_list))
     target = lax.all_to_all(target, ("y", "x"), split_axis=0, concat_axis=0, tiled=True)
 
-    turn = units[:TURN].reshape(TURN * FRAMES, FEAT)
     one, two, three = shift(turn, "y", -1), shift(turn, "y", 2), shift(turn, "y", 1)
     all_units = normalize(embeddings)
     straight = all_units.reshape(NX, PART, FRAMES, FEAT)[:, TURN:].reshape(STRAIGHT * FRAMES, FEAT)
@@ -307,6 +381,7 @@
         out_shape=jax.ShapeDtypeStruct((LIST,), jnp.int32),
         in_specs=[smem],
         out_specs=smem,
+        scratch_shapes=[pltpu.SMEM((LIST,), jnp.int32)],
         compiler_params=limit(1),
     )(codes)
     half = STRAIGHT * FRAMES // 2
@@ -337,7 +412,7 @@
             pltpu.VMEM((QBLOCKS + 1, FRAMES, 2 * CH), jnp.float32),
             pltpu.VMEM((NY * NX, SEND, CH), jnp.bfloat16),
             pltpu.VMEM((SLOTS // 2, FRAMES, 2 * FRAMES), jnp.bfloat16),
-            pltpu.SemaphoreType.DMA((11,)),
+            pltpu.SemaphoreType.DMA((12,)),
             pltpu.SemaphoreType.DMA,
             pltpu.SemaphoreType.DMA,
         ],
@@ -363,11 +438,15 @@
     send = pl.pallas_call(
         second_kernel,
         out_shape=jax.ShapeDtypeStruct((QBLOCKS, FRAMES, CH), jnp.bfloat16),
-        in_specs=[smem, far_memory, vmem, vmem],
-        out_specs=vmem,
+        in_specs=[smem, far_memory, hbm, hbm],
+        out_specs=far_memory,
         scratch_shapes=[
             pltpu.VMEM((QBLOCKS + 1, FRAMES, CH), jnp.float32),
             pltpu.VMEM((SLOTS // 2, FRAMES, 2 * FRAMES), jnp.bfloat16),
+            pltpu.VMEM((NC, NZ * PART, FRAMES, CH), jnp.bfloat16),
+            pltpu.VMEM((QBLOCKS, FRAMES, CH), jnp.bfloat16),
+            pltpu.SemaphoreType.DMA,
+            pltpu.SemaphoreType.DMA((2,)),
             pltpu.SemaphoreType.DMA,
         ],
         compiler_params=limit(57),

time: 182 us -> 177 us (0.973)
  waiting for transfers between devices: 50.1 us -> 42.6 us
  other arithmetic: 6.57 us -> 2.05 us
  Pallas kernels: 30.7 us -> 34.1 us
  starting transfers between devices: 31.4 us -> 33.3 us
    ppermute x12, waiting for transfers between devices: 25.1 us -> 20.4 us  [shift(): lax.ppermute(value, axis, [(i, (i + step) % size) for i in range(size)])]
    all_to_all x1, waiting for transfers between devices: 18.4 us -> 14 us  [body(): lax.all_to_all(send, ('y', 'x'), split_axis=0, concat_axis=0, tiled=True)]
    pallas_call x1, Pallas kernels: 6.69 us -> 10.7 us  [body(): pl.pallas_call(list_kernel, out_shape=jax.ShapeDtypeStruct((LIST,), jnp.i...]
    pallas_call x0 -> x1, Pallas kernels: none -> 3.03 us  [body(): pl.pallas_call(prep_kernel, out_shape=(jax.ShapeDtypeStruct((PIECE, WIDE)...]
    pallas_call x1, Pallas kernels: 15.7 us -> 13 us  [body(): pl.pallas_call(first_kernel, out_shape=(jax.ShapeDtypeStruct((NY * NX, SE...]
  transfers between devices with their start and end apart: 15 -> 15, of which waited for: 8 -> 8; matrix products, arithmetic and copies ran while one was open for 5% -> 5% of each run, Pallas kernels for 4% -> 7%
where the time goes in v10:
time: 177 us; the launch traced here: 175 us
  waiting for transfers between devices  42.6 us (24%)
  blocking collectives  39 us (22%)
  Pallas kernels  34.1 us (19%)
  starting transfers between devices  33.3 us (19%)
  between operations  13.7 us (8%)
  local copies, waits for them, and re-layouts  10.1 us (6%)
  other arithmetic  2.05 us (1%)
    ppermute x12, starting transfers between devices, shift(): lax.ppermute(value, axis, [(i, (i + step) % size) for i in range(size)])  22.7 us
    all_to_all x1, blocking collectives, body(): lax.all_to_all(send, ('y', 'x'), split_axis=0, concat_axis=0, tiled=True)  20.6 us
    ppermute x12, waiting for transfers between devices, shift(): lax.ppermute(value, axis, [(i, (i + step) % size) for i in range(size)])  20.4 us
    all_to_all x1, blocking collectives, body(): lax.all_to_all(masked, 'z', split_axis=0, concat_axis=0, tiled=True)  18.4 us
    all_to_all x1, waiting for transfers between devices, body(): lax.all_to_all(send, ('y', 'x'), split_axis=0, concat_axis=0, tiled=True)  14 us
    pallas_call x1, Pallas kernels, body(): pl.pallas_call(first_kernel, out_shape=(jax.ShapeDtypeStruct((NY * NX, SE...  13 us
    pallas_call x1, Pallas kernels, body(): pl.pallas_call(list_kernel, out_shape=jax.ShapeDtypeStruct((LIST,), jnp.i...  10.7 us
    all_to_all x1, starting transfers between devices, body(): lax.all_to_all(send, ('y', 'x'), split_axis=0, concat_axis=0, tiled=True)  6.38 us
  transfers between devices with their start and end apart: 15, of which 8 were waited for; matrix products, arithmetic and copies ran while one was open for 5% of the time, Pallas kernels for 7%

profile of v10, /device:TPU:1, one launch (start us, length us, event | category | flops | bytes accessed | tf_op | source)
XLA Modules:
  0.0 174.8 jit_solution(5107055764126380767)
XLA Ops:
  6.6 3.0 %shard_map.64 = (bf16[256,1280]{1,0:T(8,128)(2,1)}, bf16[128,1152]{1,0:T(8,128)(2,1)}) custom-call(bf16[16,64,1152]{2,1,0:T(8,128)(2,1)} %embeddings.1, bf16[16,64,128]{2,1,0:T(8,128)(2,1)} %prior.1, s32[16,64]{1,0:T(8,128)} %valid.1), custom_call_target="tpu_custom_call" | custom-call | tf_op jit(solution)/shard_map/pallas_call | solution.py:309
  9.7 3.8 %collective-permute-start.6 = (bf16[128,1152]{1,0:T(8,128)(2,1)}, bf16[128,1152]{1,0:T(8,128)(2,1)S(1)}, u32[]{:S(2)}, u32[]{:S(2)}) collective-permute-start(bf16[128,1152]{1,0:T(8,128)(2,1)} %get-tuple-element.26), channel_id=1, source_target_pairs={{0,128},{64,192},{128,0},{192,64},{1,129},{65,193},{129,1},{193,65... | collective-permute-start | bytes 884744 | tf_op jit(solution)/shard_map/ppermute | solution.py:38
  13.5 0.4 collective-permute-start.1
  13.9 2.3 %collective-permute-start = (bf16[128,1152]{1,0:T(8,128)(2,1)}, bf16[128,1152]{1,0:T(8,128)(2,1)S(1)}, u32[]{:S(2)}, u32[]{:S(2)}) collective-permute-start(bf16[128,1152]{1,0:T(8,128)(2,1)} %get-tuple-element.26), channel_id=1, source_target_pairs={{0,192},{64,0},{128,64},{192,128},{1,193},{65,1},{129,65},{193,129... | collective-permute-start | bytes 884744 | tf_op jit(solution)/shard_map/ppermute | solution.py:38
  16.3 0.1 reshape.402
  16.5 0.1 lt.99
  16.6 1.0 gather_fusion
  17.6 0.6 broadcast_in_dim.53
  18.2 4.1 %all-to-all-start = ((s32[16,1,128]{2,1,0:T(1,128)}), s32[16,1,128]{2,1,0:T(1,128)S(1)}, u32[]{:S(2)}, u32[]{:S(2)}) async-start(s32[16,1,128]{2,1,0:T(1,128)} %broadcast_in_dim.53), calls=%async_computation | async-start | bytes 16384 | tf_op jit(solution)/shard_map/all_to_all | solution.py:338
  22.4 0.5 fusion
  22.9 0.5 fusion.1
  23.4 1.4 copy-done.5
  24.8 1.1 slice.22
  25.9 2.8 %all-to-all-done = s32[16,1,128]{2,1,0:T(1,128)S(1)} async-done(((s32[16,1,128]{2,1,0:T(1,128)}), s32[16,1,128]{2,1,0:T(1,128)S(1)}, u32[]{:S(2)}, u32[]{:S(2)}) %all-to-all-start) | async-done | bytes 8224 | tf_op jit(solution)/shard_map/all_to_all | solution.py:338
  28.7 1.6 collective-permute-start.3
  30.5 0.1 or.31
  30.6 0.2 shard_map.66.refs_5_
  30.8 1.3 collective-permute-start.8
  32.1 1.5 collective-permute-start.7
  33.8 0.1 or.34
  34.0 10.7 %shard_map.65.lst = s32[640]{0:T(1024)S(1)} custom-call(s32[2048]{0:T(1024)S(1)} %fusion.11.codes), custom_call_target="tpu_custom_call" | custom-call | tf_op jit(solution)/shard_map/pallas_call | solution.py:379
  44.6 0.6 copy-done.3
  45.2 8.4 %collective-permute-done.3.refs_1_ = bf16[512,1152]{1,0:T(8,128)(2,1)S(1)} collective-permute-done((bf16[512,1152]{1,0:T(8,128)(2,1)}, bf16[512,1152]{1,0:T(8,128)(2,1)S(1)}, u32[]{:S(2)}, u32[]{:S(2)}) %collective-permute-start.3) | collective-permute-done | bytes 1179680 | tf_op jit(solution)/shard_map/ppermute | solution.py:38
  53.6 3.1 %collective-permute-done.2.refs_4_ = bf16[512,1152]{1,0:T(8,128)(2,1)} collective-permute-done((bf16[512,1152]{1,0:T(8,128)(2,1)}, bf16[512,1152]{1,0:T(8,128)(2,1)}, u32[]{:S(2)}, u32[]{:S(2)}) %collective-permute-start.2) | collective-permute-done | bytes 1179680 | tf_op jit(solution)/shard_map/ppermute | solution.py:38
  56.8 1.1 slice.16
  58.0 2.7 %collective-permute-start.5 = (bf16[256,1152]{1,0:T(8,128)(2,1)S(1)}, bf16[256,1152]{1,0:T(8,128)(2,1)}, u32[]{:S(2)}, u32[]{:S(2)}) collective-permute-start(bf16[256,1152]{1,0:T(8,128)(2,1)S(1)} %slice.17), channel_id=1, source_target_pairs={{0,192},{64,0},{128,64},{192,128},{1,193},{65,1},{129,65},{193,129... | collective-permute-start | bytes 1769480 | tf_op jit(solution)/shard_map/ppermute | solution.py:38
  60.7 2.3 %collective-permute-start.9 = (bf16[192,1152]{1,0:T(8,128)(2,1)S(1)}, bf16[192,1152]{1,0:T(8,128)(2,1)S(1)}, u32[]{:S(2)}, u32[]{:S(2)}) collective-permute-start(bf16[192,1152]{1,0:T(8,128)(2,1)S(1)} %slice.23), channel_id=1, source_target_pairs={{0,1},{1,2},{2,3},{3,0},{4,5},{5,6},{6,7},{7,4},{8,9},{9,10},{10,1... | collective-permute-start | bytes 1327112 | tf_op jit(solution)/shard_map/ppermute | solution.py:38
  63.0 1.1 slice.24
  64.1 2.2 %collective-permute-start.10 = (bf16[192,1152]{1,0:T(8,128)(2,1)S(1)}, bf16[192,1152]{1,0:T(8,128)(2,1)S(1)}, u32[]{:S(2)}, u32[]{:S(2)}) collective-permute-start(bf16[192,1152]{1,0:T(8,128)(2,1)S(1)} %slice.24), channel_id=1, source_target_pairs={{0,3},{1,0},{2,1},{3,2},{4,7},{5,4},{6,5},{7,6},{8,11},{9,8},{10,9... | collective-permute-start | bytes 1327112 | tf_op jit(solution)/shard_map/ppermute | solution.py:38
  66.3 6.3 %collective-permute-done.9.refs_7_ = bf16[192,1152]{1,0:T(8,128)(2,1)S(1)} collective-permute-done((bf16[192,1152]{1,0:T(8,128)(2,1)S(1)}, bf16[192,1152]{1,0:T(8,128)(2,1)S(1)}, u32[]{:S(2)}, u32[]{:S(2)}) %collective-permute-start.9) | collective-permute-done | bytes 442400 | tf_op jit(solution)/shard_map/ppermute | solution.py:38
  72.6 1.0 collective-permute-done.10.refs_8_
  73.6 0.8 copy-done.12
  74.4 5.4 %all-gather.2.cloned.1.call-done.keys = bf16[4096,1280]{1,0:T(8,128)(2,1)} async-done(((bf16[256,1280]{1,0:T(8,128)(2,1)}), bf16[4096,1280]{1,0:T(8,128)(2,1)}) %all-gather.2.cloned.1.call-update) | async-done | bytes 10485776 | tf_op jit(solution)/shard_map/all_gather | solution.py:325
  79.8 13.0 %shard_map.67 = (bf16[16,272,128]{2,1,0:T(8,128)(2,1)}, bf16[264,64,128]{2,1,0:T(8,128)(2,1)}) custom-call(s32[640]{0:T(1024)} %copy-done.3, bf16[4096,1280]{1,0:T(8,128)(2,1)} %all-gather.2.cloned.1.call-done.keys, bf16[1024,1152]{1,0:T(8,128)(2,1)} %bitcast.59, bf16[512,1152]{1,0:T(8,128)(2,1)} %copy-done.6, bf16[256,1152]{1,0:T(8,128)(2,1)} %copy-done.9, ...), custom_call_target="tpu_custom_call" | custom-call | tf_op jit(solution)/shard_map/pallas_call | solution.py:401
  92.8 6.4 %all-to-all-start.1 = ((bf16[16,272,128]{2,1,0:T(8,128)(2,1)}), bf16[16,272,128]{2,1,0:T(8,128)(2,1)S(1)}, u32[]{:S(2)}, u32[]{:S(2)}) async-start(bf16[16,272,128]{2,1,0:T(8,128)(2,1)} %get-tuple-element.39), calls=%async_computation.1 | async-start | bytes 2228224 | tf_op jit(solution)/shard_map/all_to_all | solution.py:421
  99.2 0.9 shard_map.68
  100.2 0.7 dynamic-slice_convert_fusion
  100.9 0.8 constant_dynamic-slice_fusion.prior
  101.7 14.0 %all-to-all-done.1.got = bf16[16,272,128]{2,1,0:T(8,128)(2,1)S(1)} async-done(((bf16[16,272,128]{2,1,0:T(8,128)(2,1)}), bf16[16,272,128]{2,1,0:T(8,128)(2,1)S(1)}, u32[]{:S(2)}, u32[]{:S(2)}) %all-to-all-start.1) | async-done | bytes 1114144 | tf_op jit(solution)/shard_map/all_to_all | solution.py:421
  115.7 0.1 broadcast_in_dim.56.marks
  115.8 0.4 shard_map.69
  116.2 18.4 %all_to_all.24 = bf16[8,4,64,128]{3,2,1,0:T(8,128)(2,1)S(1)} all-to-all(bf16[8,4,64,128]{3,2,1,0:T(8,128)(2,1)S(1)} %get-tuple-element.44), channel_id=1, replica_groups=mesh['y'=4,'z'=8,'c'=2,'x'=4] {'z'}, dimensions={0} | all-to-all | bytes 1048576 | tf_op jit(solution)/shard_map/all_to_all | solution.py:434
  134.6 4.6 %collective-permute-start.11 = (bf16[32,64,128]{2,1,0:T(8,128)(2,1)S(1)}, bf16[32,64,128]{2,1,0:T(8,128)(2,1)S(1)}, u32[]{:S(2)}, u32[]{:S(2)}) collective-permute-start(bf16[32,64,128]{2,1,0:T(8,128)(2,1)S(1)} %bitcast.60), channel_id=1, source_target_pairs={{0,4},{4,0},{1,5},{5,1},{2,6},{6,2},{3,7},{7,3},{8,12},{12,8},{9,1... | collective-permute-start | bytes 1572872 | tf_op jit(solution)/shard_map/ppermute | solution.py:38
  139.2 1.5 collective-permute-done.11.far
  140.7 0.8 copy-done.10
  141.5 5.1 %shard_map.70 = bf16[64,64,128]{2,1,0:T(8,128)(2,1)} custom-call(s32[640]{0:T(1024)} %copy-done.3, bf16[264,64,128]{2,1,0:T(8,128)(2,1)} %get-tuple-element.38.w_in, bf16[32,64,128]{2,1,0:T(8,128)(2,1)} %bitcast.61, bf16[32,64,128]{2,1,0:T(8,128)(2,1)} %copy-done.10), custom_call_target="tpu_custom_call" | custom-call | tf_op jit(solution)/shard_map/pallas_call | solution.py:438
  146.6 20.6 %all_to_all.25 = bf16[64,64,128]{2,1,0:T(8,128)(2,1)S(1)} all-to-all(bf16[64,64,128]{2,1,0:T(8,128)(2,1)} %shard_map.70), channel_id=1, replica_groups=mesh['y'=4,'z'=8,'c'=2,'x'=4] {'y','x'}, dimensions={0} | all-to-all | bytes 2097152 | tf_op jit(solution)/shard_map/all_to_all | solution.py:454
  167.2 0.8 shard_map.71
  (58 shorter events, 0.9 us)
Async XLA Ops:
  6.5 10.1 %copy-start = (s32[1024]{0:T(1024)S(1)}, s32[1024]{0:T(1024)}, u32[]{:S(2)}) copy-start(s32[1024]{0:T(1024)} %param.11) | copy-start | bytes 12292
  6.5 15.8 %copy-start.4 = (bf16[16,64,1152]{2,1,0:T(8,128)(2,1)S(1)}, bf16[16,64,1152]{2,1,0:T(8,128)(2,1)}, u32[]{:S(2)}) copy-start(bf16[16,64,1152]{2,1,0:T(8,128)(2,1)} %embeddings.1) | copy-start | bytes 7077892
  6.5 9.6 %copy-start.13 = (s32[16,8]{0,1:T(8,128)S(1)}, s32[16,8]{0,1:T(8,128)}, u32[]{:S(2)}) copy-start(s32[16,8]{0,1:T(8,128)} %param.9) | copy-start | bytes 1540
  6.5 9.9 %copy-start.14 = (s32[16]{0:T(128)S(1)}, s32[16]{0:T(128)}, u32[]{:S(2)}) copy-start(s32[16]{0:T(128)} %param.10) | copy-start | bytes 196
  6.5 73.3 %all-gather.2.cloned.1.call-start = ((), (), s32[]{:S(2)}) async-start(), calls=%async_computation.4 | async-start | bytes 11141120 | tf_op jit(solution)/shard_map/all_gather | solution.py:325
  9.7 21.0 %collective-permute-start.6 = (bf16[128,1152]{1,0:T(8,128)(2,1)}, bf16[128,1152]{1,0:T(8,128)(2,1)S(1)}, u32[]{:S(2)}, u32[]{:S(2)}) collective-permute-start(bf16[128,1152]{1,0:T(8,128)(2,1)} %get-tuple-element.26), channel_id=1, source_target_pairs={{0,128},{64,192},{128,0},{192,64},{1,129},{65,193},{129,1},{193,65... | collective-permute-start | bytes 884744 | tf_op jit(solution)/shard_map/ppermute | solution.py:38
  13.5 15.2 %collective-permute-start.1 = (bf16[128,1152]{1,0:T(8,128)(2,1)}, bf16[128,1152]{1,0:T(8,128)(2,1)S(1)}, u32[]{:S(2)}, u32[]{:S(2)}) collective-permute-start(bf16[128,1152]{1,0:T(8,128)(2,1)} %get-tuple-element.26), channel_id=1, source_target_pairs={{0,64},{64,128},{128,192},{192,0},{1,65},{65,129},{129,193},{193,1... | collective-permute-start | bytes 884744 | tf_op jit(solution)/shard_map/ppermute | solution.py:38
  13.9 14.8 %collective-permute-start = (bf16[128,1152]{1,0:T(8,128)(2,1)}, bf16[128,1152]{1,0:T(8,128)(2,1)S(1)}, u32[]{:S(2)}, u32[]{:S(2)}) collective-permute-start(bf16[128,1152]{1,0:T(8,128)(2,1)} %get-tuple-element.26), channel_id=1, source_target_pairs={{0,192},{64,0},{128,64},{192,128},{1,193},{65,1},{129,65},{193,129... | collective-permute-start | bytes 884744 | tf_op jit(solution)/shard_map/ppermute | solution.py:38
  18.2 10.5 %all-to-all-start = ((s32[16,1,128]{2,1,0:T(1,128)}), s32[16,1,128]{2,1,0:T(1,128)S(1)}, u32[]{:S(2)}, u32[]{:S(2)}) async-start(s32[16,1,128]{2,1,0:T(1,128)} %broadcast_in_dim.53), calls=%async_computation | async-start | bytes 16384 | tf_op jit(solution)/shard_map/all_to_all | solution.py:338
  23.4 1.4 copy-start.5
  28.7 24.9 %collective-permute-start.3 = (bf16[512,1152]{1,0:T(8,128)(2,1)}, bf16[512,1152]{1,0:T(8,128)(2,1)S(1)}, u32[]{:S(2)}, u32[]{:S(2)}) collective-permute-start(bf16[512,1152]{1,0:T(8,128)(2,1)} %bitcast.62), channel_id=1, source_target_pairs={{0,192},{64,0},{128,64},{192,128},{1,193},{65,1},{129,65},{193,129... | collective-permute-start | bytes 3538952 | tf_op jit(solution)/shard_map/ppermute | solution.py:38
  30.3 26.4 %collective-permute-start.2 = (bf16[512,1152]{1,0:T(8,128)(2,1)}, bf16[512,1152]{1,0:T(8,128)(2,1)}, u32[]{:S(2)}, u32[]{:S(2)}) collective-permute-start(bf16[512,1152]{1,0:T(8,128)(2,1)} %bitcast.63), channel_id=1, source_target_pairs={{0,64},{64,128},{128,192},{192,0},{1,65},{65,129},{129,193},{193,1... | collective-permute-start | bytes 3538952 | tf_op jit(solution)/shard_map/ppermute | solution.py:38
  30.8 49.0 %copy-start.1 = (bf16[384,1152]{1,0:T(8,128)(2,1)}, bf16[384,1152]{1,0:T(8,128)(2,1)S(1)}, u32[]{:S(2)}) copy-start(bf16[384,1152]{1,0:T(8,128)(2,1)S(1)} %shard_map.66.refs_5_) | copy-start | bytes 2654212
  30.8 29.8 %collective-permute-start.8 = (bf16[384,1152]{1,0:T(8,128)(2,1)S(1)}, bf16[384,1152]{1,0:T(8,128)(2,1)S(1)}, u32[]{:S(2)}, u32[]{:S(2)}) collective-permute-start(bf16[384,1152]{1,0:T(8,128)(2,1)S(1)} %shard_map.66.refs_5_), channel_id=1, source_target_pairs={{0,1},{1,2},{2,3},{3,0},{4,5},{5,6},{6,7},{7,4},{8,9},{9,10},{10,1... | collective-permute-start | bytes 2654216 | tf_op jit(solution)/shard_map/ppermute | solution.py:38
  32.1 30.9 %collective-permute-start.7 = (bf16[384,1152]{1,0:T(8,128)(2,1)S(1)}, bf16[384,1152]{1,0:T(8,128)(2,1)}, u32[]{:S(2)}, u32[]{:S(2)}) collective-permute-start(bf16[384,1152]{1,0:T(8,128)(2,1)S(1)} %shard_map.66.refs_5_), channel_id=1, source_target_pairs={{0,3},{1,0},{2,1},{3,2},{4,7},{5,4},{6,5},{7,6},{8,11},{9,8},{10,9... | collective-permute-start | bytes 2654216 | tf_op jit(solution)/shard_map/ppermute | solution.py:38
  44.6 0.6 copy-start.3
  53.6 26.2 %copy-start.6 = (bf16[512,1152]{1,0:T(8,128)(2,1)}, bf16[512,1152]{1,0:T(8,128)(2,1)S(1)}, u32[]{:S(2)}) copy-start(bf16[512,1152]{1,0:T(8,128)(2,1)S(1)} %collective-permute-done.3.refs_1_) | copy-start | bytes 3538948
  57.9 15.7 %collective-permute-start.4 = (bf16[256,1152]{1,0:T(8,128)(2,1)S(1)}, bf16[256,1152]{1,0:T(8,128)(2,1)S(1)}, u32[]{:S(2)}, u32[]{:S(2)}) collective-permute-start(bf16[256,1152]{1,0:T(8,128)(2,1)S(1)} %slice.16), channel_id=1, source_target_pairs={{0,64},{64,128},{128,192},{192,0},{1,65},{65,129},{129,193},{193,1... | collective-permute-start | bytes 1769480 | tf_op jit(solution)/shard_map/ppermute | solution.py:38
  58.0 16.4 %collective-permute-start.5 = (bf16[256,1152]{1,0:T(8,128)(2,1)S(1)}, bf16[256,1152]{1,0:T(8,128)(2,1)}, u32[]{:S(2)}, u32[]{:S(2)}) collective-permute-start(bf16[256,1152]{1,0:T(8,128)(2,1)S(1)} %slice.17), channel_id=1, source_target_pairs={{0,192},{64,0},{128,64},{192,128},{1,193},{65,1},{129,65},{193,129... | collective-permute-start | bytes 1769480 | tf_op jit(solution)/shard_map/ppermute | solution.py:38
  60.7 19.2 %copy-start.8 = (bf16[384,1152]{1,0:T(8,128)(2,1)}, bf16[384,1152]{1,0:T(8,128)(2,1)S(1)}, u32[]{:S(2)}) copy-start(bf16[384,1152]{1,0:T(8,128)(2,1)S(1)} %collective-permute-done.8.refs_9_) | copy-start | bytes 2654212
  60.7 11.9 %collective-permute-start.9 = (bf16[192,1152]{1,0:T(8,128)(2,1)S(1)}, bf16[192,1152]{1,0:T(8,128)(2,1)S(1)}, u32[]{:S(2)}, u32[]{:S(2)}) collective-permute-start(bf16[192,1152]{1,0:T(8,128)(2,1)S(1)} %slice.23), channel_id=1, source_target_pairs={{0,1},{1,2},{2,3},{3,0},{4,5},{5,6},{6,7},{7,4},{8,9},{9,10},{10,1... | collective-permute-start | bytes 1327112 | tf_op jit(solution)/shard_map/ppermute | solution.py:38
  64.1 9.5 %collective-permute-start.10 = (bf16[192,1152]{1,0:T(8,128)(2,1)S(1)}, bf16[192,1152]{1,0:T(8,128)(2,1)S(1)}, u32[]{:S(2)}, u32[]{:S(2)}) collective-permute-start(bf16[192,1152]{1,0:T(8,128)(2,1)S(1)} %slice.24), channel_id=1, source_target_pairs={{0,3},{1,0},{2,1},{3,2},{4,7},{5,4},{6,5},{7,6},{8,11},{9,8},{10,9... | collective-permute-start | bytes 1327112 | tf_op jit(solution)/shard_map/ppermute | solution.py:38
  72.6 1.0 copy-start.11
  73.6 0.8 copy-start.12
  74.4 5.5 %copy-start.9 = (bf16[256,1152]{1,0:T(8,128)(2,1)}, bf16[256,1152]{1,0:T(8,128)(2,1)S(1)}, u32[]{:S(2)}) copy-start(bf16[256,1152]{1,0:T(8,128)(2,1)S(1)} %collective-permute-done.4.refs_2_) | copy-start | bytes 1769476
  92.8 6.4 %copy-start.2 = (bf16[256,1280]{1,0:T(8,128)(2,1)S(1)}, bf16[256,1280]{1,0:T(8,128)(2,1)}, u32[]{:S(2)}) copy-start(bf16[256,1280]{1,0:T(8,128)(2,1)} %get-tuple-element.40.piece) | copy-start | bytes 1966084
  92.8 22.9 %all-to-all-start.1 = ((bf16[16,272,128]{2,1,0:T(8,128)(2,1)}), bf16[16,272,128]{2,1,0:T(8,128)(2,1)S(1)}, u32[]{:S(2)}, u32[]{:S(2)}) async-start(bf16[16,272,128]{2,1,0:T(8,128)(2,1)} %get-tuple-element.39), calls=%async_computation.1 | async-start | bytes 2228224 | tf_op jit(solution)/shard_map/all_to_all | solution.py:421
  134.6 6.1 %copy-start.7 = (bf16[8,4,64,128]{3,2,1,0:T(8,128)(2,1)}, bf16[8,4,64,128]{3,2,1,0:T(8,128)(2,1)S(1)}, u32[]{:S(2)}) copy-start(bf16[8,4,64,128]{3,2,1,0:T(8,128)(2,1)S(1)} %all_to_all.24) | copy-start | bytes 1572868
  134.6 6.1 %collective-permute-start.11 = (bf16[32,64,128]{2,1,0:T(8,128)(2,1)S(1)}, bf16[32,64,128]{2,1,0:T(8,128)(2,1)S(1)}, u32[]{:S(2)}, u32[]{:S(2)}) collective-permute-start(bf16[32,64,128]{2,1,0:T(8,128)(2,1)S(1)} %bitcast.60), channel_id=1, source_target_pairs={{0,4},{4,0},{1,5},{5,1},{2,6},{6,2},{3,7},{7,3},{8,12},{12,8},{9,1... | collective-permute-start | bytes 1572872 | tf_op jit(solution)/shard_map/ppermute | solution.py:38
  140.7 0.8 copy-start.10
Sparse Core Ops, SparseCore 0:
  9.8 69.9 all-gather.1

commit v11 on v10

--- a/solution.py
+++ b/solution.py
@@ -23,6 +23,7 @@
 Q_TURN = ROWS + (NY - 1) * STRAIGHT
 UNROLL = 8
 SLOTS = 528
+HELD = 4608
 WIDE = FEAT + CH
 PIECE = PART * FRAMES
 SEND = PIECE + 16
@@ -217,14 +218,8 @@
     lax.fori_loop(0, steps, drain, 0)
 
 
-def second_kernel(lst, w_in, near, far, send_out, acc, w, scores, send, w_sem, sems, send_sem):
+def second_kernel(lst, w_in, near, far, send, acc, w, w_sem):
     steps = lst[STEPS_AT]
-    copies = [
-        pltpu.make_async_copy(near, scores.at[0], sems.at[0]),
-        pltpu.make_async_copy(far, scores.at[1], sems.at[1]),
-    ]
-    for copy in copies:
-        copy.start()
 
     def fetch(i, carry):
         pairs_copy(w_in, w, w_sem, i).start()
@@ -232,8 +227,6 @@
 
     lax.fori_loop(0, steps, fetch, 0)
     acc[...] = jnp.zeros_like(acc)
-    for copy in copies:
-        copy.wait()
 
     def drain(i, carry):
         pairs_copy(w_in, w, w_sem, i).wait()
@@ -246,22 +239,16 @@
         sums = []
         for u, code in enumerate(codes):
             weights = w[i * (UNROLL // 2) + u // 2][:, (u % 2) * FRAMES:(u % 2 + 1) * FRAMES]
-            sums.append(
-                jnp.dot(
-                    weights, scores[(code >> 20) & 1, (code >> 21) & 31], preferred_element_type=jnp.float32
-                )
-            )
+            block = (code >> 21) & 31
+            scores = jnp.where(((code >> 20) & 1) == 0, near[block], far[block])
+            sums.append(jnp.dot(weights, scores, preferred_element_type=jnp.float32))
         for u, code in enumerate(codes):
             acc[code & 127] += sums[u]
         return carry
 
     lax.fori_loop(0, steps, step, 0)
-    groups = [pl.ds(d * PART, PART) for d in range(NY * NX)]
-    for group in groups:
-        send[group] = acc[group].astype(jnp.bfloat16)
-        pltpu.make_async_copy(send.at[group], send_out.at[group], send_sem).start()
-    for group in groups:
-        pltpu.make_async_copy(send.at[group], send_out.at[group], send_sem).wait()
+    for b in range(QBLOCKS):
+        send[b] = acc[b].astype(jnp.bfloat16)
 
 
 def mix_kernel(got, base, weights, prior, marks, masked, denominator, own_second):
@@ -402,7 +389,7 @@
         first_kernel,
         out_shape=(
             jax.ShapeDtypeStruct((NY * NX, SEND, CH), jnp.bfloat16),
-            jax.ShapeDtypeStruct((SLOTS // 2, FRAMES, 2 * FRAMES), jnp.bfloat16),
+            jax.ShapeDtypeStruct((HELD, FRAMES, 2 * FRAMES), jnp.bfloat16),
         ),
         in_specs=[smem] + [hbm] * 11,
         out_specs=(far_memory, far_memory),
@@ -438,18 +425,14 @@
     send = pl.pallas_call(
         second_kernel,
         out_shape=jax.ShapeDtypeStruct((QBLOCKS, FRAMES, CH), jnp.bfloat16),
-        in_specs=[smem, far_memory, hbm, hbm],
-        out_specs=far_memory,
+        in_specs=[smem, far_memory, vmem, vmem],
+        out_specs=vmem,
         scratch_shapes=[
             pltpu.VMEM((QBLOCKS + 1, FRAMES, CH), jnp.float32),
             pltpu.VMEM((SLOTS // 2, FRAMES, 2 * FRAMES), jnp.bfloat16),
-            pltpu.VMEM((NC, NZ * PART, FRAMES, CH), jnp.bfloat16),
-            pltpu.VMEM((QBLOCKS, FRAMES, CH), jnp.bfloat16),
-            pltpu.SemaphoreType.DMA,
-            pltpu.SemaphoreType.DMA((2,)),
             pltpu.SemaphoreType.DMA,
         ],
-        compiler_params=limit(57),
+        compiler_params=limit(16),
     )(lst, weights, near_scores, far_scores)
     got = lax.all_to_all(send, ("y", "x"), split_axis=0, concat_axis=0, tiled=True)
     return pl.pallas_call(

time: 177 us -> 176 us (level)
    all_to_all x1, blocking collectives: 18.4 us -> 20.8 us  [body(): lax.all_to_all(masked, 'z', split_axis=0, concat_axis=0, tiled=True)]
where the time goes in v11:
time: 176 us; the launch traced here: 174 us
  waiting for transfers between devices  43.5 us (25%)
  blocking collectives  40.1 us (23%)
  Pallas kernels  32.8 us (19%)
  starting transfers between devices  32.3 us (18%)
  between operations  13.7 us (8%)
  local copies, waits for them, and re-layouts  9.45 us (5%)
  other arithmetic  2.05 us (1%)
    ppermute x12, starting transfers between devices, shift(): lax.ppermute(value, axis, [(i, (i + step) % size) for i in range(size)])  21.1 us
    all_to_all x1, blocking collectives, body(): lax.all_to_all(masked, 'z', split_axis=0, concat_axis=0, tiled=True)  20.8 us
    ppermute x12, waiting for transfers between devices, shift(): lax.ppermute(value, axis, [(i, (i + step) % size) for i in range(size)])  20.4 us
    all_to_all x1, blocking collectives, body(): lax.all_to_all(send, ('y', 'x'), split_axis=0, concat_axis=0, tiled=True)  19.2 us
    all_to_all x1, waiting for transfers between devices, body(): lax.all_to_all(send, ('y', 'x'), split_axis=0, concat_axis=0, tiled=True)  14.9 us
    pallas_call x1, Pallas kernels, body(): pl.pallas_call(first_kernel, out_shape=(jax.ShapeDtypeStruct((NY * NX, SE...  12.9 us
    pallas_call x1, Pallas kernels, body(): pl.pallas_call(list_kernel, out_shape=jax.ShapeDtypeStruct((LIST,), jnp.i...  10.7 us
    all_to_all x1, starting transfers between devices, body(): lax.all_to_all(send, ('y', 'x'), split_axis=0, concat_axis=0, tiled=True)  7.01 us
  transfers between devices with their start and end apart: 15, of which 8 were waited for; matrix products, arithmetic and copies ran while one was open for 5% of the time, Pallas kernels for 7%

profile of v11, /device:TPU:1, one launch (start us, length us, event | category | flops | bytes accessed | tf_op | source)
XLA Modules:
  0.0 173.8 jit_solution(14688683077055923583)
XLA Ops:
  6.6 3.1 %shard_map.64 = (bf16[256,1280]{1,0:T(8,128)(2,1)}, bf16[128,1152]{1,0:T(8,128)(2,1)}) custom-call(bf16[16,64,1152]{2,1,0:T(8,128)(2,1)} %embeddings.1, bf16[16,64,128]{2,1,0:T(8,128)(2,1)} %prior.1, s32[16,64]{1,0:T(8,128)} %valid.1), custom_call_target="tpu_custom_call" | custom-call | tf_op jit(solution)/shard_map/pallas_call | solution.py:296
  9.7 3.8 %collective-permute-start.6 = (bf16[128,1152]{1,0:T(8,128)(2,1)}, bf16[128,1152]{1,0:T(8,128)(2,1)S(1)}, u32[]{:S(2)}, u32[]{:S(2)}) collective-permute-start(bf16[128,1152]{1,0:T(8,128)(2,1)} %get-tuple-element.26), channel_id=1, source_target_pairs={{0,128},{64,192},{128,0},{192,64},{1,129},{65,193},{129,1},{193,65... | collective-permute-start | bytes 884744 | tf_op jit(solution)/shard_map/ppermute | solution.py:39
  13.5 0.4 collective-permute-start.1
  13.9 2.3 %collective-permute-start = (bf16[128,1152]{1,0:T(8,128)(2,1)}, bf16[128,1152]{1,0:T(8,128)(2,1)S(1)}, u32[]{:S(2)}, u32[]{:S(2)}) collective-permute-start(bf16[128,1152]{1,0:T(8,128)(2,1)} %get-tuple-element.26), channel_id=1, source_target_pairs={{0,192},{64,0},{128,64},{192,128},{1,193},{65,1},{129,65},{193,129... | collective-permute-start | bytes 884744 | tf_op jit(solution)/shard_map/ppermute | solution.py:39
  16.3 0.1 reshape.403
  16.4 0.1 reshape.402
  16.5 0.1 lt.99
  16.7 1.0 gather_fusion
  17.7 0.6 broadcast_in_dim.53
  18.3 4.1 %all-to-all-start = ((s32[16,1,128]{2,1,0:T(1,128)}), s32[16,1,128]{2,1,0:T(1,128)S(1)}, u32[]{:S(2)}, u32[]{:S(2)}) async-start(s32[16,1,128]{2,1,0:T(1,128)} %broadcast_in_dim.53), calls=%async_computation | async-start | bytes 16384 | tf_op jit(solution)/shard_map/all_to_all | solution.py:325
  22.4 0.5 fusion
  23.0 0.5 fusion.1
  23.4 1.4 copy-done.6
  24.9 1.1 slice.22
  26.0 2.7 %all-to-all-done = s32[16,1,128]{2,1,0:T(1,128)S(1)} async-done(((s32[16,1,128]{2,1,0:T(1,128)}), s32[16,1,128]{2,1,0:T(1,128)S(1)}, u32[]{:S(2)}, u32[]{:S(2)}) %all-to-all-start) | async-done | bytes 8224 | tf_op jit(solution)/shard_map/all_to_all | solution.py:325
  28.7 1.6 collective-permute-start.3
  30.5 0.1 or.31
  30.6 0.2 shard_map.66.refs_5_
  30.9 1.3 collective-permute-start.8
  32.2 1.5 collective-permute-start.7
  33.8 0.1 or.34
  34.0 10.7 %shard_map.65.lst = s32[640]{0:T(1024)S(1)} custom-call(s32[2048]{0:T(1024)S(1)} %fusion.11.codes), custom_call_target="tpu_custom_call" | custom-call | tf_op jit(solution)/shard_map/pallas_call | solution.py:366
  44.7 0.6 copy-done.3
  45.3 8.4 %collective-permute-done.3.refs_1_ = bf16[512,1152]{1,0:T(8,128)(2,1)S(1)} collective-permute-done((bf16[512,1152]{1,0:T(8,128)(2,1)}, bf16[512,1152]{1,0:T(8,128)(2,1)S(1)}, u32[]{:S(2)}, u32[]{:S(2)}) %collective-permute-start.3) | collective-permute-done | bytes 1179680 | tf_op jit(solution)/shard_map/ppermute | solution.py:39
  53.6 3.1 %collective-permute-done.2.refs_4_ = bf16[512,1152]{1,0:T(8,128)(2,1)} collective-permute-done((bf16[512,1152]{1,0:T(8,128)(2,1)}, bf16[512,1152]{1,0:T(8,128)(2,1)}, u32[]{:S(2)}, u32[]{:S(2)}) %collective-permute-start.2) | collective-permute-done | bytes 1179680 | tf_op jit(solution)/shard_map/ppermute | solution.py:39
  56.8 1.1 slice.16
  58.0 2.7 %collective-permute-start.5 = (bf16[256,1152]{1,0:T(8,128)(2,1)S(1)}, bf16[256,1152]{1,0:T(8,128)(2,1)}, u32[]{:S(2)}, u32[]{:S(2)}) collective-permute-start(bf16[256,1152]{1,0:T(8,128)(2,1)S(1)} %slice.17), channel_id=1, source_target_pairs={{0,192},{64,0},{128,64},{192,128},{1,193},{65,1},{129,65},{193,129... | collective-permute-start | bytes 1769480 | tf_op jit(solution)/shard_map/ppermute | solution.py:39
  60.7 2.3 %collective-permute-start.9 = (bf16[192,1152]{1,0:T(8,128)(2,1)S(1)}, bf16[192,1152]{1,0:T(8,128)(2,1)S(1)}, u32[]{:S(2)}, u32[]{:S(2)}) collective-permute-start(bf16[192,1152]{1,0:T(8,128)(2,1)S(1)} %slice.23), channel_id=1, source_target_pairs={{0,1},{1,2},{2,3},{3,0},{4,5},{5,6},{6,7},{7,4},{8,9},{9,10},{10,1... | collective-permute-start | bytes 1327112 | tf_op jit(solution)/shard_map/ppermute | solution.py:39
  63.0 1.1 slice.24
  64.1 2.2 %collective-permute-start.10 = (bf16[192,1152]{1,0:T(8,128)(2,1)S(1)}, bf16[192,1152]{1,0:T(8,128)(2,1)S(1)}, u32[]{:S(2)}, u32[]{:S(2)}) collective-permute-start(bf16[192,1152]{1,0:T(8,128)(2,1)S(1)} %slice.24), channel_id=1, source_target_pairs={{0,3},{1,0},{2,1},{3,2},{4,7},{5,4},{6,5},{7,6},{8,11},{9,8},{10,9... | collective-permute-start | bytes 1327112 | tf_op jit(solution)/shard_map/ppermute | solution.py:39
  66.3 6.3 %collective-permute-done.9.refs_7_ = bf16[192,1152]{1,0:T(8,128)(2,1)S(1)} collective-permute-done((bf16[192,1152]{1,0:T(8,128)(2,1)S(1)}, bf16[192,1152]{1,0:T(8,128)(2,1)S(1)}, u32[]{:S(2)}, u32[]{:S(2)}) %collective-permute-start.9) | collective-permute-done | bytes 442400 | tf_op jit(solution)/shard_map/ppermute | solution.py:39
  72.6 1.0 collective-permute-done.10.refs_8_
  73.6 0.8 copy-done.11
  74.4 5.4 %all-gather.2.cloned.1.call-done.keys = bf16[4096,1280]{1,0:T(8,128)(2,1)} async-done(((bf16[256,1280]{1,0:T(8,128)(2,1)}), bf16[4096,1280]{1,0:T(8,128)(2,1)}) %all-gather.2.cloned.1.call-update) | async-done | bytes 10485776 | tf_op jit(solution)/shard_map/all_gather | solution.py:312
  79.9 12.9 %shard_map.67 = (bf16[16,272,128]{2,1,0:T(8,128)(2,1)}, bf16[4608,64,128]{2,1,0:T(8,128)(2,1)}) custom-call(s32[640]{0:T(1024)} %copy-done.3, bf16[4096,1280]{1,0:T(8,128)(2,1)} %all-gather.2.cloned.1.call-done.keys, bf16[1024,1152]{1,0:T(8,128)(2,1)} %bitcast.61, bf16[512,1152]{1,0:T(8,128)(2,1)} %copy-done.7, bf16[256,1152]{1,0:T(8,128)(2,1)} %copy-done.9, ...), custom_call_target="tpu_custom_call" | custom-call | tf_op jit(solution)/shard_map/pallas_call | solution.py:388
  92.8 7.0 %all-to-all-start.1 = ((bf16[16,272,128]{2,1,0:T(8,128)(2,1)}), bf16[16,272,128]{2,1,0:T(8,128)(2,1)S(1)}, u32[]{:S(2)}, u32[]{:S(2)}) async-start(bf16[16,272,128]{2,1,0:T(8,128)(2,1)} %get-tuple-element.39), calls=%async_computation.1 | async-start | bytes 2228224 | tf_op jit(solution)/shard_map/all_to_all | solution.py:408
  99.9 0.9 shard_map.68
  100.8 0.7 dynamic-slice_convert_fusion
  101.5 0.8 constant_dynamic-slice_fusion.prior
  102.3 14.9 %all-to-all-done.1.got = bf16[16,272,128]{2,1,0:T(8,128)(2,1)S(1)} async-done(((bf16[16,272,128]{2,1,0:T(8,128)(2,1)}), bf16[16,272,128]{2,1,0:T(8,128)(2,1)S(1)}, u32[]{:S(2)}, u32[]{:S(2)}) %all-to-all-start.1) | async-done | bytes 1114144 | tf_op jit(solution)/shard_map/all_to_all | solution.py:408
  117.2 0.1 broadcast_in_dim.56.marks
  117.3 0.4 shard_map.69
  117.7 20.8 %all_to_all.24 = bf16[8,4,64,128]{3,2,1,0:T(8,128)(2,1)S(1)} all-to-all(bf16[8,4,64,128]{3,2,1,0:T(8,128)(2,1)S(1)} %get-tuple-element.44), channel_id=1, replica_groups=mesh['y'=4,'z'=8,'c'=2,'x'=4] {'z'}, dimensions={0} | all-to-all | bytes 1048576 | tf_op jit(solution)/shard_map/all_to_all | solution.py:421
  138.5 3.0 %collective-permute-start.11 = (bf16[32,64,128]{2,1,0:T(8,128)(2,1)S(1)}, bf16[32,64,128]{2,1,0:T(8,128)(2,1)S(1)}, u32[]{:S(2)}, u32[]{:S(2)}) collective-permute-start(bf16[32,64,128]{2,1,0:T(8,128)(2,1)S(1)} %bitcast.58), channel_id=1, source_target_pairs={{0,4},{4,0},{1,5},{5,1},{2,6},{6,2},{3,7},{7,3},{8,12},{12,8},{9,1... | collective-permute-start | bytes 1572872 | tf_op jit(solution)/shard_map/ppermute | solution.py:39
  141.5 1.5 collective-permute-done.11.far
  143.1 3.9 %shard_map.70 = bf16[64,64,128]{2,1,0:T(8,128)(2,1)S(1)} custom-call(s32[640]{0:T(1024)S(1)} %copy-done.4, bf16[4608,64,128]{2,1,0:T(8,128)(2,1)} %get-tuple-element.38.w_in, bf16[32,64,128]{2,1,0:T(8,128)(2,1)S(1)} %bitcast.59, bf16[32,64,128]{2,1,0:T(8,128)(2,1)S(1)} %collective-permute-done.11.far), custom_call_target="tpu_custom_call" | custom-call | tf_op jit(solution)/shard_map/pallas_call | solution.py:425
  146.9 19.2 %all_to_all.25 = bf16[64,64,128]{2,1,0:T(8,128)(2,1)S(1)} all-to-all(bf16[64,64,128]{2,1,0:T(8,128)(2,1)S(1)} %shard_map.70), channel_id=1, replica_groups=mesh['y'=4,'z'=8,'c'=2,'x'=4] {'y','x'}, dimensions={0} | all-to-all | bytes 2097152 | tf_op jit(solution)/shard_map/all_to_all | solution.py:437
  166.2 0.8 shard_map.71
  (56 shorter events, 0.9 us)
Async XLA Ops:
  6.5 10.1 %copy-start = (s32[1024]{0:T(1024)S(1)}, s32[1024]{0:T(1024)}, u32[]{:S(2)}) copy-start(s32[1024]{0:T(1024)} %param.11) | copy-start | bytes 12292
  6.5 15.9 %copy-start.5 = (bf16[16,64,1152]{2,1,0:T(8,128)(2,1)S(1)}, bf16[16,64,1152]{2,1,0:T(8,128)(2,1)}, u32[]{:S(2)}) copy-start(bf16[16,64,1152]{2,1,0:T(8,128)(2,1)} %embeddings.1) | copy-start | bytes 7077892
  6.5 9.7 %copy-start.12 = (s32[16,8]{0,1:T(8,128)S(1)}, s32[16,8]{0,1:T(8,128)}, u32[]{:S(2)}) copy-start(s32[16,8]{0,1:T(8,128)} %param.9) | copy-start | bytes 1540
  6.5 9.9 %copy-start.13 = (s32[16]{0:T(128)S(1)}, s32[16]{0:T(128)}, u32[]{:S(2)}) copy-start(s32[16]{0:T(128)} %param.10) | copy-start | bytes 196
  6.5 73.3 %all-gather.2.cloned.1.call-start = ((), (), s32[]{:S(2)}) async-start(), calls=%async_computation.4 | async-start | bytes 11141120 | tf_op jit(solution)/shard_map/all_gather | solution.py:312
  9.7 21.0 %collective-permute-start.6 = (bf16[128,1152]{1,0:T(8,128)(2,1)}, bf16[128,1152]{1,0:T(8,128)(2,1)S(1)}, u32[]{:S(2)}, u32[]{:S(2)}) collective-permute-start(bf16[128,1152]{1,0:T(8,128)(2,1)} %get-tuple-element.26), channel_id=1, source_target_pairs={{0,128},{64,192},{128,0},{192,64},{1,129},{65,193},{129,1},{193,65... | collective-permute-start | bytes 884744 | tf_op jit(solution)/shard_map/ppermute | solution.py:39
  13.5 15.2 %collective-permute-start.1 = (bf16[128,1152]{1,0:T(8,128)(2,1)}, bf16[128,1152]{1,0:T(8,128)(2,1)S(1)}, u32[]{:S(2)}, u32[]{:S(2)}) collective-permute-start(bf16[128,1152]{1,0:T(8,128)(2,1)} %get-tuple-element.26), channel_id=1, source_target_pairs={{0,64},{64,128},{128,192},{192,0},{1,65},{65,129},{129,193},{193,1... | collective-permute-start | bytes 884744 | tf_op jit(solution)/shard_map/ppermute | solution.py:39
  13.9 14.8 %collective-permute-start = (bf16[128,1152]{1,0:T(8,128)(2,1)}, bf16[128,1152]{1,0:T(8,128)(2,1)S(1)}, u32[]{:S(2)}, u32[]{:S(2)}) collective-permute-start(bf16[128,1152]{1,0:T(8,128)(2,1)} %get-tuple-element.26), channel_id=1, source_target_pairs={{0,192},{64,0},{128,64},{192,128},{1,193},{65,1},{129,65},{193,129... | collective-permute-start | bytes 884744 | tf_op jit(solution)/shard_map/ppermute | solution.py:39
  18.3 10.5 %all-to-all-start = ((s32[16,1,128]{2,1,0:T(1,128)}), s32[16,1,128]{2,1,0:T(1,128)S(1)}, u32[]{:S(2)}, u32[]{:S(2)}) async-start(s32[16,1,128]{2,1,0:T(1,128)} %broadcast_in_dim.53), calls=%async_computation | async-start | bytes 16384 | tf_op jit(solution)/shard_map/all_to_all | solution.py:325
  23.4 1.5 copy-start.6
  28.7 24.9 %collective-permute-start.3 = (bf16[512,1152]{1,0:T(8,128)(2,1)}, bf16[512,1152]{1,0:T(8,128)(2,1)S(1)}, u32[]{:S(2)}, u32[]{:S(2)}) collective-permute-start(bf16[512,1152]{1,0:T(8,128)(2,1)} %bitcast.62), channel_id=1, source_target_pairs={{0,192},{64,0},{128,64},{192,128},{1,193},{65,1},{129,65},{193,129... | collective-permute-start | bytes 3538952 | tf_op jit(solution)/shard_map/ppermute | solution.py:39
  30.3 26.4 %collective-permute-start.2 = (bf16[512,1152]{1,0:T(8,128)(2,1)}, bf16[512,1152]{1,0:T(8,128)(2,1)}, u32[]{:S(2)}, u32[]{:S(2)}) collective-permute-start(bf16[512,1152]{1,0:T(8,128)(2,1)} %bitcast.63), channel_id=1, source_target_pairs={{0,64},{64,128},{128,192},{192,0},{1,65},{65,129},{129,193},{193,1... | collective-permute-start | bytes 3538952 | tf_op jit(solution)/shard_map/ppermute | solution.py:39
  30.9 49.0 %copy-start.1 = (bf16[384,1152]{1,0:T(8,128)(2,1)}, bf16[384,1152]{1,0:T(8,128)(2,1)S(1)}, u32[]{:S(2)}) copy-start(bf16[384,1152]{1,0:T(8,128)(2,1)S(1)} %shard_map.66.refs_5_) | copy-start | bytes 2654212
  30.9 29.8 %collective-permute-start.8 = (bf16[384,1152]{1,0:T(8,128)(2,1)S(1)}, bf16[384,1152]{1,0:T(8,128)(2,1)S(1)}, u32[]{:S(2)}, u32[]{:S(2)}) collective-permute-start(bf16[384,1152]{1,0:T(8,128)(2,1)S(1)} %shard_map.66.refs_5_), channel_id=1, source_target_pairs={{0,1},{1,2},{2,3},{3,0},{4,5},{5,6},{6,7},{7,4},{8,9},{9,10},{10,1... | collective-permute-start | bytes 2654216 | tf_op jit(solution)/shard_map/ppermute | solution.py:39
  32.2 30.9 %collective-permute-start.7 = (bf16[384,1152]{1,0:T(8,128)(2,1)S(1)}, bf16[384,1152]{1,0:T(8,128)(2,1)}, u32[]{:S(2)}, u32[]{:S(2)}) collective-permute-start(bf16[384,1152]{1,0:T(8,128)(2,1)S(1)} %shard_map.66.refs_5_), channel_id=1, source_target_pairs={{0,3},{1,0},{2,1},{3,2},{4,7},{5,4},{6,5},{7,6},{8,11},{9,8},{10,9... | collective-permute-start | bytes 2654216 | tf_op jit(solution)/shard_map/ppermute | solution.py:39
  44.7 0.6 copy-start.3
  53.6 26.2 %copy-start.7 = (bf16[512,1152]{1,0:T(8,128)(2,1)}, bf16[512,1152]{1,0:T(8,128)(2,1)S(1)}, u32[]{:S(2)}) copy-start(bf16[512,1152]{1,0:T(8,128)(2,1)S(1)} %collective-permute-done.3.refs_1_) | copy-start | bytes 3538948
  57.9 15.7 %collective-permute-start.4 = (bf16[256,1152]{1,0:T(8,128)(2,1)S(1)}, bf16[256,1152]{1,0:T(8,128)(2,1)S(1)}, u32[]{:S(2)}, u32[]{:S(2)}) collective-permute-start(bf16[256,1152]{1,0:T(8,128)(2,1)S(1)} %slice.16), channel_id=1, source_target_pairs={{0,64},{64,128},{128,192},{192,0},{1,65},{65,129},{129,193},{193,1... | collective-permute-start | bytes 1769480 | tf_op jit(solution)/shard_map/ppermute | solution.py:39
  58.0 16.4 %collective-permute-start.5 = (bf16[256,1152]{1,0:T(8,128)(2,1)S(1)}, bf16[256,1152]{1,0:T(8,128)(2,1)}, u32[]{:S(2)}, u32[]{:S(2)}) collective-permute-start(bf16[256,1152]{1,0:T(8,128)(2,1)S(1)} %slice.17), channel_id=1, source_target_pairs={{0,192},{64,0},{128,64},{192,128},{1,193},{65,1},{129,65},{193,129... | collective-permute-start | bytes 1769480 | tf_op jit(solution)/shard_map/ppermute | solution.py:39
  60.7 19.2 %copy-start.8 = (bf16[384,1152]{1,0:T(8,128)(2,1)}, bf16[384,1152]{1,0:T(8,128)(2,1)S(1)}, u32[]{:S(2)}) copy-start(bf16[384,1152]{1,0:T(8,128)(2,1)S(1)} %collective-permute-done.8.refs_9_) | copy-start | bytes 2654212
  60.7 11.9 %collective-permute-start.9 = (bf16[192,1152]{1,0:T(8,128)(2,1)S(1)}, bf16[192,1152]{1,0:T(8,128)(2,1)S(1)}, u32[]{:S(2)}, u32[]{:S(2)}) collective-permute-start(bf16[192,1152]{1,0:T(8,128)(2,1)S(1)} %slice.23), channel_id=1, source_target_pairs={{0,1},{1,2},{2,3},{3,0},{4,5},{5,6},{6,7},{7,4},{8,9},{9,10},{10,1... | collective-permute-start | bytes 1327112 | tf_op jit(solution)/shard_map/ppermute | solution.py:39
  64.1 9.5 %collective-permute-start.10 = (bf16[192,1152]{1,0:T(8,128)(2,1)S(1)}, bf16[192,1152]{1,0:T(8,128)(2,1)S(1)}, u32[]{:S(2)}, u32[]{:S(2)}) collective-permute-start(bf16[192,1152]{1,0:T(8,128)(2,1)S(1)} %slice.24), channel_id=1, source_target_pairs={{0,3},{1,0},{2,1},{3,2},{4,7},{5,4},{6,5},{7,6},{8,11},{9,8},{10,9... | collective-permute-start | bytes 1327112 | tf_op jit(solution)/shard_map/ppermute | solution.py:39
  72.6 1.0 copy-start.10
  73.6 0.8 copy-start.11
  74.4 5.4 %copy-start.9 = (bf16[256,1152]{1,0:T(8,128)(2,1)}, bf16[256,1152]{1,0:T(8,128)(2,1)S(1)}, u32[]{:S(2)}) copy-start(bf16[256,1152]{1,0:T(8,128)(2,1)S(1)} %collective-permute-done.4.refs_2_) | copy-start | bytes 1769476
  92.8 7.0 %copy-start.2 = (bf16[256,1280]{1,0:T(8,128)(2,1)S(1)}, bf16[256,1280]{1,0:T(8,128)(2,1)}, u32[]{:S(2)}) copy-start(bf16[256,1280]{1,0:T(8,128)(2,1)} %get-tuple-element.40.piece) | copy-start | bytes 1966084
  92.8 50.3 %copy-start.4 = (s32[640]{0:T(1024)S(1)}, s32[640]{0:T(1024)}, u32[]{:S(2)}) copy-start(s32[640]{0:T(1024)} %copy-done.3) | copy-start | bytes 7684
  92.8 24.4 %all-to-all-start.1 = ((bf16[16,272,128]{2,1,0:T(8,128)(2,1)}), bf16[16,272,128]{2,1,0:T(8,128)(2,1)S(1)}, u32[]{:S(2)}, u32[]{:S(2)}) async-start(bf16[16,272,128]{2,1,0:T(8,128)(2,1)} %get-tuple-element.39), calls=%async_computation.1 | async-start | bytes 2228224 | tf_op jit(solution)/shard_map/all_to_all | solution.py:408
  138.5 4.5 %collective-permute-start.11 = (bf16[32,64,128]{2,1,0:T(8,128)(2,1)S(1)}, bf16[32,64,128]{2,1,0:T(8,128)(2,1)S(1)}, u32[]{:S(2)}, u32[]{:S(2)}) collective-permute-start(bf16[32,64,128]{2,1,0:T(8,128)(2,1)S(1)} %bitcast.58), channel_id=1, source_target_pairs={{0,4},{4,0},{1,5},{5,1},{2,6},{6,2},{3,7},{7,3},{8,12},{12,8},{9,1... | collective-permute-start | bytes 1572872 | tf_op jit(solution)/shard_map/ppermute | solution.py:39
Sparse Core Ops, SparseCore 0:
  9.8 69.9 all-gather.1

commit v12 on v11

--- a/solution.py
+++ b/solution.py
@@ -44,29 +44,37 @@
     return (floats * lax.rsqrt(jnp.sum(floats * floats, axis=-1, keepdims=True) + epsilon)).astype(jnp.bfloat16)
 
 
-def prep_kernel(embeddings, prior, valid, piece, turn, e, p, sems):
+def prep_kernel(embeddings, prior, marks, piece_out, turn_out, e, p, valid, piece, sems, out_sems):
     first = lax.axis_index("x") * PART
-    copies = [
-        pltpu.make_async_copy(embeddings.at[pl.ds(first, PART)], e, sems.at[0]),
-        pltpu.make_async_copy(prior.at[pl.ds(first, PART)], p, sems.at[1]),
+    shared = [
+        pltpu.make_async_copy(prior.at[pl.ds(first, PART)], p, sems.at[PART]),
+        pltpu.make_async_copy(marks, valid, sems.at[PART + 1]),
     ]
-    for copy in copies:
+    blocks = [pltpu.make_async_copy(embeddings.at[first + b], e.at[b], sems.at[b]) for b in range(PART)]
+    for copy in shared + blocks:
         copy.start()
-    for copy in copies:
+    for copy in shared:
         copy.wait()
     row = lax.broadcasted_iota(jnp.int32, (FRAMES, FRAMES), 0)
     col = lax.broadcasted_iota(jnp.int32, (FRAMES, FRAMES), 1)
     pick = row == col
+    outs = []
     for b in range(PART):
-        units = normalize(e[b])
+        rows = pl.ds(b * FRAMES, FRAMES)
         real = valid[pl.ds(first + b, 1), :].astype(jnp.float32)
         column = jnp.sum(jnp.where(pick, real, 0.0), axis=1, keepdims=True)
         marked = jnp.where(column > 0.0, p[b].astype(jnp.float32), 2.0 * UNREAL).astype(jnp.bfloat16)
-        rows = pl.ds(b * FRAMES, FRAMES)
-        piece[rows, :FEAT] = units
         piece[rows, FEAT:] = marked
+        blocks[b].wait()
+        piece[rows, :FEAT] = normalize(e[b])
+        outs.append(pltpu.make_async_copy(piece.at[rows], piece_out.at[rows], out_sems.at[len(outs)]))
+        outs[-1].start()
         if b < TURN:
-            turn[rows, :] = units
+            units = piece.at[rows, pl.ds(0, FEAT)]
+            outs.append(pltpu.make_async_copy(units, turn_out.at[rows], out_sems.at[len(outs)]))
+            outs[-1].start()
+    for copy in outs:
+        copy.wait()
 
 
 def list_kernel(codes, out, late):
@@ -139,9 +147,11 @@
         copy.wait()
 
 
-def first_kernel(lst, keys, *refs):
+def first_kernel(lst_in, keys, *refs):
     queries = refs[:10]
-    send_out, w_out, q, k, acc, send, w, sems, w_sem, send_sem = refs[10:]
+    send_out, w_out, q, k, acc, send, w, lst, sems, w_sem, send_sem, lst_sem = refs[10:]
+    lst_copy = pltpu.make_async_copy(lst_in, lst, lst_sem)
+    lst_copy.start()
     half = k.shape[0] // 2
     copies = [pltpu.make_async_copy(keys.at[pl.ds(0, half)], k.at[pl.ds(0, half)], sems.at[0])]
     at = 0
@@ -156,6 +166,7 @@
     acc[...] = jnp.zeros_like(acc)
     for copy in copies:
         copy.wait()
+    lst_copy.wait()
     early_steps, steps = lst[EARLY_AT], lst[STEPS_AT]
 
     def step(i, carry):
@@ -299,12 +310,15 @@
             jax.ShapeDtypeStruct((PIECE, WIDE), jnp.bfloat16),
             jax.ShapeDtypeStruct((TURN * FRAMES, FEAT), jnp.bfloat16),
         ),
-        in_specs=[hbm, hbm, vmem],
-        out_specs=(vmem, vmem),
+        in_specs=[hbm, hbm, hbm],
+        out_specs=(far_memory, far_memory),
         scratch_shapes=[
             pltpu.VMEM((PART, FRAMES, FEAT), jnp.bfloat16),
             pltpu.VMEM((PART, FRAMES, CH), jnp.bfloat16),
-            pltpu.SemaphoreType.DMA((2,)),
+            pltpu.VMEM((ROWS, FRAMES), jnp.int32),
+            pltpu.VMEM((PIECE, WIDE), jnp.bfloat16),
+            pltpu.SemaphoreType.DMA((PART + 2,)),
+            pltpu.SemaphoreType.DMA((PART + TURN,)),
         ],
         compiler_params=limit(59),
     )(embeddings, prior_scores, frame_valid)
@@ -391,7 +405,7 @@
             jax.ShapeDtypeStruct((NY * NX, SEND, CH), jnp.bfloat16),
             jax.ShapeDtypeStruct((HELD, FRAMES, 2 * FRAMES), jnp.bfloat16),
         ),
-        in_specs=[smem] + [hbm] * 11,
+        in_specs=[hbm] * 12,
         out_specs=(far_memory, far_memory),
         scratch_shapes=[
             pltpu.VMEM((QBLOCKS * FRAMES, FEAT), jnp.bfloat16),
@@ -399,7 +413,9 @@
             pltpu.VMEM((QBLOCKS + 1, FRAMES, 2 * CH), jnp.float32),
             pltpu.VMEM((NY * NX, SEND, CH), jnp.bfloat16),
             pltpu.VMEM((SLOTS // 2, FRAMES, 2 * FRAMES), jnp.bfloat16),
+            pltpu.SMEM((LIST,), jnp.int32),
             pltpu.SemaphoreType.DMA((12,)),
+            pltpu.SemaphoreType.DMA,
             pltpu.SemaphoreType.DMA,
             pltpu.SemaphoreType.DMA,
         ],

time: 176 us -> 174 us (0.989)
  blocking collectives: 40.1 us -> 36.9 us
  starting transfers between devices: 32.3 us -> 35.1 us
  Pallas kernels: 32.8 us -> 30.6 us
    all_to_all x1, blocking collectives: 20.8 us -> 16.4 us  [body(): lax.all_to_all(masked, 'z', split_axis=0, concat_axis=0, tiled=True)]
    ppermute x12, starting transfers between devices: 21.1 us -> 23.3 us  [shift(): lax.ppermute(value, axis, [(i, (i + step) % size) for i in range(size)])]
where the time goes in v12:
time: 174 us; the launch traced here: 171 us
  waiting for transfers between devices  43.5 us (25%)
  blocking collectives  36.9 us (21%)
  starting transfers between devices  35.1 us (20%)
  Pallas kernels  30.6 us (18%)
  between operations  13.7 us (8%)
  local copies, waits for them, and re-layouts  9.45 us (5%)
  other arithmetic  2.05 us (1%)
    ppermute x12, starting transfers between devices, shift(): lax.ppermute(value, axis, [(i, (i + step) % size) for i in range(size)])  23.3 us
    all_to_all x1, blocking collectives, body(): lax.all_to_all(send, ('y', 'x'), split_axis=0, concat_axis=0, tiled=True)  20.5 us
    ppermute x12, waiting for transfers between devices, shift(): lax.ppermute(value, axis, [(i, (i + step) % size) for i in range(size)])  20.4 us
    all_to_all x1, blocking collectives, body(): lax.all_to_all(masked, 'z', split_axis=0, concat_axis=0, tiled=True)  16.4 us
    all_to_all x1, waiting for transfers between devices, body(): lax.all_to_all(send, ('y', 'x'), split_axis=0, concat_axis=0, tiled=True)  14.8 us
    pallas_call x1, Pallas kernels, body(): pl.pallas_call(first_kernel, out_shape=(jax.ShapeDtypeStruct((NY * NX, SE...  11.6 us
    pallas_call x1, Pallas kernels, body(): pl.pallas_call(list_kernel, out_shape=jax.ShapeDtypeStruct((LIST,), jnp.i...  10.7 us
    all_to_all x1, starting transfers between devices, body(): lax.all_to_all(send, ('y', 'x'), split_axis=0, concat_axis=0, tiled=True)  7.63 us
  transfers between devices with their start and end apart: 15, of which 8 were waited for; matrix products, arithmetic and copies ran while one was open for 5% of the time, Pallas kernels for 7%

profile of v12, /device:TPU:1, one launch (start us, length us, event | category | flops | bytes accessed | tf_op | source)
XLA Modules:
  0.0 171.2 jit_solution(16404022620384388309)
XLA Ops:
  6.6 2.4 %shard_map.64 = (bf16[256,1280]{1,0:T(8,128)(2,1)}, bf16[128,1152]{1,0:T(8,128)(2,1)}) custom-call(bf16[16,64,1152]{2,1,0:T(8,128)(2,1)} %embeddings.1, bf16[16,64,128]{2,1,0:T(8,128)(2,1)} %prior.1, s32[16,64]{1,0:T(8,128)} %marks.1), custom_call_target="tpu_custom_call" | custom-call | tf_op jit(solution)/shard_map/pallas_call | solution.py:307
  9.0 3.8 %collective-permute-start.6 = (bf16[128,1152]{1,0:T(8,128)(2,1)}, bf16[128,1152]{1,0:T(8,128)(2,1)S(1)}, u32[]{:S(2)}, u32[]{:S(2)}) collective-permute-start(bf16[128,1152]{1,0:T(8,128)(2,1)} %get-tuple-element.26), channel_id=1, source_target_pairs={{0,128},{64,192},{128,0},{192,64},{1,129},{65,193},{129,1},{193,65... | collective-permute-start | bytes 884744 | tf_op jit(solution)/shard_map/ppermute | solution.py:39
  12.8 0.4 collective-permute-start.1
  13.2 2.3 %collective-permute-start = (bf16[128,1152]{1,0:T(8,128)(2,1)}, bf16[128,1152]{1,0:T(8,128)(2,1)S(1)}, u32[]{:S(2)}, u32[]{:S(2)}) collective-permute-start(bf16[128,1152]{1,0:T(8,128)(2,1)} %get-tuple-element.26), channel_id=1, source_target_pairs={{0,192},{64,0},{128,64},{192,128},{1,193},{65,1},{129,65},{193,129... | collective-permute-start | bytes 884744 | tf_op jit(solution)/shard_map/ppermute | solution.py:39
  15.6 0.1 reshape.403
  15.7 0.1 reshape.402
  15.9 0.1 lt.99
  16.0 1.0 gather_fusion
  17.0 0.6 broadcast_in_dim.53
  17.6 4.1 %all-to-all-start = ((s32[16,1,128]{2,1,0:T(1,128)}), s32[16,1,128]{2,1,0:T(1,128)S(1)}, u32[]{:S(2)}, u32[]{:S(2)}) async-start(s32[16,1,128]{2,1,0:T(1,128)} %broadcast_in_dim.53), calls=%async_computation | async-start | bytes 16384 | tf_op jit(solution)/shard_map/all_to_all | solution.py:339
  21.7 0.5 fusion
  22.3 0.5 fusion.1
  22.8 1.4 copy-done.6
  24.2 1.1 slice.22
  25.3 2.7 %all-to-all-done = s32[16,1,128]{2,1,0:T(1,128)S(1)} async-done(((s32[16,1,128]{2,1,0:T(1,128)}), s32[16,1,128]{2,1,0:T(1,128)S(1)}, u32[]{:S(2)}, u32[]{:S(2)}) %all-to-all-start) | async-done | bytes 8224 | tf_op jit(solution)/shard_map/all_to_all | solution.py:339
  28.1 1.6 collective-permute-start.3
  29.8 0.1 or.31
  30.0 0.2 shard_map.66.refs_5_
  30.2 1.3 collective-permute-start.8
  31.5 1.5 collective-permute-start.7
  33.1 0.1 or.34
  33.3 10.7 %shard_map.65.lst_in.lst = s32[640]{0:T(1024)S(1)} custom-call(s32[2048]{0:T(1024)S(1)} %fusion.11.codes), custom_call_target="tpu_custom_call" | custom-call | tf_op jit(solution)/shard_map/pallas_call | solution.py:380
  44.0 0.6 copy-done.3
  44.6 8.4 %collective-permute-done.3.refs_1_ = bf16[512,1152]{1,0:T(8,128)(2,1)S(1)} collective-permute-done((bf16[512,1152]{1,0:T(8,128)(2,1)}, bf16[512,1152]{1,0:T(8,128)(2,1)S(1)}, u32[]{:S(2)}, u32[]{:S(2)}) %collective-permute-start.3) | collective-permute-done | bytes 1179680 | tf_op jit(solution)/shard_map/ppermute | solution.py:39
  53.0 3.1 %collective-permute-done.2.refs_4_ = bf16[512,1152]{1,0:T(8,128)(2,1)} collective-permute-done((bf16[512,1152]{1,0:T(8,128)(2,1)}, bf16[512,1152]{1,0:T(8,128)(2,1)}, u32[]{:S(2)}, u32[]{:S(2)}) %collective-permute-start.2) | collective-permute-done | bytes 1179680 | tf_op jit(solution)/shard_map/ppermute | solution.py:39
  56.2 1.1 slice.16
  57.4 2.7 %collective-permute-start.5 = (bf16[256,1152]{1,0:T(8,128)(2,1)S(1)}, bf16[256,1152]{1,0:T(8,128)(2,1)}, u32[]{:S(2)}, u32[]{:S(2)}) collective-permute-start(bf16[256,1152]{1,0:T(8,128)(2,1)S(1)} %slice.17), channel_id=1, source_target_pairs={{0,192},{64,0},{128,64},{192,128},{1,193},{65,1},{129,65},{193,129... | collective-permute-start | bytes 1769480 | tf_op jit(solution)/shard_map/ppermute | solution.py:39
  60.1 2.2 %collective-permute-start.9 = (bf16[192,1152]{1,0:T(8,128)(2,1)S(1)}, bf16[192,1152]{1,0:T(8,128)(2,1)S(1)}, u32[]{:S(2)}, u32[]{:S(2)}) collective-permute-start(bf16[192,1152]{1,0:T(8,128)(2,1)S(1)} %slice.23), channel_id=1, source_target_pairs={{0,1},{1,2},{2,3},{3,0},{4,5},{5,6},{6,7},{7,4},{8,9},{9,10},{10,1... | collective-permute-start | bytes 1327112 | tf_op jit(solution)/shard_map/ppermute | solution.py:39
  62.4 1.1 slice.24
  63.4 2.3 %collective-permute-start.10 = (bf16[192,1152]{1,0:T(8,128)(2,1)S(1)}, bf16[192,1152]{1,0:T(8,128)(2,1)S(1)}, u32[]{:S(2)}, u32[]{:S(2)}) collective-permute-start(bf16[192,1152]{1,0:T(8,128)(2,1)S(1)} %slice.24), channel_id=1, source_target_pairs={{0,3},{1,0},{2,1},{3,2},{4,7},{5,4},{6,5},{7,6},{8,11},{9,8},{10,9... | collective-permute-start | bytes 1327112 | tf_op jit(solution)/shard_map/ppermute | solution.py:39
  65.7 6.4 %collective-permute-done.9.refs_7_ = bf16[192,1152]{1,0:T(8,128)(2,1)S(1)} collective-permute-done((bf16[192,1152]{1,0:T(8,128)(2,1)S(1)}, bf16[192,1152]{1,0:T(8,128)(2,1)S(1)}, u32[]{:S(2)}, u32[]{:S(2)}) %collective-permute-start.9) | collective-permute-done | bytes 442400 | tf_op jit(solution)/shard_map/ppermute | solution.py:39
  72.1 0.9 collective-permute-done.10.refs_8_
  72.9 0.8 copy-done.11
  73.7 5.5 %all-gather.2.cloned.1.call-done.keys = bf16[4096,1280]{1,0:T(8,128)(2,1)} async-done(((bf16[256,1280]{1,0:T(8,128)(2,1)}), bf16[4096,1280]{1,0:T(8,128)(2,1)}) %all-gather.2.cloned.1.call-update) | async-done | bytes 10485776 | tf_op jit(solution)/shard_map/all_gather | solution.py:326
  79.3 11.6 %shard_map.67 = (bf16[16,272,128]{2,1,0:T(8,128)(2,1)}, bf16[4608,64,128]{2,1,0:T(8,128)(2,1)}) custom-call(s32[640]{0:T(1024)} %copy-done.3, bf16[4096,1280]{1,0:T(8,128)(2,1)} %all-gather.2.cloned.1.call-done.keys, bf16[1024,1152]{1,0:T(8,128)(2,1)} %bitcast.61, bf16[512,1152]{1,0:T(8,128)(2,1)} %copy-done.7, bf16[256,1152]{1,0:T(8,128)(2,1)} %copy-done.9, ...), custom_call_target="tpu_custom_call" | custom-call | tf_op jit(solution)/shard_map/pallas_call | solution.py:402
  90.9 7.6 %all-to-all-start.1 = ((bf16[16,272,128]{2,1,0:T(8,128)(2,1)}), bf16[16,272,128]{2,1,0:T(8,128)(2,1)S(1)}, u32[]{:S(2)}, u32[]{:S(2)}) async-start(bf16[16,272,128]{2,1,0:T(8,128)(2,1)} %get-tuple-element.39), calls=%async_computation.1 | async-start | bytes 2228224 | tf_op jit(solution)/shard_map/all_to_all | solution.py:424
  98.6 0.9 shard_map.68
  99.5 0.7 dynamic-slice_convert_fusion
  100.2 0.8 constant_dynamic-slice_fusion.prior
  101.1 14.8 %all-to-all-done.1.got = bf16[16,272,128]{2,1,0:T(8,128)(2,1)S(1)} async-done(((bf16[16,272,128]{2,1,0:T(8,128)(2,1)}), bf16[16,272,128]{2,1,0:T(8,128)(2,1)S(1)}, u32[]{:S(2)}, u32[]{:S(2)}) %all-to-all-start.1) | async-done | bytes 1114144 | tf_op jit(solution)/shard_map/all_to_all | solution.py:424
  115.9 0.1 broadcast_in_dim.56.marks
  116.0 0.4 shard_map.69
  116.4 16.4 %all_to_all.24 = bf16[8,4,64,128]{3,2,1,0:T(8,128)(2,1)S(1)} all-to-all(bf16[8,4,64,128]{3,2,1,0:T(8,128)(2,1)S(1)} %get-tuple-element.44), channel_id=1, replica_groups=mesh['y'=4,'z'=8,'c'=2,'x'=4] {'z'}, dimensions={0} | all-to-all | bytes 1048576 | tf_op jit(solution)/shard_map/all_to_all | solution.py:437
  132.7 5.2 %collective-permute-start.11 = (bf16[32,64,128]{2,1,0:T(8,128)(2,1)S(1)}, bf16[32,64,128]{2,1,0:T(8,128)(2,1)S(1)}, u32[]{:S(2)}, u32[]{:S(2)}) collective-permute-start(bf16[32,64,128]{2,1,0:T(8,128)(2,1)S(1)} %bitcast.58), channel_id=1, source_target_pairs={{0,4},{4,0},{1,5},{5,1},{2,6},{6,2},{3,7},{7,3},{8,12},{12,8},{9,1... | collective-permute-start | bytes 1572872 | tf_op jit(solution)/shard_map/ppermute | solution.py:39
  137.9 1.5 collective-permute-done.11.far
  139.4 3.6 %shard_map.70 = bf16[64,64,128]{2,1,0:T(8,128)(2,1)S(1)} custom-call(s32[640]{0:T(1024)S(1)} %copy-done.4, bf16[4608,64,128]{2,1,0:T(8,128)(2,1)} %get-tuple-element.38.w_in, bf16[32,64,128]{2,1,0:T(8,128)(2,1)S(1)} %bitcast.59, bf16[32,64,128]{2,1,0:T(8,128)(2,1)S(1)} %collective-permute-done.11.far), custom_call_target="tpu_custom_call" | custom-call | tf_op jit(solution)/shard_map/pallas_call | solution.py:441
  143.0 20.5 %all_to_all.25 = bf16[64,64,128]{2,1,0:T(8,128)(2,1)S(1)} all-to-all(bf16[64,64,128]{2,1,0:T(8,128)(2,1)S(1)} %shard_map.70), channel_id=1, replica_groups=mesh['y'=4,'z'=8,'c'=2,'x'=4] {'y','x'}, dimensions={0} | all-to-all | bytes 2097152 | tf_op jit(solution)/shard_map/all_to_all | solution.py:453
  163.6 0.8 shard_map.71
  (56 shorter events, 0.9 us)
Async XLA Ops:
  6.5 9.4 %copy-start = (s32[1024]{0:T(1024)S(1)}, s32[1024]{0:T(1024)}, u32[]{:S(2)}) copy-start(s32[1024]{0:T(1024)} %param.11) | copy-start | bytes 12292
  6.5 15.2 %copy-start.5 = (bf16[16,64,1152]{2,1,0:T(8,128)(2,1)S(1)}, bf16[16,64,1152]{2,1,0:T(8,128)(2,1)}, u32[]{:S(2)}) copy-start(bf16[16,64,1152]{2,1,0:T(8,128)(2,1)} %embeddings.1) | copy-start | bytes 7077892
  6.5 9.0 %copy-start.12 = (s32[16,8]{0,1:T(8,128)S(1)}, s32[16,8]{0,1:T(8,128)}, u32[]{:S(2)}) copy-start(s32[16,8]{0,1:T(8,128)} %param.9) | copy-start | bytes 1540
  6.5 9.2 %copy-start.13 = (s32[16]{0:T(128)S(1)}, s32[16]{0:T(128)}, u32[]{:S(2)}) copy-start(s32[16]{0:T(128)} %param.10) | copy-start | bytes 196
  6.5 72.7 %all-gather.2.cloned.1.call-start = ((), (), s32[]{:S(2)}) async-start(), calls=%async_computation.4 | async-start | bytes 11141120 | tf_op jit(solution)/shard_map/all_gather | solution.py:326
  9.0 21.0 %collective-permute-start.6 = (bf16[128,1152]{1,0:T(8,128)(2,1)}, bf16[128,1152]{1,0:T(8,128)(2,1)S(1)}, u32[]{:S(2)}, u32[]{:S(2)}) collective-permute-start(bf16[128,1152]{1,0:T(8,128)(2,1)} %get-tuple-element.26), channel_id=1, source_target_pairs={{0,128},{64,192},{128,0},{192,64},{1,129},{65,193},{129,1},{193,65... | collective-permute-start | bytes 884744 | tf_op jit(solution)/shard_map/ppermute | solution.py:39
  12.8 15.2 %collective-permute-start.1 = (bf16[128,1152]{1,0:T(8,128)(2,1)}, bf16[128,1152]{1,0:T(8,128)(2,1)S(1)}, u32[]{:S(2)}, u32[]{:S(2)}) collective-permute-start(bf16[128,1152]{1,0:T(8,128)(2,1)} %get-tuple-element.26), channel_id=1, source_target_pairs={{0,64},{64,128},{128,192},{192,0},{1,65},{65,129},{129,193},{193,1... | collective-permute-start | bytes 884744 | tf_op jit(solution)/shard_map/ppermute | solution.py:39
  13.2 14.8 %collective-permute-start = (bf16[128,1152]{1,0:T(8,128)(2,1)}, bf16[128,1152]{1,0:T(8,128)(2,1)S(1)}, u32[]{:S(2)}, u32[]{:S(2)}) collective-permute-start(bf16[128,1152]{1,0:T(8,128)(2,1)} %get-tuple-element.26), channel_id=1, source_target_pairs={{0,192},{64,0},{128,64},{192,128},{1,193},{65,1},{129,65},{193,129... | collective-permute-start | bytes 884744 | tf_op jit(solution)/shard_map/ppermute | solution.py:39
  17.6 10.5 %all-to-all-start = ((s32[16,1,128]{2,1,0:T(1,128)}), s32[16,1,128]{2,1,0:T(1,128)S(1)}, u32[]{:S(2)}, u32[]{:S(2)}) async-start(s32[16,1,128]{2,1,0:T(1,128)} %broadcast_in_dim.53), calls=%async_computation | async-start | bytes 16384 | tf_op jit(solution)/shard_map/all_to_all | solution.py:339
  22.7 1.5 copy-start.6
  28.1 24.9 %collective-permute-start.3 = (bf16[512,1152]{1,0:T(8,128)(2,1)}, bf16[512,1152]{1,0:T(8,128)(2,1)S(1)}, u32[]{:S(2)}, u32[]{:S(2)}) collective-permute-start(bf16[512,1152]{1,0:T(8,128)(2,1)} %bitcast.62), channel_id=1, source_target_pairs={{0,192},{64,0},{128,64},{192,128},{1,193},{65,1},{129,65},{193,129... | collective-permute-start | bytes 3538952 | tf_op jit(solution)/shard_map/ppermute | solution.py:39
  29.7 26.5 %collective-permute-start.2 = (bf16[512,1152]{1,0:T(8,128)(2,1)}, bf16[512,1152]{1,0:T(8,128)(2,1)}, u32[]{:S(2)}, u32[]{:S(2)}) collective-permute-start(bf16[512,1152]{1,0:T(8,128)(2,1)} %bitcast.63), channel_id=1, source_target_pairs={{0,64},{64,128},{128,192},{192,0},{1,65},{65,129},{129,193},{193,1... | collective-permute-start | bytes 3538952 | tf_op jit(solution)/shard_map/ppermute | solution.py:39
  30.2 49.1 %copy-start.1 = (bf16[384,1152]{1,0:T(8,128)(2,1)}, bf16[384,1152]{1,0:T(8,128)(2,1)S(1)}, u32[]{:S(2)}) copy-start(bf16[384,1152]{1,0:T(8,128)(2,1)S(1)} %shard_map.66.refs_5_) | copy-start | bytes 2654212
  30.2 29.9 %collective-permute-start.8 = (bf16[384,1152]{1,0:T(8,128)(2,1)S(1)}, bf16[384,1152]{1,0:T(8,128)(2,1)S(1)}, u32[]{:S(2)}, u32[]{:S(2)}) collective-permute-start(bf16[384,1152]{1,0:T(8,128)(2,1)S(1)} %shard_map.66.refs_5_), channel_id=1, source_target_pairs={{0,1},{1,2},{2,3},{3,0},{4,5},{5,6},{6,7},{7,4},{8,9},{9,10},{10,1... | collective-permute-start | bytes 2654216 | tf_op jit(solution)/shard_map/ppermute | solution.py:39
  31.5 30.9 %collective-permute-start.7 = (bf16[384,1152]{1,0:T(8,128)(2,1)S(1)}, bf16[384,1152]{1,0:T(8,128)(2,1)}, u32[]{:S(2)}, u32[]{:S(2)}) collective-permute-start(bf16[384,1152]{1,0:T(8,128)(2,1)S(1)} %shard_map.66.refs_5_), channel_id=1, source_target_pairs={{0,3},{1,0},{2,1},{3,2},{4,7},{5,4},{6,5},{7,6},{8,11},{9,8},{10,9... | collective-permute-start | bytes 2654216 | tf_op jit(solution)/shard_map/ppermute | solution.py:39
  44.0 0.6 copy-start.3
  53.0 26.2 %copy-start.7 = (bf16[512,1152]{1,0:T(8,128)(2,1)}, bf16[512,1152]{1,0:T(8,128)(2,1)S(1)}, u32[]{:S(2)}) copy-start(bf16[512,1152]{1,0:T(8,128)(2,1)S(1)} %collective-permute-done.3.refs_1_) | copy-start | bytes 3538948
  57.3 15.6 %collective-permute-start.4 = (bf16[256,1152]{1,0:T(8,128)(2,1)S(1)}, bf16[256,1152]{1,0:T(8,128)(2,1)S(1)}, u32[]{:S(2)}, u32[]{:S(2)}) collective-permute-start(bf16[256,1152]{1,0:T(8,128)(2,1)S(1)} %slice.16), channel_id=1, source_target_pairs={{0,64},{64,128},{128,192},{192,0},{1,65},{65,129},{129,193},{193,1... | collective-permute-start | bytes 1769480 | tf_op jit(solution)/shard_map/ppermute | solution.py:39
  57.4 16.3 %collective-permute-start.5 = (bf16[256,1152]{1,0:T(8,128)(2,1)S(1)}, bf16[256,1152]{1,0:T(8,128)(2,1)}, u32[]{:S(2)}, u32[]{:S(2)}) collective-permute-start(bf16[256,1152]{1,0:T(8,128)(2,1)S(1)} %slice.17), channel_id=1, source_target_pairs={{0,192},{64,0},{128,64},{192,128},{1,193},{65,1},{129,65},{193,129... | collective-permute-start | bytes 1769480 | tf_op jit(solution)/shard_map/ppermute | solution.py:39
  60.1 19.2 %copy-start.8 = (bf16[384,1152]{1,0:T(8,128)(2,1)}, bf16[384,1152]{1,0:T(8,128)(2,1)S(1)}, u32[]{:S(2)}) copy-start(bf16[384,1152]{1,0:T(8,128)(2,1)S(1)} %collective-permute-done.8.refs_9_) | copy-start | bytes 2654212
  60.1 12.0 %collective-permute-start.9 = (bf16[192,1152]{1,0:T(8,128)(2,1)S(1)}, bf16[192,1152]{1,0:T(8,128)(2,1)S(1)}, u32[]{:S(2)}, u32[]{:S(2)}) collective-permute-start(bf16[192,1152]{1,0:T(8,128)(2,1)S(1)} %slice.23), channel_id=1, source_target_pairs={{0,1},{1,2},{2,3},{3,0},{4,5},{5,6},{6,7},{7,4},{8,9},{9,10},{10,1... | collective-permute-start | bytes 1327112 | tf_op jit(solution)/shard_map/ppermute | solution.py:39
  63.4 9.5 %collective-permute-start.10 = (bf16[192,1152]{1,0:T(8,128)(2,1)S(1)}, bf16[192,1152]{1,0:T(8,128)(2,1)S(1)}, u32[]{:S(2)}, u32[]{:S(2)}) collective-permute-start(bf16[192,1152]{1,0:T(8,128)(2,1)S(1)} %slice.24), channel_id=1, source_target_pairs={{0,3},{1,0},{2,1},{3,2},{4,7},{5,4},{6,5},{7,6},{8,11},{9,8},{10,9... | collective-permute-start | bytes 1327112 | tf_op jit(solution)/shard_map/ppermute | solution.py:39
  72.1 0.9 copy-start.10
  72.9 0.8 copy-start.11
  73.7 5.5 %copy-start.9 = (bf16[256,1152]{1,0:T(8,128)(2,1)}, bf16[256,1152]{1,0:T(8,128)(2,1)S(1)}, u32[]{:S(2)}) copy-start(bf16[256,1152]{1,0:T(8,128)(2,1)S(1)} %collective-permute-done.4.refs_2_) | copy-start | bytes 1769476
  90.9 7.7 %copy-start.2 = (bf16[256,1280]{1,0:T(8,128)(2,1)S(1)}, bf16[256,1280]{1,0:T(8,128)(2,1)}, u32[]{:S(2)}) copy-start(bf16[256,1280]{1,0:T(8,128)(2,1)} %get-tuple-element.40.piece) | copy-start | bytes 1966084
  90.9 48.5 %copy-start.4 = (s32[640]{0:T(1024)S(1)}, s32[640]{0:T(1024)}, u32[]{:S(2)}) copy-start(s32[640]{0:T(1024)} %copy-done.3) | copy-start | bytes 7684
  90.9 25.0 %all-to-all-start.1 = ((bf16[16,272,128]{2,1,0:T(8,128)(2,1)}), bf16[16,272,128]{2,1,0:T(8,128)(2,1)S(1)}, u32[]{:S(2)}, u32[]{:S(2)}) async-start(bf16[16,272,128]{2,1,0:T(8,128)(2,1)} %get-tuple-element.39), calls=%async_computation.1 | async-start | bytes 2228224 | tf_op jit(solution)/shard_map/all_to_all | solution.py:424
  132.7 6.7 %collective-permute-start.11 = (bf16[32,64,128]{2,1,0:T(8,128)(2,1)S(1)}, bf16[32,64,128]{2,1,0:T(8,128)(2,1)S(1)}, u32[]{:S(2)}, u32[]{:S(2)}) collective-permute-start(bf16[32,64,128]{2,1,0:T(8,128)(2,1)S(1)} %bitcast.58), channel_id=1, source_target_pairs={{0,4},{4,0},{1,5},{5,1},{2,6},{6,2},{3,7},{7,3},{8,12},{12,8},{9,1... | collective-permute-start | bytes 1572872 | tf_op jit(solution)/shard_map/ppermute | solution.py:39
Sparse Core Ops, SparseCore 0:
  9.2 69.9 all-gather.1

commit v13 on v12

--- a/solution.py
+++ b/solution.py
@@ -28,7 +28,7 @@
 PIECE = PART * FRAMES
 SEND = PIECE + 16
 LIST = 640
-EARLY_AT, STEPS_AT = 600, 601
+FIRST_AT, SECOND_AT, STEPS_AT = 600, 601, 602
 SPARE = QBLOCKS
 UNREAL = 1024.0
 sharpness = 2.0 * math.sqrt(FEAT)
@@ -77,35 +77,37 @@
         copy.wait()
 
 
-def list_kernel(codes, out, late):
-    def eight(i, counts):
-        early_count, late_count = counts
+def list_kernel(codes, out, found):
+    def eight(i, count):
         for u in range(8):
             code = codes[i * 8 + u]
-            out[early_count] = code
-            late[late_count] = code
-            is_late = (code >> 12) & 1
-            real = jnp.where(code >= 0, 1, 0)
-            early_count = early_count + (real & (1 - is_late))
-            late_count = late_count + (real & is_late)
-        return early_count, late_count
-
-    early_count, late_count = lax.fori_loop(0, QBLOCKS * 32 // 8, eight, (0, 0))
+            found[count] = code
+            count = count + jnp.where(code >= 0, 1, 0)
+        return count
+
+    count = lax.fori_loop(0, QBLOCKS * 32 // 8, eight, 0)
+
+    def kind_of(code):
+        return ((code >> 12) & 1) + jnp.where(((code >> 13) & 63) >= Q_TURN, 2, 0)
+
+    def tally(i, counts):
+        kind = kind_of(found[i])
+        return tuple(n + jnp.where(kind == j, 1, 0) for j, n in enumerate(counts))
+
+    one, two, three = lax.fori_loop(0, count, tally, (0, 0, 0))
+
+    def place(i, at):
+        code = found[i]
+        kind = kind_of(code)
+        out[jnp.where(kind < 2, jnp.where(kind == 0, at[0], at[1]), jnp.where(kind == 2, at[2], at[3]))] = code
+        return tuple(n + jnp.where(kind == j, 1, 0) for j, n in enumerate(at))
+
+    lax.fori_loop(0, count, place, (0, one, one + two, one + two + three))
     for u in range(UNROLL):
-        out[early_count + u] = SPARE
-        late[late_count + u] = SPARE
-    early_steps = (early_count + UNROLL - 1) // UNROLL
-    late_steps = (late_count + UNROLL - 1) // UNROLL
-    start = early_steps * UNROLL
-
-    def copy(i, carry):
-        for u in range(UNROLL):
-            out[start + i * UNROLL + u] = late[i * UNROLL + u]
-        return carry
-
-    lax.fori_loop(0, late_steps, copy, 0)
-    out[EARLY_AT] = early_steps
-    out[STEPS_AT] = early_steps + late_steps
+        out[count + u] = SPARE
+    out[FIRST_AT] = one // UNROLL
+    out[SECOND_AT] = (one + two) // UNROLL
+    out[STEPS_AT] = (count + UNROLL - 1) // UNROLL
 
 
 def own_kernel(piece, own_weights, own_base):
@@ -153,21 +155,24 @@
     lst_copy = pltpu.make_async_copy(lst_in, lst, lst_sem)
     lst_copy.start()
     half = k.shape[0] // 2
-    copies = [pltpu.make_async_copy(keys.at[pl.ds(0, half)], k.at[pl.ds(0, half)], sems.at[0])]
+    q_copies = []
     at = 0
     for part in queries:
         rows = part.shape[0]
-        copies.append(pltpu.make_async_copy(part, q.at[pl.ds(at, rows)], sems.at[len(copies)]))
+        q_copies.append(pltpu.make_async_copy(part, q.at[pl.ds(at, rows)], sems.at[len(q_copies)]))
         at += rows
-    rest = pltpu.make_async_copy(keys.at[pl.ds(half, half)], k.at[pl.ds(half, half)], sems.at[len(copies)])
-    for copy in copies:
+    k_copies = [
+        pltpu.make_async_copy(keys.at[pl.ds(i * half, half)], k.at[pl.ds(i * half, half)], sems.at[10 + i])
+        for i in range(2)
+    ]
+    straight, turned = q_copies[:5], q_copies[5:]
+    for copy in straight + k_copies + turned:
         copy.start()
-    rest.start()
     acc[...] = jnp.zeros_like(acc)
-    for copy in copies:
+    lst_copy.wait()
+    for copy in straight + k_copies[:1]:
         copy.wait()
-    lst_copy.wait()
-    early_steps, steps = lst[EARLY_AT], lst[STEPS_AT]
+    steps = lst[STEPS_AT]
 
     def step(i, carry):
         codes = [lst[i * UNROLL + u] for u in range(UNROLL)]
@@ -193,9 +198,12 @@
         pairs_copy(w, w_out, w_sem, i).start()
         return carry
 
-    lax.fori_loop(0, early_steps, step, 0)
-    rest.wait()
-    lax.fori_loop(early_steps, steps, step, 0)
+    lax.fori_loop(0, lst[FIRST_AT], step, 0)
+    k_copies[1].wait()
+    lax.fori_loop(lst[FIRST_AT], lst[SECOND_AT], step, 0)
+    for copy in turned:
+        copy.wait()
+    lax.fori_loop(lst[SECOND_AT], steps, step, 0)
     row = lax.broadcasted_iota(jnp.int32, (FRAMES, CH), 0)
     lane = lax.broadcasted_iota(jnp.int32, (FRAMES, CH), 1)
     pick = row == lane % FRAMES

time: 174 us -> 174 us (level); the launches traced: 171 us -> 173 us
  blocking collectives: 36.9 us -> 45.1 us
  starting transfers between devices: 35.1 us -> 31.6 us
  Pallas kernels: 30.6 us -> 27.6 us
    all_to_all x1, blocking collectives: 16.4 us -> 26.3 us  [body(): lax.all_to_all(masked, 'z', split_axis=0, concat_axis=0, tiled=True)]
    ppermute x12, starting transfers between devices: 23.3 us -> 20.7 us  [shift(): lax.ppermute(value, axis, [(i, (i + step) % size) for i in range(size)])]
    ppermute x12, waiting for transfers between devices: 20.4 us -> 22.5 us  [shift(): lax.ppermute(value, axis, [(i, (i + step) % size) for i in range(size)])]
    pallas_call x1, Pallas kernels: 10.7 us -> 8.54 us  [body(): pl.pallas_call(list_kernel, out_shape=jax.ShapeDtypeStruct((LIST,), jnp.i...]
    all_to_all x1, waiting for transfers between devices: 14.8 us -> 13 us  [body(): lax.all_to_all(send, ('y', 'x'), split_axis=0, concat_axis=0, tiled=True)]
  transfers between devices with their start and end apart: 15 -> 15, of which waited for: 8 -> 8; matrix products, arithmetic and copies ran while one was open for 5% -> 5% of each run, Pallas kernels for 7% -> 6%
where the time goes in v13:
time: 174 us; the launch traced here: 173 us
  blocking collectives  45.1 us (26%)
  waiting for transfers between devices  43.8 us (25%)
  starting transfers between devices  31.6 us (18%)
  Pallas kernels  27.6 us (16%)
  between operations  13.7 us (8%)
  local copies, waits for them, and re-layouts  9.45 us (5%)
  other arithmetic  2.05 us (1%)
    all_to_all x1, blocking collectives, body(): lax.all_to_all(masked, 'z', split_axis=0, concat_axis=0, tiled=True)  26.3 us
    ppermute x12, waiting for transfers between devices, shift(): lax.ppermute(value, axis, [(i, (i + step) % size) for i in range(size)])  22.5 us
    ppermute x12, starting transfers between devices, shift(): lax.ppermute(value, axis, [(i, (i + step) % size) for i in range(size)])  20.7 us
    all_to_all x1, blocking collectives, body(): lax.all_to_all(send, ('y', 'x'), split_axis=0, concat_axis=0, tiled=True)  18.8 us
    all_to_all x1, waiting for transfers between devices, body(): lax.all_to_all(send, ('y', 'x'), split_axis=0, concat_axis=0, tiled=True)  13 us
    pallas_call x1, Pallas kernels, body(): pl.pallas_call(first_kernel, out_shape=(jax.ShapeDtypeStruct((NY * NX, SE...  10.8 us
    pallas_call x1, Pallas kernels, body(): pl.pallas_call(list_kernel, out_shape=jax.ShapeDtypeStruct((LIST,), jnp.i...  8.54 us
    all_to_all x1, starting transfers between devices, body(): lax.all_to_all(send, ('y', 'x'), split_axis=0, concat_axis=0, tiled=True)  6.67 us
  transfers between devices with their start and end apart: 15, of which 8 were waited for; matrix products, arithmetic and copies ran while one was open for 5% of the time, Pallas kernels for 6%

profile of v13, /device:TPU:1, one launch (start us, length us, event | category | flops | bytes accessed | tf_op | source)
XLA Modules:
  0.0 173.3 jit_solution(13302668685995209385)
XLA Ops:
  6.6 2.4 %shard_map.64 = (bf16[256,1280]{1,0:T(8,128)(2,1)}, bf16[128,1152]{1,0:T(8,128)(2,1)}) custom-call(bf16[16,64,1152]{2,1,0:T(8,128)(2,1)} %embeddings.1, bf16[16,64,128]{2,1,0:T(8,128)(2,1)} %prior.1, s32[16,64]{1,0:T(8,128)} %marks.1), custom_call_target="tpu_custom_call" | custom-call | tf_op jit(solution)/shard_map/pallas_call | solution.py:315
  9.0 3.8 %collective-permute-start.6 = (bf16[128,1152]{1,0:T(8,128)(2,1)}, bf16[128,1152]{1,0:T(8,128)(2,1)S(1)}, u32[]{:S(2)}, u32[]{:S(2)}) collective-permute-start(bf16[128,1152]{1,0:T(8,128)(2,1)} %get-tuple-element.26), channel_id=1, source_target_pairs={{0,128},{64,192},{128,0},{192,64},{1,129},{65,193},{129,1},{193,65... | collective-permute-start | bytes 884744 | tf_op jit(solution)/shard_map/ppermute | solution.py:39
  12.8 0.4 collective-permute-start.1
  13.2 2.3 %collective-permute-start = (bf16[128,1152]{1,0:T(8,128)(2,1)}, bf16[128,1152]{1,0:T(8,128)(2,1)S(1)}, u32[]{:S(2)}, u32[]{:S(2)}) collective-permute-start(bf16[128,1152]{1,0:T(8,128)(2,1)} %get-tuple-element.26), channel_id=1, source_target_pairs={{0,192},{64,0},{128,64},{192,128},{1,193},{65,1},{129,65},{193,129... | collective-permute-start | bytes 884744 | tf_op jit(solution)/shard_map/ppermute | solution.py:39
  15.6 0.1 reshape.403
  15.7 0.1 reshape.402
  15.9 0.1 lt.99
  16.0 1.0 gather_fusion
  17.0 0.6 broadcast_in_dim.53
  17.6 4.1 %all-to-all-start = ((s32[16,1,128]{2,1,0:T(1,128)}), s32[16,1,128]{2,1,0:T(1,128)S(1)}, u32[]{:S(2)}, u32[]{:S(2)}) async-start(s32[16,1,128]{2,1,0:T(1,128)} %broadcast_in_dim.53), calls=%async_computation | async-start | bytes 16384 | tf_op jit(solution)/shard_map/all_to_all | solution.py:347
  21.7 0.5 fusion
  22.3 0.5 fusion.1
  22.8 1.4 copy-done.6
  24.2 1.1 slice.22
  25.3 2.7 %all-to-all-done = s32[16,1,128]{2,1,0:T(1,128)S(1)} async-done(((s32[16,1,128]{2,1,0:T(1,128)}), s32[16,1,128]{2,1,0:T(1,128)S(1)}, u32[]{:S(2)}, u32[]{:S(2)}) %all-to-all-start) | async-done | bytes 8224 | tf_op jit(solution)/shard_map/all_to_all | solution.py:347
  28.1 1.6 collective-permute-start.3
  29.8 0.1 or.31
  30.0 0.2 shard_map.66.refs_5_
  30.2 1.3 collective-permute-start.8
  31.5 1.5 collective-permute-start.7
  33.1 0.1 or.34
  33.3 8.5 %shard_map.65.lst_in.lst = s32[640]{0:T(1024)S(1)} custom-call(s32[2048]{0:T(1024)S(1)} %fusion.11.codes), custom_call_target="tpu_custom_call" | custom-call | tf_op jit(solution)/shard_map/pallas_call | solution.py:388
  41.9 0.6 copy-done.3
  42.4 10.6 %collective-permute-done.3.refs_1_ = bf16[512,1152]{1,0:T(8,128)(2,1)S(1)} collective-permute-done((bf16[512,1152]{1,0:T(8,128)(2,1)}, bf16[512,1152]{1,0:T(8,128)(2,1)S(1)}, u32[]{:S(2)}, u32[]{:S(2)}) %collective-permute-start.3) | collective-permute-done | bytes 1179680 | tf_op jit(solution)/shard_map/ppermute | solution.py:39
  53.0 3.1 %collective-permute-done.2.refs_4_ = bf16[512,1152]{1,0:T(8,128)(2,1)} collective-permute-done((bf16[512,1152]{1,0:T(8,128)(2,1)}, bf16[512,1152]{1,0:T(8,128)(2,1)}, u32[]{:S(2)}, u32[]{:S(2)}) %collective-permute-start.2) | collective-permute-done | bytes 1179680 | tf_op jit(solution)/shard_map/ppermute | solution.py:39
  56.2 1.1 slice.16
  57.4 2.7 %collective-permute-start.5 = (bf16[256,1152]{1,0:T(8,128)(2,1)S(1)}, bf16[256,1152]{1,0:T(8,128)(2,1)}, u32[]{:S(2)}, u32[]{:S(2)}) collective-permute-start(bf16[256,1152]{1,0:T(8,128)(2,1)S(1)} %slice.17), channel_id=1, source_target_pairs={{0,192},{64,0},{128,64},{192,128},{1,193},{65,1},{129,65},{193,129... | collective-permute-start | bytes 1769480 | tf_op jit(solution)/shard_map/ppermute | solution.py:39
  60.1 2.2 %collective-permute-start.9 = (bf16[192,1152]{1,0:T(8,128)(2,1)S(1)}, bf16[192,1152]{1,0:T(8,128)(2,1)S(1)}, u32[]{:S(2)}, u32[]{:S(2)}) collective-permute-start(bf16[192,1152]{1,0:T(8,128)(2,1)S(1)} %slice.23), channel_id=1, source_target_pairs={{0,1},{1,2},{2,3},{3,0},{4,5},{5,6},{6,7},{7,4},{8,9},{9,10},{10,1... | collective-permute-start | bytes 1327112 | tf_op jit(solution)/shard_map/ppermute | solution.py:39
  62.4 1.1 slice.24
  63.4 2.3 %collective-permute-start.10 = (bf16[192,1152]{1,0:T(8,128)(2,1)S(1)}, bf16[192,1152]{1,0:T(8,128)(2,1)S(1)}, u32[]{:S(2)}, u32[]{:S(2)}) collective-permute-start(bf16[192,1152]{1,0:T(8,128)(2,1)S(1)} %slice.24), channel_id=1, source_target_pairs={{0,3},{1,0},{2,1},{3,2},{4,7},{5,4},{6,5},{7,6},{8,11},{9,8},{10,9... | collective-permute-start | bytes 1327112 | tf_op jit(solution)/shard_map/ppermute | solution.py:39
  65.7 6.4 %collective-permute-done.9.refs_7_ = bf16[192,1152]{1,0:T(8,128)(2,1)S(1)} collective-permute-done((bf16[192,1152]{1,0:T(8,128)(2,1)S(1)}, bf16[192,1152]{1,0:T(8,128)(2,1)S(1)}, u32[]{:S(2)}, u32[]{:S(2)}) %collective-permute-start.9) | collective-permute-done | bytes 442400 | tf_op jit(solution)/shard_map/ppermute | solution.py:39
  72.1 0.9 collective-permute-done.10.refs_8_
  72.9 0.8 copy-done.11
  73.7 5.5 %all-gather.2.cloned.1.call-done.keys = bf16[4096,1280]{1,0:T(8,128)(2,1)} async-done(((bf16[256,1280]{1,0:T(8,128)(2,1)}), bf16[4096,1280]{1,0:T(8,128)(2,1)}) %all-gather.2.cloned.1.call-update) | async-done | bytes 10485776 | tf_op jit(solution)/shard_map/all_gather | solution.py:334
  79.3 10.8 %shard_map.67 = (bf16[16,272,128]{2,1,0:T(8,128)(2,1)}, bf16[4608,64,128]{2,1,0:T(8,128)(2,1)}) custom-call(s32[640]{0:T(1024)} %copy-done.3, bf16[4096,1280]{1,0:T(8,128)(2,1)} %all-gather.2.cloned.1.call-done.keys, bf16[1024,1152]{1,0:T(8,128)(2,1)} %bitcast.61, bf16[512,1152]{1,0:T(8,128)(2,1)} %copy-done.7, bf16[256,1152]{1,0:T(8,128)(2,1)} %copy-done.9, ...), custom_call_target="tpu_custom_call" | custom-call | tf_op jit(solution)/shard_map/pallas_call | solution.py:410
  90.1 6.7 %all-to-all-start.1 = ((bf16[16,272,128]{2,1,0:T(8,128)(2,1)}), bf16[16,272,128]{2,1,0:T(8,128)(2,1)S(1)}, u32[]{:S(2)}, u32[]{:S(2)}) async-start(bf16[16,272,128]{2,1,0:T(8,128)(2,1)} %get-tuple-element.39), calls=%async_computation.1 | async-start | bytes 2228224 | tf_op jit(solution)/shard_map/all_to_all | solution.py:432
  96.8 0.9 shard_map.68
  97.7 0.7 dynamic-slice_convert_fusion
  98.4 0.8 constant_dynamic-slice_fusion.prior
  99.3 13.0 %all-to-all-done.1.got = bf16[16,272,128]{2,1,0:T(8,128)(2,1)S(1)} async-done(((bf16[16,272,128]{2,1,0:T(8,128)(2,1)}), bf16[16,272,128]{2,1,0:T(8,128)(2,1)S(1)}, u32[]{:S(2)}, u32[]{:S(2)}) %all-to-all-start.1) | async-done | bytes 1114144 | tf_op jit(solution)/shard_map/all_to_all | solution.py:432
  112.3 0.1 broadcast_in_dim.56.marks
  112.4 0.4 shard_map.69
  112.8 26.3 %all_to_all.24 = bf16[8,4,64,128]{3,2,1,0:T(8,128)(2,1)S(1)} all-to-all(bf16[8,4,64,128]{3,2,1,0:T(8,128)(2,1)S(1)} %get-tuple-element.44), channel_id=1, replica_groups=mesh['y'=4,'z'=8,'c'=2,'x'=4] {'z'}, dimensions={0} | all-to-all | bytes 1048576 | tf_op jit(solution)/shard_map/all_to_all | solution.py:445
  139.1 2.6 %collective-permute-start.11 = (bf16[32,64,128]{2,1,0:T(8,128)(2,1)S(1)}, bf16[32,64,128]{2,1,0:T(8,128)(2,1)S(1)}, u32[]{:S(2)}, u32[]{:S(2)}) collective-permute-start(bf16[32,64,128]{2,1,0:T(8,128)(2,1)S(1)} %bitcast.58), channel_id=1, source_target_pairs={{0,4},{4,0},{1,5},{5,1},{2,6},{6,2},{3,7},{7,3},{8,12},{12,8},{9,1... | collective-permute-start | bytes 1572872 | tf_op jit(solution)/shard_map/ppermute | solution.py:39
  141.7 1.5 collective-permute-done.11.far
  143.2 3.6 %shard_map.70 = bf16[64,64,128]{2,1,0:T(8,128)(2,1)S(1)} custom-call(s32[640]{0:T(1024)S(1)} %copy-done.4, bf16[4608,64,128]{2,1,0:T(8,128)(2,1)} %get-tuple-element.38.w_in, bf16[32,64,128]{2,1,0:T(8,128)(2,1)S(1)} %bitcast.59, bf16[32,64,128]{2,1,0:T(8,128)(2,1)S(1)} %collective-permute-done.11.far), custom_call_target="tpu_custom_call" | custom-call | tf_op jit(solution)/shard_map/pallas_call | solution.py:449
  146.8 18.8 %all_to_all.25 = bf16[64,64,128]{2,1,0:T(8,128)(2,1)S(1)} all-to-all(bf16[64,64,128]{2,1,0:T(8,128)(2,1)S(1)} %shard_map.70), channel_id=1, replica_groups=mesh['y'=4,'z'=8,'c'=2,'x'=4] {'y','x'}, dimensions={0} | all-to-all | bytes 2097152 | tf_op jit(solution)/shard_map/all_to_all | solution.py:461
  165.6 0.8 shard_map.71
  (56 shorter events, 0.9 us)
Async XLA Ops:
  6.5 9.4 %copy-start = (s32[1024]{0:T(1024)S(1)}, s32[1024]{0:T(1024)}, u32[]{:S(2)}) copy-start(s32[1024]{0:T(1024)} %param.11) | copy-start | bytes 12292
  6.5 15.2 %copy-start.5 = (bf16[16,64,1152]{2,1,0:T(8,128)(2,1)S(1)}, bf16[16,64,1152]{2,1,0:T(8,128)(2,1)}, u32[]{:S(2)}) copy-start(bf16[16,64,1152]{2,1,0:T(8,128)(2,1)} %embeddings.1) | copy-start | bytes 7077892
  6.5 9.0 %copy-start.12 = (s32[16,8]{0,1:T(8,128)S(1)}, s32[16,8]{0,1:T(8,128)}, u32[]{:S(2)}) copy-start(s32[16,8]{0,1:T(8,128)} %param.9) | copy-start | bytes 1540
  6.5 9.2 %copy-start.13 = (s32[16]{0:T(128)S(1)}, s32[16]{0:T(128)}, u32[]{:S(2)}) copy-start(s32[16]{0:T(128)} %param.10) | copy-start | bytes 196
  6.5 72.7 %all-gather.2.cloned.1.call-start = ((), (), s32[]{:S(2)}) async-start(), calls=%async_computation.4 | async-start | bytes 11141120 | tf_op jit(solution)/shard_map/all_gather | solution.py:334
  9.0 21.0 %collective-permute-start.6 = (bf16[128,1152]{1,0:T(8,128)(2,1)}, bf16[128,1152]{1,0:T(8,128)(2,1)S(1)}, u32[]{:S(2)}, u32[]{:S(2)}) collective-permute-start(bf16[128,1152]{1,0:T(8,128)(2,1)} %get-tuple-element.26), channel_id=1, source_target_pairs={{0,128},{64,192},{128,0},{192,64},{1,129},{65,193},{129,1},{193,65... | collective-permute-start | bytes 884744 | tf_op jit(solution)/shard_map/ppermute | solution.py:39
  12.8 15.2 %collective-permute-start.1 = (bf16[128,1152]{1,0:T(8,128)(2,1)}, bf16[128,1152]{1,0:T(8,128)(2,1)S(1)}, u32[]{:S(2)}, u32[]{:S(2)}) collective-permute-start(bf16[128,1152]{1,0:T(8,128)(2,1)} %get-tuple-element.26), channel_id=1, source_target_pairs={{0,64},{64,128},{128,192},{192,0},{1,65},{65,129},{129,193},{193,1... | collective-permute-start | bytes 884744 | tf_op jit(solution)/shard_map/ppermute | solution.py:39
  13.2 14.8 %collective-permute-start = (bf16[128,1152]{1,0:T(8,128)(2,1)}, bf16[128,1152]{1,0:T(8,128)(2,1)S(1)}, u32[]{:S(2)}, u32[]{:S(2)}) collective-permute-start(bf16[128,1152]{1,0:T(8,128)(2,1)} %get-tuple-element.26), channel_id=1, source_target_pairs={{0,192},{64,0},{128,64},{192,128},{1,193},{65,1},{129,65},{193,129... | collective-permute-start | bytes 884744 | tf_op jit(solution)/shard_map/ppermute | solution.py:39
  17.6 10.5 %all-to-all-start = ((s32[16,1,128]{2,1,0:T(1,128)}), s32[16,1,128]{2,1,0:T(1,128)S(1)}, u32[]{:S(2)}, u32[]{:S(2)}) async-start(s32[16,1,128]{2,1,0:T(1,128)} %broadcast_in_dim.53), calls=%async_computation | async-start | bytes 16384 | tf_op jit(solution)/shard_map/all_to_all | solution.py:347
  22.7 1.5 copy-start.6
  28.1 24.9 %collective-permute-start.3 = (bf16[512,1152]{1,0:T(8,128)(2,1)}, bf16[512,1152]{1,0:T(8,128)(2,1)S(1)}, u32[]{:S(2)}, u32[]{:S(2)}) collective-permute-start(bf16[512,1152]{1,0:T(8,128)(2,1)} %bitcast.62), channel_id=1, source_target_pairs={{0,192},{64,0},{128,64},{192,128},{1,193},{65,1},{129,65},{193,129... | collective-permute-start | bytes 3538952 | tf_op jit(solution)/shard_map/ppermute | solution.py:39
  29.7 26.5 %collective-permute-start.2 = (bf16[512,1152]{1,0:T(8,128)(2,1)}, bf16[512,1152]{1,0:T(8,128)(2,1)}, u32[]{:S(2)}, u32[]{:S(2)}) collective-permute-start(bf16[512,1152]{1,0:T(8,128)(2,1)} %bitcast.63), channel_id=1, source_target_pairs={{0,64},{64,128},{128,192},{192,0},{1,65},{65,129},{129,193},{193,1... | collective-permute-start | bytes 3538952 | tf_op jit(solution)/shard_map/ppermute | solution.py:39
  30.2 49.1 %copy-start.1 = (bf16[384,1152]{1,0:T(8,128)(2,1)}, bf16[384,1152]{1,0:T(8,128)(2,1)S(1)}, u32[]{:S(2)}) copy-start(bf16[384,1152]{1,0:T(8,128)(2,1)S(1)} %shard_map.66.refs_5_) | copy-start | bytes 2654212
  30.2 29.9 %collective-permute-start.8 = (bf16[384,1152]{1,0:T(8,128)(2,1)S(1)}, bf16[384,1152]{1,0:T(8,128)(2,1)S(1)}, u32[]{:S(2)}, u32[]{:S(2)}) collective-permute-start(bf16[384,1152]{1,0:T(8,128)(2,1)S(1)} %shard_map.66.refs_5_), channel_id=1, source_target_pairs={{0,1},{1,2},{2,3},{3,0},{4,5},{5,6},{6,7},{7,4},{8,9},{9,10},{10,1... | collective-permute-start | bytes 2654216 | tf_op jit(solution)/shard_map/ppermute | solution.py:39
  31.5 30.9 %collective-permute-start.7 = (bf16[384,1152]{1,0:T(8,128)(2,1)S(1)}, bf16[384,1152]{1,0:T(8,128)(2,1)}, u32[]{:S(2)}, u32[]{:S(2)}) collective-permute-start(bf16[384,1152]{1,0:T(8,128)(2,1)S(1)} %shard_map.66.refs_5_), channel_id=1, source_target_pairs={{0,3},{1,0},{2,1},{3,2},{4,7},{5,4},{6,5},{7,6},{8,11},{9,8},{10,9... | collective-permute-start | bytes 2654216 | tf_op jit(solution)/shard_map/ppermute | solution.py:39
  41.9 0.6 copy-start.3
  53.0 26.2 %copy-start.7 = (bf16[512,1152]{1,0:T(8,128)(2,1)}, bf16[512,1152]{1,0:T(8,128)(2,1)S(1)}, u32[]{:S(2)}) copy-start(bf16[512,1152]{1,0:T(8,128)(2,1)S(1)} %collective-permute-done.3.refs_1_) | copy-start | bytes 3538948
  57.3 15.6 %collective-permute-start.4 = (bf16[256,1152]{1,0:T(8,128)(2,1)S(1)}, bf16[256,1152]{1,0:T(8,128)(2,1)S(1)}, u32[]{:S(2)}, u32[]{:S(2)}) collective-permute-start(bf16[256,1152]{1,0:T(8,128)(2,1)S(1)} %slice.16), channel_id=1, source_target_pairs={{0,64},{64,128},{128,192},{192,0},{1,65},{65,129},{129,193},{193,1... | collective-permute-start | bytes 1769480 | tf_op jit(solution)/shard_map/ppermute | solution.py:39
  57.4 16.3 %collective-permute-start.5 = (bf16[256,1152]{1,0:T(8,128)(2,1)S(1)}, bf16[256,1152]{1,0:T(8,128)(2,1)}, u32[]{:S(2)}, u32[]{:S(2)}) collective-permute-start(bf16[256,1152]{1,0:T(8,128)(2,1)S(1)} %slice.17), channel_id=1, source_target_pairs={{0,192},{64,0},{128,64},{192,128},{1,193},{65,1},{129,65},{193,129... | collective-permute-start | bytes 1769480 | tf_op jit(solution)/shard_map/ppermute | solution.py:39
  60.1 19.2 %copy-start.8 = (bf16[384,1152]{1,0:T(8,128)(2,1)}, bf16[384,1152]{1,0:T(8,128)(2,1)S(1)}, u32[]{:S(2)}) copy-start(bf16[384,1152]{1,0:T(8,128)(2,1)S(1)} %collective-permute-done.8.refs_9_) | copy-start | bytes 2654212
  60.1 12.0 %collective-permute-start.9 = (bf16[192,1152]{1,0:T(8,128)(2,1)S(1)}, bf16[192,1152]{1,0:T(8,128)(2,1)S(1)}, u32[]{:S(2)}, u32[]{:S(2)}) collective-permute-start(bf16[192,1152]{1,0:T(8,128)(2,1)S(1)} %slice.23), channel_id=1, source_target_pairs={{0,1},{1,2},{2,3},{3,0},{4,5},{5,6},{6,7},{7,4},{8,9},{9,10},{10,1... | collective-permute-start | bytes 1327112 | tf_op jit(solution)/shard_map/ppermute | solution.py:39
  63.4 9.5 %collective-permute-start.10 = (bf16[192,1152]{1,0:T(8,128)(2,1)S(1)}, bf16[192,1152]{1,0:T(8,128)(2,1)S(1)}, u32[]{:S(2)}, u32[]{:S(2)}) collective-permute-start(bf16[192,1152]{1,0:T(8,128)(2,1)S(1)} %slice.24), channel_id=1, source_target_pairs={{0,3},{1,0},{2,1},{3,2},{4,7},{5,4},{6,5},{7,6},{8,11},{9,8},{10,9... | collective-permute-start | bytes 1327112 | tf_op jit(solution)/shard_map/ppermute | solution.py:39
  72.1 0.9 copy-start.10
  72.9 0.8 copy-start.11
  73.7 5.5 %copy-start.9 = (bf16[256,1152]{1,0:T(8,128)(2,1)}, bf16[256,1152]{1,0:T(8,128)(2,1)S(1)}, u32[]{:S(2)}) copy-start(bf16[256,1152]{1,0:T(8,128)(2,1)S(1)} %collective-permute-done.4.refs_2_) | copy-start | bytes 1769476
  90.1 6.7 %copy-start.2 = (bf16[256,1280]{1,0:T(8,128)(2,1)S(1)}, bf16[256,1280]{1,0:T(8,128)(2,1)}, u32[]{:S(2)}) copy-start(bf16[256,1280]{1,0:T(8,128)(2,1)} %get-tuple-element.40.piece) | copy-start | bytes 1966084
  90.1 53.1 %copy-start.4 = (s32[640]{0:T(1024)S(1)}, s32[640]{0:T(1024)}, u32[]{:S(2)}) copy-start(s32[640]{0:T(1024)} %copy-done.3) | copy-start | bytes 7684
  90.1 22.2 %all-to-all-start.1 = ((bf16[16,272,128]{2,1,0:T(8,128)(2,1)}), bf16[16,272,128]{2,1,0:T(8,128)(2,1)S(1)}, u32[]{:S(2)}, u32[]{:S(2)}) async-start(bf16[16,272,128]{2,1,0:T(8,128)(2,1)} %get-tuple-element.39), calls=%async_computation.1 | async-start | bytes 2228224 | tf_op jit(solution)/shard_map/all_to_all | solution.py:432
  139.1 4.1 %collective-permute-start.11 = (bf16[32,64,128]{2,1,0:T(8,128)(2,1)S(1)}, bf16[32,64,128]{2,1,0:T(8,128)(2,1)S(1)}, u32[]{:S(2)}, u32[]{:S(2)}) collective-permute-start(bf16[32,64,128]{2,1,0:T(8,128)(2,1)S(1)} %bitcast.58), channel_id=1, source_target_pairs={{0,4},{4,0},{1,5},{5,1},{2,6},{6,2},{3,7},{7,3},{8,12},{12,8},{9,1... | collective-permute-start | bytes 1572872 | tf_op jit(solution)/shard_map/ppermute | solution.py:39
Sparse Core Ops, SparseCore 0:
  9.2 69.9 all-gather.1

commit v14 on v13

--- a/solution.py
+++ b/solution.py
@@ -28,7 +28,8 @@
 PIECE = PART * FRAMES
 SEND = PIECE + 16
 LIST = 640
-FIRST_AT, SECOND_AT, STEPS_AT = 600, 601, 602
+QUARTERS = 4
+PARTS_AT, STEPS_AT = 600, 610
 SPARE = QBLOCKS
 UNREAL = 1024.0
 sharpness = 2.0 * math.sqrt(FEAT)
@@ -88,25 +89,31 @@
     count = lax.fori_loop(0, QBLOCKS * 32 // 8, eight, 0)
 
     def kind_of(code):
-        return ((code >> 12) & 1) + jnp.where(((code >> 13) & 63) >= Q_TURN, 2, 0)
+        return jnp.where(((code >> 13) & 63) >= Q_TURN, QUARTERS, (code >> 11) & 3)
 
     def tally(i, counts):
         kind = kind_of(found[i])
         return tuple(n + jnp.where(kind == j, 1, 0) for j, n in enumerate(counts))
 
-    one, two, three = lax.fori_loop(0, count, tally, (0, 0, 0))
+    counts = lax.fori_loop(0, count, tally, (0,) * QUARTERS)
+    starts = [0]
+    for n in counts:
+        starts.append(starts[-1] + n)
 
     def place(i, at):
         code = found[i]
         kind = kind_of(code)
-        out[jnp.where(kind < 2, jnp.where(kind == 0, at[0], at[1]), jnp.where(kind == 2, at[2], at[3]))] = code
+        slot = at[QUARTERS]
+        for j in range(QUARTERS):
+            slot = jnp.where(kind == j, at[j], slot)
+        out[slot] = code
         return tuple(n + jnp.where(kind == j, 1, 0) for j, n in enumerate(at))
 
-    lax.fori_loop(0, count, place, (0, one, one + two, one + two + three))
+    lax.fori_loop(0, count, place, tuple(starts))
     for u in range(UNROLL):
         out[count + u] = SPARE
-    out[FIRST_AT] = one // UNROLL
-    out[SECOND_AT] = (one + two) // UNROLL
+    for j in range(QUARTERS):
+        out[PARTS_AT + j] = starts[j + 1] // UNROLL
     out[STEPS_AT] = (count + UNROLL - 1) // UNROLL
 
 
@@ -154,7 +161,7 @@
     send_out, w_out, q, k, acc, send, w, lst, sems, w_sem, send_sem, lst_sem = refs[10:]
     lst_copy = pltpu.make_async_copy(lst_in, lst, lst_sem)
     lst_copy.start()
-    half = k.shape[0] // 2
+    quarter = k.shape[0] // QUARTERS
     q_copies = []
     at = 0
     for part in queries:
@@ -162,15 +169,17 @@
         q_copies.append(pltpu.make_async_copy(part, q.at[pl.ds(at, rows)], sems.at[len(q_copies)]))
         at += rows
     k_copies = [
-        pltpu.make_async_copy(keys.at[pl.ds(i * half, half)], k.at[pl.ds(i * half, half)], sems.at[10 + i])
-        for i in range(2)
+        pltpu.make_async_copy(
+            keys.at[pl.ds(i * quarter, quarter)], k.at[pl.ds(i * quarter, quarter)], sems.at[10 + i]
+        )
+        for i in range(QUARTERS)
     ]
     straight, turned = q_copies[:5], q_copies[5:]
     for copy in straight + k_copies + turned:
         copy.start()
     acc[...] = jnp.zeros_like(acc)
     lst_copy.wait()
-    for copy in straight + k_copies[:1]:
+    for copy in straight:
         copy.wait()
     steps = lst[STEPS_AT]
 
@@ -198,12 +207,14 @@
         pairs_copy(w, w_out, w_sem, i).start()
         return carry
 
-    lax.fori_loop(0, lst[FIRST_AT], step, 0)
-    k_copies[1].wait()
-    lax.fori_loop(lst[FIRST_AT], lst[SECOND_AT], step, 0)
+    done = 0
+    for j in range(QUARTERS):
+        k_copies[j].wait()
+        lax.fori_loop(done, lst[PARTS_AT + j], step, 0)
+        done = lst[PARTS_AT + j]
     for copy in turned:
         copy.wait()
-    lax.fori_loop(lst[SECOND_AT], steps, step, 0)
+    lax.fori_loop(done, steps, step, 0)
     row = lax.broadcasted_iota(jnp.int32, (FRAMES, CH), 0)
     lane = lax.broadcasted_iota(jnp.int32, (FRAMES, CH), 1)
     pick = row == lane % FRAMES
@@ -422,7 +433,7 @@
             pltpu.VMEM((NY * NX, SEND, CH), jnp.bfloat16),
             pltpu.VMEM((SLOTS // 2, FRAMES, 2 * FRAMES), jnp.bfloat16),
             pltpu.SMEM((LIST,), jnp.int32),
-            pltpu.SemaphoreType.DMA((12,)),
+            pltpu.SemaphoreType.DMA((14,)),
             pltpu.SemaphoreType.DMA,
             pltpu.SemaphoreType.DMA,
             pltpu.SemaphoreType.DMA,

time: 174 us -> 172 us (0.989)
  blocking collectives: 45.1 us -> 40.2 us
    all_to_all x1, blocking collectives: 26.3 us -> 20.6 us  [body(): lax.all_to_all(masked, 'z', split_axis=0, concat_axis=0, tiled=True)]
    all_to_all x1, waiting for transfers between devices: 13 us -> 15.1 us  [body(): lax.all_to_all(send, ('y', 'x'), split_axis=0, concat_axis=0, tiled=True)]
where the time goes in v14:
time: 172 us; the launch traced here: 171 us
  waiting for transfers between devices  45.1 us (26%)
  blocking collectives  40.2 us (23%)
  starting transfers between devices  31.7 us (18%)
  Pallas kernels  29.3 us (17%)
  between operations  13.7 us (8%)
  local copies, waits for them, and re-layouts  9.45 us (5%)
  other arithmetic  2.05 us (1%)
    ppermute x12, waiting for transfers between devices, shift(): lax.ppermute(value, axis, [(i, (i + step) % size) for i in range(size)])  21.8 us
    ppermute x12, starting transfers between devices, shift(): lax.ppermute(value, axis, [(i, (i + step) % size) for i in range(size)])  21.1 us
    all_to_all x1, blocking collectives, body(): lax.all_to_all(masked, 'z', split_axis=0, concat_axis=0, tiled=True)  20.6 us
    all_to_all x1, blocking collectives, body(): lax.all_to_all(send, ('y', 'x'), split_axis=0, concat_axis=0, tiled=True)  19.6 us
    all_to_all x1, waiting for transfers between devices, body(): lax.all_to_all(send, ('y', 'x'), split_axis=0, concat_axis=0, tiled=True)  15.1 us
    pallas_call x1, Pallas kernels, body(): pl.pallas_call(first_kernel, out_shape=(jax.ShapeDtypeStruct((NY * NX, SE...  11.3 us
    pallas_call x1, Pallas kernels, body(): pl.pallas_call(list_kernel, out_shape=jax.ShapeDtypeStruct((LIST,), jnp.i...  9.2 us
    all_to_all x1, starting transfers between devices, body(): lax.all_to_all(send, ('y', 'x'), split_axis=0, concat_axis=0, tiled=True)  6.46 us
  transfers between devices with their start and end apart: 15, of which 8 were waited for; matrix products, arithmetic and copies ran while one was open for 5% of the time, Pallas kernels for 6%

profile of v14, /device:TPU:1, one launch (start us, length us, event | category | flops | bytes accessed | tf_op | source)
XLA Modules:
  0.0 171.5 jit_solution(11790180693691569683)
XLA Ops:
  6.6 2.4 %shard_map.64 = (bf16[256,1280]{1,0:T(8,128)(2,1)}, bf16[128,1152]{1,0:T(8,128)(2,1)}) custom-call(bf16[16,64,1152]{2,1,0:T(8,128)(2,1)} %embeddings.1, bf16[16,64,128]{2,1,0:T(8,128)(2,1)} %prior.1, s32[16,64]{1,0:T(8,128)} %marks.1), custom_call_target="tpu_custom_call" | custom-call | tf_op jit(solution)/shard_map/pallas_call | solution.py:326
  9.0 3.8 %collective-permute-start.6 = (bf16[128,1152]{1,0:T(8,128)(2,1)}, bf16[128,1152]{1,0:T(8,128)(2,1)S(1)}, u32[]{:S(2)}, u32[]{:S(2)}) collective-permute-start(bf16[128,1152]{1,0:T(8,128)(2,1)} %get-tuple-element.26), channel_id=1, source_target_pairs={{0,128},{64,192},{128,0},{192,64},{1,129},{65,193},{129,1},{193,65... | collective-permute-start | bytes 884744 | tf_op jit(solution)/shard_map/ppermute | solution.py:40
  12.8 0.4 collective-permute-start.1
  13.2 2.3 %collective-permute-start = (bf16[128,1152]{1,0:T(8,128)(2,1)}, bf16[128,1152]{1,0:T(8,128)(2,1)S(1)}, u32[]{:S(2)}, u32[]{:S(2)}) collective-permute-start(bf16[128,1152]{1,0:T(8,128)(2,1)} %get-tuple-element.26), channel_id=1, source_target_pairs={{0,192},{64,0},{128,64},{192,128},{1,193},{65,1},{129,65},{193,129... | collective-permute-start | bytes 884744 | tf_op jit(solution)/shard_map/ppermute | solution.py:40
  15.6 0.1 reshape.403
  15.7 0.1 reshape.402
  15.9 0.1 lt.99
  16.0 1.0 gather_fusion
  17.0 0.6 broadcast_in_dim.53
  17.6 4.1 %all-to-all-start = ((s32[16,1,128]{2,1,0:T(1,128)}), s32[16,1,128]{2,1,0:T(1,128)S(1)}, u32[]{:S(2)}, u32[]{:S(2)}) async-start(s32[16,1,128]{2,1,0:T(1,128)} %broadcast_in_dim.53), calls=%async_computation | async-start | bytes 16384 | tf_op jit(solution)/shard_map/all_to_all | solution.py:358
  21.7 0.5 fusion
  22.3 0.5 fusion.1
  22.8 1.4 copy-done.6
  24.2 1.1 slice.22
  25.3 2.7 %all-to-all-done = s32[16,1,128]{2,1,0:T(1,128)S(1)} async-done(((s32[16,1,128]{2,1,0:T(1,128)}), s32[16,1,128]{2,1,0:T(1,128)S(1)}, u32[]{:S(2)}, u32[]{:S(2)}) %all-to-all-start) | async-done | bytes 8224 | tf_op jit(solution)/shard_map/all_to_all | solution.py:358
  28.1 1.6 collective-permute-start.3
  29.8 0.1 or.31
  30.0 0.2 shard_map.66.refs_5_
  30.2 1.3 collective-permute-start.8
  31.5 1.5 collective-permute-start.7
  33.1 0.1 or.34
  33.3 9.2 %shard_map.65.lst_in.lst = s32[640]{0:T(1024)S(1)} custom-call(s32[2048]{0:T(1024)S(1)} %fusion.11.codes), custom_call_target="tpu_custom_call" | custom-call | tf_op jit(solution)/shard_map/pallas_call | solution.py:399
  42.5 0.6 copy-done.3
  43.1 9.9 %collective-permute-done.3.refs_1_ = bf16[512,1152]{1,0:T(8,128)(2,1)S(1)} collective-permute-done((bf16[512,1152]{1,0:T(8,128)(2,1)}, bf16[512,1152]{1,0:T(8,128)(2,1)S(1)}, u32[]{:S(2)}, u32[]{:S(2)}) %collective-permute-start.3) | collective-permute-done | bytes 1179680 | tf_op jit(solution)/shard_map/ppermute | solution.py:40
  53.0 3.1 %collective-permute-done.2.refs_4_ = bf16[512,1152]{1,0:T(8,128)(2,1)} collective-permute-done((bf16[512,1152]{1,0:T(8,128)(2,1)}, bf16[512,1152]{1,0:T(8,128)(2,1)}, u32[]{:S(2)}, u32[]{:S(2)}) %collective-permute-start.2) | collective-permute-done | bytes 1179680 | tf_op jit(solution)/shard_map/ppermute | solution.py:40
  56.2 1.1 slice.16
  57.4 2.7 %collective-permute-start.5 = (bf16[256,1152]{1,0:T(8,128)(2,1)S(1)}, bf16[256,1152]{1,0:T(8,128)(2,1)}, u32[]{:S(2)}, u32[]{:S(2)}) collective-permute-start(bf16[256,1152]{1,0:T(8,128)(2,1)S(1)} %slice.17), channel_id=1, source_target_pairs={{0,192},{64,0},{128,64},{192,128},{1,193},{65,1},{129,65},{193,129... | collective-permute-start | bytes 1769480 | tf_op jit(solution)/shard_map/ppermute | solution.py:40
  60.1 2.2 %collective-permute-start.9 = (bf16[192,1152]{1,0:T(8,128)(2,1)S(1)}, bf16[192,1152]{1,0:T(8,128)(2,1)S(1)}, u32[]{:S(2)}, u32[]{:S(2)}) collective-permute-start(bf16[192,1152]{1,0:T(8,128)(2,1)S(1)} %slice.23), channel_id=1, source_target_pairs={{0,1},{1,2},{2,3},{3,0},{4,5},{5,6},{6,7},{7,4},{8,9},{9,10},{10,1... | collective-permute-start | bytes 1327112 | tf_op jit(solution)/shard_map/ppermute | solution.py:40
  62.4 1.1 slice.24
  63.4 2.3 %collective-permute-start.10 = (bf16[192,1152]{1,0:T(8,128)(2,1)S(1)}, bf16[192,1152]{1,0:T(8,128)(2,1)S(1)}, u32[]{:S(2)}, u32[]{:S(2)}) collective-permute-start(bf16[192,1152]{1,0:T(8,128)(2,1)S(1)} %slice.24), channel_id=1, source_target_pairs={{0,3},{1,0},{2,1},{3,2},{4,7},{5,4},{6,5},{7,6},{8,11},{9,8},{10,9... | collective-permute-start | bytes 1327112 | tf_op jit(solution)/shard_map/ppermute | solution.py:40
  65.7 6.4 %collective-permute-done.9.refs_7_ = bf16[192,1152]{1,0:T(8,128)(2,1)S(1)} collective-permute-done((bf16[192,1152]{1,0:T(8,128)(2,1)S(1)}, bf16[192,1152]{1,0:T(8,128)(2,1)S(1)}, u32[]{:S(2)}, u32[]{:S(2)}) %collective-permute-start.9) | collective-permute-done | bytes 442400 | tf_op jit(solution)/shard_map/ppermute | solution.py:40
  72.1 0.9 collective-permute-done.10.refs_8_
  72.9 0.8 copy-done.11
  73.7 5.5 %all-gather.2.cloned.1.call-done.keys = bf16[4096,1280]{1,0:T(8,128)(2,1)} async-done(((bf16[256,1280]{1,0:T(8,128)(2,1)}), bf16[4096,1280]{1,0:T(8,128)(2,1)}) %all-gather.2.cloned.1.call-update) | async-done | bytes 10485776 | tf_op jit(solution)/shard_map/all_gather | solution.py:345
  79.3 11.3 %shard_map.67 = (bf16[16,272,128]{2,1,0:T(8,128)(2,1)}, bf16[4608,64,128]{2,1,0:T(8,128)(2,1)}) custom-call(s32[640]{0:T(1024)} %copy-done.3, bf16[4096,1280]{1,0:T(8,128)(2,1)} %all-gather.2.cloned.1.call-done.keys, bf16[1024,1152]{1,0:T(8,128)(2,1)} %bitcast.61, bf16[512,1152]{1,0:T(8,128)(2,1)} %copy-done.7, bf16[256,1152]{1,0:T(8,128)(2,1)} %copy-done.9, ...), custom_call_target="tpu_custom_call" | custom-call | tf_op jit(solution)/shard_map/pallas_call | solution.py:421
  90.6 6.5 %all-to-all-start.1 = ((bf16[16,272,128]{2,1,0:T(8,128)(2,1)}), bf16[16,272,128]{2,1,0:T(8,128)(2,1)S(1)}, u32[]{:S(2)}, u32[]{:S(2)}) async-start(bf16[16,272,128]{2,1,0:T(8,128)(2,1)} %get-tuple-element.39), calls=%async_computation.1 | async-start | bytes 2228224 | tf_op jit(solution)/shard_map/all_to_all | solution.py:443
  97.0 0.9 shard_map.68
  98.0 0.7 dynamic-slice_convert_fusion
  98.7 0.8 constant_dynamic-slice_fusion.prior
  99.5 15.1 %all-to-all-done.1.got = bf16[16,272,128]{2,1,0:T(8,128)(2,1)S(1)} async-done(((bf16[16,272,128]{2,1,0:T(8,128)(2,1)}), bf16[16,272,128]{2,1,0:T(8,128)(2,1)S(1)}, u32[]{:S(2)}, u32[]{:S(2)}) %all-to-all-start.1) | async-done | bytes 1114144 | tf_op jit(solution)/shard_map/all_to_all | solution.py:443
  114.6 0.1 broadcast_in_dim.56.marks
  114.7 0.4 shard_map.69
  115.0 20.6 %all_to_all.24 = bf16[8,4,64,128]{3,2,1,0:T(8,128)(2,1)S(1)} all-to-all(bf16[8,4,64,128]{3,2,1,0:T(8,128)(2,1)S(1)} %get-tuple-element.44), channel_id=1, replica_groups=mesh['y'=4,'z'=8,'c'=2,'x'=4] {'z'}, dimensions={0} | all-to-all | bytes 1048576 | tf_op jit(solution)/shard_map/all_to_all | solution.py:456
  135.7 2.9 %collective-permute-start.11 = (bf16[32,64,128]{2,1,0:T(8,128)(2,1)S(1)}, bf16[32,64,128]{2,1,0:T(8,128)(2,1)S(1)}, u32[]{:S(2)}, u32[]{:S(2)}) collective-permute-start(bf16[32,64,128]{2,1,0:T(8,128)(2,1)S(1)} %bitcast.58), channel_id=1, source_target_pairs={{0,4},{4,0},{1,5},{5,1},{2,6},{6,2},{3,7},{7,3},{8,12},{12,8},{9,1... | collective-permute-start | bytes 1572872 | tf_op jit(solution)/shard_map/ppermute | solution.py:40
  138.6 1.5 collective-permute-done.11.far
  140.2 4.1 %shard_map.70 = bf16[64,64,128]{2,1,0:T(8,128)(2,1)S(1)} custom-call(s32[640]{0:T(1024)S(1)} %copy-done.4, bf16[4608,64,128]{2,1,0:T(8,128)(2,1)} %get-tuple-element.38.w_in, bf16[32,64,128]{2,1,0:T(8,128)(2,1)S(1)} %bitcast.59, bf16[32,64,128]{2,1,0:T(8,128)(2,1)S(1)} %collective-permute-done.11.far), custom_call_target="tpu_custom_call" | custom-call | tf_op jit(solution)/shard_map/pallas_call | solution.py:460
  144.3 19.6 %all_to_all.25 = bf16[64,64,128]{2,1,0:T(8,128)(2,1)S(1)} all-to-all(bf16[64,64,128]{2,1,0:T(8,128)(2,1)S(1)} %shard_map.70), channel_id=1, replica_groups=mesh['y'=4,'z'=8,'c'=2,'x'=4] {'y','x'}, dimensions={0} | all-to-all | bytes 2097152 | tf_op jit(solution)/shard_map/all_to_all | solution.py:472
  163.8 0.8 shard_map.71
  (56 shorter events, 0.9 us)
Async XLA Ops:
  6.5 9.4 %copy-start = (s32[1024]{0:T(1024)S(1)}, s32[1024]{0:T(1024)}, u32[]{:S(2)}) copy-start(s32[1024]{0:T(1024)} %param.11) | copy-start | bytes 12292
  6.5 15.2 %copy-start.5 = (bf16[16,64,1152]{2,1,0:T(8,128)(2,1)S(1)}, bf16[16,64,1152]{2,1,0:T(8,128)(2,1)}, u32[]{:S(2)}) copy-start(bf16[16,64,1152]{2,1,0:T(8,128)(2,1)} %embeddings.1) | copy-start | bytes 7077892
  6.5 9.0 %copy-start.12 = (s32[16,8]{0,1:T(8,128)S(1)}, s32[16,8]{0,1:T(8,128)}, u32[]{:S(2)}) copy-start(s32[16,8]{0,1:T(8,128)} %param.9) | copy-start | bytes 1540
  6.5 9.2 %copy-start.13 = (s32[16]{0:T(128)S(1)}, s32[16]{0:T(128)}, u32[]{:S(2)}) copy-start(s32[16]{0:T(128)} %param.10) | copy-start | bytes 196
  6.5 72.7 %all-gather.2.cloned.1.call-start = ((), (), s32[]{:S(2)}) async-start(), calls=%async_computation.4 | async-start | bytes 11141120 | tf_op jit(solution)/shard_map/all_gather | solution.py:345
  9.0 21.0 %collective-permute-start.6 = (bf16[128,1152]{1,0:T(8,128)(2,1)}, bf16[128,1152]{1,0:T(8,128)(2,1)S(1)}, u32[]{:S(2)}, u32[]{:S(2)}) collective-permute-start(bf16[128,1152]{1,0:T(8,128)(2,1)} %get-tuple-element.26), channel_id=1, source_target_pairs={{0,128},{64,192},{128,0},{192,64},{1,129},{65,193},{129,1},{193,65... | collective-permute-start | bytes 884744 | tf_op jit(solution)/shard_map/ppermute | solution.py:40
  12.8 15.2 %collective-permute-start.1 = (bf16[128,1152]{1,0:T(8,128)(2,1)}, bf16[128,1152]{1,0:T(8,128)(2,1)S(1)}, u32[]{:S(2)}, u32[]{:S(2)}) collective-permute-start(bf16[128,1152]{1,0:T(8,128)(2,1)} %get-tuple-element.26), channel_id=1, source_target_pairs={{0,64},{64,128},{128,192},{192,0},{1,65},{65,129},{129,193},{193,1... | collective-permute-start | bytes 884744 | tf_op jit(solution)/shard_map/ppermute | solution.py:40
  13.2 14.8 %collective-permute-start = (bf16[128,1152]{1,0:T(8,128)(2,1)}, bf16[128,1152]{1,0:T(8,128)(2,1)S(1)}, u32[]{:S(2)}, u32[]{:S(2)}) collective-permute-start(bf16[128,1152]{1,0:T(8,128)(2,1)} %get-tuple-element.26), channel_id=1, source_target_pairs={{0,192},{64,0},{128,64},{192,128},{1,193},{65,1},{129,65},{193,129... | collective-permute-start | bytes 884744 | tf_op jit(solution)/shard_map/ppermute | solution.py:40
  17.6 10.5 %all-to-all-start = ((s32[16,1,128]{2,1,0:T(1,128)}), s32[16,1,128]{2,1,0:T(1,128)S(1)}, u32[]{:S(2)}, u32[]{:S(2)}) async-start(s32[16,1,128]{2,1,0:T(1,128)} %broadcast_in_dim.53), calls=%async_computation | async-start | bytes 16384 | tf_op jit(solution)/shard_map/all_to_all | solution.py:358
  22.7 1.5 copy-start.6
  28.1 24.9 %collective-permute-start.3 = (bf16[512,1152]{1,0:T(8,128)(2,1)}, bf16[512,1152]{1,0:T(8,128)(2,1)S(1)}, u32[]{:S(2)}, u32[]{:S(2)}) collective-permute-start(bf16[512,1152]{1,0:T(8,128)(2,1)} %bitcast.62), channel_id=1, source_target_pairs={{0,192},{64,0},{128,64},{192,128},{1,193},{65,1},{129,65},{193,129... | collective-permute-start | bytes 3538952 | tf_op jit(solution)/shard_map/ppermute | solution.py:40
  29.7 26.5 %collective-permute-start.2 = (bf16[512,1152]{1,0:T(8,128)(2,1)}, bf16[512,1152]{1,0:T(8,128)(2,1)}, u32[]{:S(2)}, u32[]{:S(2)}) collective-permute-start(bf16[512,1152]{1,0:T(8,128)(2,1)} %bitcast.63), channel_id=1, source_target_pairs={{0,64},{64,128},{128,192},{192,0},{1,65},{65,129},{129,193},{193,1... | collective-permute-start | bytes 3538952 | tf_op jit(solution)/shard_map/ppermute | solution.py:40
  30.2 49.1 %copy-start.1 = (bf16[384,1152]{1,0:T(8,128)(2,1)}, bf16[384,1152]{1,0:T(8,128)(2,1)S(1)}, u32[]{:S(2)}) copy-start(bf16[384,1152]{1,0:T(8,128)(2,1)S(1)} %shard_map.66.refs_5_) | copy-start | bytes 2654212
  30.2 29.9 %collective-permute-start.8 = (bf16[384,1152]{1,0:T(8,128)(2,1)S(1)}, bf16[384,1152]{1,0:T(8,128)(2,1)S(1)}, u32[]{:S(2)}, u32[]{:S(2)}) collective-permute-start(bf16[384,1152]{1,0:T(8,128)(2,1)S(1)} %shard_map.66.refs_5_), channel_id=1, source_target_pairs={{0,1},{1,2},{2,3},{3,0},{4,5},{5,6},{6,7},{7,4},{8,9},{9,10},{10,1... | collective-permute-start | bytes 2654216 | tf_op jit(solution)/shard_map/ppermute | solution.py:40
  31.5 30.9 %collective-permute-start.7 = (bf16[384,1152]{1,0:T(8,128)(2,1)S(1)}, bf16[384,1152]{1,0:T(8,128)(2,1)}, u32[]{:S(2)}, u32[]{:S(2)}) collective-permute-start(bf16[384,1152]{1,0:T(8,128)(2,1)S(1)} %shard_map.66.refs_5_), channel_id=1, source_target_pairs={{0,3},{1,0},{2,1},{3,2},{4,7},{5,4},{6,5},{7,6},{8,11},{9,8},{10,9... | collective-permute-start | bytes 2654216 | tf_op jit(solution)/shard_map/ppermute | solution.py:40
  42.5 0.6 copy-start.3
  53.0 26.2 %copy-start.7 = (bf16[512,1152]{1,0:T(8,128)(2,1)}, bf16[512,1152]{1,0:T(8,128)(2,1)S(1)}, u32[]{:S(2)}) copy-start(bf16[512,1152]{1,0:T(8,128)(2,1)S(1)} %collective-permute-done.3.refs_1_) | copy-start | bytes 3538948
  57.3 15.6 %collective-permute-start.4 = (bf16[256,1152]{1,0:T(8,128)(2,1)S(1)}, bf16[256,1152]{1,0:T(8,128)(2,1)S(1)}, u32[]{:S(2)}, u32[]{:S(2)}) collective-permute-start(bf16[256,1152]{1,0:T(8,128)(2,1)S(1)} %slice.16), channel_id=1, source_target_pairs={{0,64},{64,128},{128,192},{192,0},{1,65},{65,129},{129,193},{193,1... | collective-permute-start | bytes 1769480 | tf_op jit(solution)/shard_map/ppermute | solution.py:40
  57.4 16.3 %collective-permute-start.5 = (bf16[256,1152]{1,0:T(8,128)(2,1)S(1)}, bf16[256,1152]{1,0:T(8,128)(2,1)}, u32[]{:S(2)}, u32[]{:S(2)}) collective-permute-start(bf16[256,1152]{1,0:T(8,128)(2,1)S(1)} %slice.17), channel_id=1, source_target_pairs={{0,192},{64,0},{128,64},{192,128},{1,193},{65,1},{129,65},{193,129... | collective-permute-start | bytes 1769480 | tf_op jit(solution)/shard_map/ppermute | solution.py:40
  60.1 19.2 %copy-start.8 = (bf16[384,1152]{1,0:T(8,128)(2,1)}, bf16[384,1152]{1,0:T(8,128)(2,1)S(1)}, u32[]{:S(2)}) copy-start(bf16[384,1152]{1,0:T(8,128)(2,1)S(1)} %collective-permute-done.8.refs_9_) | copy-start | bytes 2654212
  60.1 12.0 %collective-permute-start.9 = (bf16[192,1152]{1,0:T(8,128)(2,1)S(1)}, bf16[192,1152]{1,0:T(8,128)(2,1)S(1)}, u32[]{:S(2)}, u32[]{:S(2)}) collective-permute-start(bf16[192,1152]{1,0:T(8,128)(2,1)S(1)} %slice.23), channel_id=1, source_target_pairs={{0,1},{1,2},{2,3},{3,0},{4,5},{5,6},{6,7},{7,4},{8,9},{9,10},{10,1... | collective-permute-start | bytes 1327112 | tf_op jit(solution)/shard_map/ppermute | solution.py:40
  63.4 9.5 %collective-permute-start.10 = (bf16[192,1152]{1,0:T(8,128)(2,1)S(1)}, bf16[192,1152]{1,0:T(8,128)(2,1)S(1)}, u32[]{:S(2)}, u32[]{:S(2)}) collective-permute-start(bf16[192,1152]{1,0:T(8,128)(2,1)S(1)} %slice.24), channel_id=1, source_target_pairs={{0,3},{1,0},{2,1},{3,2},{4,7},{5,4},{6,5},{7,6},{8,11},{9,8},{10,9... | collective-permute-start | bytes 1327112 | tf_op jit(solution)/shard_map/ppermute | solution.py:40
  72.1 0.9 copy-start.10
  72.9 0.8 copy-start.11
  73.7 5.5 %copy-start.9 = (bf16[256,1152]{1,0:T(8,128)(2,1)}, bf16[256,1152]{1,0:T(8,128)(2,1)S(1)}, u32[]{:S(2)}) copy-start(bf16[256,1152]{1,0:T(8,128)(2,1)S(1)} %collective-permute-done.4.refs_2_) | copy-start | bytes 1769476
  90.6 6.5 %copy-start.2 = (bf16[256,1280]{1,0:T(8,128)(2,1)S(1)}, bf16[256,1280]{1,0:T(8,128)(2,1)}, u32[]{:S(2)}) copy-start(bf16[256,1280]{1,0:T(8,128)(2,1)} %get-tuple-element.40.piece) | copy-start | bytes 1966084
  90.6 49.6 %copy-start.4 = (s32[640]{0:T(1024)S(1)}, s32[640]{0:T(1024)}, u32[]{:S(2)}) copy-start(s32[640]{0:T(1024)} %copy-done.3) | copy-start | bytes 7684
  90.6 24.0 %all-to-all-start.1 = ((bf16[16,272,128]{2,1,0:T(8,128)(2,1)}), bf16[16,272,128]{2,1,0:T(8,128)(2,1)S(1)}, u32[]{:S(2)}, u32[]{:S(2)}) async-start(bf16[16,272,128]{2,1,0:T(8,128)(2,1)} %get-tuple-element.39), calls=%async_computation.1 | async-start | bytes 2228224 | tf_op jit(solution)/shard_map/all_to_all | solution.py:443
  135.7 4.5 %collective-permute-start.11 = (bf16[32,64,128]{2,1,0:T(8,128)(2,1)S(1)}, bf16[32,64,128]{2,1,0:T(8,128)(2,1)S(1)}, u32[]{:S(2)}, u32[]{:S(2)}) collective-permute-start(bf16[32,64,128]{2,1,0:T(8,128)(2,1)S(1)} %bitcast.58), channel_id=1, source_target_pairs={{0,4},{4,0},{1,5},{5,1},{2,6},{6,2},{3,7},{7,3},{8,12},{12,8},{9,1... | collective-permute-start | bytes 1572872 | tf_op jit(solution)/shard_map/ppermute | solution.py:40
Sparse Core Ops, SparseCore 0:
  9.2 69.9 all-gather.1

commit v15 on v14

--- a/solution.py
+++ b/solution.py
@@ -405,8 +405,6 @@
         compiler_params=limit(1),
     )(codes)
     half = STRAIGHT * FRAMES // 2
-    behind, ahead, lst = lax.optimization_barrier((behind, ahead, lst))
-    across = [shift(behind[:half], "y", 1), shift(ahead[half:], "y", -1)]
     own_weights, own_base = pl.pallas_call(
         own_kernel,
         out_shape=(
@@ -417,6 +415,10 @@
         out_specs=(vmem, vmem),
         compiler_params=limit(4),
     )(piece)
+    behind, ahead, lst, own_weights, own_base, prior, marks = lax.optimization_barrier(
+        (behind, ahead, lst, own_weights, own_base, prior, marks)
+    )
+    across = [shift(behind[:half], "y", 1), shift(ahead[half:], "y", -1)]
 
     send, weights = pl.pallas_call(
         first_kernel,

time: 172 us -> 169 us (0.983)
  blocking collectives: 40.2 us -> 59 us
  waiting for transfers between devices: 45.1 us -> 26.9 us
  starting transfers between devices: 31.7 us -> 27.3 us
    all_to_all x1 -> x2, blocking collectives: 19.6 us -> 42.7 us  [body(): lax.all_to_all(send, ('y', 'x'), split_axis=0, concat_axis=0, tiled=True)]
    all_to_all x1 -> x0, waiting for transfers between devices: 15.1 us -> none  [body(): lax.all_to_all(send, ('y', 'x'), split_axis=0, concat_axis=0, tiled=True)]
    all_to_all x1 -> x0, starting transfers between devices: 6.46 us -> none  [body(): lax.all_to_all(send, ('y', 'x'), split_axis=0, concat_axis=0, tiled=True)]
    all_to_all x1, blocking collectives: 20.6 us -> 16.3 us  [body(): lax.all_to_all(masked, 'z', split_axis=0, concat_axis=0, tiled=True)]
    ppermute x12, waiting for transfers between devices: 21.8 us -> 19.7 us  [shift(): lax.ppermute(value, axis, [(i, (i + step) % size) for i in range(size)])]
    ppermute x12, starting transfers between devices: 21.1 us -> 23.1 us  [shift(): lax.ppermute(value, axis, [(i, (i + step) % size) for i in range(size)])]
  transfers between devices with their start and end apart: 15 -> 14, of which waited for: 8 -> 7; matrix products, arithmetic and copies ran while one was open for 5% -> 6% of each run, Pallas kernels for 6% -> 6%
where the time goes in v15:
time: 169 us; the launch traced here: 168 us
  blocking collectives  59 us (35%)
  Pallas kernels  28.2 us (17%)
  starting transfers between devices  27.3 us (16%)
  waiting for transfers between devices  26.9 us (16%)
  between operations  13.7 us (8%)
  local copies, waits for them, and re-layouts  10.5 us (6%)
  other arithmetic  2.04 us (1%)
    all_to_all x2, blocking collectives, body(): lax.all_to_all(send, ('y', 'x'), split_axis=0, concat_axis=0, tiled=True)  42.7 us
    ppermute x12, starting transfers between devices, shift(): lax.ppermute(value, axis, [(i, (i + step) % size) for i in range(size)])  23.1 us
    ppermute x12, waiting for transfers between devices, shift(): lax.ppermute(value, axis, [(i, (i + step) % size) for i in range(size)])  19.7 us
    all_to_all x1, blocking collectives, body(): lax.all_to_all(masked, 'z', split_axis=0, concat_axis=0, tiled=True)  16.3 us
    pallas_call x1, Pallas kernels, body(): pl.pallas_call(first_kernel, out_shape=(jax.ShapeDtypeStruct((NY * NX, SE...  10.8 us
    pallas_call x1, Pallas kernels, body(): pl.pallas_call(list_kernel, out_shape=jax.ShapeDtypeStruct((LIST,), jnp.i...  8.89 us
    all_gather x1, waiting for transfers between devices, body(): keys = lax.all_gather(piece, ('z', 'c'), axis=0, tiled=True)  4.42 us
    all_to_all x1, starting transfers between devices, body(): lax.all_to_all(target, ('y', 'x'), split_axis=0, concat_axis=0, tiled=True)  4.12 us
  transfers between devices with their start and end apart: 14, of which 7 were waited for; matrix products, arithmetic and copies ran while one was open for 6% of the time, Pallas kernels for 6%

profile of v15, /device:TPU:1, one launch (start us, length us, event | category | flops | bytes accessed | tf_op | source)
XLA Modules:
  0.0 167.5 jit_solution(6688841459962596429)
XLA Ops:
  6.6 2.4 %shard_map.64 = (bf16[256,1280]{1,0:T(8,128)(2,1)}, bf16[128,1152]{1,0:T(8,128)(2,1)}) custom-call(bf16[16,64,1152]{2,1,0:T(8,128)(2,1)} %embeddings.1, bf16[16,64,128]{2,1,0:T(8,128)(2,1)} %prior.1, s32[16,64]{1,0:T(8,128)} %marks.1), custom_call_target="tpu_custom_call" | custom-call | tf_op jit(solution)/shard_map/pallas_call | solution.py:326
  9.0 3.8 %collective-permute-start.6 = (bf16[128,1152]{1,0:T(8,128)(2,1)}, bf16[128,1152]{1,0:T(8,128)(2,1)S(1)}, u32[]{:S(2)}, u32[]{:S(2)}) collective-permute-start(bf16[128,1152]{1,0:T(8,128)(2,1)} %get-tuple-element.30), channel_id=1, source_target_pairs={{0,128},{64,192},{128,0},{192,64},{1,129},{65,193},{129,1},{193,65... | collective-permute-start | bytes 884744 | tf_op jit(solution)/shard_map/ppermute | solution.py:40
  12.8 0.4 collective-permute-start.1
  13.2 2.3 %collective-permute-start = (bf16[128,1152]{1,0:T(8,128)(2,1)}, bf16[128,1152]{1,0:T(8,128)(2,1)S(1)}, u32[]{:S(2)}, u32[]{:S(2)}) collective-permute-start(bf16[128,1152]{1,0:T(8,128)(2,1)} %get-tuple-element.30), channel_id=1, source_target_pairs={{0,192},{64,0},{128,64},{192,128},{1,193},{65,1},{129,65},{193,129... | collective-permute-start | bytes 884744 | tf_op jit(solution)/shard_map/ppermute | solution.py:40
  15.6 0.1 reshape.403
  15.7 0.1 reshape.402
  15.8 0.1 lt.99
  16.0 1.0 gather_fusion
  17.0 0.6 broadcast_in_dim.53
  17.6 4.1 %all-to-all-start = ((s32[16,1,128]{2,1,0:T(1,128)}), s32[16,1,128]{2,1,0:T(1,128)S(1)}, u32[]{:S(2)}, u32[]{:S(2)}) async-start(s32[16,1,128]{2,1,0:T(1,128)} %broadcast_in_dim.53), calls=%async_computation | async-start | bytes 16384 | tf_op jit(solution)/shard_map/all_to_all | solution.py:358
  21.7 0.5 fusion
  22.3 0.5 fusion.1
  22.8 1.3 copy-done.6
  24.2 1.1 slice.22
  25.3 2.7 %all-to-all-done = s32[16,1,128]{2,1,0:T(1,128)S(1)} async-done(((s32[16,1,128]{2,1,0:T(1,128)}), s32[16,1,128]{2,1,0:T(1,128)S(1)}, u32[]{:S(2)}, u32[]{:S(2)}) %all-to-all-start) | async-done | bytes 8224 | tf_op jit(solution)/shard_map/all_to_all | solution.py:358
  28.0 1.6 collective-permute-start.3
  29.7 0.1 or.31
  29.9 0.2 shard_map.67.refs_5_
  30.1 1.3 collective-permute-start.8
  31.4 1.5 collective-permute-start.7
  33.0 0.1 or.34
  33.2 0.9 shard_map.66
  34.1 0.7 dynamic-slice_convert_fusion
  34.8 0.8 constant_dynamic-slice_fusion.prior
  35.7 8.9 %shard_map.65.lst_in.lst = s32[640]{0:T(1024)S(1)} custom-call(s32[2048]{0:T(1024)S(1)} %fusion.11.codes), custom_call_target="tpu_custom_call" | custom-call | tf_op jit(solution)/shard_map/pallas_call | solution.py:399
  44.6 0.6 copy-done.3
  45.2 7.8 %collective-permute-done.3.refs_1_ = bf16[512,1152]{1,0:T(8,128)(2,1)} collective-permute-done((bf16[512,1152]{1,0:T(8,128)(2,1)}, bf16[512,1152]{1,0:T(8,128)(2,1)}, u32[]{:S(2)}, u32[]{:S(2)}) %collective-permute-start.3) | collective-permute-done | bytes 1179680 | tf_op jit(solution)/shard_map/ppermute | solution.py:40
  53.0 3.1 %collective-permute-done.2.refs_4_ = bf16[512,1152]{1,0:T(8,128)(2,1)} collective-permute-done((bf16[512,1152]{1,0:T(8,128)(2,1)}, bf16[512,1152]{1,0:T(8,128)(2,1)}, u32[]{:S(2)}, u32[]{:S(2)}) %collective-permute-start.2) | collective-permute-done | bytes 1179680 | tf_op jit(solution)/shard_map/ppermute | solution.py:40
  56.1 0.1 broadcast_in_dim.56.marks
  56.2 1.1 slice.17
  57.3 1.1 slice.16
  58.5 2.7 %collective-permute-start.5 = (bf16[256,1152]{1,0:T(8,128)(2,1)S(1)}, bf16[256,1152]{1,0:T(8,128)(2,1)}, u32[]{:S(2)}, u32[]{:S(2)}) collective-permute-start(bf16[256,1152]{1,0:T(8,128)(2,1)S(1)} %slice.17), channel_id=1, source_target_pairs={{0,192},{64,0},{128,64},{192,128},{1,193},{65,1},{129,65},{193,129... | collective-permute-start | bytes 1769480 | tf_op jit(solution)/shard_map/ppermute | solution.py:40
  61.3 2.3 %collective-permute-start.9 = (bf16[192,1152]{1,0:T(8,128)(2,1)S(1)}, bf16[192,1152]{1,0:T(8,128)(2,1)S(1)}, u32[]{:S(2)}, u32[]{:S(2)}) collective-permute-start(bf16[192,1152]{1,0:T(8,128)(2,1)S(1)} %slice.23), channel_id=1, source_target_pairs={{0,1},{1,2},{2,3},{3,0},{4,5},{5,6},{6,7},{7,4},{8,9},{9,10},{10,1... | collective-permute-start | bytes 1327112 | tf_op jit(solution)/shard_map/ppermute | solution.py:40
  63.5 1.1 slice.24
  64.6 2.2 %collective-permute-start.10 = (bf16[192,1152]{1,0:T(8,128)(2,1)S(1)}, bf16[192,1152]{1,0:T(8,128)(2,1)S(1)}, u32[]{:S(2)}, u32[]{:S(2)}) collective-permute-start(bf16[192,1152]{1,0:T(8,128)(2,1)S(1)} %slice.24), channel_id=1, source_target_pairs={{0,3},{1,0},{2,1},{3,2},{4,7},{5,4},{6,5},{7,6},{8,11},{9,8},{10,9... | collective-permute-start | bytes 1327112 | tf_op jit(solution)/shard_map/ppermute | solution.py:40
  66.8 6.3 %collective-permute-done.9.refs_7_ = bf16[192,1152]{1,0:T(8,128)(2,1)S(1)} collective-permute-done((bf16[192,1152]{1,0:T(8,128)(2,1)S(1)}, bf16[192,1152]{1,0:T(8,128)(2,1)S(1)}, u32[]{:S(2)}, u32[]{:S(2)}) %collective-permute-start.9) | collective-permute-done | bytes 442400 | tf_op jit(solution)/shard_map/ppermute | solution.py:40
  73.2 0.9 collective-permute-done.10.refs_8_
  74.0 0.8 copy-done.10
  74.8 4.4 %all-gather.2.cloned.1.call-done.keys = bf16[4096,1280]{1,0:T(8,128)(2,1)} async-done(((bf16[256,1280]{1,0:T(8,128)(2,1)}), bf16[4096,1280]{1,0:T(8,128)(2,1)}) %all-gather.2.cloned.1.call-update) | async-done | bytes 10485776 | tf_op jit(solution)/shard_map/all_gather | solution.py:345
  79.2 10.8 %shard_map.68 = (bf16[16,272,128]{2,1,0:T(8,128)(2,1)}, bf16[4608,64,128]{2,1,0:T(8,128)(2,1)}) custom-call(s32[640]{0:T(1024)} %copy-done.3, bf16[4096,1280]{1,0:T(8,128)(2,1)} %all-gather.2.cloned.1.call-done.keys, bf16[1024,1152]{1,0:T(8,128)(2,1)} %bitcast.61, bf16[512,1152]{1,0:T(8,128)(2,1)} %collective-permute-done.3.refs_1_, ...), custom_call_target="tpu_custom_call" | custom-call | tf_op jit(solution)/shard_map/pallas_call | solution.py:423
  90.1 23.5 %all_to_all.24.got = bf16[16,272,128]{2,1,0:T(8,128)(2,1)S(1)} all-to-all(bf16[16,272,128]{2,1,0:T(8,128)(2,1)} %get-tuple-element.47), channel_id=1, replica_groups=mesh['y'=4,'z'=8,'c'=2,'x'=4] {'y','x'}, dimensions={0} | all-to-all | bytes 2228224 | tf_op jit(solution)/shard_map/all_to_all | solution.py:445
  113.6 0.4 shard_map.69
  114.0 16.3 %all_to_all.25 = bf16[8,4,64,128]{3,2,1,0:T(8,128)(2,1)S(1)} all-to-all(bf16[8,4,64,128]{3,2,1,0:T(8,128)(2,1)S(1)} %get-tuple-element.52), channel_id=1, replica_groups=mesh['y'=4,'z'=8,'c'=2,'x'=4] {'z'}, dimensions={0} | all-to-all | bytes 1048576 | tf_op jit(solution)/shard_map/all_to_all | solution.py:458
  130.3 5.1 %collective-permute-start.11 = (bf16[32,64,128]{2,1,0:T(8,128)(2,1)S(1)}, bf16[32,64,128]{2,1,0:T(8,128)(2,1)S(1)}, u32[]{:S(2)}, u32[]{:S(2)}) collective-permute-start(bf16[32,64,128]{2,1,0:T(8,128)(2,1)S(1)} %bitcast.58), channel_id=1, source_target_pairs={{0,4},{4,0},{1,5},{5,1},{2,6},{6,2},{3,7},{7,3},{8,12},{12,8},{9,1... | collective-permute-start | bytes 1572872 | tf_op jit(solution)/shard_map/ppermute | solution.py:40
  135.4 1.5 collective-permute-done.11.far
  136.9 3.9 %shard_map.70 = bf16[64,64,128]{2,1,0:T(8,128)(2,1)S(1)} custom-call(s32[640]{0:T(1024)S(1)} %copy-done.4, bf16[4608,64,128]{2,1,0:T(8,128)(2,1)} %get-tuple-element.46.w_in, bf16[32,64,128]{2,1,0:T(8,128)(2,1)S(1)} %bitcast.59, bf16[32,64,128]{2,1,0:T(8,128)(2,1)S(1)} %collective-permute-done.11.far), custom_call_target="tpu_custom_call" | custom-call | tf_op jit(solution)/shard_map/pallas_call | solution.py:462
  140.8 19.1 %all_to_all.26 = bf16[64,64,128]{2,1,0:T(8,128)(2,1)S(1)} all-to-all(bf16[64,64,128]{2,1,0:T(8,128)(2,1)S(1)} %shard_map.70), channel_id=1, replica_groups=mesh['y'=4,'z'=8,'c'=2,'x'=4] {'y','x'}, dimensions={0} | all-to-all | bytes 2097152 | tf_op jit(solution)/shard_map/all_to_all | solution.py:474
  159.9 0.8 shard_map.71
  (53 shorter events, 0.8 us)
Async XLA Ops:
  6.5 9.4 %copy-start = (s32[1024]{0:T(1024)S(1)}, s32[1024]{0:T(1024)}, u32[]{:S(2)}) copy-start(s32[1024]{0:T(1024)} %param.11) | copy-start | bytes 12292
  6.5 15.2 %copy-start.5 = (bf16[16,64,1152]{2,1,0:T(8,128)(2,1)S(1)}, bf16[16,64,1152]{2,1,0:T(8,128)(2,1)}, u32[]{:S(2)}) copy-start(bf16[16,64,1152]{2,1,0:T(8,128)(2,1)} %embeddings.1) | copy-start | bytes 7077892
  6.5 9.0 %copy-start.11 = (s32[16,8]{0,1:T(8,128)S(1)}, s32[16,8]{0,1:T(8,128)}, u32[]{:S(2)}) copy-start(s32[16,8]{0,1:T(8,128)} %param.9) | copy-start | bytes 1540
  6.5 9.2 %copy-start.12 = (s32[16]{0:T(128)S(1)}, s32[16]{0:T(128)}, u32[]{:S(2)}) copy-start(s32[16]{0:T(128)} %param.10) | copy-start | bytes 196
  6.5 72.7 %all-gather.2.cloned.1.call-start = ((), (), s32[]{:S(2)}) async-start(), calls=%async_computation.4 | async-start | bytes 11141120 | tf_op jit(solution)/shard_map/all_gather | solution.py:345
  9.0 20.9 %collective-permute-start.6 = (bf16[128,1152]{1,0:T(8,128)(2,1)}, bf16[128,1152]{1,0:T(8,128)(2,1)S(1)}, u32[]{:S(2)}, u32[]{:S(2)}) collective-permute-start(bf16[128,1152]{1,0:T(8,128)(2,1)} %get-tuple-element.30), channel_id=1, source_target_pairs={{0,128},{64,192},{128,0},{192,64},{1,129},{65,193},{129,1},{193,65... | collective-permute-start | bytes 884744 | tf_op jit(solution)/shard_map/ppermute | solution.py:40
  12.8 15.2 %collective-permute-start.1 = (bf16[128,1152]{1,0:T(8,128)(2,1)}, bf16[128,1152]{1,0:T(8,128)(2,1)S(1)}, u32[]{:S(2)}, u32[]{:S(2)}) collective-permute-start(bf16[128,1152]{1,0:T(8,128)(2,1)} %get-tuple-element.30), channel_id=1, source_target_pairs={{0,64},{64,128},{128,192},{192,0},{1,65},{65,129},{129,193},{193,1... | collective-permute-start | bytes 884744 | tf_op jit(solution)/shard_map/ppermute | solution.py:40
  13.2 14.8 %collective-permute-start = (bf16[128,1152]{1,0:T(8,128)(2,1)}, bf16[128,1152]{1,0:T(8,128)(2,1)S(1)}, u32[]{:S(2)}, u32[]{:S(2)}) collective-permute-start(bf16[128,1152]{1,0:T(8,128)(2,1)} %get-tuple-element.30), channel_id=1, source_target_pairs={{0,192},{64,0},{128,64},{192,128},{1,193},{65,1},{129,65},{193,129... | collective-permute-start | bytes 884744 | tf_op jit(solution)/shard_map/ppermute | solution.py:40
  17.6 10.5 %all-to-all-start = ((s32[16,1,128]{2,1,0:T(1,128)}), s32[16,1,128]{2,1,0:T(1,128)S(1)}, u32[]{:S(2)}, u32[]{:S(2)}) async-start(s32[16,1,128]{2,1,0:T(1,128)} %broadcast_in_dim.53), calls=%async_computation | async-start | bytes 16384 | tf_op jit(solution)/shard_map/all_to_all | solution.py:358
  22.7 1.4 copy-start.6
  24.2 9.0 %copy-start.2 = (bf16[256,1280]{1,0:T(8,128)(2,1)S(1)}, bf16[256,1280]{1,0:T(8,128)(2,1)}, u32[]{:S(2)}) copy-start(bf16[256,1280]{1,0:T(8,128)(2,1)} %get-tuple-element.37.piece) | copy-start | bytes 1966084
  28.0 24.9 %collective-permute-start.3 = (bf16[512,1152]{1,0:T(8,128)(2,1)}, bf16[512,1152]{1,0:T(8,128)(2,1)}, u32[]{:S(2)}, u32[]{:S(2)}) collective-permute-start(bf16[512,1152]{1,0:T(8,128)(2,1)} %bitcast.1), channel_id=1, source_target_pairs={{0,192},{64,0},{128,64},{192,128},{1,193},{65,1},{129,65},{193,129... | collective-permute-start | bytes 3538952 | tf_op jit(solution)/shard_map/ppermute | solution.py:40
  29.6 26.5 %collective-permute-start.2 = (bf16[512,1152]{1,0:T(8,128)(2,1)}, bf16[512,1152]{1,0:T(8,128)(2,1)}, u32[]{:S(2)}, u32[]{:S(2)}) collective-permute-start(bf16[512,1152]{1,0:T(8,128)(2,1)} %bitcast.1), channel_id=1, source_target_pairs={{0,64},{64,128},{128,192},{192,0},{1,65},{65,129},{129,193},{193,1... | collective-permute-start | bytes 3538952 | tf_op jit(solution)/shard_map/ppermute | solution.py:40
  30.1 34.5 %copy-start.1 = (bf16[384,1152]{1,0:T(8,128)(2,1)}, bf16[384,1152]{1,0:T(8,128)(2,1)S(1)}, u32[]{:S(2)}) copy-start(bf16[384,1152]{1,0:T(8,128)(2,1)S(1)} %shard_map.67.refs_5_) | copy-start | bytes 2654212
  30.1 31.1 %collective-permute-start.8 = (bf16[384,1152]{1,0:T(8,128)(2,1)S(1)}, bf16[384,1152]{1,0:T(8,128)(2,1)S(1)}, u32[]{:S(2)}, u32[]{:S(2)}) collective-permute-start(bf16[384,1152]{1,0:T(8,128)(2,1)S(1)} %shard_map.67.refs_5_), channel_id=1, source_target_pairs={{0,1},{1,2},{2,3},{3,0},{4,5},{5,6},{6,7},{7,4},{8,9},{9,10},{10,1... | collective-permute-start | bytes 2654216 | tf_op jit(solution)/shard_map/ppermute | solution.py:40
  31.4 32.1 %collective-permute-start.7 = (bf16[384,1152]{1,0:T(8,128)(2,1)S(1)}, bf16[384,1152]{1,0:T(8,128)(2,1)}, u32[]{:S(2)}, u32[]{:S(2)}) collective-permute-start(bf16[384,1152]{1,0:T(8,128)(2,1)S(1)} %shard_map.67.refs_5_), channel_id=1, source_target_pairs={{0,3},{1,0},{2,1},{3,2},{4,7},{5,4},{6,5},{7,6},{8,11},{9,8},{10,9... | collective-permute-start | bytes 2654216 | tf_op jit(solution)/shard_map/ppermute | solution.py:40
  44.6 0.6 copy-start.3
  58.5 15.6 %collective-permute-start.4 = (bf16[256,1152]{1,0:T(8,128)(2,1)S(1)}, bf16[256,1152]{1,0:T(8,128)(2,1)S(1)}, u32[]{:S(2)}, u32[]{:S(2)}) collective-permute-start(bf16[256,1152]{1,0:T(8,128)(2,1)S(1)} %slice.16), channel_id=1, source_target_pairs={{0,64},{64,128},{128,192},{192,0},{1,65},{65,129},{129,193},{193,1... | collective-permute-start | bytes 1769480 | tf_op jit(solution)/shard_map/ppermute | solution.py:40
  58.5 16.3 %collective-permute-start.5 = (bf16[256,1152]{1,0:T(8,128)(2,1)S(1)}, bf16[256,1152]{1,0:T(8,128)(2,1)}, u32[]{:S(2)}, u32[]{:S(2)}) collective-permute-start(bf16[256,1152]{1,0:T(8,128)(2,1)S(1)} %slice.17), channel_id=1, source_target_pairs={{0,192},{64,0},{128,64},{192,128},{1,193},{65,1},{129,65},{193,129... | collective-permute-start | bytes 1769480 | tf_op jit(solution)/shard_map/ppermute | solution.py:40
  61.2 18.0 %copy-start.7 = (bf16[384,1152]{1,0:T(8,128)(2,1)}, bf16[384,1152]{1,0:T(8,128)(2,1)S(1)}, u32[]{:S(2)}) copy-start(bf16[384,1152]{1,0:T(8,128)(2,1)S(1)} %collective-permute-done.8.refs_9_) | copy-start | bytes 2654212
  61.3 11.9 %collective-permute-start.9 = (bf16[192,1152]{1,0:T(8,128)(2,1)S(1)}, bf16[192,1152]{1,0:T(8,128)(2,1)S(1)}, u32[]{:S(2)}, u32[]{:S(2)}) collective-permute-start(bf16[192,1152]{1,0:T(8,128)(2,1)S(1)} %slice.23), channel_id=1, source_target_pairs={{0,1},{1,2},{2,3},{3,0},{4,5},{5,6},{6,7},{7,4},{8,9},{9,10},{10,1... | collective-permute-start | bytes 1327112 | tf_op jit(solution)/shard_map/ppermute | solution.py:40
  64.6 9.4 %collective-permute-start.10 = (bf16[192,1152]{1,0:T(8,128)(2,1)S(1)}, bf16[192,1152]{1,0:T(8,128)(2,1)S(1)}, u32[]{:S(2)}, u32[]{:S(2)}) collective-permute-start(bf16[192,1152]{1,0:T(8,128)(2,1)S(1)} %slice.24), channel_id=1, source_target_pairs={{0,3},{1,0},{2,1},{3,2},{4,7},{5,4},{6,5},{7,6},{8,11},{9,8},{10,9... | collective-permute-start | bytes 1327112 | tf_op jit(solution)/shard_map/ppermute | solution.py:40
  73.1 0.9 copy-start.9
  74.0 0.8 copy-start.10
  74.8 4.4 %copy-start.8 = (bf16[256,1152]{1,0:T(8,128)(2,1)}, bf16[256,1152]{1,0:T(8,128)(2,1)S(1)}, u32[]{:S(2)}) copy-start(bf16[256,1152]{1,0:T(8,128)(2,1)S(1)} %collective-permute-done.4.refs_2_) | copy-start | bytes 1769476
  90.1 46.8 %copy-start.4 = (s32[640]{0:T(1024)S(1)}, s32[640]{0:T(1024)}, u32[]{:S(2)}) copy-start(s32[640]{0:T(1024)} %copy-done.3) | copy-start | bytes 7684
  130.3 6.6 %collective-permute-start.11 = (bf16[32,64,128]{2,1,0:T(8,128)(2,1)S(1)}, bf16[32,64,128]{2,1,0:T(8,128)(2,1)S(1)}, u32[]{:S(2)}, u32[]{:S(2)}) collective-permute-start(bf16[32,64,128]{2,1,0:T(8,128)(2,1)S(1)} %bitcast.58), channel_id=1, source_target_pairs={{0,4},{4,0},{1,5},{5,1},{2,6},{6,2},{3,7},{7,3},{8,12},{12,8},{9,1... | collective-permute-start | bytes 1572872 | tf_op jit(solution)/shard_map/ppermute | solution.py:40
Sparse Core Ops, SparseCore 0:
  9.2 69.9 all-gather.1
